TPU v7x, 256 devices: a whole 4x4x8 slice. The times are simulated.
256 devices in a mesh: dp: 16 (over x, y), zero: 16 (over z, core).
Axes of the slice: x: 4, y: 4, z: 8, core: 2. Of those that a mesh axis runs over, the one named last changes fastest.
Arguments:
- frames: bfloat16 [16, 16, 768, 1536], P('dp', 'zero')
- segments: int32 [16, 16, 768], P('dp', 'zero'), may hold values from 0 to 2, never falling along the last dimension, each value on 1 to 384 neighbouring positions
- targets: int32 [16, 16, 12], P('dp', 'zero'), may hold values from -1 to 15, as said below
- cotangent: bfloat16 [16, 16, 512, 1536], P('dp', 'zero'), may hold values from -6 to 6
- w_out: bfloat16 [1536, 1536], P(None, 'zero'), may hold values from -0.15625 to 0.15625
- kernel: bfloat16 [32, 1536], P(None, 'zero'), may hold values from -1 to 1
- norm_params: bfloat16 [2, 1536], P(None, 'zero'), may hold values from 0.29882812 to 1.5
Outputs:
- module_out: bfloat16 [16, 16, 512, 1536], P('dp', 'zero')
- grad_out_weight: float32 [1536, 1536], P(None, 'zero')
- grad_kernel: float32 [32, 1536], P(None, 'zero')
- grad_norm: float32 [2, 1536], P(None, 'zero')
Inputs may be any that keep to these rules, and one draw needn't show every extreme that they name: `targets`: within each device's slots the padding blocks come after the live ones. For each zero index, counting the live blocks in order of dp index and then block, the n-th goes to data group n mod 16; every data group receives exactly 8 blocks; a device sends at most 1 block to one data group.
All inputs are finite; a program needn't handle non-finite values.
Results may differ from a plain program's by a relative error of at most 0.005.
Values may be sent and summed in bfloat16 or wider, within the bound.
No kernel may reach another device: no remote copies, remote signals or barrier semaphores. Data moves between devices by JAX's collectives and lax.ppermute only.
A program may use at most 128 MiB of HBM per device.

v0:
```python
import jax
import jax.numpy as jnp
from jax import lax
from jax.experimental import pallas as pl
from jax.experimental.pallas import tpu as pltpu
from jax.sharding import PartitionSpec as P

KER = 32
BLOCK = 64
BLOCKS = 8
NB = 12
LEFT = 16
WIN = 96
CHUNK = 32
LANES = 128
EPS = 1e-05
F32 = jnp.float32
BF16 = jnp.bfloat16
SMEM_SPEC = pl.BlockSpec(memory_space=pltpu.SMEM)


def row_iota(rows):
    return lax.broadcasted_iota(jnp.int32, (rows, LANES), 0)


def spread_taps(kern_ref, taps):
    for k in range(KER):
        taps[pl.ds(8 * k, 8), :] = jnp.broadcast_to(kern_ref[pl.ds(k, 1), :], (8, LANES))


def shifted(window, p):
    return [window[pl.ds(p + 8 * i, 8), :] for i in range(7)]


def conv_chunk(window, taps):
    acc = [jnp.zeros((8, LANES), F32) for _ in range(4)]
    for p in range(8):
        xs = shifted(window, p)
        for q in range(4):
            tap = taps[pl.ds(8 * (8 * q + p), 8), :]
            for i in range(4):
                acc[i] = acc[i] + tap * xs[i + q]
    return acc


def pack_kernel(block_ref, x_ref, out_ref, sems):
    def copies(r):
        b = block_ref[r]
        before = pl.multiple_of(jnp.maximum(b * BLOCK - LEFT, 0), 16)
        start = pl.multiple_of(b * BLOCK, 16)
        after = pl.multiple_of(jnp.minimum((b + 1) * BLOCK, NB * BLOCK - 16), 16)
        return [
            pltpu.make_async_copy(
                x_ref.at[pl.ds(before, 16)], out_ref.at[r, pl.ds(0, 16)], sems.at[r, 0]
            ),
            pltpu.make_async_copy(
                x_ref.at[pl.ds(start, 64)], out_ref.at[r, pl.ds(16, 64)], sems.at[r, 1]
            ),
            pltpu.make_async_copy(
                x_ref.at[pl.ds(after, 16)], out_ref.at[r, pl.ds(80, 16)], sems.at[r, 2]
            ),
        ]

    for r in range(16):
        @pl.when(block_ref[r] >= 0)
        def _():
            for copy in copies(r):
                copy.start()

    for r in range(16):
        @pl.when(block_ref[r] >= 0)
        def _():
            for copy in copies(r):
                copy.wait()


def pack(block_of, x):
    return pl.pallas_call(
        pack_kernel,
        out_shape=jax.ShapeDtypeStruct((16, WIN, x.shape[1]), BF16),
        in_specs=[SMEM_SPEC, pl.BlockSpec(memory_space=pl.ANY)],
        out_specs=pl.BlockSpec(memory_space=pl.ANY),
        scratch_shapes=[pltpu.SemaphoreType.DMA((16, 3))],
        name="pack",
    )(block_of, x)


def stats_kernel(bounds_ref, x_ref, kern_ref, out_ref, full, window, taps, sums):
    spread_taps(kern_ref, taps)
    full[pl.ds(0, 16), :] = jnp.zeros((16, LANES), F32)
    full[pl.ds(16 + NB * BLOCK, 16), :] = jnp.zeros((16, LANES), F32)
    full[pl.ds(16, NB * BLOCK), :] = x_ref[...].astype(F32)
    sums[...] = jnp.zeros_like(sums)
    first, second, end = bounds_ref[1], bounds_ref[2], bounds_ref[3]

    def chunk(c, carry):
        row = c * CHUNK
        low = (first <= row).astype(jnp.int32) + (second <= row).astype(jnp.int32)
        top = row + CHUNK - 1
        high = (first <= top).astype(jnp.int32) + (second <= top).astype(jnp.int32)

        def part(u, inner):
            begin, stop = bounds_ref[u], bounds_ref[u + 1]
            rows = row_iota(64) + (row - LEFT)
            source = full[pl.ds(pl.multiple_of(row, 32), 64), :]
            window[...] = jnp.where((rows >= begin) & (rows < stop), source, 0.0)
            acc = conv_chunk(window, taps)
            total, square = sums[pl.ds(0, 8), :], sums[pl.ds(8, 8), :]
            for i in range(4):
                at = row_iota(8) + (row + 8 * i)
                h = jnp.where((at >= begin) & (at < stop), acc[i], 0.0)
                total = total + h
                square = square + h * h
            sums[pl.ds(0, 8), :] = total
            sums[pl.ds(8, 8), :] = square
            return inner

        return lax.fori_loop(low, high + 1, part, carry)

    lax.fori_loop(0, end // CHUNK, chunk, 0)
    out_ref[pl.ds(0, 1), :] = jnp.sum(sums[pl.ds(0, 8), :], axis=0, keepdims=True)
    out_ref[pl.ds(1, 1), :] = jnp.sum(sums[pl.ds(8, 8), :], axis=0, keepdims=True)


def stats(bounds, x, kern):
    width = x.shape[1]
    return pl.pallas_call(
        stats_kernel,
        grid=(width // LANES,),
        out_shape=jax.ShapeDtypeStruct((2, width), F32),
        in_specs=[
            SMEM_SPEC,
            pl.BlockSpec((NB * BLOCK, LANES), lambda c: (0, c)),
            pl.BlockSpec((KER, LANES), lambda c: (0, c)),
        ],
        out_specs=pl.BlockSpec((2, LANES), lambda c: (0, c)),
        scratch_shapes=[
            pltpu.VMEM((32 + NB * BLOCK, LANES), F32),
            pltpu.VMEM((64, LANES), F32),
            pltpu.VMEM((8 * KER, LANES), F32),
            pltpu.VMEM((16, LANES), F32),
        ],
        cost_estimate=pl.CostEstimate(flops=100_000_000, bytes_accessed=3_000_000, transcendentals=0),
        name="stats",
    )(bounds, x, kern)


def live_parts(info_ref, got_ref, window, per_part):
    def slot(s, n):
        valid = info_ref[8 * s] > 0

        @pl.when(valid)
        def _():
            for c in range(2):
                row = LEFT + CHUNK * c
                top = row + CHUNK - 1
                first, second = info_ref[8 * s + 2], info_ref[8 * s + 3]
                low = (first <= row).astype(jnp.int32) + (second <= row).astype(jnp.int32)
                high = (first <= top).astype(jnp.int32) + (second <= top).astype(jnp.int32)
                at = pl.multiple_of(n * BLOCK + c * CHUNK, CHUNK)

                def part(u, carry):
                    begin, stop = info_ref[8 * s + 1 + u], info_ref[8 * s + 2 + u]
                    rows = row_iota(64) + CHUNK * c
                    source = got_ref[s, pl.ds(CHUNK * c, 64), :].astype(F32)
                    window[...] = jnp.where((rows >= begin) & (rows < stop), source, 0.0)
                    per_part(row, at, begin, stop)
                    return carry

                lax.fori_loop(low, high + 1, part, 0)

        return n + valid.astype(jnp.int32)

    lax.fori_loop(0, 16, slot, 0)


def hidden_kernel(info_ref, got_ref, kern_ref, h_ref, window, taps):
    spread_taps(kern_ref, taps)

    def per_part(row, at, begin, stop):
        acc = conv_chunk(window, taps)
        for i in range(4):
            rows = row_iota(8) + (row + 8 * i)
            place = pl.ds(pl.multiple_of(at + 8 * i, 8), 8)
            h_ref[place, :] = jnp.where((rows >= begin) & (rows < stop), acc[i], h_ref[place, :])

    live_parts(info_ref, got_ref, window, per_part)


def hidden(info, got, kern):
    width = got.shape[2]
    return pl.pallas_call(
        hidden_kernel,
        grid=(width // LANES,),
        out_shape=jax.ShapeDtypeStruct((BLOCKS * BLOCK, width), F32),
        in_specs=[
            SMEM_SPEC,
            pl.BlockSpec((16, WIN, LANES), lambda c: (0, 0, c)),
            pl.BlockSpec((KER, LANES), lambda c: (0, c)),
        ],
        out_specs=pl.BlockSpec((BLOCKS * BLOCK, LANES), lambda c: (0, c)),
        scratch_shapes=[pltpu.VMEM((64, LANES), F32), pltpu.VMEM((8 * KER, LANES), F32)],
        cost_estimate=pl.CostEstimate(flops=60_000_000, bytes_accessed=8_000_000, transcendentals=0),
        name="hidden",
    )(info, got, kern)


def terms_kernel(info_ref, got_ref, h_ref, back_ref, norm_ref, out_ref, window, acc_a, acc_x, sums):
    acc_a[...] = jnp.zeros_like(acc_a)
    acc_x[...] = jnp.zeros_like(acc_x)
    sums[...] = jnp.zeros_like(sums)
    mean, inverse = norm_ref[pl.ds(0, 1), :], norm_ref[pl.ds(1, 1), :]
    scale, shift = norm_ref[pl.ds(2, 1), :], norm_ref[pl.ds(3, 1), :]

    def per_part(row, at, begin, stop):
        das, hats = [], []
        sum_x, sum_1 = sums[pl.ds(0, 8), :], sums[pl.ds(8, 8), :]
        for i in range(4):
            place = pl.ds(pl.multiple_of(at + 8 * i, 8), 8)
            rows = row_iota(8) + (row + 8 * i)
            keep = (rows >= begin) & (rows < stop)
            hat = (h_ref[place, :] - mean) * inverse
            a = hat * scale + shift
            sig = jax.nn.sigmoid(a)
            da = back_ref[place, :] * (sig * (1.0 + a * (1.0 - sig)))
            da = jnp.where(keep, da, 0.0)
            hat = jnp.where(keep, hat, 0.0)
            sum_x = sum_x + da * hat
            sum_1 = sum_1 + da
            das.append(da)
            hats.append(hat)
        sums[pl.ds(0, 8), :] = sum_x
        sums[pl.ds(8, 8), :] = sum_1
        for p in range(8):
            xs = shifted(window, p)
            for q in range(4):
                place = pl.ds(8 * (8 * q + p), 8)
                acc_a[place, :] += (das[0] * xs[q] + das[1] * xs[q + 1]) + (
                    das[2] * xs[q + 2] + das[3] * xs[q + 3]
                )
                acc_x[place, :] += (hats[0] * xs[q] + hats[1] * xs[q + 1]) + (
                    hats[2] * xs[q + 2] + hats[3] * xs[q + 3]
                )

    live_parts(info_ref, got_ref, window, per_part)
    out_ref[pl.ds(0, 32), :] = jnp.sum(acc_a[...].reshape(KER, 8, LANES), axis=1)
    out_ref[pl.ds(32, 32), :] = jnp.sum(acc_x[...].reshape(KER, 8, LANES), axis=1)
    out_ref[pl.ds(64, 1), :] = jnp.sum(sums[pl.ds(0, 8), :], axis=0, keepdims=True)
    out_ref[pl.ds(65, 1), :] = jnp.sum(sums[pl.ds(8, 8), :], axis=0, keepdims=True)
    out_ref[pl.ds(66, 6), :] = jnp.zeros((6, LANES), F32)


def terms(info, got, h, back, norm):
    width = got.shape[2]
    return pl.pallas_call(
        terms_kernel,
        grid=(width // LANES,),
        out_shape=jax.ShapeDtypeStruct((72, width), F32),
        in_specs=[
            SMEM_SPEC,
            pl.BlockSpec((16, WIN, LANES), lambda c: (0, 0, c)),
            pl.BlockSpec((BLOCKS * BLOCK, LANES), lambda c: (0, c)),
            pl.BlockSpec((BLOCKS * BLOCK, LANES), lambda c: (0, c)),
            pl.BlockSpec((4, LANES), lambda c: (0, c)),
        ],
        out_specs=pl.BlockSpec((72, LANES), lambda c: (0, c)),
        scratch_shapes=[
            pltpu.VMEM((64, LANES), F32),
            pltpu.VMEM((8 * KER, LANES), F32),
            pltpu.VMEM((8 * KER, LANES), F32),
            pltpu.VMEM((16, LANES), F32),
        ],
        cost_estimate=pl.CostEstimate(
            flops=110_000_000, bytes_accessed=12_000_000, transcendentals=800_000
        ),
        name="terms",
    )(info, got, h, back, norm)


def gather_sum(x, axis):
    copies = jnp.broadcast_to(x[None], (16,) + x.shape)
    return jnp.sum(lax.all_to_all(copies, axis, 0, 0, tiled=True), axis=0)


def per_device(frames, segments, targets, cotangent, w_out, kernel, norm_params):
    x, seg, target_row, cot = frames[0, 0], segments[0, 0], targets[0, 0], cotangent[0, 0]
    width = x.shape[1]
    share = width // 16
    zero_id = lax.axis_index("zero")
    core = lax.rem(zero_id, 2)

    groups = jnp.arange(16, dtype=jnp.int32)
    hit = target_row[None, :] == groups[:, None]
    valid = jnp.any(hit, axis=1)
    block_of = jnp.sum(jnp.where(hit, jnp.arange(NB, dtype=jnp.int32)[None, :], 0), axis=1)
    end = BLOCK * jnp.sum((target_row >= 0).astype(jnp.int32))
    ends = [jnp.minimum(jnp.sum((seg < u).astype(jnp.int32)), end) for u in (1, 2)]
    bounds = jnp.stack([jnp.int32(0), ends[0], ends[1], end])
    base = BLOCK * block_of - LEFT
    info = jnp.clip(bounds[None, :] - base[:, None], 0, WIN)
    info = jnp.concatenate(
        [valid.astype(jnp.int32)[:, None], info, jnp.zeros((16, 3), jnp.int32)], axis=1
    )

    small = jnp.concatenate([kernel, norm_params, jnp.zeros((14, share), BF16)], axis=0)
    small_full = lax.all_to_all(
        jnp.broadcast_to(small[None], (16,) + small.shape), "zero", 0, 0, tiled=True
    )
    small_full = jnp.transpose(small_full, (1, 0, 2)).reshape(48, width).astype(F32)
    kern_full = small_full[:KER]
    info = lax.all_to_all(info, "dp", 0, 0, tiled=True).reshape(128)

    send = pack(jnp.where(valid, block_of, -1), x)
    got = lax.all_to_all(send, "dp", 0, 0, tiled=True)

    w_t = lax.all_gather(w_out.T, "zero", axis=0, tiled=True)

    sums = stats(bounds, x, kern_full)
    sums = gather_sum(gather_sum(sums, "zero"), "dp")
    frame_count = jnp.float32(BLOCKS * BLOCK * 256)
    mean = sums[0] / frame_count
    var = sums[1] / frame_count - mean * mean
    inverse = lax.rsqrt(var + EPS)
    norm = jnp.stack([mean, inverse, small_full[KER], small_full[KER + 1]])

    label = jnp.where(jnp.arange(NB * BLOCK) < end, seg, -1)
    padded = jnp.pad(label, (KER - 1 - LEFT, LEFT), constant_values=-1)
    meets = jnp.stack(
        [
            (padded[KER - 1 - k : KER - 1 - k + NB * BLOCK] == label) & (label >= 0)
            for k in range(KER)
        ]
    )
    x_sums = jnp.dot(meets.astype(BF16), x, preferred_element_type=F32)

    halves = cot.reshape(BLOCKS * BLOCK, 8, 2, share)
    cot_own = lax.dynamic_index_in_dim(halves, core, 2, False).reshape(-1, width // 2)
    cot_send = lax.dynamic_index_in_dim(halves, 1 - core, 2, False).reshape(-1, width // 2)
    swap = [(i, i ^ 1) for i in range(16)]
    cot_other = lax.ppermute(cot_send, "zero", swap)
    back = jnp.dot(cot, w_t, preferred_element_type=F32)

    h = hidden(info, got, kern_full)
    a = (h - mean) * inverse * norm[2] + norm[3]
    sw = (a * jax.nn.sigmoid(a)).astype(BF16)
    sw_other = lax.ppermute(sw, "zero", swap)
    contract = (((0,), (0,)), ((), ()))
    term = lax.dot_general(sw, cot_own, contract, preferred_element_type=F32)
    term = term + lax.dot_general(sw_other, cot_other, contract, preferred_element_type=F32)
    term = term.astype(BF16).reshape(16, share, width // 2)
    term = lax.all_to_all(term, "dp", 0, 0, tiled=True)

    grads = terms(info, got, h, back, norm)
    out = lax.dot_general(
        sw, w_t, (((1,), (1,)), ((), ())), preferred_element_type=F32
    ).astype(BF16)

    grads = jnp.concatenate([grads, x_sums], axis=0)
    grads = jnp.transpose(grads.reshape(104, 16, share), (1, 0, 2))
    grads = jnp.sum(lax.all_to_all(grads, "zero", 0, 0, tiled=True), axis=0)

    term = jnp.sum(term.astype(F32), axis=0)
    term = jnp.transpose(term.reshape(share, 8, share), (1, 0, 2))
    term = lax.all_to_all(
        term,
        "zero",
        0,
        0,
        axis_index_groups=[[i for i in range(16) if i % 2 == c] for c in range(2)],
        tiled=True,
    )
    term = jnp.sum(term, axis=0)

    last = jnp.concatenate([term, grads], axis=0)
    last = lax.all_to_all(
        jnp.broadcast_to(last[None], (16,) + last.shape), "dp", 0, 0, tiled=True
    )
    part_w = last[:, :share].reshape(width, share)
    grads = jnp.sum(last[:, share:], axis=0)

    own = lax.dynamic_slice_in_dim(norm, zero_id * share, share, 1)
    da_x, hat_x, x_k = grads[:KER], grads[KER : 2 * KER], grads[72 : 72 + KER]
    sum_x, sum_1 = grads[64], grads[65]
    part_k = (own[2] * own[1]) * (da_x - (sum_1 / frame_count) * x_k - (sum_x / frame_count) * hat_x)
    return out[None, None], part_w, part_k, jnp.stack([sum_x, sum_1])


def solution(mesh):
    return jax.shard_map(
        per_device,
        mesh=mesh,
        in_specs=(
            P("dp", "zero", None, None),
            P("dp", "zero", None),
            P("dp", "zero", None),
            P("dp", "zero", None, None),
            P(None, "zero"),
            P(None, "zero"),
            P(None, "zero"),
        ),
        out_specs=(P("dp", "zero", None, None), P(None, "zero"), P(None, "zero"), P(None, "zero")),
        check_vma=False,
    )
```

profile of v0, /device:TPU:8, one launch (start us, length us, event | category | flops | bytes accessed | tf_op | source)
XLA Modules:
  0.0 451.4 jit_solution(3904374452556932485)
XLA Ops:
  7.3 0.8 maximum_maximum_fusion
  8.0 0.7 broadcast_in_dim.70
  8.7 8.6 %all-to-all-start.2 = ((bf16[16,48,96]{2,1,0:T(8,128)(2,1)}), bf16[16,48,96]{2,1,0:T(8,128)(2,1)S(1)}, u32[]{:S(2)}, u32[]{:S(2)}) async-start(bf16[16,48,96]{2,1,0:T(8,128)(2,1)} %broadcast_in_dim.70), calls=%async_computation.2 | async-start | bytes 393216 | tf_op jit(solution)/shard_map/all_to_all | solution.py:306
  17.3 1.3 fusion.43
  18.6 0.8 fusion.8
  19.4 0.8 select_reduce_fusion
  20.8 0.7 reduce
  21.5 0.6 convert_reduce_fusion.2
  23.5 0.5 broadcast_select_fusion
  24.2 3.1 all-to-all-done.2
  27.3 0.2 copy.49
  27.5 0.8 slice.149.kern_ref
  28.3 16.6 %stats.1 = f32[2,1536]{1,0:T(2,128)} custom-call(s32[4]{0:T(128)} %copy-done.6, bf16[768,1536]{1,0:T(8,128)(2,1)} %bitcast.40, f32[32,1536]{1,0:T(8,128)} %slice.149.kern_ref), custom_call_target="tpu_custom_call" | custom-call | flops 100000000 | bytes 3000000 | tf_op jit(solution)/shard_map/stats/pallas_call | solution.py:127
  44.9 1.4 broadcast_in_dim.71
  46.4 7.7 %all-to-all-start.3 = ((f32[16,2,1536]{2,1,0:T(2,128)}), f32[16,2,1536]{2,1,0:T(2,128)S(1)}, u32[]{:S(2)}, u32[]{:S(2)}) async-start(f32[16,2,1536]{2,1,0:T(2,128)} %broadcast_in_dim.71), calls=%async_computation.3 | async-start | bytes 393216 | tf_op jit(solution)/shard_map/all_to_all | solution.py:282
  54.1 0.7 copy.48
  54.8 9.2 %all-to-all-done.3 = f32[16,2,1536]{2,1,0:T(2,128)S(1)} async-done(((f32[16,2,1536]{2,1,0:T(2,128)}), f32[16,2,1536]{2,1,0:T(2,128)S(1)}, u32[]{:S(2)}, u32[]{:S(2)}) %all-to-all-start.3) | async-done | bytes 196640 | tf_op jit(solution)/shard_map/all_to_all | solution.py:282
  64.0 8.8 %all-to-all-start = ((s32[16,1,8]{2,1,0:T(1,128)}), s32[16,1,8]{2,1,0:T(1,128)S(1)}, u32[]{:S(2)}, u32[]{:S(2)}) async-start(s32[16,1,8]{2,1,0:T(1,128)} %copy.48), calls=%async_computation | async-start | bytes 16384 | tf_op jit(solution)/shard_map/all_to_all | solution.py:311
  72.9 6.0 %all-to-all-done = s32[16,1,8]{2,1,0:T(1,128)S(1)} async-done(((s32[16,1,8]{2,1,0:T(1,128)}), s32[16,1,8]{2,1,0:T(1,128)S(1)}, u32[]{:S(2)}, u32[]{:S(2)}) %all-to-all-start) | async-done | bytes 544 | tf_op jit(solution)/shard_map/all_to_all | solution.py:311
  78.9 0.7 broadcast_in_dim.72
  79.7 4.8 %all-to-all-start.4 = ((f32[16,2,1536]{2,1,0:T(2,128)}), f32[16,2,1536]{2,1,0:T(2,128)S(1)}, u32[]{:S(2)}, u32[]{:S(2)}) async-start(f32[16,2,1536]{2,1,0:T(2,128)} %broadcast_in_dim.72), calls=%async_computation.4 | async-start | bytes 393216 | tf_op jit(solution)/shard_map/all_to_all | solution.py:282
  84.5 82.6 %pack.1 = bf16[16,96,1536]{2,1,0:T(8,128)(2,1)} custom-call(s32[16]{0:T(128)} %get-tuple-element.66.block_ref, bf16[768,1536]{1,0:T(8,128)(2,1)} %bitcast.41), custom_call_target="tpu_custom_call" | custom-call | tf_op jit(solution)/shard_map/pack/pallas_call | solution.py:78
  167.1 31.7 %all-to-all-start.1 = ((bf16[16,96,1536]{2,1,0:T(8,128)(2,1)}), bf16[16,96,1536]{2,1,0:T(8,128)(2,1)}, u32[]{:S(2)}, u32[]{:S(2)}) async-start(bf16[16,96,1536]{2,1,0:T(8,128)(2,1)} %pack.1), calls=%async_computation.1 | async-start | bytes 9437184 | tf_op jit(solution)/shard_map/all_to_all | solution.py:314
  198.8 0.7 all-gather.2.cloned.1.call-update
  199.5 0.5 broadcast.174
  200.0 0.7 reduce.19
  200.7 0.6 reshape.81.info_ref
  201.5 0.6 slice_multiply_fusion.5
  202.2 55.7 %all-to-all-done.1.got_ref = bf16[16,96,1536]{2,1,0:T(8,128)(2,1)} async-done(((bf16[16,96,1536]{2,1,0:T(8,128)(2,1)}), bf16[16,96,1536]{2,1,0:T(8,128)(2,1)}, u32[]{:S(2)}, u32[]{:S(2)}) %all-to-all-start.1) | async-done | bytes 4718624 | tf_op jit(solution)/shard_map/all_to_all | solution.py:314
  257.9 15.6 %hidden.1.h_ref = f32[512,1536]{1,0:T(8,128)} custom-call(s32[128]{0:T(128)} %reshape.81.info_ref, bf16[16,96,1536]{2,1,0:T(8,128)(2,1)} %all-to-all-done.1.got_ref, f32[32,1536]{1,0:T(8,128)} %slice.149.kern_ref), custom_call_target="tpu_custom_call" | custom-call | flops 60000000 | bytes 8000000 | tf_op jit(solution)/shard_map/hidden/pallas_call | solution.py:192
  273.4 2.9 multiply_convert_fusion
  276.4 2.2 copy.52
  278.7 0.1 collective-permute-start.1
  278.8 1.4 fusion.48
  280.3 0.8 collective-permute-done.1
  281.1 4.3 add_convert_fusion
  285.4 10.1 %all-to-all-start.5 = ((bf16[16,96,768]{2,1,0:T(8,128)(2,1)}), bf16[16,96,768]{2,1,0:T(8,128)(2,1)}, u32[]{:S(2)}, u32[]{:S(2)}) async-start(bf16[16,96,768]{2,1,0:T(8,128)(2,1)} %bitcast.42), calls=%async_computation.5 | async-start | bytes 4718592 | tf_op jit(solution)/shard_map/all_to_all | solution.py:351
  296.3 0.9 stack.153
  297.2 0.5 fusion.44
  297.8 0.6 pad_maximum_fusion.2.norm_ref
  298.5 29.7 %all-to-all-done.5 = bf16[16,96,768]{2,1,0:T(8,128)(2,1)} async-done(((bf16[16,96,768]{2,1,0:T(8,128)(2,1)}), bf16[16,96,768]{2,1,0:T(8,128)(2,1)}, u32[]{:S(2)}, u32[]{:S(2)}) %all-to-all-start.5) | async-done | bytes 2359328 | tf_op jit(solution)/shard_map/all_to_all | solution.py:351
  328.1 2.0 convert_reduce_fusion
  330.2 0.2 reshape.85
  330.4 0.8 copy.53
  331.2 15.9 %all-to-all-start.6 = ((f32[8,96,96]{2,1,0:T(8,128)}), f32[8,96,96]{2,1,0:T(8,128)S(1)}, u32[]{:S(2)}, u32[]{:S(2)}) async-start(f32[8,96,96]{2,1,0:T(8,128)} %copy.53), calls=%async_computation.6 | async-start | bytes 786432 | tf_op jit(solution)/shard_map/all_to_all | solution.py:364
  347.1 6.6 %fusion.1.back_ref = f32[512,1536]{1,0:T(8,128)} fusion(bf16[1536,1536]{1,0:T(8,128)(2,1)} %all-gather.2.cloned.1.call-done, bf16[1,1,512,1536]{3,2,1,0:T(8,128)(2,1)S(1)} %copy-done.3), kind=kOutput, calls=%fused_computation.5 | convolution fusion | flops 2415919104 | bytes 9437184 | tf_op jit(solution)/shard_map/dot_general | solution.py:341
  353.7 24.7 %terms.1 = f32[72,1536]{1,0:T(8,128)} custom-call(s32[128]{0:T(128)} %reshape.81.info_ref, bf16[16,96,1536]{2,1,0:T(8,128)(2,1)} %all-to-all-done.1.got_ref, f32[512,1536]{1,0:T(8,128)} %hidden.1.h_ref, f32[512,1536]{1,0:T(8,128)} %fusion.1.back_ref, f32[4,1536]{1,0:T(4,128)} %pad_maximum_fusion.2.norm_ref), custom_call_target="tpu_custom_call" | custom-call | flops 110000000 | bytes 12000000 | tf_op jit(solution)/shard_map/terms/pallas_call | solution.py:255
  378.4 1.1 pad_maximum_fusion
  379.5 0.3 reshape.86
  379.8 1.3 copy.55
  381.0 9.5 %all-to-all-start.7 = ((f32[16,104,96]{1,2,0:T(8,128)}), f32[16,104,96]{1,2,0:T(8,128)S(1)}, u32[]{:S(2)}, u32[]{:S(2)}) async-start(f32[16,104,96]{1,2,0:T(8,128)} %copy.55), calls=%async_computation.7 | async-start | bytes 1572864 | tf_op jit(solution)/shard_map/all_to_all | solution.py:360
  390.6 20.6 %all-to-all-done.7 = f32[16,104,96]{1,2,0:T(8,128)S(1)} async-done(((f32[16,104,96]{1,2,0:T(8,128)}), f32[16,104,96]{1,2,0:T(8,128)S(1)}, u32[]{:S(2)}, u32[]{:S(2)}) %all-to-all-start.7) | async-done | bytes 639008 | tf_op jit(solution)/shard_map/all_to_all | solution.py:360
  411.5 1.3 broadcast_in_dim.76
  412.8 6.3 %all-to-all-start.8 = ((f32[16,200,96]{1,2,0:T(8,128)}), f32[16,200,96]{1,2,0:T(8,128)S(1)}, u32[]{:S(2)}, u32[]{:S(2)}) async-start(f32[16,200,96]{1,2,0:T(8,128)} %broadcast_in_dim.76), calls=%async_computation.8 | async-start | bytes 3145728 | tf_op jit(solution)/shard_map/all_to_all | solution.py:375
  419.1 0.7 constant_dynamic-slice_fusion
  419.8 6.1 %fusion = bf16[1,1,512,1536]{3,2,1,0:T(8,128)(2,1)} fusion(bf16[512,1536]{1,0:T(8,128)(2,1)S(1)} %copy-done.2, bf16[1536,1536]{1,0:T(8,128)(2,1)} %all-gather.2.cloned.1.call-done), kind=kOutput, calls=%fused_computation.4 | convolution fusion | flops 2416705536 | bytes 7864320 | tf_op jit(solution)/shard_map/dot_general | solution.py:354
  425.9 15.0 %all-to-all-done.8 = f32[16,200,96]{1,2,0:T(8,128)S(1)} async-done(((f32[16,200,96]{1,2,0:T(8,128)}), f32[16,200,96]{1,2,0:T(8,128)S(1)}, u32[]{:S(2)}, u32[]{:S(2)}) %all-to-all-start.8) | async-done | bytes 1228832 | tf_op jit(solution)/shard_map/all_to_all | solution.py:375
  440.9 0.3 slice_reduce_fusion
  441.1 0.2 fusion.7
  441.4 0.1 fusion.4
  441.6 0.7 copy.60
  442.3 0.5 copy.58
  442.8 1.1 reshape.87
  443.9 0.6 copy.61
  (83 shorter events, 2.1 us)
Async XLA Ops:
  8.7 18.5 %all-to-all-start.2 = ((bf16[16,48,96]{2,1,0:T(8,128)(2,1)}), bf16[16,48,96]{2,1,0:T(8,128)(2,1)S(1)}, u32[]{:S(2)}, u32[]{:S(2)}) async-start(bf16[16,48,96]{2,1,0:T(8,128)(2,1)} %broadcast_in_dim.70), calls=%async_computation.2 | async-start | bytes 393216 | tf_op jit(solution)/shard_map/all_to_all | solution.py:306
  24.1 4.3 copy-start.6
  46.4 17.7 %all-to-all-start.3 = ((f32[16,2,1536]{2,1,0:T(2,128)}), f32[16,2,1536]{2,1,0:T(2,128)S(1)}, u32[]{:S(2)}, u32[]{:S(2)}) async-start(f32[16,2,1536]{2,1,0:T(2,128)} %broadcast_in_dim.71), calls=%async_computation.3 | async-start | bytes 393216 | tf_op jit(solution)/shard_map/all_to_all | solution.py:282
  64.0 14.9 %all-to-all-start = ((s32[16,1,8]{2,1,0:T(1,128)}), s32[16,1,8]{2,1,0:T(1,128)S(1)}, u32[]{:S(2)}, u32[]{:S(2)}) async-start(s32[16,1,8]{2,1,0:T(1,128)} %copy.48), calls=%async_computation | async-start | bytes 16384 | tf_op jit(solution)/shard_map/all_to_all | solution.py:311
  79.7 87.4 %all-to-all-start.4 = ((f32[16,2,1536]{2,1,0:T(2,128)}), f32[16,2,1536]{2,1,0:T(2,128)S(1)}, u32[]{:S(2)}, u32[]{:S(2)}) async-start(f32[16,2,1536]{2,1,0:T(2,128)} %broadcast_in_dim.72), calls=%async_computation.4 | async-start | bytes 393216 | tf_op jit(solution)/shard_map/all_to_all | solution.py:282
  167.1 90.8 %all-to-all-start.1 = ((bf16[16,96,1536]{2,1,0:T(8,128)(2,1)}), bf16[16,96,1536]{2,1,0:T(8,128)(2,1)}, u32[]{:S(2)}, u32[]{:S(2)}) async-start(bf16[16,96,1536]{2,1,0:T(8,128)(2,1)} %pack.1), calls=%async_computation.1 | async-start | bytes 9437184 | tf_op jit(solution)/shard_map/all_to_all | solution.py:314
  198.7 148.4 %all-gather.2.cloned.1.call-start = ((), (), s32[]{:S(2)}) async-start(), calls=%async_computation.9 | async-start | bytes 5013504 | tf_op jit(solution)/shard_map/all_gather | solution.py:316
  276.3 2.5 copy-start.1
  276.3 4.8 %collective-permute-start = (bf16[512,1536]{1,0:T(8,128)(2,1)S(1)}, bf16[512,1536]{1,0:T(8,128)(2,1)}, u32[]{:S(2)}, u32[]{:S(2)}) collective-permute-start(bf16[512,1536]{1,0:T(8,128)(2,1)S(1)} %multiply_convert_fusion), channel_id=1, source_target_pairs={{0,1},{1,0},{2,3},{3,2},{4,5},{5,4},{6,7},{7,6},{8,9},{9,8},{10,11... | collective-permute-start | bytes 4718600 | tf_op jit(solution)/shard_map/ppermute | solution.py:346
  278.7 2.4 collective-permute-start.1
  285.4 10.9 %copy-start.5 = (s32[1,1,768]{2,1,0:T(1,128)S(1)}, s32[1,1,768]{2,1,0:T(1,128)}, u32[]{:S(2)}) copy-start(s32[1,1,768]{2,1,0:T(1,128)} %param.8) | copy-start | bytes 9220
  285.4 11.8 %copy-start = (bf16[1,1,768,1536]{3,2,1,0:T(8,128)(2,1)S(1)}, bf16[1,1,768,1536]{3,2,1,0:T(8,128)(2,1)}, u32[]{:S(2)}) copy-start(bf16[1,1,768,1536]{3,2,1,0:T(8,128)(2,1)} %param.7) | copy-start | bytes 7077892
  285.4 12.4 %copy-start.4 = (f32[1,1536]{1,0:T(1,128)S(1)}, f32[1,1536]{1,0:T(1,128)}, u32[]{:S(2)}) copy-start(f32[1,1536]{1,0:T(1,128)} %get-tuple-element.33) | copy-start | bytes 18436
  285.4 42.8 %all-to-all-start.5 = ((bf16[16,96,768]{2,1,0:T(8,128)(2,1)}), bf16[16,96,768]{2,1,0:T(8,128)(2,1)}, u32[]{:S(2)}, u32[]{:S(2)}) async-start(bf16[16,96,768]{2,1,0:T(8,128)(2,1)} %bitcast.42), calls=%async_computation.5 | async-start | bytes 4718592 | tf_op jit(solution)/shard_map/all_to_all | solution.py:351
  297.7 49.4 %copy-start.3 = (bf16[1,1,512,1536]{3,2,1,0:T(8,128)(2,1)S(1)}, bf16[1,1,512,1536]{3,2,1,0:T(8,128)(2,1)}, u32[]{:S(2)}) copy-start(bf16[1,1,512,1536]{3,2,1,0:T(8,128)(2,1)} %param.10) | copy-start | bytes 4718596
  331.2 49.8 %all-to-all-start.6 = ((f32[8,96,96]{2,1,0:T(8,128)}), f32[8,96,96]{2,1,0:T(8,128)S(1)}, u32[]{:S(2)}, u32[]{:S(2)}) async-start(f32[8,96,96]{2,1,0:T(8,128)} %copy.53), calls=%async_computation.6 | async-start | bytes 786432 | tf_op jit(solution)/shard_map/all_to_all | solution.py:364
  381.0 30.2 %all-to-all-start.7 = ((f32[16,104,96]{1,2,0:T(8,128)}), f32[16,104,96]{1,2,0:T(8,128)S(1)}, u32[]{:S(2)}, u32[]{:S(2)}) async-start(f32[16,104,96]{1,2,0:T(8,128)} %copy.55), calls=%async_computation.7 | async-start | bytes 1572864 | tf_op jit(solution)/shard_map/all_to_all | solution.py:360
  390.5 29.3 %copy-start.2 = (bf16[512,1536]{1,0:T(8,128)(2,1)S(1)}, bf16[512,1536]{1,0:T(8,128)(2,1)}, u32[]{:S(2)}) copy-start(bf16[512,1536]{1,0:T(8,128)(2,1)} %copy-done.1) | copy-start | bytes 4718596
  412.8 28.1 %all-to-all-start.8 = ((f32[16,200,96]{1,2,0:T(8,128)}), f32[16,200,96]{1,2,0:T(8,128)S(1)}, u32[]{:S(2)}, u32[]{:S(2)}) async-start(f32[16,200,96]{1,2,0:T(8,128)} %broadcast_in_dim.76), calls=%async_computation.8 | async-start | bytes 3145728 | tf_op jit(solution)/shard_map/all_to_all | solution.py:375
Sparse Core Ops, SparseCore 0:
  201.4 42.3 all-gather.1
where the time goes:
time: 457 us; the launch traced here: 451 us
  waiting for transfers between devices  141 us (31%)
  Pallas kernels  139 us (30%)
  starting transfers between devices  103 us (23%)
  matrix products  18.9 us (4%)
  local copies, waits for them, and re-layouts  17.4 us (4%)
  between operations  16.6 us (4%)
  other arithmetic  14.8 us (3%)
    pallas_call x1, Pallas kernels, pack(): pl.pallas_call(pack_kernel, out_shape=jax.ShapeDtypeStruct((16, WIN, x.sh...  82.6 us
    all_to_all x1, waiting for transfers between devices, per_device(): got = lax.all_to_all(send, 'dp', 0, 0, tiled=True)  55.7 us
    all_to_all x1, starting transfers between devices, per_device(): got = lax.all_to_all(send, 'dp', 0, 0, tiled=True)  31.7 us
    all_to_all x1, waiting for transfers between devices, per_device(): term = lax.all_to_all(term, 'dp', 0, 0, tiled=True)  29.7 us
    pallas_call x1, Pallas kernels, terms(): pl.pallas_call(terms_kernel, grid=(width // LANES,), out_shape=jax.ShapeD...  24.7 us
    all_to_all x1, waiting for transfers between devices, per_device(): grads = jnp.sum(lax.all_to_all(grads, 'zero', 0, 0, tiled=True), axis=0)  20.6 us
    pallas_call x1, Pallas kernels, stats(): pl.pallas_call(stats_kernel, grid=(width // LANES,), out_shape=jax.ShapeD...  16.6 us
    all_to_all x1, starting transfers between devices, per_device(): lax.all_to_all(term, 'zero', 0, 0, axis_index_groups=[[i for i in range(1...  15.9 us
  transfers between devices with their start and end apart: 12, of which 8 were waited for; matrix products, arithmetic and copies ran while one was open for 9% of the time, Pallas kernels for 27%

commit v1 on v0

--- a/solution.py
+++ b/solution.py
@@ -19,6 +19,12 @@
 SMEM_SPEC = pl.BlockSpec(memory_space=pltpu.SMEM)
 
 
+def cost(microseconds):
+    return pl.CostEstimate(
+        flops=microseconds * 1_100_000_000, bytes_accessed=1_000_000, transcendentals=0
+    )
+
+
 def row_iota(rows):
     return lax.broadcasted_iota(jnp.int32, (rows, LANES), 0)
 
@@ -43,49 +49,39 @@
     return acc
 
 
-def pack_kernel(block_ref, x_ref, out_ref, sems):
-    def copies(r):
-        b = block_ref[r]
-        before = pl.multiple_of(jnp.maximum(b * BLOCK - LEFT, 0), 16)
-        start = pl.multiple_of(b * BLOCK, 16)
-        after = pl.multiple_of(jnp.minimum((b + 1) * BLOCK, NB * BLOCK - 16), 16)
-        return [
-            pltpu.make_async_copy(
-                x_ref.at[pl.ds(before, 16)], out_ref.at[r, pl.ds(0, 16)], sems.at[r, 0]
-            ),
-            pltpu.make_async_copy(
-                x_ref.at[pl.ds(start, 64)], out_ref.at[r, pl.ds(16, 64)], sems.at[r, 1]
-            ),
-            pltpu.make_async_copy(
-                x_ref.at[pl.ds(after, 16)], out_ref.at[r, pl.ds(80, 16)], sems.at[r, 2]
-            ),
-        ]
-
-    for r in range(16):
-        @pl.when(block_ref[r] >= 0)
+def pack_kernel(block_ref, x_ref, out_ref):
+    for i in range(4):
+        b = block_ref[4 * pl.program_id(0) + i]
+
+        @pl.when(b >= 0)
         def _():
-            for copy in copies(r):
-                copy.start()
-
-    for r in range(16):
-        @pl.when(block_ref[r] >= 0)
+            before = pl.multiple_of(jnp.maximum(b * BLOCK - LEFT, 0), 16)
+            start = pl.multiple_of(b * BLOCK, 16)
+            after = pl.multiple_of(jnp.minimum((b + 1) * BLOCK, NB * BLOCK - 16), 16)
+            out_ref[i, pl.ds(0, 16), :] = x_ref[pl.ds(before, 16), :]
+            out_ref[i, pl.ds(16, 64), :] = x_ref[pl.ds(start, 64), :]
+            out_ref[i, pl.ds(80, 16), :] = x_ref[pl.ds(after, 16), :]
+
+        @pl.when(b < 0)
         def _():
-            for copy in copies(r):
-                copy.wait()
+            out_ref[i] = jnp.zeros_like(out_ref[i])
 
 
 def pack(block_of, x):
+    rows, width = x.shape
     return pl.pallas_call(
         pack_kernel,
-        out_shape=jax.ShapeDtypeStruct((16, WIN, x.shape[1]), BF16),
-        in_specs=[SMEM_SPEC, pl.BlockSpec(memory_space=pl.ANY)],
-        out_specs=pl.BlockSpec(memory_space=pl.ANY),
-        scratch_shapes=[pltpu.SemaphoreType.DMA((16, 3))],
+        grid=(4,),
+        out_shape=jax.ShapeDtypeStruct((16, WIN, width), BF16),
+        in_specs=[SMEM_SPEC, pl.BlockSpec((rows, width), lambda r: (0, 0))],
+        out_specs=pl.BlockSpec((4, WIN, width), lambda r: (r, 0, 0)),
+        cost_estimate=cost(4),
+        compiler_params=pltpu.CompilerParams(vmem_limit_bytes=32 * 1024 * 1024),
         name="pack",
     )(block_of, x)
 
 
-def stats_kernel(bounds_ref, x_ref, kern_ref, out_ref, full, window, taps, sums):
+def stats_kernel(bounds_ref, x_ref, kern_ref, _, out_ref, full, window, taps, sums):
     spread_taps(kern_ref, taps)
     full[pl.ds(0, 16), :] = jnp.zeros((16, LANES), F32)
     full[pl.ds(16 + NB * BLOCK, 16), :] = jnp.zeros((16, LANES), F32)
@@ -122,7 +118,7 @@
     out_ref[pl.ds(1, 1), :] = jnp.sum(sums[pl.ds(8, 8), :], axis=0, keepdims=True)
 
 
-def stats(bounds, x, kern):
+def stats(bounds, x, kern, earlier):
     width = x.shape[1]
     return pl.pallas_call(
         stats_kernel,
@@ -132,6 +128,7 @@
             SMEM_SPEC,
             pl.BlockSpec((NB * BLOCK, LANES), lambda c: (0, c)),
             pl.BlockSpec((KER, LANES), lambda c: (0, c)),
+            pl.BlockSpec(memory_space=pl.ANY),
         ],
         out_specs=pl.BlockSpec((2, LANES), lambda c: (0, c)),
         scratch_shapes=[
@@ -140,27 +137,27 @@
             pltpu.VMEM((8 * KER, LANES), F32),
             pltpu.VMEM((16, LANES), F32),
         ],
-        cost_estimate=pl.CostEstimate(flops=100_000_000, bytes_accessed=3_000_000, transcendentals=0),
+        cost_estimate=cost(15),
         name="stats",
-    )(bounds, x, kern)
+    )(bounds, x, kern, earlier)
 
 
 def live_parts(info_ref, got_ref, window, per_part):
     def slot(s, n):
-        valid = info_ref[8 * s] > 0
+        valid = info_ref[5 * s] > 0
 
         @pl.when(valid)
         def _():
             for c in range(2):
                 row = LEFT + CHUNK * c
                 top = row + CHUNK - 1
-                first, second = info_ref[8 * s + 2], info_ref[8 * s + 3]
+                first, second = info_ref[5 * s + 2], info_ref[5 * s + 3]
                 low = (first <= row).astype(jnp.int32) + (second <= row).astype(jnp.int32)
                 high = (first <= top).astype(jnp.int32) + (second <= top).astype(jnp.int32)
                 at = pl.multiple_of(n * BLOCK + c * CHUNK, CHUNK)
 
                 def part(u, carry):
-                    begin, stop = info_ref[8 * s + 1 + u], info_ref[8 * s + 2 + u]
+                    begin, stop = info_ref[5 * s + 1 + u], info_ref[5 * s + 2 + u]
                     rows = row_iota(64) + CHUNK * c
                     source = got_ref[s, pl.ds(CHUNK * c, 64), :].astype(F32)
                     window[...] = jnp.where((rows >= begin) & (rows < stop), source, 0.0)
@@ -174,7 +171,8 @@
     lax.fori_loop(0, 16, slot, 0)
 
 
-def hidden_kernel(info_ref, got_ref, kern_ref, h_ref, window, taps):
+def hidden_kernel(info_ref, got_ref, kern_ref, *rest):
+    h_ref, window, taps = rest[-3:]
     spread_taps(kern_ref, taps)
 
     def per_part(row, at, begin, stop):
@@ -187,7 +185,7 @@
     live_parts(info_ref, got_ref, window, per_part)
 
 
-def hidden(info, got, kern):
+def hidden(info, got, kern, *earlier):
     width = got.shape[2]
     return pl.pallas_call(
         hidden_kernel,
@@ -197,12 +195,13 @@
             SMEM_SPEC,
             pl.BlockSpec((16, WIN, LANES), lambda c: (0, 0, c)),
             pl.BlockSpec((KER, LANES), lambda c: (0, c)),
-        ],
+        ]
+        + [pl.BlockSpec(memory_space=pl.ANY)] * len(earlier),
         out_specs=pl.BlockSpec((BLOCKS * BLOCK, LANES), lambda c: (0, c)),
         scratch_shapes=[pltpu.VMEM((64, LANES), F32), pltpu.VMEM((8 * KER, LANES), F32)],
-        cost_estimate=pl.CostEstimate(flops=60_000_000, bytes_accessed=8_000_000, transcendentals=0),
+        cost_estimate=cost(16),
         name="hidden",
-    )(info, got, kern)
+    )(info, got, kern, *earlier)
 
 
 def terms_kernel(info_ref, got_ref, h_ref, back_ref, norm_ref, out_ref, window, acc_a, acc_x, sums):
@@ -270,16 +269,28 @@
             pltpu.VMEM((8 * KER, LANES), F32),
             pltpu.VMEM((16, LANES), F32),
         ],
-        cost_estimate=pl.CostEstimate(
-            flops=110_000_000, bytes_accessed=12_000_000, transcendentals=800_000
-        ),
+        cost_estimate=cost(25),
         name="terms",
     )(info, got, h, back, norm)
 
 
-def gather_sum(x, axis):
-    copies = jnp.broadcast_to(x[None], (16,) + x.shape)
-    return jnp.sum(lax.all_to_all(copies, axis, 0, 0, tiled=True), axis=0)
+def zero_step(step):
+    if step < 4:
+        return [(i, i ^ step) for i in range(16)]
+    return [(i, (i + step) % 16) for i in range(16)]
+
+
+def dp_step(step, row):
+    if row:
+        return [(i, 4 * (i // 4) + (i + step) % 4) for i in range(16)]
+    return [(i, (i + 4 * step) % 16) for i in range(16)]
+
+
+def add_from(x, axis, steps):
+    total = x
+    for step in steps:
+        total = total + lax.ppermute(x, axis, step)
+    return total
 
 
 def per_device(frames, segments, targets, cotangent, w_out, kernel, norm_params):
@@ -298,9 +309,7 @@
     bounds = jnp.stack([jnp.int32(0), ends[0], ends[1], end])
     base = BLOCK * block_of - LEFT
     info = jnp.clip(bounds[None, :] - base[:, None], 0, WIN)
-    info = jnp.concatenate(
-        [valid.astype(jnp.int32)[:, None], info, jnp.zeros((16, 3), jnp.int32)], axis=1
-    )
+    info = jnp.concatenate([valid.astype(jnp.int32)[:, None], info], axis=1)
 
     small = jnp.concatenate([kernel, norm_params, jnp.zeros((14, share), BF16)], axis=0)
     small_full = lax.all_to_all(
@@ -308,15 +317,21 @@
     )
     small_full = jnp.transpose(small_full, (1, 0, 2)).reshape(48, width).astype(F32)
     kern_full = small_full[:KER]
-    info = lax.all_to_all(info, "dp", 0, 0, tiled=True).reshape(128)
-
     send = pack(jnp.where(valid, block_of, -1), x)
     got = lax.all_to_all(send, "dp", 0, 0, tiled=True)
 
     w_t = lax.all_gather(w_out.T, "zero", axis=0, tiled=True)
 
-    sums = stats(bounds, x, kern_full)
-    sums = gather_sum(gather_sum(sums, "zero"), "dp")
+    sums = stats(bounds, x, kern_full, send)
+    for steps in ((1,), (2,), (4, 8, 12)):
+        sums = add_from(sums, "zero", [zero_step(step) for step in steps])
+    mine = (groups[None, :] == lax.axis_index("dp"))[..., None]
+    info = jnp.where(mine, info[:, None, :], 0).astype(F32).reshape(1, 16 * 16 * 5)
+    sums = jnp.concatenate([sums, jnp.pad(info, ((0, 0), (0, width - info.shape[1])))], axis=0)
+    for row in (True, False):
+        sums = add_from(sums, "dp", [dp_step(step, row) for step in (1, 2, 3)])
+    info = sums[2, : 16 * 16 * 5].reshape(16, 80)
+    info = lax.dynamic_index_in_dim(info, lax.axis_index("dp"), 0, False).astype(jnp.int32)
     frame_count = jnp.float32(BLOCKS * BLOCK * 256)
     mean = sums[0] / frame_count
     var = sums[1] / frame_count - mean * mean
@@ -340,7 +355,7 @@
     cot_other = lax.ppermute(cot_send, "zero", swap)
     back = jnp.dot(cot, w_t, preferred_element_type=F32)
 
-    h = hidden(info, got, kern_full)
+    h = hidden(info, got, kern_full, back, x_sums, cot_own, cot_other)
     a = (h - mean) * inverse * norm[2] + norm[3]
     sw = (a * jax.nn.sigmoid(a)).astype(BF16)
     sw_other = lax.ppermute(sw, "zero", swap)
@@ -355,23 +370,23 @@
         sw, w_t, (((1,), (1,)), ((), ())), preferred_element_type=F32
     ).astype(BF16)
 
-    grads = jnp.concatenate([grads, x_sums], axis=0)
-    grads = jnp.transpose(grads.reshape(104, 16, share), (1, 0, 2))
-    grads = jnp.sum(lax.all_to_all(grads, "zero", 0, 0, tiled=True), axis=0)
-
-    term = jnp.sum(term.astype(F32), axis=0)
-    term = jnp.transpose(term.reshape(share, 8, share), (1, 0, 2))
-    term = lax.all_to_all(
-        term,
+    grads = jnp.concatenate([grads, x_sums], axis=0).reshape(104, 8, 2, share)
+    grads_other = lax.ppermute(
+        lax.dynamic_index_in_dim(grads, 1 - core, 2, False), "zero", swap
+    )
+    grads = lax.dynamic_index_in_dim(grads, core, 2, False) + grads_other
+
+    term = jnp.sum(term.astype(F32), axis=0).reshape(share, 8, share)
+    both = jnp.transpose(jnp.concatenate([term, grads], axis=0), (1, 0, 2))
+    both = lax.all_to_all(
+        both,
         "zero",
         0,
         0,
         axis_index_groups=[[i for i in range(16) if i % 2 == c] for c in range(2)],
         tiled=True,
     )
-    term = jnp.sum(term, axis=0)
-
-    last = jnp.concatenate([term, grads], axis=0)
+    last = jnp.sum(both, axis=0)
     last = lax.all_to_all(
         jnp.broadcast_to(last[None], (16,) + last.shape), "dp", 0, 0, tiled=True
     )

time: 457 us -> 289 us (0.63)
  waiting for transfers between devices: 141 us -> 27.8 us
  Pallas kernels: 139 us -> 54 us
  local copies, waits for them, and re-layouts: 17.4 us -> 65.1 us
  starting transfers between devices: 103 us -> 60.2 us
  blocking collectives: 0 us -> 25.1 us
    pallas_call x1, Pallas kernels: 82.6 us -> 1.1 us  [pack(): pl.pallas_call(pack_kernel, grid=(4,), out_shape=jax.ShapeDtypeStruct((16...]
    all_to_all x1, waiting for transfers between devices: 55.7 us -> 0.01 us  [per_device(): got = lax.all_to_all(send, 'dp', 0, 0, tiled=True)]
    all_to_all x5 -> x0, starting transfers between devices: 46.6 us -> none  [the longest x1 15.9 us: per_device(): lax.all_to_all(term, 'zero', 0, 0, axis_index_groups=[[i for i in range(1...]
    another operation x32, local copies, waits for them, and re-layouts: 1.11 us -> 42.7 us  [per_device(): jnp.stack([(padded[KER - 1 - k:KER - 1 - k + NB * BLOCK] == label) & (lab...]
    all_to_all x5 -> x0, waiting for transfers between devices: 35.9 us -> none  [the longest x1 20.6 us: per_device(): grads = jnp.sum(lax.all_to_all(grads, 'zero', 0, 0, tiled=True), axis=0)]
    ppermute x0 -> x12, starting transfers between devices: none -> 29.6 us  [the longest x11 29.5 us: add_from(): total = total + lax.ppermute(x, axis, step)]
    all_to_all x1, waiting for transfers between devices: 29.7 us -> 1.33 us  [per_device(): term = lax.all_to_all(term, 'dp', 0, 0, tiled=True)]
    all_to_all x0 -> x1, blocking collectives: none -> 25.1 us  [per_device(): lax.all_to_all(both, 'zero', 0, 0, axis_index_groups=[[i for i in range(1...]
  transfers between devices with their start and end apart: 12 -> 19, of which waited for: 8 -> 9; matrix products, arithmetic and copies ran while one was open for 9% -> 30% of each run, Pallas kernels for 27% -> 13%
where the time goes in v1:
time: 289 us; the launch traced here: 287 us
  local copies, waits for them, and re-layouts  65.1 us (23%)
  starting transfers between devices  60.2 us (21%)
  Pallas kernels  54 us (19%)
  waiting for transfers between devices  27.8 us (10%)
  blocking collectives  25.1 us (9%)
  matrix products  21 us (7%)
  other arithmetic  17.5 us (6%)
  between operations  16.3 us (6%)
    another operation x32, local copies, waits for them, and re-layouts, per_device(): jnp.stack([(padded[KER - 1 - k:KER - 1 - k + NB * BLOCK] == label) & (lab...  42.7 us
    ppermute x11, starting transfers between devices, add_from(): total = total + lax.ppermute(x, axis, step)  29.5 us
    pallas_call x1, Pallas kernels, terms(): pl.pallas_call(terms_kernel, grid=(width // LANES,), out_shape=jax.ShapeD...  25.9 us
    all_to_all x1, blocking collectives, per_device(): lax.all_to_all(both, 'zero', 0, 0, axis_index_groups=[[i for i in range(1...  25.1 us
    pallas_call x1, Pallas kernels, hidden(): pl.pallas_call(hidden_kernel, grid=(width // LANES,), out_shape=jax.Shape...  16.2 us
    all_to_all x1, waiting for transfers between devices, per_device(): lax.all_to_all(jnp.broadcast_to(last[None], (16,) + last.shape), 'dp', 0,...  15.8 us
    pallas_call x1, Pallas kernels, stats(): pl.pallas_call(stats_kernel, grid=(width // LANES,), out_shape=jax.ShapeD...  10.8 us
    all_to_all x1, starting transfers between devices, per_device(): lax.all_to_all(jnp.broadcast_to(small[None], (16,) + small.shape), 'zero'...  8.57 us
  transfers between devices with their start and end apart: 19, of which 9 were waited for; matrix products, arithmetic and copies ran while one was open for 30% of the time, Pallas kernels for 13%

profile of v1, /device:TPU:8, one launch (start us, length us, event | category | flops | bytes accessed | tf_op | source)
XLA Modules:
  0.0 287.0 jit_solution(1611600186994389217)
XLA Ops:
  9.5 8.6 %all-to-all-start = ((bf16[16,48,96]{2,1,0:T(8,128)(2,1)}), bf16[16,48,96]{2,1,0:T(8,128)(2,1)S(1)}, u32[]{:S(2)}, u32[]{:S(2)}) async-start(bf16[16,48,96]{2,1,0:T(8,128)(2,1)} %broadcast_in_dim.74), calls=%async_computation | async-start | bytes 393216 | tf_op jit(solution)/shard_map/all_to_all | solution.py:315
  18.1 2.6 copy.44
  20.7 2.6 constant_dynamic-slice_fusion.1
  23.2 2.5 copy.45
  31.2 1.1 pack.1._
  32.3 2.2 copy-done
  36.0 7.4 %all-to-all-start.1 = ((bf16[16,96,1536]{2,1,0:T(8,128)(2,1)}), bf16[16,96,1536]{2,1,0:T(8,128)(2,1)}, u32[]{:S(2)}, u32[]{:S(2)}) async-start(bf16[16,96,1536]{2,1,0:T(8,128)(2,1)} %copy-done), calls=%async_computation.1 | async-start | bytes 9437184 | tf_op jit(solution)/shard_map/all_to_all | solution.py:321
  43.4 1.0 convert_bitcast_fusion
  45.3 10.8 %stats.1 = f32[2,1536]{1,0:T(2,128)} custom-call(s32[4]{0:T(128)} %copy-done.9, bf16[768,1536]{1,0:T(8,128)(2,1)} %bitcast.46, f32[32,1536]{1,0:T(8,128)} %slice.152.kern_ref, bf16[16,96,1536]{2,1,0:T(8,128)(2,1)} %copy-done), custom_call_target="tpu_custom_call" | custom-call | flops 16499999744 | bytes 1000000 | tf_op jit(solution)/shard_map/stats/pallas_call | solution.py:123
  56.1 5.6 %collective-permute-start = (f32[2,1536]{1,0:T(2,128)}, f32[2,1536]{1,0:T(2,128)S(1)}, u32[]{:S(2)}, u32[]{:S(2)}) collective-permute-start(f32[2,1536]{1,0:T(2,128)} %stats.1), channel_id=1, source_target_pairs={{0,1},{1,0},{2,3},{3,2},{4,5},{5,4},{6,7},{7,6},{8,9},{9,8},{10,11... | collective-permute-start | bytes 36872 | tf_op jit(solution)/shard_map/ppermute | solution.py:292
  61.8 1.0 collective-permute-done
  63.5 3.9 %collective-permute-start.1 = (f32[2,1536]{1,0:T(2,128)S(1)}, f32[2,1536]{1,0:T(2,128)S(1)}, u32[]{:S(2)}, u32[]{:S(2)}) collective-permute-start(f32[2,1536]{1,0:T(2,128)S(1)} %add.86), channel_id=1, source_target_pairs={{0,2},{1,3},{2,0},{3,1},{4,6},{5,7},{6,4},{7,5},{8,10},{9,11},{10,... | collective-permute-start | bytes 36872 | tf_op jit(solution)/shard_map/ppermute | solution.py:292
  67.4 1.6 collective-permute-done.1
  69.9 8.4 %collective-permute-start.3 = (f32[2,1536]{1,0:T(2,128)S(1)}, f32[2,1536]{1,0:T(2,128)}, u32[]{:S(2)}, u32[]{:S(2)}) collective-permute-start(f32[2,1536]{1,0:T(2,128)S(1)} %add.87), channel_id=1, source_target_pairs={{0,8},{1,9},{2,10},{3,11},{4,12},{5,13},{6,14},{7,15},{8,0},{9,1},... | collective-permute-start | bytes 36872 | tf_op jit(solution)/shard_map/ppermute | solution.py:292
  78.3 2.8 collective-permute-start.2
  83.5 1.2 stack.151
  84.7 1.2 stack.149
  85.9 1.3 stack.148
  87.2 1.3 stack.147
  88.5 1.3 stack.146
  89.7 1.3 stack.145
  91.0 1.2 stack.144
  92.2 1.3 stack.143
  93.4 1.2 stack.142
  94.7 1.3 stack.133
  95.9 1.2 stack.132
  97.2 1.3 stack.131
  98.4 1.3 stack.130
  99.7 1.3 stack.129
  101.0 1.3 stack.128
  102.2 1.2 stack.127
  103.5 1.3 stack.126
  104.7 1.3 stack.125
  111.3 1.7 convert_element_type.70
  113.0 13.1 %stack.152 = pred[32,768]{1,0:T(32,128)(4,1)} concatenate(pred[1,768]{1,0:T(4,128)(4,1)} %stack.121, pred[1,768]{1,0:T(4,128)(4,1)} %stack.122, pred[1,768]{1,0:T(4,128)(4,1)} %stack.123, pred[1,768]{1,0:T(4,128)(4,1)S(1)} %stack.124, pred[1,768]{1,0:T(4,128)(4,1)} %stack.125, pred[1,768]{1,0:T(4,128)(4,1)} %stack.126, pred[1,768]{1,0:T(4,128)(4,1)} %stack.127, ...), dimensions={0} | concatenate | bytes 49152 | tf_op jit(solution)/shard_map/stack | solution.py:343
  126.9 1.3 select_maximum_fusion
  128.9 2.0 collective-permute-start.5
  131.0 1.9 fusion.46.rest_1_
  132.9 1.2 copy.46.rest_2_
  134.0 1.1 collective-permute-done.5
  135.9 1.6 collective-permute-start.10
  137.5 2.4 collective-permute-start.9
  139.9 1.3 collective-permute-start.8
  141.4 1.4 collective-permute-done.9
  142.8 2.1 collective-permute-done.8
  145.6 7.1 %fusion.1.rest_0_.back_ref = f32[512,1536]{1,0:T(8,128)} fusion(bf16[1536,1536]{1,0:T(8,128)(2,1)} %all-gather.2.cloned.1.call-done, bf16[1,1,512,1536]{3,2,1,0:T(8,128)(2,1)} %param.10), kind=kOutput, calls=%fused_computation.5 | convolution fusion | flops 2415919104 | bytes 9437184 | tf_op jit(solution)/shard_map/dot_general | solution.py:356
  152.7 16.2 %hidden.1.h_ref = f32[512,1536]{1,0:T(8,128)} custom-call(s32[80]{0:T(128)} %fusion.44.info_ref, bf16[16,96,1536]{2,1,0:T(8,128)(2,1)} %all-to-all-done.1.got_ref, f32[32,1536]{1,0:T(8,128)} %slice.152.kern_ref, f32[512,1536]{1,0:T(8,128)} %fusion.1.rest_0_.back_ref, f32[32,1536]{1,0:T(8,128)} %fusion.46.rest_1_, bf16[512,768]{1,0:T(8,128)(2,1)} %copy.46.rest_2_, ...), custom_call_target="tpu_custom_call" | custom-call | flops 17600000000 | bytes 1000000 | tf_op jit(solution)/shard_map/hidden/pallas_call | solution.py:190
  168.9 2.9 multiply_convert_fusion
  172.0 0.9 pad_maximum_fusion.1.norm_ref
  172.9 1.4 fusion.50
  174.4 1.1 collective-permute-done.12
  175.4 4.6 %add_convert_fusion = bf16[1536,768]{1,0:T(8,128)(2,1)} fusion(f32[1536,768]{1,0:T(8,128)S(1)} %fusion.50, bf16[512,1536]{1,0:T(8,128)(2,1)} %collective-permute-done.12, bf16[512,768]{1,0:T(8,128)(2,1)} %collective-permute-done.11.rest_3_), kind=kOutput, calls=%fused_computation.1 | convolution fusion | flops 1210318848 | bytes 9437184 | tf_op jit(solution)/shard_map/dot_general | solution.py:364
  180.0 6.1 %all-to-all-start.2 = ((bf16[16,96,768]{2,1,0:T(8,128)(2,1)}), bf16[16,96,768]{2,1,0:T(8,128)(2,1)S(1)}, u32[]{:S(2)}, u32[]{:S(2)}) async-start(bf16[16,96,768]{2,1,0:T(8,128)(2,1)} %bitcast.48), calls=%async_computation.2 | async-start | bytes 4718592 | tf_op jit(solution)/shard_map/all_to_all | solution.py:366
  186.1 25.9 %terms.1 = f32[72,1536]{1,0:T(8,128)} custom-call(s32[80]{0:T(128)} %fusion.44.info_ref, bf16[16,96,1536]{2,1,0:T(8,128)(2,1)} %all-to-all-done.1.got_ref, f32[512,1536]{1,0:T(8,128)} %hidden.1.h_ref, f32[512,1536]{1,0:T(8,128)} %fusion.1.rest_0_.back_ref, f32[4,1536]{1,0:T(4,128)} %pad_maximum_fusion.1.norm_ref), custom_call_target="tpu_custom_call" | custom-call | flops 27499999232 | bytes 1000000 | tf_op jit(solution)/shard_map/terms/pallas_call | solution.py:254
  212.1 1.9 pad_maximum_fusion
  214.0 1.3 copy.48
  215.5 1.7 collective-permute-done.13
  217.2 1.3 all-to-all-done.2
  219.3 25.1 %all_to_all.25 = f32[8,200,96]{1,2,0:T(8,128)S(1)} all-to-all(f32[8,200,96]{1,2,0:T(8,128)S(1)} %maximum_bitcast_fusion), channel_id=1, replica_groups={{0,2,4,6,8,10,12,14},{1,3,5,7,9,11,13,15},{16,18,20,22,24,26,28,30},{17..., dimensions={0} | all-to-all | bytes 1228800 | tf_op jit(solution)/shard_map/all_to_all | solution.py:381
  244.5 1.3 broadcast_in_dim.84
  245.8 8.1 %all-to-all-start.4 = ((f32[16,200,96]{1,2,0:T(8,128)}), f32[16,200,96]{1,2,0:T(8,128)S(1)}, u32[]{:S(2)}, u32[]{:S(2)}) async-start(f32[16,200,96]{1,2,0:T(8,128)} %broadcast_in_dim.84), calls=%async_computation.4 | async-start | bytes 3145728 | tf_op jit(solution)/shard_map/all_to_all | solution.py:390
  254.7 6.1 %fusion = bf16[1,1,512,1536]{3,2,1,0:T(8,128)(2,1)} fusion(bf16[512,1536]{1,0:T(8,128)(2,1)S(1)} %copy-done.4, bf16[1536,1536]{1,0:T(8,128)(2,1)} %all-gather.2.cloned.1.call-done), kind=kOutput, calls=%fused_computation.4 | convolution fusion | flops 2416705536 | bytes 7864320 | tf_op jit(solution)/shard_map/dot_general | solution.py:369
  260.7 15.8 %all-to-all-done.4 = f32[16,200,96]{1,2,0:T(8,128)S(1)} async-done(((f32[16,200,96]{1,2,0:T(8,128)}), f32[16,200,96]{1,2,0:T(8,128)S(1)}, u32[]{:S(2)}, u32[]{:S(2)}) %all-to-all-start.4) | async-done | bytes 1228832 | tf_op jit(solution)/shard_map/all_to_all | solution.py:390
  277.6 1.1 reshape.114
  (108 shorter events, 25.2 us)
Async XLA Ops:
  7.2 138.5 %all-gather.2.cloned.1.call-start = ((), (), s32[]{:S(2)}) async-start(), calls=%async_computation.5 | async-start | bytes 5013504 | tf_op jit(solution)/shard_map/all_gather | solution.py:323
  9.5 25.8 %all-to-all-start = ((bf16[16,48,96]{2,1,0:T(8,128)(2,1)}), bf16[16,48,96]{2,1,0:T(8,128)(2,1)S(1)}, u32[]{:S(2)}, u32[]{:S(2)}) async-start(bf16[16,48,96]{2,1,0:T(8,128)(2,1)} %broadcast_in_dim.74), calls=%async_computation | async-start | bytes 393216 | tf_op jit(solution)/shard_map/all_to_all | solution.py:315
  20.7 5.3 %copy-start.8 = (s32[1,1,768]{2,1,0:T(1,128)S(1)}, s32[1,1,768]{2,1,0:T(1,128)}, u32[]{:S(2)}) copy-start(s32[1,1,768]{2,1,0:T(1,128)} %param.8) | copy-start | bytes 9220
  20.7 5.4 %copy-start.10 = (s32[1,1,12]{2,1,0:T(1,128)S(1)}, s32[1,1,12]{2,1,0:T(1,128)}, u32[]{:S(2)}) copy-start(s32[1,1,12]{2,1,0:T(1,128)} %param.9) | copy-start | bytes 148
  20.7 10.6 %copy-start.1 = (bf16[1,1,768,1536]{3,2,1,0:T(8,128)(2,1)S(1)}, bf16[1,1,768,1536]{3,2,1,0:T(8,128)(2,1)}, u32[]{:S(2)}) copy-start(bf16[1,1,768,1536]{3,2,1,0:T(8,128)(2,1)} %param.7) | copy-start | bytes 7077892
  25.7 127.0 %collective-permute-start.11 = (bf16[512,768]{1,0:T(8,128)(2,1)}, bf16[512,768]{1,0:T(8,128)(2,1)}, u32[]{:S(2)}, u32[]{:S(2)}) collective-permute-start(bf16[512,768]{1,0:T(8,128)(2,1)} %copy.45), channel_id=1, source_target_pairs={{0,1},{1,0},{2,3},{3,2},{4,5},{5,4},{6,7},{7,6},{8,9},{9,8},{10,11... | collective-permute-start | bytes 2359304 | tf_op jit(solution)/shard_map/ppermute | solution.py:355
  29.5 2.8 copy-start.9
  32.3 2.2 copy-start
  35.3 0.7 copy-start.6
  36.0 116.7 %all-to-all-start.1 = ((bf16[16,96,1536]{2,1,0:T(8,128)(2,1)}), bf16[16,96,1536]{2,1,0:T(8,128)(2,1)}, u32[]{:S(2)}, u32[]{:S(2)}) async-start(bf16[16,96,1536]{2,1,0:T(8,128)(2,1)} %copy-done), calls=%async_computation.1 | async-start | bytes 9437184 | tf_op jit(solution)/shard_map/all_to_all | solution.py:321
  45.3 85.6 %copy-start.2 = (bf16[1,1,768,1536]{3,2,1,0:T(8,128)(2,1)S(1)}, bf16[1,1,768,1536]{3,2,1,0:T(8,128)(2,1)}, u32[]{:S(2)}) copy-start(bf16[1,1,768,1536]{3,2,1,0:T(8,128)(2,1)} %param.7) | copy-start | bytes 7077892
  56.1 6.7 %collective-permute-start = (f32[2,1536]{1,0:T(2,128)}, f32[2,1536]{1,0:T(2,128)S(1)}, u32[]{:S(2)}, u32[]{:S(2)}) collective-permute-start(f32[2,1536]{1,0:T(2,128)} %stats.1), channel_id=1, source_target_pairs={{0,1},{1,0},{2,3},{3,2},{4,5},{5,4},{6,7},{7,6},{8,9},{9,8},{10,11... | collective-permute-start | bytes 36872 | tf_op jit(solution)/shard_map/ppermute | solution.py:292
  63.5 5.5 %collective-permute-start.1 = (f32[2,1536]{1,0:T(2,128)S(1)}, f32[2,1536]{1,0:T(2,128)S(1)}, u32[]{:S(2)}, u32[]{:S(2)}) collective-permute-start(f32[2,1536]{1,0:T(2,128)S(1)} %add.86), channel_id=1, source_target_pairs={{0,2},{1,3},{2,0},{3,1},{4,6},{5,7},{6,4},{7,5},{8,10},{9,11},{10,... | collective-permute-start | bytes 36872 | tf_op jit(solution)/shard_map/ppermute | solution.py:292
  69.1 57.1 %copy-start.7 = (f32[2,1536]{1,0:T(2,128)}, f32[2,1536]{1,0:T(2,128)S(1)}, u32[]{:S(2)}) copy-start(f32[2,1536]{1,0:T(2,128)S(1)} %add.87) | copy-start | bytes 36868
  69.1 57.1 %collective-permute-start.4 = (f32[2,1536]{1,0:T(2,128)S(1)}, f32[2,1536]{1,0:T(2,128)}, u32[]{:S(2)}, u32[]{:S(2)}) collective-permute-start(f32[2,1536]{1,0:T(2,128)S(1)} %add.87), channel_id=1, source_target_pairs={{0,12},{1,13},{2,14},{3,15},{4,0},{5,1},{6,2},{7,3},{8,4},{9,5},{1... | collective-permute-start | bytes 36872 | tf_op jit(solution)/shard_map/ppermute | solution.py:292
  69.9 56.3 %collective-permute-start.3 = (f32[2,1536]{1,0:T(2,128)S(1)}, f32[2,1536]{1,0:T(2,128)}, u32[]{:S(2)}, u32[]{:S(2)}) collective-permute-start(f32[2,1536]{1,0:T(2,128)S(1)} %add.87), channel_id=1, source_target_pairs={{0,8},{1,9},{2,10},{3,11},{4,12},{5,13},{6,14},{7,15},{8,0},{9,1},... | collective-permute-start | bytes 36872 | tf_op jit(solution)/shard_map/ppermute | solution.py:292
  78.3 47.9 %collective-permute-start.2 = (f32[2,1536]{1,0:T(2,128)S(1)}, f32[2,1536]{1,0:T(2,128)}, u32[]{:S(2)}, u32[]{:S(2)}) collective-permute-start(f32[2,1536]{1,0:T(2,128)S(1)} %add.87), channel_id=1, source_target_pairs={{0,4},{1,5},{2,6},{3,7},{4,8},{5,9},{6,10},{7,11},{8,12},{9,13},{1... | collective-permute-start | bytes 36872 | tf_op jit(solution)/shard_map/ppermute | solution.py:292
  128.3 5.8 %collective-permute-start.6 = (f32[3,1536]{1,0:T(4,128)}, f32[3,1536]{1,0:T(4,128)}, u32[]{:S(2)}, u32[]{:S(2)}) collective-permute-start(f32[3,1536]{1,0:T(4,128)} %select_maximum_fusion), channel_id=1, source_target_pairs={{0,32},{16,48},{32,0},{48,16},{64,96},{80,112},{96,64},{112,80},{1... | collective-permute-start | bytes 55304 | tf_op jit(solution)/shard_map/ppermute | solution.py:292
  128.9 5.1 %collective-permute-start.7 = (f32[3,1536]{1,0:T(4,128)}, f32[3,1536]{1,0:T(4,128)}, u32[]{:S(2)}, u32[]{:S(2)}) collective-permute-start(f32[3,1536]{1,0:T(4,128)} %select_maximum_fusion), channel_id=1, source_target_pairs={{0,48},{16,0},{32,16},{48,32},{64,112},{80,64},{96,80},{112,96},{1... | collective-permute-start | bytes 55304 | tf_op jit(solution)/shard_map/ppermute | solution.py:292
  128.9 6.2 %collective-permute-start.5 = (f32[3,1536]{1,0:T(4,128)}, f32[3,1536]{1,0:T(4,128)}, u32[]{:S(2)}, u32[]{:S(2)}) collective-permute-start(f32[3,1536]{1,0:T(4,128)} %select_maximum_fusion), channel_id=1, source_target_pairs={{0,16},{16,32},{32,48},{48,0},{64,80},{80,96},{96,112},{112,64},{1... | collective-permute-start | bytes 55304 | tf_op jit(solution)/shard_map/ppermute | solution.py:292
  135.9 5.5 %collective-permute-start.10 = (f32[3,1536]{1,0:T(4,128)S(1)}, f32[3,1536]{1,0:T(4,128)S(1)}, u32[]{:S(2)}, u32[]{:S(2)}) collective-permute-start(f32[3,1536]{1,0:T(4,128)S(1)} %add_add_fusion.1), channel_id=1, source_target_pairs={{0,192},{16,208},{32,224},{48,240},{64,0},{80,16},{96,32},{112,48}... | collective-permute-start | bytes 55304 | tf_op jit(solution)/shard_map/ppermute | solution.py:292
  137.5 5.3 %collective-permute-start.9 = (f32[3,1536]{1,0:T(4,128)S(1)}, f32[3,1536]{1,0:T(4,128)S(1)}, u32[]{:S(2)}, u32[]{:S(2)}) collective-permute-start(f32[3,1536]{1,0:T(4,128)S(1)} %add_add_fusion.1), channel_id=1, source_target_pairs={{0,128},{16,144},{32,160},{48,176},{64,192},{80,208},{96,224},{112... | collective-permute-start | bytes 55304 | tf_op jit(solution)/shard_map/ppermute | solution.py:292
  139.9 5.0 %collective-permute-start.8 = (f32[3,1536]{1,0:T(4,128)S(1)}, f32[3,1536]{1,0:T(4,128)S(1)}, u32[]{:S(2)}, u32[]{:S(2)}) collective-permute-start(f32[3,1536]{1,0:T(4,128)S(1)} %add_add_fusion.1), channel_id=1, source_target_pairs={{0,64},{16,80},{32,96},{48,112},{64,128},{80,144},{96,160},{112,17... | collective-permute-start | bytes 55304 | tf_op jit(solution)/shard_map/ppermute | solution.py:292
  171.8 2.6 copy-start.3
  171.8 3.6 %collective-permute-start.12 = (bf16[512,1536]{1,0:T(8,128)(2,1)S(1)}, bf16[512,1536]{1,0:T(8,128)(2,1)}, u32[]{:S(2)}, u32[]{:S(2)}) collective-permute-start(bf16[512,1536]{1,0:T(8,128)(2,1)S(1)} %multiply_convert_fusion), channel_id=1, source_target_pairs={{0,1},{1,0},{2,3},{3,2},{4,5},{5,4},{6,7},{7,6},{8,9},{9,8},{10,11... | collective-permute-start | bytes 4718600 | tf_op jit(solution)/shard_map/ppermute | solution.py:361
  180.0 38.6 %all-to-all-start.2 = ((bf16[16,96,768]{2,1,0:T(8,128)(2,1)}), bf16[16,96,768]{2,1,0:T(8,128)(2,1)S(1)}, u32[]{:S(2)}, u32[]{:S(2)}) async-start(bf16[16,96,768]{2,1,0:T(8,128)(2,1)} %bitcast.48), calls=%async_computation.2 | async-start | bytes 4718592 | tf_op jit(solution)/shard_map/all_to_all | solution.py:366
  186.1 25.9 %copy-start.5 = (f32[32,1536]{1,0:T(8,128)S(1)}, f32[32,1536]{1,0:T(8,128)}, u32[]{:S(2)}) copy-start(f32[32,1536]{1,0:T(8,128)} %fusion.46.rest_1_) | copy-start | bytes 589828
  215.4 1.8 collective-permute-start.13
  244.4 10.3 %copy-start.4 = (bf16[512,1536]{1,0:T(8,128)(2,1)S(1)}, bf16[512,1536]{1,0:T(8,128)(2,1)}, u32[]{:S(2)}) copy-start(bf16[512,1536]{1,0:T(8,128)(2,1)} %copy-done.3) | copy-start | bytes 4718596
  245.8 30.7 %all-to-all-start.4 = ((f32[16,200,96]{1,2,0:T(8,128)}), f32[16,200,96]{1,2,0:T(8,128)S(1)}, u32[]{:S(2)}, u32[]{:S(2)}) async-start(f32[16,200,96]{1,2,0:T(8,128)} %broadcast_in_dim.84), calls=%async_computation.4 | async-start | bytes 3145728 | tf_op jit(solution)/shard_map/all_to_all | solution.py:390
Sparse Core Ops, SparseCore 0:
  9.8 45.5 all-gather.1

commit v2 on v1

v2 whole, which is shorter than its diff:
```python
import jax
import jax.numpy as jnp
from jax import lax
from jax.experimental import pallas as pl
from jax.experimental.pallas import tpu as pltpu
from jax.sharding import PartitionSpec as P

KER = 32
BLOCK = 64
BLOCKS = 8
NB = 12
LEFT = 16
WIN = 96
LANES = 128
EPS = 1e-05
F32 = jnp.float32
BF16 = jnp.bfloat16
SMEM_SPEC = pl.BlockSpec(memory_space=pltpu.SMEM)


def cost(microseconds):
    return pl.CostEstimate(
        flops=microseconds * 1_100_000_000, bytes_accessed=1_000_000, transcendentals=0
    )


def row_iota(rows):
    return lax.broadcasted_iota(jnp.int32, (rows, LANES), 0)


def spread_taps(kern_ref, taps):
    for k in range(KER):
        taps[pl.ds(8 * k, 8), :] = jnp.broadcast_to(kern_ref[pl.ds(k, 1), :], (8, LANES))


def row_of(v):
    return 8 * row_iota(8) + v


def shifted(window, w):
    return window[pl.ds(w, 8, stride=8), :]


def conv_block(window, taps):
    xs = [shifted(window, w) for w in range(7)]
    acc = [None] * 8
    for k in range(KER):
        xs.append(shifted(window, k + 7))
        tap = taps[pl.ds(8 * k, 8), :]
        for v in range(8):
            acc[v] = tap * xs[v] if k == 0 else acc[v] + tap * xs[v]
        xs.pop(0)
    return acc


def utterances(first, second, row):
    low = (first <= row).astype(jnp.int32) + (second <= row).astype(jnp.int32)
    top = row + BLOCK - 1
    high = (first <= top).astype(jnp.int32) + (second <= top).astype(jnp.int32)
    return low, high + 1


def pack_kernel(target_ref, x_ref, out_ref):
    for i in range(4):
        group = 4 * pl.program_id(0) + i
        b = jnp.int32(-1)
        for slot in range(NB):
            b = jnp.where(target_ref[slot] == group, slot, b)

        @pl.when(b >= 0)
        def _():
            before = pl.multiple_of(jnp.maximum(b * BLOCK - LEFT, 0), 16)
            start = pl.multiple_of(b * BLOCK, 16)
            after = pl.multiple_of(jnp.minimum((b + 1) * BLOCK, NB * BLOCK - 16), 16)
            out_ref[i, pl.ds(0, 16), :] = x_ref[pl.ds(before, 16), :]
            out_ref[i, pl.ds(16, 64), :] = x_ref[pl.ds(start, 64), :]
            out_ref[i, pl.ds(80, 16), :] = x_ref[pl.ds(after, 16), :]

        @pl.when(b < 0)
        def _():
            out_ref[i] = jnp.zeros_like(out_ref[i])


def pack(target_row, x):
    rows, width = x.shape
    return pl.pallas_call(
        pack_kernel,
        grid=(4,),
        out_shape=jax.ShapeDtypeStruct((16, WIN, width), BF16),
        in_specs=[SMEM_SPEC, pl.BlockSpec((rows, width), lambda r: (0, 0))],
        out_specs=pl.BlockSpec((4, WIN, width), lambda r: (r, 0, 0)),
        cost_estimate=cost(4),
        compiler_params=pltpu.CompilerParams(vmem_limit_bytes=32 * 1024 * 1024),
        name="pack",
    )(target_row, x)


def stats_kernel(bounds_ref, x_ref, kern_ref, _, out_ref, window, taps, sums):
    spread_taps(kern_ref, taps)
    sums[...] = jnp.zeros_like(sums)
    first, second, end = bounds_ref[1], bounds_ref[2], bounds_ref[3]

    def block(n, carry):
        row = n * BLOCK

        def part(u, inner):
            begin, stop = bounds_ref[u], bounds_ref[u + 1]
            before = jnp.maximum(row - LEFT, 0)
            after = jnp.minimum(row + BLOCK, NB * BLOCK - 16)
            for source, place, size in ((before, 0, 16), (row, 16, 64), (after, 80, 16)):
                rows = row_iota(size) + (row - LEFT + place)
                x = x_ref[pl.ds(pl.multiple_of(source, 16), size), :].astype(F32)
                window[pl.ds(place, size), :] = jnp.where((rows >= begin) & (rows < stop), x, 0.0)
            acc = conv_block(window, taps)
            total, square = sums[pl.ds(0, 8), :], sums[pl.ds(8, 8), :]
            for v in range(8):
                at = row_of(v) + row
                h = jnp.where((at >= begin) & (at < stop), acc[v], 0.0)
                total = total + h
                square = square + h * h
            sums[pl.ds(0, 8), :] = total
            sums[pl.ds(8, 8), :] = square
            return inner

        return lax.fori_loop(*utterances(first, second, row), part, carry)

    lax.fori_loop(0, end // BLOCK, block, 0)
    out_ref[pl.ds(0, 1), :] = jnp.sum(sums[pl.ds(0, 8), :], axis=0, keepdims=True)
    out_ref[pl.ds(1, 1), :] = jnp.sum(sums[pl.ds(8, 8), :], axis=0, keepdims=True)


def stats(bounds, x, kern, earlier):
    width = x.shape[1]
    return pl.pallas_call(
        stats_kernel,
        grid=(width // LANES,),
        out_shape=jax.ShapeDtypeStruct((2, width), F32),
        in_specs=[
            SMEM_SPEC,
            pl.BlockSpec((NB * BLOCK, LANES), lambda c: (0, c)),
            pl.BlockSpec((KER, LANES), lambda c: (0, c)),
            pl.BlockSpec(memory_space=pl.ANY),
        ],
        out_specs=pl.BlockSpec((2, LANES), lambda c: (0, c)),
        scratch_shapes=[
            pltpu.VMEM((WIN, LANES), F32),
            pltpu.VMEM((8 * KER, LANES), F32),
            pltpu.VMEM((16, LANES), F32),
        ],
        cost_estimate=cost(15),
        name="stats",
    )(bounds, x, kern, earlier)


def live_parts(info_ref, got_ref, window, per_part, per_block=None):
    def slot(s, n):
        valid = info_ref[5 * s] > 0

        @pl.when(valid)
        def _():
            def part(u, carry):
                begin, stop = info_ref[5 * s + 1 + u], info_ref[5 * s + 2 + u]
                rows = row_iota(WIN)
                source = got_ref[s].astype(F32)
                window[...] = jnp.where((rows >= begin) & (rows < stop), source, 0.0)
                per_part(pl.multiple_of(n * BLOCK, BLOCK), begin - LEFT, stop - LEFT)
                return carry

            lax.fori_loop(
                *utterances(info_ref[5 * s + 2], info_ref[5 * s + 3], LEFT), part, 0
            )
            if per_block is not None:
                per_block(pl.multiple_of(n * BLOCK, BLOCK))

        return n + valid.astype(jnp.int32)

    lax.fori_loop(0, 16, slot, 0)


def hidden_kernel(info_ref, got_ref, kern_ref, norm_ref, *rest):
    h_ref, sw_ref, window, taps = rest[-4:]
    spread_taps(kern_ref, taps)
    mean, inverse = norm_ref[pl.ds(0, 1), :], norm_ref[pl.ds(1, 1), :]
    scale, shift = norm_ref[pl.ds(2, 1), :], norm_ref[pl.ds(3, 1), :]

    def per_part(at, begin, stop):
        acc = conv_block(window, taps)
        for v in range(8):
            place = pl.ds(at + v, 8, stride=8)
            keep = (row_of(v) >= begin) & (row_of(v) < stop)
            h_ref[place, :] = jnp.where(keep, acc[v], h_ref[place, :])

    def per_block(at):
        a = (h_ref[pl.ds(at, BLOCK), :] - mean) * inverse * scale + shift
        sw_ref[pl.ds(at, BLOCK), :] = (a * jax.nn.sigmoid(a)).astype(BF16)

    live_parts(info_ref, got_ref, window, per_part, per_block)


def hidden(info, got, kern, norm, *earlier):
    width = got.shape[2]
    rows = BLOCKS * BLOCK
    return pl.pallas_call(
        hidden_kernel,
        grid=(width // LANES,),
        out_shape=(
            jax.ShapeDtypeStruct((rows, width), F32),
            jax.ShapeDtypeStruct((rows, width), BF16),
        ),
        in_specs=[
            SMEM_SPEC,
            pl.BlockSpec((16, WIN, LANES), lambda c: (0, 0, c)),
            pl.BlockSpec((KER, LANES), lambda c: (0, c)),
            pl.BlockSpec((4, LANES), lambda c: (0, c)),
        ]
        + [pl.BlockSpec(memory_space=pl.ANY)] * len(earlier),
        out_specs=(
            pl.BlockSpec((rows, LANES), lambda c: (0, c)),
            pl.BlockSpec((rows, LANES), lambda c: (0, c)),
        ),
        scratch_shapes=[pltpu.VMEM((WIN, LANES), F32), pltpu.VMEM((8 * KER, LANES), F32)],
        cost_estimate=cost(16),
        name="hidden",
    )(info, got, kern, norm, *earlier)


def terms_kernel(info_ref, got_ref, h_ref, back_ref, norm_ref, out_ref, window, acc_a, acc_x, sums):
    acc_a[...] = jnp.zeros_like(acc_a)
    acc_x[...] = jnp.zeros_like(acc_x)
    sums[...] = jnp.zeros_like(sums)
    mean, inverse = norm_ref[pl.ds(0, 1), :], norm_ref[pl.ds(1, 1), :]
    scale, shift = norm_ref[pl.ds(2, 1), :], norm_ref[pl.ds(3, 1), :]

    def per_part(at, begin, stop):
        das, hats = [], []
        sum_x, sum_1 = sums[pl.ds(0, 8), :], sums[pl.ds(8, 8), :]
        for v in range(8):
            place = pl.ds(at + v, 8, stride=8)
            keep = (row_of(v) >= begin) & (row_of(v) < stop)
            hat = (h_ref[place, :] - mean) * inverse
            a = hat * scale + shift
            sig = jax.nn.sigmoid(a)
            da = back_ref[place, :] * (sig * (1.0 + a * (1.0 - sig)))
            da = jnp.where(keep, da, 0.0)
            hat = jnp.where(keep, hat, 0.0)
            sum_x = sum_x + da * hat
            sum_1 = sum_1 + da
            das.append(da)
            hats.append(hat)
        sums[pl.ds(0, 8), :] = sum_x
        sums[pl.ds(8, 8), :] = sum_1
        xs = [shifted(window, w) for w in range(7)]
        for k in range(KER):
            xs.append(shifted(window, k + 7))
            place = pl.ds(8 * k, 8)
            for acc, rows in ((acc_a, das), (acc_x, hats)):
                terms_k = [rows[v] * xs[v] for v in range(8)]
                while len(terms_k) > 1:
                    terms_k = [p + q for p, q in zip(terms_k[::2], terms_k[1::2])]
                acc[place, :] += terms_k[0]
            xs.pop(0)

    live_parts(info_ref, got_ref, window, per_part)
    out_ref[pl.ds(0, 32), :] = jnp.sum(acc_a[...].reshape(KER, 8, LANES), axis=1)
    out_ref[pl.ds(32, 32), :] = jnp.sum(acc_x[...].reshape(KER, 8, LANES), axis=1)
    out_ref[pl.ds(64, 1), :] = jnp.sum(sums[pl.ds(0, 8), :], axis=0, keepdims=True)
    out_ref[pl.ds(65, 1), :] = jnp.sum(sums[pl.ds(8, 8), :], axis=0, keepdims=True)
    out_ref[pl.ds(66, 6), :] = jnp.zeros((6, LANES), F32)


def terms(info, got, h, back, norm):
    width = got.shape[2]
    return pl.pallas_call(
        terms_kernel,
        grid=(width // LANES,),
        out_shape=jax.ShapeDtypeStruct((72, width), F32),
        in_specs=[
            SMEM_SPEC,
            pl.BlockSpec((16, WIN, LANES), lambda c: (0, 0, c)),
            pl.BlockSpec((BLOCKS * BLOCK, LANES), lambda c: (0, c)),
            pl.BlockSpec((BLOCKS * BLOCK, LANES), lambda c: (0, c)),
            pl.BlockSpec((4, LANES), lambda c: (0, c)),
        ],
        out_specs=pl.BlockSpec((72, LANES), lambda c: (0, c)),
        scratch_shapes=[
            pltpu.VMEM((WIN, LANES), F32),
            pltpu.VMEM((8 * KER, LANES), F32),
            pltpu.VMEM((8 * KER, LANES), F32),
            pltpu.VMEM((16, LANES), F32),
        ],
        cost_estimate=cost(25),
        name="terms",
    )(info, got, h, back, norm)


def zero_step(step):
    if step < 4:
        return [(i, i ^ step) for i in range(16)]
    return [(i, (i + step) % 16) for i in range(16)]


def dp_step(step, row):
    if row:
        return [(i, 4 * (i // 4) + (i + step) % 4) for i in range(16)]
    return [(i, (i + 4 * step) % 16) for i in range(16)]


def add_from(x, axis, steps, *meanwhile):
    parts = [lax.ppermute(x, axis, step) for step in steps]
    parts, meanwhile = lax.optimization_barrier((parts, meanwhile))
    return sum(parts, x), meanwhile


def per_device(frames, segments, targets, cotangent, w_out, kernel, norm_params):
    x, seg, target_row, cot = frames[0, 0], segments[0, 0], targets[0, 0], cotangent[0, 0]
    width = x.shape[1]
    share = width // 16
    zero_id = lax.axis_index("zero")
    core = lax.rem(zero_id, 2)

    groups = jnp.arange(16, dtype=jnp.int32)
    hit = target_row[None, :] == groups[:, None]
    valid = jnp.any(hit, axis=1)
    block_of = jnp.sum(jnp.where(hit, jnp.arange(NB, dtype=jnp.int32)[None, :], 0), axis=1)
    end = BLOCK * jnp.sum((target_row >= 0).astype(jnp.int32))
    ends = [jnp.minimum(jnp.sum((seg < u).astype(jnp.int32)), end) for u in (1, 2)]
    bounds = jnp.stack([jnp.int32(0), ends[0], ends[1], end])
    base = BLOCK * block_of - LEFT
    info = jnp.clip(bounds[None, :] - base[:, None], 0, WIN)
    info = jnp.concatenate([valid.astype(jnp.int32)[:, None], info], axis=1)

    small = jnp.concatenate([kernel, norm_params, jnp.zeros((14, share), BF16)], axis=0)
    small_full = lax.all_to_all(
        jnp.broadcast_to(small[None], (16,) + small.shape), "zero", 0, 0, tiled=True
    )
    small_full = jnp.transpose(small_full, (1, 0, 2)).reshape(48, width).astype(F32)
    kern_full = small_full[:KER]
    send = pack(target_row, x)
    got = lax.all_to_all(send, "dp", 0, 0, tiled=True)

    w_t = lax.all_gather(w_out.T, "zero", axis=0, tiled=True)

    sums = stats(bounds, x, kern_full, send)
    for steps in ((1,), (2,), (4, 8, 12)):
        sums, _ = add_from(sums, "zero", [zero_step(step) for step in steps])
    mine = (groups[None, :] == lax.axis_index("dp"))[..., None]
    info = jnp.where(mine, info[:, None, :], 0).astype(F32).reshape(1, 16 * 16 * 5)
    sums = jnp.concatenate([sums, jnp.pad(info, ((0, 0), (0, width - info.shape[1])))], axis=0)
    back = jnp.dot(cot, w_t, preferred_element_type=F32)
    sums, _ = add_from(sums, "dp", [dp_step(step, True) for step in (1, 2, 3)])
    sums, (back,) = add_from(sums, "dp", [dp_step(step, False) for step in (1, 2, 3)], back)
    info = sums[2, : 16 * 16 * 5].reshape(16, 80)
    info = lax.dynamic_index_in_dim(info, lax.axis_index("dp"), 0, False).astype(jnp.int32)
    frame_count = jnp.float32(BLOCKS * BLOCK * 256)
    mean = sums[0] / frame_count
    var = sums[1] / frame_count - mean * mean
    inverse = lax.rsqrt(var + EPS)
    norm = jnp.stack([mean, inverse, small_full[KER], small_full[KER + 1]])

    frame = lax.broadcasted_iota(jnp.int32, (KER, NB * BLOCK), 1)
    centre = frame - lax.broadcasted_iota(jnp.int32, (KER, NB * BLOCK), 0) + LEFT
    meets = jnp.zeros((KER, NB * BLOCK), jnp.bool_)
    for u in range(3):
        begin, stop = bounds[u], bounds[u + 1]
        within = (jnp.minimum(frame, centre) >= begin) & (jnp.maximum(frame, centre) < stop)
        meets = meets | within
    x_sums = jnp.dot(meets.astype(BF16), x, preferred_element_type=F32)

    half = width // 2
    cot_own = lax.dynamic_slice_in_dim(cot, core * half, half, 1)
    cot_send = lax.dynamic_slice_in_dim(cot, (1 - core) * half, half, 1)
    swap = [(i, i ^ 1) for i in range(16)]
    cot_other = lax.ppermute(cot_send, "zero", swap)

    h, sw = hidden(info, got, kern_full, norm, back, x_sums)
    sw_other = lax.ppermute(sw, "zero", swap)
    contract = (((0,), (0,)), ((), ()))
    term = lax.dot_general(sw, cot_own, contract, preferred_element_type=F32)
    term = term + lax.dot_general(sw_other, cot_other, contract, preferred_element_type=F32)
    term = term.astype(BF16).reshape(16, share, half)
    term = lax.all_to_all(term, "dp", 0, 0, tiled=True)

    grads = terms(info, got, h, back, norm)
    out = lax.dot_general(
        sw, w_t, (((1,), (1,)), ((), ())), preferred_element_type=F32
    ).astype(BF16)

    grads = jnp.concatenate([grads, x_sums], axis=0)
    grads_other = lax.ppermute(
        lax.dynamic_slice_in_dim(grads, (1 - core) * half, half, 1), "zero", swap
    )
    grads = lax.dynamic_slice_in_dim(grads, core * half, half, 1) + grads_other

    term = jnp.sum(term.astype(F32), axis=0)
    both = jnp.concatenate([term, grads], axis=0).reshape(-1, 8, share)
    both = jnp.transpose(both, (1, 0, 2))
    both = lax.dynamic_slice_in_dim(jnp.concatenate([both, both], axis=0), zero_id // 2, 8, 0)
    last = jnp.zeros(both.shape[1:], F32)
    for i in range(8):
        to_owner = [(2 * z + c, 8 * c + (i + z) % 8) for z in range(8) for c in range(2)]
        last = last + lax.ppermute(both[i], "zero", to_owner)
    last = lax.all_to_all(
        jnp.broadcast_to(last[None], (16,) + last.shape), "dp", 0, 0, tiled=True
    )
    part_w = last[:, :share].reshape(width, share)
    grads = jnp.sum(last[:, share:], axis=0)

    own = lax.dynamic_slice_in_dim(norm, zero_id * share, share, 1)
    da_x, hat_x, x_k = grads[:KER], grads[KER : 2 * KER], grads[72 : 72 + KER]
    sum_x, sum_1 = grads[64], grads[65]
    part_k = (own[2] * own[1]) * (da_x - (sum_1 / frame_count) * x_k - (sum_x / frame_count) * hat_x)
    return out[None, None], part_w, part_k, jnp.stack([sum_x, sum_1])


def solution(mesh):
    return jax.shard_map(
        per_device,
        mesh=mesh,
        in_specs=(
            P("dp", "zero", None, None),
            P("dp", "zero", None),
            P("dp", "zero", None),
            P("dp", "zero", None, None),
            P(None, "zero"),
            P(None, "zero"),
            P(None, "zero"),
        ),
        out_specs=(P("dp", "zero", None, None), P(None, "zero"), P(None, "zero"), P(None, "zero")),
        check_vma=False,
    )
```

time: 289 us -> 265 us (0.917); the launches traced: 287 us -> 260 us
  local copies, waits for them, and re-layouts: 65.1 us -> 14.3 us
  starting transfers between devices: 60.2 us -> 89.3 us
  blocking collectives: 25.1 us -> 0 us
  waiting for transfers between devices: 27.8 us -> 47.7 us
  other arithmetic: 17.5 us -> 12.2 us
  Pallas kernels: 54 us -> 57.3 us
    another operation x32 -> x0, local copies, waits for them, and re-layouts: 42.7 us -> none  [per_device(): jnp.stack([(padded[KER - 1 - k:KER - 1 - k + NB * BLOCK] == label) & (lab...]
    ppermute x12 -> x20, starting transfers between devices: 29.6 us -> 57 us  [the longest x8 29.7 us: per_device(): last = last + lax.ppermute(both[i], 'zero', to_owner)]
    all_to_all x1 -> x0, blocking collectives: 25.1 us -> none  [per_device(): lax.all_to_all(both, 'zero', 0, 0, axis_index_groups=[[i for i in range(1...]
    ppermute x12 -> x20, waiting for transfers between devices: 8.87 us -> 31.1 us  [the longest x11 23.3 us: add_from(): parts = [lax.ppermute(x, axis, step) for step in steps]]
    reshape x3 -> x1, local copies, waits for them, and re-layouts: 3.8 us -> 0.39 us  [per_device(): both = jnp.concatenate([term, grads], axis=0).reshape(-1, 8, share)]
    all_to_all x1, waiting for transfers between devices: 15.8 us -> 12.7 us  [per_device(): lax.all_to_all(jnp.broadcast_to(last[None], (16,) + last.shape), 'dp', 0,...]
    unnamed x25 -> x14, local copies, waits for them, and re-layouts: 6.85 us -> 6.27 us
  transfers between devices with their start and end apart: 19 -> 27, of which waited for: 9 -> 12; matrix products, arithmetic and copies ran while one was open for 30% -> 12% of each run, Pallas kernels for 13% -> 15%
where the time goes in v2:
time: 265 us; the launch traced here: 260 us
  starting transfers between devices  89.3 us (34%)
  Pallas kernels  57.3 us (22%)
  waiting for transfers between devices  47.7 us (18%)
  matrix products  22.9 us (9%)
  between operations  16.4 us (6%)
  local copies, waits for them, and re-layouts  14.3 us (5%)
  other arithmetic  12.2 us (5%)
    ppermute x8, starting transfers between devices, per_device(): last = last + lax.ppermute(both[i], 'zero', to_owner)  29.7 us
    ppermute x11, starting transfers between devices, add_from(): parts = [lax.ppermute(x, axis, step) for step in steps]  27.2 us
    pallas_call x1, Pallas kernels, terms(): pl.pallas_call(terms_kernel, grid=(width // LANES,), out_shape=jax.ShapeD...  26.5 us
    ppermute x11, waiting for transfers between devices, add_from(): parts = [lax.ppermute(x, axis, step) for step in steps]  23.3 us
    pallas_call x1, Pallas kernels, hidden(): pl.pallas_call(hidden_kernel, grid=(width // LANES,), out_shape=(jax.Shap...  18.4 us
    all_to_all x1, waiting for transfers between devices, per_device(): lax.all_to_all(jnp.broadcast_to(last[None], (16,) + last.shape), 'dp', 0,...  12.7 us
    pallas_call x1, Pallas kernels, stats(): pl.pallas_call(stats_kernel, grid=(width // LANES,), out_shape=jax.ShapeD...  11.3 us
    all_to_all x1, starting transfers between devices, per_device(): lax.all_to_all(jnp.broadcast_to(last[None], (16,) + last.shape), 'dp', 0,...  8.9 us
  transfers between devices with their start and end apart: 27, of which 12 were waited for; matrix products, arithmetic and copies ran while one was open for 12% of the time, Pallas kernels for 15%

profile of v2, /device:TPU:8, one launch (start us, length us, event | category | flops | bytes accessed | tf_op | source)
XLA Modules:
  0.0 260.1 jit_solution(4462131733946412150)
XLA Ops:
  7.2 0.7 all-gather.2.cloned.1.call-update
  8.0 0.8 maximum_maximum_fusion
  8.8 0.7 broadcast_in_dim.41
  9.5 8.6 %all-to-all-start = ((bf16[16,48,96]{2,1,0:T(8,128)(2,1)}), bf16[16,48,96]{2,1,0:T(8,128)(2,1)S(1)}, u32[]{:S(2)}, u32[]{:S(2)}) async-start(bf16[16,48,96]{2,1,0:T(8,128)(2,1)} %broadcast_in_dim.41), calls=%async_computation | async-start | bytes 393216 | tf_op jit(solution)/shard_map/all_to_all | solution.py:333
  18.1 1.3 fusion.42
  20.0 1.3 fusion.38
  22.7 0.8 fusion.36
  23.4 0.8 select_reduce_fusion
  24.2 1.7 copy-done.2
  25.9 0.7 copy-done.3
  26.5 1.2 pack.1._
  27.8 2.2 copy-done.1
  30.6 7.4 %all-to-all-start.1 = ((bf16[16,96,1536]{2,1,0:T(8,128)(2,1)}), bf16[16,96,1536]{2,1,0:T(8,128)(2,1)}, u32[]{:S(2)}, u32[]{:S(2)}) async-start(bf16[16,96,1536]{2,1,0:T(8,128)(2,1)} %copy-done.1), calls=%async_computation.1 | async-start | bytes 9437184 | tf_op jit(solution)/shard_map/all_to_all | solution.py:339
  38.3 0.8 slice.76.kern_ref
  39.1 11.3 %stats.1 = f32[2,1536]{1,0:T(2,128)} custom-call(s32[4]{0:T(128)} %copy-done.5, bf16[768,1536]{1,0:T(8,128)(2,1)} %bitcast.59, f32[32,1536]{1,0:T(8,128)} %slice.76.kern_ref, bf16[16,96,1536]{2,1,0:T(8,128)(2,1)} %copy-done.1), custom_call_target="tpu_custom_call" | custom-call | flops 16499999744 | bytes 1000000 | tf_op jit(solution)/shard_map/stats/pallas_call | solution.py:134
  50.4 0.7 collective-permute-start
  51.1 1.0 collective-permute-done
  52.1 0.7 add.109
  52.8 11.3 %collective-permute-start.1 = (f32[2,1536]{1,0:T(2,128)S(1)}, f32[2,1536]{1,0:T(2,128)S(1)}, u32[]{:S(2)}, u32[]{:S(2)}) collective-permute-start(f32[2,1536]{1,0:T(2,128)S(1)} %add.109), channel_id=1, source_target_pairs={{0,2},{1,3},{2,0},{3,1},{4,6},{5,7},{6,4},{7,5},{8,10},{9,11},{10,... | collective-permute-start | bytes 36872 | tf_op jit(solution)/shard_map/ppermute | solution.py:309
  64.1 1.7 collective-permute-done.1
  65.8 1.3 collective-permute-start.2
  67.0 4.6 %collective-permute-start.3 = (f32[2,1536]{1,0:T(2,128)S(1)}, f32[2,1536]{1,0:T(2,128)S(1)}, u32[]{:S(2)}, u32[]{:S(2)}) collective-permute-start(f32[2,1536]{1,0:T(2,128)S(1)} %add.110), channel_id=1, source_target_pairs={{0,8},{1,9},{2,10},{3,11},{4,12},{5,13},{6,14},{7,15},{8,0},{9,1},... | collective-permute-start | bytes 36872 | tf_op jit(solution)/shard_map/ppermute | solution.py:309
  71.6 1.7 collective-permute-start.4
  73.6 1.1 collective-permute-done.3
  74.6 1.6 collective-permute-done.4
  76.3 1.1 collective-permute-start.5
  77.3 2.2 collective-permute-start.7
  79.5 2.8 %fusion.22.rest_1_ = f32[32,1536]{1,0:T(8,128)} fusion(s32[]{:T(128)} %mul.59, s32[]{:T(128)} %min.24, s32[]{:T(128)} %min.23, bf16[1,1,768,1536]{3,2,1,0:T(8,128)(2,1)} %param.7), kind=kOutput, calls=%fused_computation.40 | convolution fusion | flops 75866112 | bytes 2555916 | tf_op jit(solution)/shard_map/dot_general | solution.py:367
  82.6 17.8 %collective-permute-done.6 = f32[3,1536]{1,0:T(4,128)S(1)} collective-permute-done((f32[3,1536]{1,0:T(4,128)S(1)}, f32[3,1536]{1,0:T(4,128)S(1)}, u32[]{:S(2)}, u32[]{:S(2)}) %collective-permute-start.6) | collective-permute-done | bytes 18464 | tf_op jit(solution)/shard_map/ppermute | solution.py:309
  100.5 3.2 %collective-permute-start.9 = (f32[3,1536]{1,0:T(4,128)S(1)}, f32[3,1536]{1,0:T(4,128)S(1)}, u32[]{:S(2)}, u32[]{:S(2)}) collective-permute-start(f32[3,1536]{1,0:T(4,128)S(1)} %add_add_fusion.2), channel_id=1, source_target_pairs={{0,128},{16,144},{32,160},{48,176},{64,192},{80,208},{96,224},{112... | collective-permute-start | bytes 55304 | tf_op jit(solution)/shard_map/ppermute | solution.py:309
  103.6 1.3 collective-permute-start.10
  104.9 6.6 %fusion.1.rest_0_.back_ref = f32[512,1536]{1,0:T(8,128)} fusion(bf16[1536,1536]{1,0:T(8,128)(2,1)} %all-gather.2.cloned.1.call-done, bf16[1,1,512,1536]{3,2,1,0:T(8,128)(2,1)S(1)} %copy-done), kind=kOutput, calls=%fused_computation.6 | convolution fusion | flops 2415919104 | bytes 9437184 | tf_op jit(solution)/shard_map/dot_general | solution.py:349
  112.2 0.6 pad_maximum_fusion.1.norm_ref
  112.8 18.4 %hidden.1 = (f32[512,1536]{1,0:T(8,128)}, bf16[512,1536]{1,0:T(8,128)(2,1)}) custom-call(s32[80]{0:T(128)} %fusion.44.info_ref, bf16[16,96,1536]{2,1,0:T(8,128)(2,1)} %all-to-all-done.1.got_ref, f32[32,1536]{1,0:T(8,128)} %slice.76.kern_ref, f32[4,1536]{1,0:T(4,128)} %pad_maximum_fusion.1.norm_ref, f32[512,1536]{1,0:T(8,128)} %fusion.1.rest_0_.back_ref, ...), custom_call_target="tpu_custom_call" | custom-call | flops 17600000000 | bytes 1000000 | tf_op jit(solution)/shard_map/hidden/pallas_call | solution.py:203
  131.2 0.9 dynamic-slice_bitcast_fusion
  132.6 2.8 %fusion.4 = f32[1536,768]{1,0:T(8,128)S(1)} fusion(bf16[512,1536]{1,0:T(8,128)(2,1)} %get-tuple-element.26, bf16[1,1,512,1536]{3,2,1,0:T(8,128)(2,1)S(1)} %copy-done, s32[]{:T(128)S(6)} %select_n.42), kind=kOutput, calls=%fused_computation.12 | convolution fusion | flops 1207959552 | bytes 7077892 | tf_op jit(solution)/shard_map/dot_general | solution.py:378
  135.5 0.6 collective-permute-done.12
  136.1 4.1 %add_convert_fusion = bf16[1536,768]{1,0:T(8,128)(2,1)} fusion(f32[1536,768]{1,0:T(8,128)S(1)} %fusion.4, bf16[512,1536]{1,0:T(8,128)(2,1)S(1)} %collective-permute-done.11, bf16[512,768]{1,0:T(8,128)(2,1)} %collective-permute-done.12), kind=kOutput, calls=%fused_computation.1 | convolution fusion | flops 1210318848 | bytes 9437184 | tf_op jit(solution)/shard_map/dot_general | solution.py:379
  140.1 6.9 %all-to-all-start.2 = ((bf16[16,96,768]{2,1,0:T(8,128)(2,1)}), bf16[16,96,768]{2,1,0:T(8,128)(2,1)}, u32[]{:S(2)}, u32[]{:S(2)}) async-start(bf16[16,96,768]{2,1,0:T(8,128)(2,1)} %bitcast.64), calls=%async_computation.2 | async-start | bytes 4718592 | tf_op jit(solution)/shard_map/all_to_all | solution.py:381
  147.0 26.5 %terms.1 = f32[72,1536]{1,0:T(8,128)} custom-call(s32[80]{0:T(128)} %fusion.44.info_ref, bf16[16,96,1536]{2,1,0:T(8,128)(2,1)} %all-to-all-done.1.got_ref, f32[512,1536]{1,0:T(8,128)} %get-tuple-element.27.h_ref, f32[512,1536]{1,0:T(8,128)} %fusion.1.rest_0_.back_ref, f32[4,1536]{1,0:T(4,128)} %pad_maximum_fusion.1.norm_ref), custom_call_target="tpu_custom_call" | custom-call | flops 27499999232 | bytes 1000000 | tf_op jit(solution)/shard_map/terms/pallas_call | solution.py:273
  173.5 1.0 fusion.7
  174.6 1.6 collective-permute-done.13
  176.2 1.0 fusion.9
  177.2 2.6 all-to-all-done.2
  179.7 2.0 convert_reduce_fusion
  182.5 0.5 fusion.47
  183.0 5.9 %collective-permute-start.21 = (f32[200,96]{1,0:T(8,128)S(1)}, f32[200,96]{1,0:T(8,128)S(1)}, u32[]{:S(2)}, u32[]{:S(2)}) collective-permute-start(f32[200,96]{1,0:T(8,128)S(1)} %bitcast.74), channel_id=1, source_target_pairs={{0,7},{1,15},{2,0},{3,8},{4,1},{5,9},{6,2},{7,10},{8,3},{9,11},{10... | collective-permute-start | bytes 230408 | tf_op jit(solution)/shard_map/ppermute | solution.py:401
  189.0 7.0 %collective-permute-start.20 = (f32[200,96]{1,0:T(8,128)S(1)}, f32[200,96]{1,0:T(8,128)S(1)}, u32[]{:S(2)}, u32[]{:S(2)}) collective-permute-start(f32[200,96]{1,0:T(8,128)S(1)} %bitcast.73), channel_id=1, source_target_pairs={{0,6},{1,14},{2,7},{3,15},{4,0},{5,8},{6,1},{7,9},{8,2},{9,10},{10... | collective-permute-start | bytes 230408 | tf_op jit(solution)/shard_map/ppermute | solution.py:401
  196.0 1.9 collective-permute-start.19
  197.9 0.7 collective-permute-start.18
  198.6 2.5 collective-permute-start.17
  201.2 5.6 %collective-permute-start.16 = (f32[200,96]{1,0:T(8,128)S(1)}, f32[200,96]{1,0:T(8,128)S(1)}, u32[]{:S(2)}, u32[]{:S(2)}) collective-permute-start(f32[200,96]{1,0:T(8,128)S(1)} %bitcast.69), channel_id=1, source_target_pairs={{0,2},{1,10},{2,3},{3,11},{4,4},{5,12},{6,5},{7,13},{8,6},{9,14},{... | collective-permute-start | bytes 230408 | tf_op jit(solution)/shard_map/ppermute | solution.py:401
  206.7 0.7 collective-permute-start.14
  207.4 5.4 %collective-permute-start.15 = (f32[200,96]{1,0:T(8,128)S(1)}, f32[200,96]{1,0:T(8,128)S(1)}, u32[]{:S(2)}, u32[]{:S(2)}) collective-permute-start(f32[200,96]{1,0:T(8,128)S(1)} %bitcast.67), channel_id=1, source_target_pairs={{0,1},{1,9},{2,2},{3,10},{4,3},{5,11},{6,4},{7,12},{8,5},{9,13},{1... | collective-permute-start | bytes 230408 | tf_op jit(solution)/shard_map/ppermute | solution.py:401
  212.9 3.9 %collective-permute-done.16 = f32[200,96]{1,0:T(8,128)S(1)} collective-permute-done((f32[200,96]{1,0:T(8,128)S(1)}, f32[200,96]{1,0:T(8,128)S(1)}, u32[]{:S(2)}, u32[]{:S(2)}) %collective-permute-start.16) | collective-permute-done | bytes 76832 | tf_op jit(solution)/shard_map/ppermute | solution.py:401
  216.8 2.4 collective-permute-done.15
  219.3 1.3 broadcast_in_dim.69
  220.6 8.9 %all-to-all-start.3 = ((f32[16,200,96]{1,2,0:T(8,128)}), f32[16,200,96]{1,2,0:T(8,128)S(1)}, u32[]{:S(2)}, u32[]{:S(2)}) async-start(f32[16,200,96]{1,2,0:T(8,128)} %broadcast_in_dim.69), calls=%async_computation.3 | async-start | bytes 3145728 | tf_op jit(solution)/shard_map/all_to_all | solution.py:402
  229.5 0.7 constant_dynamic-slice_fusion
  230.3 6.6 %fusion = bf16[1,1,512,1536]{3,2,1,0:T(8,128)(2,1)} fusion(bf16[512,1536]{1,0:T(8,128)(2,1)} %get-tuple-element.26, bf16[1536,1536]{1,0:T(8,128)(2,1)} %all-gather.2.cloned.1.call-done), kind=kOutput, calls=%fused_computation.3 | convolution fusion | flops 2416705536 | bytes 7864320 | tf_op jit(solution)/shard_map/dot_general | solution.py:384
  236.9 12.7 %all-to-all-done.3 = f32[16,200,96]{1,2,0:T(8,128)S(1)} async-done(((f32[16,200,96]{1,2,0:T(8,128)}), f32[16,200,96]{1,2,0:T(8,128)S(1)}, u32[]{:S(2)}, u32[]{:S(2)}) %all-to-all-start.3) | async-done | bytes 1228832 | tf_op jit(solution)/shard_map/all_to_all | solution.py:402
  250.6 1.1 reshape.84
  251.9 0.7 copy.71
  252.6 0.6 copy.72
  (69 shorter events, 5.2 us)
Async XLA Ops:
  7.2 97.8 %copy-start = (bf16[1,1,512,1536]{3,2,1,0:T(8,128)(2,1)S(1)}, bf16[1,1,512,1536]{3,2,1,0:T(8,128)(2,1)}, u32[]{:S(2)}) copy-start(bf16[1,1,512,1536]{3,2,1,0:T(8,128)(2,1)} %param.10) | copy-start | bytes 4718596
  7.2 97.7 %all-gather.2.cloned.1.call-start = ((), (), s32[]{:S(2)}) async-start(), calls=%async_computation.4 | async-start | bytes 5013504 | tf_op jit(solution)/shard_map/all_gather | solution.py:341
  9.5 20.7 %all-to-all-start = ((bf16[16,48,96]{2,1,0:T(8,128)(2,1)}), bf16[16,48,96]{2,1,0:T(8,128)(2,1)S(1)}, u32[]{:S(2)}, u32[]{:S(2)}) async-start(bf16[16,48,96]{2,1,0:T(8,128)(2,1)} %broadcast_in_dim.41), calls=%async_computation | async-start | bytes 393216 | tf_op jit(solution)/shard_map/all_to_all | solution.py:333
  24.2 1.7 copy-start.2
  25.9 0.7 copy-start.3
  27.8 2.2 copy-start.1
  30.1 0.6 copy-start.5
  30.6 82.1 %all-to-all-start.1 = ((bf16[16,96,1536]{2,1,0:T(8,128)(2,1)}), bf16[16,96,1536]{2,1,0:T(8,128)(2,1)}, u32[]{:S(2)}, u32[]{:S(2)}) async-start(bf16[16,96,1536]{2,1,0:T(8,128)(2,1)} %copy-done.1), calls=%async_computation.1 | async-start | bytes 9437184 | tf_op jit(solution)/shard_map/all_to_all | solution.py:339
  50.4 1.7 collective-permute-start
  52.8 13.0 %collective-permute-start.1 = (f32[2,1536]{1,0:T(2,128)S(1)}, f32[2,1536]{1,0:T(2,128)S(1)}, u32[]{:S(2)}, u32[]{:S(2)}) collective-permute-start(f32[2,1536]{1,0:T(2,128)S(1)} %add.109), channel_id=1, source_target_pairs={{0,2},{1,3},{2,0},{3,1},{4,6},{5,7},{6,4},{7,5},{8,10},{9,11},{10,... | collective-permute-start | bytes 36872 | tf_op jit(solution)/shard_map/ppermute | solution.py:309
  65.8 7.8 %collective-permute-start.2 = (f32[2,1536]{1,0:T(2,128)S(1)}, f32[2,1536]{1,0:T(2,128)S(1)}, u32[]{:S(2)}, u32[]{:S(2)}) collective-permute-start(f32[2,1536]{1,0:T(2,128)S(1)} %add.110), channel_id=1, source_target_pairs={{0,4},{1,5},{2,6},{3,7},{4,8},{5,9},{6,10},{7,11},{8,12},{9,13},{1... | collective-permute-start | bytes 36872 | tf_op jit(solution)/shard_map/ppermute | solution.py:309
  67.0 7.6 %collective-permute-start.3 = (f32[2,1536]{1,0:T(2,128)S(1)}, f32[2,1536]{1,0:T(2,128)S(1)}, u32[]{:S(2)}, u32[]{:S(2)}) collective-permute-start(f32[2,1536]{1,0:T(2,128)S(1)} %add.110), channel_id=1, source_target_pairs={{0,8},{1,9},{2,10},{3,11},{4,12},{5,13},{6,14},{7,15},{8,0},{9,1},... | collective-permute-start | bytes 36872 | tf_op jit(solution)/shard_map/ppermute | solution.py:309
  71.6 4.6 %collective-permute-start.4 = (f32[2,1536]{1,0:T(2,128)S(1)}, f32[2,1536]{1,0:T(2,128)S(1)}, u32[]{:S(2)}, u32[]{:S(2)}) collective-permute-start(f32[2,1536]{1,0:T(2,128)S(1)} %add.110), channel_id=1, source_target_pairs={{0,12},{1,13},{2,14},{3,15},{4,0},{5,1},{6,2},{7,3},{8,4},{9,5},{1... | collective-permute-start | bytes 36872 | tf_op jit(solution)/shard_map/ppermute | solution.py:309
  76.3 6.4 %collective-permute-start.5 = (f32[3,1536]{1,0:T(4,128)S(1)}, f32[3,1536]{1,0:T(4,128)S(1)}, u32[]{:S(2)}, u32[]{:S(2)}) collective-permute-start(f32[3,1536]{1,0:T(4,128)S(1)} %select_maximum_fusion), channel_id=1, source_target_pairs={{0,16},{16,32},{32,48},{48,0},{64,80},{80,96},{96,112},{112,64},{1... | collective-permute-start | bytes 55304 | tf_op jit(solution)/shard_map/ppermute | solution.py:309
  77.3 23.1 %collective-permute-start.6 = (f32[3,1536]{1,0:T(4,128)S(1)}, f32[3,1536]{1,0:T(4,128)S(1)}, u32[]{:S(2)}, u32[]{:S(2)}) collective-permute-start(f32[3,1536]{1,0:T(4,128)S(1)} %select_maximum_fusion), channel_id=1, source_target_pairs={{0,32},{16,48},{32,0},{48,16},{64,96},{80,112},{96,64},{112,80},{1... | collective-permute-start | bytes 55304 | tf_op jit(solution)/shard_map/ppermute | solution.py:309
  77.3 23.1 %collective-permute-start.7 = (f32[3,1536]{1,0:T(4,128)S(1)}, f32[3,1536]{1,0:T(4,128)S(1)}, u32[]{:S(2)}, u32[]{:S(2)}) collective-permute-start(f32[3,1536]{1,0:T(4,128)S(1)} %select_maximum_fusion), channel_id=1, source_target_pairs={{0,48},{16,0},{32,16},{48,32},{64,112},{80,64},{96,80},{112,96},{1... | collective-permute-start | bytes 55304 | tf_op jit(solution)/shard_map/ppermute | solution.py:309
  100.4 11.1 %collective-permute-start.8 = (f32[3,1536]{1,0:T(4,128)S(1)}, f32[3,1536]{1,0:T(4,128)S(1)}, u32[]{:S(2)}, u32[]{:S(2)}) collective-permute-start(f32[3,1536]{1,0:T(4,128)S(1)} %add_add_fusion.2), channel_id=1, source_target_pairs={{0,64},{16,80},{32,96},{48,112},{64,128},{80,144},{96,160},{112,17... | collective-permute-start | bytes 55304 | tf_op jit(solution)/shard_map/ppermute | solution.py:309
  100.5 11.0 %collective-permute-start.9 = (f32[3,1536]{1,0:T(4,128)S(1)}, f32[3,1536]{1,0:T(4,128)S(1)}, u32[]{:S(2)}, u32[]{:S(2)}) collective-permute-start(f32[3,1536]{1,0:T(4,128)S(1)} %add_add_fusion.2), channel_id=1, source_target_pairs={{0,128},{16,144},{32,160},{48,176},{64,192},{80,208},{96,224},{112... | collective-permute-start | bytes 55304 | tf_op jit(solution)/shard_map/ppermute | solution.py:309
  103.6 7.8 %collective-permute-start.10 = (f32[3,1536]{1,0:T(4,128)S(1)}, f32[3,1536]{1,0:T(4,128)S(1)}, u32[]{:S(2)}, u32[]{:S(2)}) collective-permute-start(f32[3,1536]{1,0:T(4,128)S(1)} %add_add_fusion.2), channel_id=1, source_target_pairs={{0,192},{16,208},{32,224},{48,240},{64,0},{80,16},{96,32},{112,48}... | collective-permute-start | bytes 55304 | tf_op jit(solution)/shard_map/ppermute | solution.py:309
  131.2 4.9 %collective-permute-start.11 = (bf16[512,1536]{1,0:T(8,128)(2,1)}, bf16[512,1536]{1,0:T(8,128)(2,1)S(1)}, u32[]{:S(2)}, u32[]{:S(2)}) collective-permute-start(bf16[512,1536]{1,0:T(8,128)(2,1)} %get-tuple-element.26), channel_id=1, source_target_pairs={{0,1},{1,0},{2,3},{3,2},{4,5},{5,4},{6,7},{7,6},{8,9},{9,8},{10,11... | collective-permute-start | bytes 4718600 | tf_op jit(solution)/shard_map/ppermute | solution.py:376
  132.1 3.9 %collective-permute-start.12 = (bf16[512,768]{1,0:T(8,128)(2,1)}, bf16[512,768]{1,0:T(8,128)(2,1)}, u32[]{:S(2)}, u32[]{:S(2)}) collective-permute-start(bf16[512,768]{1,0:T(8,128)(2,1)} %dynamic-slice_bitcast_fusion), channel_id=1, source_target_pairs={{0,1},{1,0},{2,3},{3,2},{4,5},{5,4},{6,7},{7,6},{8,9},{9,8},{10,11... | collective-permute-start | bytes 2359304 | tf_op jit(solution)/shard_map/ppermute | solution.py:373
  140.1 39.6 %all-to-all-start.2 = ((bf16[16,96,768]{2,1,0:T(8,128)(2,1)}), bf16[16,96,768]{2,1,0:T(8,128)(2,1)}, u32[]{:S(2)}, u32[]{:S(2)}) async-start(bf16[16,96,768]{2,1,0:T(8,128)(2,1)} %bitcast.64), calls=%async_computation.2 | async-start | bytes 4718592 | tf_op jit(solution)/shard_map/all_to_all | solution.py:381
  147.0 26.5 %copy-start.4 = (f32[32,1536]{1,0:T(8,128)S(1)}, f32[32,1536]{1,0:T(8,128)}, u32[]{:S(2)}) copy-start(f32[32,1536]{1,0:T(8,128)} %fusion.22.rest_1_) | copy-start | bytes 589828
  174.5 1.7 collective-permute-start.13
  183.0 18.1 %collective-permute-start.21 = (f32[200,96]{1,0:T(8,128)S(1)}, f32[200,96]{1,0:T(8,128)S(1)}, u32[]{:S(2)}, u32[]{:S(2)}) collective-permute-start(f32[200,96]{1,0:T(8,128)S(1)} %bitcast.74), channel_id=1, source_target_pairs={{0,7},{1,15},{2,0},{3,8},{4,1},{5,9},{6,2},{7,10},{8,3},{9,11},{10... | collective-permute-start | bytes 230408 | tf_op jit(solution)/shard_map/ppermute | solution.py:401
  189.0 17.8 %collective-permute-start.20 = (f32[200,96]{1,0:T(8,128)S(1)}, f32[200,96]{1,0:T(8,128)S(1)}, u32[]{:S(2)}, u32[]{:S(2)}) collective-permute-start(f32[200,96]{1,0:T(8,128)S(1)} %bitcast.73), channel_id=1, source_target_pairs={{0,6},{1,14},{2,7},{3,15},{4,0},{5,8},{6,1},{7,9},{8,2},{9,10},{10... | collective-permute-start | bytes 230408 | tf_op jit(solution)/shard_map/ppermute | solution.py:401
  196.0 11.5 %collective-permute-start.19 = (f32[200,96]{1,0:T(8,128)S(1)}, f32[200,96]{1,0:T(8,128)S(1)}, u32[]{:S(2)}, u32[]{:S(2)}) collective-permute-start(f32[200,96]{1,0:T(8,128)S(1)} %bitcast.72), channel_id=1, source_target_pairs={{0,5},{1,13},{2,6},{3,14},{4,7},{5,15},{6,0},{7,8},{8,1},{9,9},{10... | collective-permute-start | bytes 230408 | tf_op jit(solution)/shard_map/ppermute | solution.py:401
  197.9 15.0 %collective-permute-start.18 = (f32[200,96]{1,0:T(8,128)S(1)}, f32[200,96]{1,0:T(8,128)S(1)}, u32[]{:S(2)}, u32[]{:S(2)}) collective-permute-start(f32[200,96]{1,0:T(8,128)S(1)} %bitcast.71), channel_id=1, source_target_pairs={{0,4},{1,12},{2,5},{3,13},{4,6},{5,14},{6,7},{7,15},{8,0},{9,8},{1... | collective-permute-start | bytes 230408 | tf_op jit(solution)/shard_map/ppermute | solution.py:401
  198.6 14.3 %collective-permute-start.17 = (f32[200,96]{1,0:T(8,128)S(1)}, f32[200,96]{1,0:T(8,128)S(1)}, u32[]{:S(2)}, u32[]{:S(2)}) collective-permute-start(f32[200,96]{1,0:T(8,128)S(1)} %bitcast.70), channel_id=1, source_target_pairs={{0,3},{1,11},{2,4},{3,12},{4,5},{5,13},{6,6},{7,14},{8,7},{9,15},{... | collective-permute-start | bytes 230408 | tf_op jit(solution)/shard_map/ppermute | solution.py:401
  201.2 15.6 %collective-permute-start.16 = (f32[200,96]{1,0:T(8,128)S(1)}, f32[200,96]{1,0:T(8,128)S(1)}, u32[]{:S(2)}, u32[]{:S(2)}) collective-permute-start(f32[200,96]{1,0:T(8,128)S(1)} %bitcast.69), channel_id=1, source_target_pairs={{0,2},{1,10},{2,3},{3,11},{4,4},{5,12},{6,5},{7,13},{8,6},{9,14},{... | collective-permute-start | bytes 230408 | tf_op jit(solution)/shard_map/ppermute | solution.py:401
  206.7 10.0 %collective-permute-start.14 = (f32[200,96]{1,0:T(8,128)S(1)}, f32[200,96]{1,0:T(8,128)S(1)}, u32[]{:S(2)}, u32[]{:S(2)}) collective-permute-start(f32[200,96]{1,0:T(8,128)S(1)} %bitcast.68), channel_id=1, source_target_pairs={{0,0},{1,8},{2,1},{3,9},{4,2},{5,10},{6,3},{7,11},{8,4},{9,12},{10... | collective-permute-start | bytes 230408 | tf_op jit(solution)/shard_map/ppermute | solution.py:401
  207.4 11.7 %collective-permute-start.15 = (f32[200,96]{1,0:T(8,128)S(1)}, f32[200,96]{1,0:T(8,128)S(1)}, u32[]{:S(2)}, u32[]{:S(2)}) collective-permute-start(f32[200,96]{1,0:T(8,128)S(1)} %bitcast.67), channel_id=1, source_target_pairs={{0,1},{1,9},{2,2},{3,10},{4,3},{5,11},{6,4},{7,12},{8,5},{9,13},{1... | collective-permute-start | bytes 230408 | tf_op jit(solution)/shard_map/ppermute | solution.py:401
  220.6 28.9 %all-to-all-start.3 = ((f32[16,200,96]{1,2,0:T(8,128)}), f32[16,200,96]{1,2,0:T(8,128)S(1)}, u32[]{:S(2)}, u32[]{:S(2)}) async-start(f32[16,200,96]{1,2,0:T(8,128)} %broadcast_in_dim.69), calls=%async_computation.3 | async-start | bytes 3145728 | tf_op jit(solution)/shard_map/all_to_all | solution.py:402
Sparse Core Ops, SparseCore 0:
  9.8 45.6 all-gather.1

commit v3 on v2

--- a/solution.py
+++ b/solution.py
@@ -58,6 +58,51 @@
     top = row + BLOCK - 1
     high = (first <= top).astype(jnp.int32) + (second <= top).astype(jnp.int32)
     return low, high + 1
+
+
+def places_kernel(target_ref, group_ref, segment_ref, bounds_ref, row_ref):
+    live = jnp.int32(0)
+    for slot in range(NB):
+        live = live + (target_ref[slot] >= 0).astype(jnp.int32)
+    segment = segment_ref[...]
+    bounds = [jnp.int32(0)]
+    for u in (1, 2):
+        bounds.append(jnp.minimum(jnp.sum((segment < u).astype(jnp.int32)), BLOCK * live))
+    bounds.append(BLOCK * live)
+    for u in range(4):
+        bounds_ref[u] = bounds[u]
+
+    lane = lax.broadcasted_iota(jnp.int32, row_ref.shape, 1)
+    group = sum((lane >= 96 * m).astype(jnp.int32) for m in range(1, 16))
+    lane = lane - 96 * group
+    source = sum((lane >= 5 * m).astype(jnp.int32) for m in range(1, 17))
+    field = lane - 5 * source
+    valid = jnp.zeros(row_ref.shape, jnp.int32)
+    block = jnp.zeros(row_ref.shape, jnp.int32)
+    for slot in range(NB):
+        here = group == target_ref[slot]
+        valid = jnp.where(here, 1, valid)
+        block = jnp.where(here, slot, block)
+    bound = jnp.zeros(row_ref.shape, jnp.int32)
+    for u in range(4):
+        bound = jnp.where(field == u + 1, bounds[u], bound)
+    bound = jnp.clip(bound - (BLOCK * block - LEFT), 0, WIN)
+    value = jnp.where(field == 0, valid, bound)
+    row_ref[...] = jnp.where(source == group_ref[0], value, 0).astype(F32)
+
+
+def places(target_row, group, segment, width):
+    return pl.pallas_call(
+        places_kernel,
+        out_shape=(
+            jax.ShapeDtypeStruct((4,), jnp.int32),
+            jax.ShapeDtypeStruct((1, width), F32),
+        ),
+        in_specs=[SMEM_SPEC, SMEM_SPEC, pl.BlockSpec(memory_space=pltpu.VMEM)],
+        out_specs=(SMEM_SPEC, pl.BlockSpec(memory_space=pltpu.VMEM)),
+        cost_estimate=cost(1),
+        name="places",
+    )(target_row, group, segment)
 
 
 def pack_kernel(target_ref, x_ref, out_ref):
@@ -318,44 +363,18 @@
     zero_id = lax.axis_index("zero")
     core = lax.rem(zero_id, 2)
 
-    groups = jnp.arange(16, dtype=jnp.int32)
-    hit = target_row[None, :] == groups[:, None]
-    valid = jnp.any(hit, axis=1)
-    block_of = jnp.sum(jnp.where(hit, jnp.arange(NB, dtype=jnp.int32)[None, :], 0), axis=1)
-    end = BLOCK * jnp.sum((target_row >= 0).astype(jnp.int32))
-    ends = [jnp.minimum(jnp.sum((seg < u).astype(jnp.int32)), end) for u in (1, 2)]
-    bounds = jnp.stack([jnp.int32(0), ends[0], ends[1], end])
-    base = BLOCK * block_of - LEFT
-    info = jnp.clip(bounds[None, :] - base[:, None], 0, WIN)
-    info = jnp.concatenate([valid.astype(jnp.int32)[:, None], info], axis=1)
-
+    bounds, info = places(
+        target_row, lax.axis_index("dp").reshape(1), seg.reshape(NB // 2, 2 * BLOCK), width
+    )
+    send = pack(target_row, x)
     small = jnp.concatenate([kernel, norm_params, jnp.zeros((14, share), BF16)], axis=0)
-    small_full = lax.all_to_all(
-        jnp.broadcast_to(small[None], (16,) + small.shape), "zero", 0, 0, tiled=True
-    )
+    send, small = lax.optimization_barrier((send, small))
+    got = lax.all_to_all(send, "dp", 0, 0, tiled=True)
+    small_full = lax.all_gather(small, "zero", axis=0)
     small_full = jnp.transpose(small_full, (1, 0, 2)).reshape(48, width).astype(F32)
     kern_full = small_full[:KER]
-    send = pack(target_row, x)
-    got = lax.all_to_all(send, "dp", 0, 0, tiled=True)
 
     w_t = lax.all_gather(w_out.T, "zero", axis=0, tiled=True)
-
-    sums = stats(bounds, x, kern_full, send)
-    for steps in ((1,), (2,), (4, 8, 12)):
-        sums, _ = add_from(sums, "zero", [zero_step(step) for step in steps])
-    mine = (groups[None, :] == lax.axis_index("dp"))[..., None]
-    info = jnp.where(mine, info[:, None, :], 0).astype(F32).reshape(1, 16 * 16 * 5)
-    sums = jnp.concatenate([sums, jnp.pad(info, ((0, 0), (0, width - info.shape[1])))], axis=0)
-    back = jnp.dot(cot, w_t, preferred_element_type=F32)
-    sums, _ = add_from(sums, "dp", [dp_step(step, True) for step in (1, 2, 3)])
-    sums, (back,) = add_from(sums, "dp", [dp_step(step, False) for step in (1, 2, 3)], back)
-    info = sums[2, : 16 * 16 * 5].reshape(16, 80)
-    info = lax.dynamic_index_in_dim(info, lax.axis_index("dp"), 0, False).astype(jnp.int32)
-    frame_count = jnp.float32(BLOCKS * BLOCK * 256)
-    mean = sums[0] / frame_count
-    var = sums[1] / frame_count - mean * mean
-    inverse = lax.rsqrt(var + EPS)
-    norm = jnp.stack([mean, inverse, small_full[KER], small_full[KER + 1]])
 
     frame = lax.broadcasted_iota(jnp.int32, (KER, NB * BLOCK), 1)
     centre = frame - lax.broadcasted_iota(jnp.int32, (KER, NB * BLOCK), 0) + LEFT
@@ -364,13 +383,36 @@
         begin, stop = bounds[u], bounds[u + 1]
         within = (jnp.minimum(frame, centre) >= begin) & (jnp.maximum(frame, centre) < stop)
         meets = meets | within
+
+    half = width // 2
+    column = lax.broadcasted_iota(jnp.int32, (width, half), 0)
+    place = lax.broadcasted_iota(jnp.int32, (width, half), 1)
+    even = column == place + share * (place // share)
+    odd = column == place + share * (place // share) + share
+    own_columns = jnp.where(core == 0, even, odd).astype(BF16)
+    other_columns = jnp.where(core == 0, odd, even).astype(BF16)
+    swap = [(i, i ^ 1) for i in range(16)]
+
+    sums = stats(bounds, x, kern_full, send)
+    for steps in ((1,), (2,), (4, 8, 12)):
+        sums, _ = add_from(sums, "zero", [zero_step(step) for step in steps])
+    sums = jnp.concatenate([sums, info], axis=0)
+    sums, cot, x = lax.optimization_barrier((sums, cot, x))
     x_sums = jnp.dot(meets.astype(BF16), x, preferred_element_type=F32)
-
-    half = width // 2
-    cot_own = lax.dynamic_slice_in_dim(cot, core * half, half, 1)
-    cot_send = lax.dynamic_slice_in_dim(cot, (1 - core) * half, half, 1)
-    swap = [(i, i ^ 1) for i in range(16)]
+    cot_own = jnp.dot(cot, own_columns, preferred_element_type=F32).astype(BF16)
+    cot_send = jnp.dot(cot, other_columns, preferred_element_type=F32).astype(BF16)
+    back = jnp.dot(cot, w_t, preferred_element_type=F32)
+    sums, (x_sums, cot_own, cot_send) = add_from(
+        sums, "dp", [dp_step(step, True) for step in (1, 2, 3)], x_sums, cot_own, cot_send
+    )
     cot_other = lax.ppermute(cot_send, "zero", swap)
+    sums, (back,) = add_from(sums, "dp", [dp_step(step, False) for step in (1, 2, 3)], back)
+    info = lax.dynamic_slice_in_dim(sums[2], lax.axis_index("dp") * 96, 80, 0).astype(jnp.int32)
+    frame_count = jnp.float32(BLOCKS * BLOCK * 256)
+    mean = sums[0] / frame_count
+    var = sums[1] / frame_count - mean * mean
+    inverse = lax.rsqrt(var + EPS)
+    norm = jnp.stack([mean, inverse, small_full[KER], small_full[KER + 1]])
 
     h, sw = hidden(info, got, kern_full, norm, back, x_sums)
     sw_other = lax.ppermute(sw, "zero", swap)
@@ -385,20 +427,24 @@
         sw, w_t, (((1,), (1,)), ((), ())), preferred_element_type=F32
     ).astype(BF16)
 
-    grads = jnp.concatenate([grads, x_sums], axis=0)
+    grads = jnp.concatenate([grads, x_sums], axis=0).reshape(104, 8, 2, share)
+    grads = jnp.transpose(grads, (2, 1, 0, 3))
     grads_other = lax.ppermute(
-        lax.dynamic_slice_in_dim(grads, (1 - core) * half, half, 1), "zero", swap
-    )
-    grads = lax.dynamic_slice_in_dim(grads, core * half, half, 1) + grads_other
-
-    term = jnp.sum(term.astype(F32), axis=0)
-    both = jnp.concatenate([term, grads], axis=0).reshape(-1, 8, share)
-    both = jnp.transpose(both, (1, 0, 2))
-    both = lax.dynamic_slice_in_dim(jnp.concatenate([both, both], axis=0), zero_id // 2, 8, 0)
-    last = jnp.zeros(both.shape[1:], F32)
-    for i in range(8):
-        to_owner = [(2 * z + c, 8 * c + (i + z) % 8) for z in range(8) for c in range(2)]
-        last = last + lax.ppermute(both[i], "zero", to_owner)
+        lax.dynamic_index_in_dim(grads, 1 - core, 0, False), "zero", swap
+    )
+    grads = lax.dynamic_index_in_dim(grads, core, 0, False) + grads_other
+
+    term = jnp.sum(term.astype(F32), axis=0).reshape(share, 8, share)
+    both = jnp.concatenate([jnp.transpose(term, (1, 0, 2)), grads], axis=1)
+    both = lax.all_to_all(
+        both,
+        "zero",
+        0,
+        0,
+        axis_index_groups=[[i for i in range(16) if i % 2 == c] for c in range(2)],
+        tiled=True,
+    )
+    last = jnp.sum(both, axis=0)
     last = lax.all_to_all(
         jnp.broadcast_to(last[None], (16,) + last.shape), "dp", 0, 0, tiled=True
     )

time: 265 us -> 254 us (0.958); the launches traced: 260 us -> 253 us
  blocking collectives: 0 us -> 45.6 us
  starting transfers between devices: 89.3 us -> 55.2 us
  waiting for transfers between devices: 47.7 us -> 29.5 us
  matrix products: 22.9 us -> 27.7 us
  other arithmetic: 12.2 us -> 7.46 us
  Pallas kernels: 57.3 us -> 61.2 us
    ppermute x9 -> x1, starting transfers between devices: 29.8 us -> 1.84 us  [per_device(): lax.ppermute(lax.dynamic_index_in_dim(grads, 1 - core, 0, False), 'zero',...]
    all_to_all x0 -> x1, blocking collectives: none -> 25.1 us  [per_device(): lax.all_to_all(both, 'zero', 0, 0, axis_index_groups=[[i for i in range(1...]
    all_gather x0 -> x1, blocking collectives: none -> 20.5 us  [per_device(): small_full = lax.all_gather(small, 'zero', axis=0)]
    ppermute x11, waiting for transfers between devices: 23.3 us -> 5.55 us  [add_from(): parts = [lax.ppermute(x, axis, step) for step in steps]]
    all_to_all x1 -> x0, starting transfers between devices: 8.57 us -> none  [per_device(): lax.all_to_all(jnp.broadcast_to(small[None], (16,) + small.shape), 'zero'...]
    ppermute x11, starting transfers between devices: 27.2 us -> 20.3 us  [add_from(): parts = [lax.ppermute(x, axis, step) for step in steps]]
    ppermute x9 -> x1, waiting for transfers between devices: 7.86 us -> 1.35 us  [per_device(): lax.ppermute(lax.dynamic_index_in_dim(grads, 1 - core, 0, False), 'zero',...]
    all_to_all x1, starting transfers between devices: 6.88 us -> 13.1 us  [per_device(): term = lax.all_to_all(term, 'dp', 0, 0, tiled=True)]
  transfers between devices with their start and end apart: 27 -> 18, of which waited for: 12 -> 9; matrix products, arithmetic and copies ran while one was open for 12% -> 12% of each run, Pallas kernels for 15% -> 17%
where the time goes in v3:
time: 254 us; the launch traced here: 253 us
  Pallas kernels  61.2 us (24%)
  starting transfers between devices  55.2 us (22%)
  blocking collectives  45.6 us (18%)
  waiting for transfers between devices  29.5 us (12%)
  matrix products  27.7 us (11%)
  between operations  14.3 us (6%)
  local copies, waits for them, and re-layouts  11.9 us (5%)
  other arithmetic  7.46 us (3%)
    all_to_all x1, blocking collectives, per_device(): lax.all_to_all(both, 'zero', 0, 0, axis_index_groups=[[i for i in range(1...  25.1 us
    pallas_call x1, Pallas kernels, terms(): pl.pallas_call(terms_kernel, grid=(width // LANES,), out_shape=jax.ShapeD...  24.3 us
    all_gather x1, blocking collectives, per_device(): small_full = lax.all_gather(small, 'zero', axis=0)  20.5 us
    ppermute x11, starting transfers between devices, add_from(): parts = [lax.ppermute(x, axis, step) for step in steps]  20.3 us
    pallas_call x1, Pallas kernels, hidden(): pl.pallas_call(hidden_kernel, grid=(width // LANES,), out_shape=(jax.Shap...  17.2 us
    pallas_call x1, Pallas kernels, stats(): pl.pallas_call(stats_kernel, grid=(width // LANES,), out_shape=jax.ShapeD...  16.9 us
    all_to_all x1, waiting for transfers between devices, per_device(): lax.all_to_all(jnp.broadcast_to(last[None], (16,) + last.shape), 'dp', 0,...  13.9 us
    all_to_all x1, starting transfers between devices, per_device(): term = lax.all_to_all(term, 'dp', 0, 0, tiled=True)  13.1 us
  transfers between devices with their start and end apart: 18, of which 9 were waited for; matrix products, arithmetic and copies ran while one was open for 12% of the time, Pallas kernels for 17%

profile of v3, /device:TPU:8, one launch (start us, length us, event | category | flops | bytes accessed | tf_op | source)
XLA Modules:
  0.0 252.8 jit_solution(16981138729440373107)
XLA Ops:
  7.2 0.7 all-gather.3.cloned.1.call-update
  8.0 0.8 maximum_maximum_fusion
  8.8 1.7 copy-done.2
  10.5 0.7 copy-done.4
  11.1 1.2 pack.1._
  12.4 2.2 copy-done.1
  14.6 7.5 %all-to-all-start = ((bf16[16,96,1536]{2,1,0:T(8,128)(2,1)}), bf16[16,96,1536]{2,1,0:T(8,128)(2,1)}, u32[]{:S(2)}, u32[]{:S(2)}) async-start(bf16[16,96,1536]{2,1,0:T(8,128)(2,1)} %copy-done.1), calls=%async_computation | async-start | bytes 9437184 | tf_op jit(solution)/shard_map/all_to_all | solution.py:372
  22.1 20.5 %all-gather = bf16[768,96]{1,0:T(8,128)(2,1)S(1)} all-gather(bf16[48,96]{1,0:T(8,128)(2,1)S(1)} %maximum_maximum_fusion), channel_id=2, replica_groups=mesh['dp'=16,'zero'=16] {'zero'}, dimensions={0}, use_global_device_ids=true | all-gather | bytes 156672 | tf_op jit(solution)/shard_map/all_gather | solution.py:373
  42.7 0.8 slice.66.kern_ref
  43.5 0.6 reduce
  44.1 1.5 places.1
  45.6 16.9 %stats.1 = f32[2,1536]{1,0:T(2,128)} custom-call(s32[4]{0:T(128)} %get-tuple-element.26.bounds_ref, bf16[768,1536]{1,0:T(8,128)(2,1)} %bitcast.52, f32[32,1536]{1,0:T(8,128)} %slice.66.kern_ref, bf16[16,96,1536]{2,1,0:T(8,128)(2,1)} %copy-done.1), custom_call_target="tpu_custom_call" | custom-call | flops 16499999744 | bytes 1000000 | tf_op jit(solution)/shard_map/stats/pallas_call | solution.py:179
  62.5 0.7 fusion.59
  63.2 0.7 collective-permute-done
  63.9 0.7 add.93
  64.6 2.6 %collective-permute-start.1 = (f32[2,1536]{1,0:T(2,128)S(1)}, f32[2,1536]{1,0:T(2,128)S(1)}, u32[]{:S(2)}, u32[]{:S(2)}) collective-permute-start(f32[2,1536]{1,0:T(2,128)S(1)} %add.93), channel_id=1, source_target_pairs={{0,2},{1,3},{2,0},{3,1},{4,6},{5,7},{6,4},{7,5},{8,10},{9,11},{10,... | collective-permute-start | bytes 36872 | tf_op jit(solution)/shard_map/ppermute | solution.py:354
  67.2 1.7 collective-permute-done.1
  68.9 0.6 collective-permute-start.2
  69.5 4.9 %collective-permute-start.3 = (f32[2,1536]{1,0:T(2,128)S(1)}, f32[2,1536]{1,0:T(2,128)S(1)}, u32[]{:S(2)}, u32[]{:S(2)}) collective-permute-start(f32[2,1536]{1,0:T(2,128)S(1)} %add.94), channel_id=1, source_target_pairs={{0,8},{1,9},{2,10},{3,11},{4,12},{5,13},{6,14},{7,15},{8,0},{9,1},... | collective-permute-start | bytes 36872 | tf_op jit(solution)/shard_map/ppermute | solution.py:354
  74.4 1.3 collective-permute-start.4
  75.7 0.1 slice.75
  75.8 1.3 collective-permute-done.3
  77.1 1.9 collective-permute-done.4
  79.0 1.5 collective-permute-start.5
  80.6 2.6 %collective-permute-start.6 = (f32[3,1536]{1,0:T(4,128)S(1)}, f32[3,1536]{1,0:T(4,128)S(1)}, u32[]{:S(2)}, u32[]{:S(2)}) collective-permute-start(f32[3,1536]{1,0:T(4,128)S(1)} %pad_maximum_fusion.2), channel_id=1, source_target_pairs={{0,32},{16,48},{32,0},{48,16},{64,96},{80,112},{96,64},{112,80},{1... | collective-permute-start | bytes 55304 | tf_op jit(solution)/shard_map/ppermute | solution.py:354
  83.1 2.5 %collective-permute-start.7 = (f32[3,1536]{1,0:T(4,128)S(1)}, f32[3,1536]{1,0:T(4,128)S(1)}, u32[]{:S(2)}, u32[]{:S(2)}) collective-permute-start(f32[3,1536]{1,0:T(4,128)S(1)} %pad_maximum_fusion.2), channel_id=1, source_target_pairs={{0,48},{16,0},{32,16},{48,32},{64,112},{80,64},{96,80},{112,96},{1... | collective-permute-start | bytes 55304 | tf_op jit(solution)/shard_map/ppermute | solution.py:354
  85.7 2.6 %fusion.18 = bf16[512,768]{1,0:T(8,128)(2,1)} fusion(bf16[512,1536]{1,0:T(8,128)(2,1)S(1)} %bitcast.50, s32[768]{0:T(1024)S(1)} %get-tuple-element.65, s32[768]{0:T(1024)S(1)} %get-tuple-element.66, pred[768]{0:T(1024)(128)(4,1)S(1)} %fusion.53, pred[]{:T(512)S(6)} %eq.14), kind=kOutput, calls=%fused_computation.21 | convolution fusion | flops 1216610304 | bytes 2366209 | tf_op jit(solution)/shard_map/dot_general | solution.py:402
  88.3 2.6 %fusion.21 = bf16[512,768]{1,0:T(8,128)(2,1)} fusion(bf16[512,1536]{1,0:T(8,128)(2,1)S(1)} %bitcast.51, s32[768]{0:T(1024)S(1)} %get-tuple-element.65, s32[768]{0:T(1024)S(1)} %get-tuple-element.66, pred[768]{0:T(1024)(128)(4,1)S(1)} %fusion.53, pred[]{:T(512)S(6)} %eq.14), kind=kOutput, calls=%fused_computation.22 | convolution fusion | flops 1216610304 | bytes 2366209 | tf_op jit(solution)/shard_map/dot_general | solution.py:403
  90.9 3.8 %fusion.36.rest_1_ = f32[32,1536]{1,0:T(8,128)} fusion(bf16[768,1536]{1,0:T(8,128)(2,1)S(1)} %bitcast.54, s32[]{:T(128)} %bitcast.9, s32[]{:T(128)} %bitcast.8, s32[]{:T(128)} %bitcast.7, s32[]{:T(128)} %bitcast.6), kind=kOutput, calls=%fused_computation.44 | convolution fusion | flops 75866112 | bytes 2555920 | tf_op jit(solution)/shard_map/dot_general | solution.py:401
  94.7 0.2 collective-permute-start.8
  94.9 2.7 %collective-permute-start.9 = (f32[3,1536]{1,0:T(4,128)S(1)}, f32[3,1536]{1,0:T(4,128)S(1)}, u32[]{:S(2)}, u32[]{:S(2)}) collective-permute-start(f32[3,1536]{1,0:T(4,128)S(1)} %add_add_fusion.1), channel_id=1, source_target_pairs={{0,128},{16,144},{32,160},{48,176},{64,192},{80,208},{96,224},{112... | collective-permute-start | bytes 55304 | tf_op jit(solution)/shard_map/ppermute | solution.py:354
  97.6 1.4 collective-permute-start.10
  99.0 6.6 %fusion.60.rest_0_.back_ref = f32[512,1536]{1,0:T(8,128)} fusion(bf16[512,1536]{1,0:T(8,128)(2,1)S(1)} %bitcast.49, bf16[1536,1536]{1,0:T(8,128)(2,1)} %all-gather.3.cloned.1.call-done), kind=kOutput, calls=%fused_computation.85 | convolution fusion | flops 2415919104 | bytes 9437184 | tf_op jit(solution)/shard_map/dot_general | solution.py:404
  105.7 0.6 fusion.55.info_ref
  106.2 0.6 pad_maximum_fusion.3.norm_ref
  106.9 17.2 %hidden.1 = (f32[512,1536]{1,0:T(8,128)}, bf16[512,1536]{1,0:T(8,128)(2,1)}) custom-call(s32[80]{0:T(128)} %fusion.55.info_ref, bf16[16,96,1536]{2,1,0:T(8,128)(2,1)} %all-to-all-done.got_ref, f32[32,1536]{1,0:T(8,128)} %slice.66.kern_ref, f32[4,1536]{1,0:T(4,128)} %pad_maximum_fusion.3.norm_ref, f32[512,1536]{1,0:T(8,128)} %fusion.60.rest_0_.back_ref, ...), custom_call_target="tpu_custom_call" | custom-call | flops 17600000000 | bytes 1000000 | tf_op jit(solution)/shard_map/hidden/pallas_call | solution.py:248
  124.1 0.5 collective-permute-start.12
  124.6 4.0 %collective-permute-done.12 = bf16[512,768]{1,0:T(8,128)(2,1)} collective-permute-done((bf16[512,768]{1,0:T(8,128)(2,1)}, bf16[512,768]{1,0:T(8,128)(2,1)}, u32[]{:S(2)}, u32[]{:S(2)}) %collective-permute-start.12) | collective-permute-done | bytes 786464 | tf_op jit(solution)/shard_map/ppermute | solution.py:408
  128.6 0.2 collective-permute-done.11
  128.9 2.6 %fusion.61 = f32[1536,768]{1,0:T(8,128)S(1)} fusion(bf16[512,1536]{1,0:T(8,128)(2,1)S(1)} %collective-permute-done.11, bf16[512,768]{1,0:T(8,128)(2,1)} %collective-permute-done.12), kind=kOutput, calls=%fused_computation.86 | convolution fusion | flops 1207959552 | bytes 7077888 | tf_op jit(solution)/shard_map/dot_general | solution.py:421
  131.5 3.0 %add_convert_fusion = bf16[1536,768]{1,0:T(8,128)(2,1)} fusion(f32[1536,768]{1,0:T(8,128)S(1)} %fusion.61, bf16[512,1536]{1,0:T(8,128)(2,1)S(1)} %copy-done.5, bf16[512,768]{1,0:T(8,128)(2,1)S(1)} %copy-done.6), kind=kOutput, calls=%fused_computation.1 | convolution fusion | flops 1210318848 | bytes 9437184 | tf_op jit(solution)/shard_map/dot_general | solution.py:420
  134.4 13.1 %all-to-all-start.1 = ((bf16[16,96,768]{2,1,0:T(8,128)(2,1)}), bf16[16,96,768]{2,1,0:T(8,128)(2,1)}, u32[]{:S(2)}, u32[]{:S(2)}) async-start(bf16[16,96,768]{2,1,0:T(8,128)(2,1)} %bitcast.57), calls=%async_computation.1 | async-start | bytes 4718592 | tf_op jit(solution)/shard_map/all_to_all | solution.py:423
  147.5 24.3 %terms.1 = f32[72,1536]{1,0:T(8,128)} custom-call(s32[80]{0:T(128)} %fusion.55.info_ref, bf16[16,96,1536]{2,1,0:T(8,128)(2,1)} %all-to-all-done.got_ref, f32[512,1536]{1,0:T(8,128)} %get-tuple-element.47.h_ref, f32[512,1536]{1,0:T(8,128)} %fusion.60.rest_0_.back_ref, f32[4,1536]{1,0:T(4,128)} %pad_maximum_fusion.3.norm_ref), custom_call_target="tpu_custom_call" | custom-call | flops 27499999232 | bytes 1000000 | tf_op jit(solution)/shard_map/terms/pallas_call | solution.py:318
  171.8 1.1 pad_maximum_fusion.1
  172.9 0.3 copy.25
  173.2 1.8 collective-permute-start.13
  175.0 1.3 collective-permute-done.13
  176.4 3.8 %all-to-all-done.1 = bf16[16,96,768]{2,1,0:T(8,128)(2,1)} async-done(((bf16[16,96,768]{2,1,0:T(8,128)(2,1)}), bf16[16,96,768]{2,1,0:T(8,128)(2,1)}, u32[]{:S(2)}, u32[]{:S(2)}) %all-to-all-start.1) | async-done | bytes 2359328 | tf_op jit(solution)/shard_map/all_to_all | solution.py:423
  180.2 2.0 convert_reduce_fusion
  182.2 0.2 copy.31
  182.4 0.3 pad_maximum_fusion
  182.7 25.1 %all_to_all.20 = f32[8,200,96]{1,2,0:T(8,128)S(1)} all-to-all(f32[8,200,96]{1,2,0:T(8,128)S(1)} %pad_maximum_fusion), channel_id=1, replica_groups={{0,2,4,6,8,10,12,14},{1,3,5,7,9,11,13,15},{16,18,20,22,24,26,28,30},{17..., dimensions={0} | all-to-all | bytes 1228800 | tf_op jit(solution)/shard_map/all_to_all | solution.py:439
  207.8 1.3 broadcast_in_dim.8
  209.2 11.9 %all-to-all-start.3 = ((f32[16,200,96]{1,2,0:T(8,128)}), f32[16,200,96]{1,2,0:T(8,128)S(1)}, u32[]{:S(2)}, u32[]{:S(2)}) async-start(f32[16,200,96]{1,2,0:T(8,128)} %broadcast_in_dim.8), calls=%async_computation.3 | async-start | bytes 3145728 | tf_op jit(solution)/shard_map/all_to_all | solution.py:448
  221.1 0.8 constant_dynamic-slice_fusion
  221.8 6.6 %fusion.5 = bf16[1,1,512,1536]{3,2,1,0:T(8,128)(2,1)} fusion(bf16[512,1536]{1,0:T(8,128)(2,1)} %get-tuple-element.44, bf16[1536,1536]{1,0:T(8,128)(2,1)} %all-gather.3.cloned.1.call-done), kind=kOutput, calls=%fused_computation.10 | convolution fusion | flops 2416705536 | bytes 7864320 | tf_op jit(solution)/shard_map/dot_general | solution.py:426
  228.4 13.9 %all-to-all-done.3 = f32[16,200,96]{1,2,0:T(8,128)S(1)} async-done(((f32[16,200,96]{1,2,0:T(8,128)}), f32[16,200,96]{1,2,0:T(8,128)S(1)}, u32[]{:S(2)}, u32[]{:S(2)}) %all-to-all-start.3) | async-done | bytes 1228832 | tf_op jit(solution)/shard_map/all_to_all | solution.py:448
  242.3 0.3 slice_reduce_fusion
  242.6 0.2 fusion.44
  242.9 0.5 copy.27
  243.4 1.1 reshape.34
  244.5 0.1 fusion.41
  244.7 0.7 copy.29
  245.4 0.6 copy.30
  (50 shorter events, 0.7 us)
Async XLA Ops:
  7.2 71.8 %copy-start = (bf16[1,1,512,1536]{3,2,1,0:T(8,128)(2,1)S(1)}, bf16[1,1,512,1536]{3,2,1,0:T(8,128)(2,1)}, u32[]{:S(2)}) copy-start(bf16[1,1,512,1536]{3,2,1,0:T(8,128)(2,1)} %param.10) | copy-start | bytes 4718596
  7.2 91.8 %all-gather.3.cloned.1.call-start = ((), (), s32[]{:S(2)}) async-start(), calls=%async_computation.4 | async-start | bytes 5013504 | tf_op jit(solution)/shard_map/all_gather | solution.py:377
  8.8 1.7 copy-start.2
  10.5 0.7 copy-start.4
  12.4 2.2 copy-start.1
  14.6 28.9 %copy-start.10 = (s32[1,1,768]{2,1,0:T(1,128)S(1)}, s32[1,1,768]{2,1,0:T(1,128)}, u32[]{:S(2)}) copy-start(s32[1,1,768]{2,1,0:T(1,128)} %param.8) | copy-start | bytes 9220
  14.6 92.3 %all-to-all-start = ((bf16[16,96,1536]{2,1,0:T(8,128)(2,1)}), bf16[16,96,1536]{2,1,0:T(8,128)(2,1)}, u32[]{:S(2)}, u32[]{:S(2)}) async-start(bf16[16,96,1536]{2,1,0:T(8,128)(2,1)} %copy-done.1), calls=%async_computation | async-start | bytes 9437184 | tf_op jit(solution)/shard_map/all_to_all | solution.py:372
  45.6 16.9 %copy-start.8 = (s32[4]{0:T(128)S(1)}, s32[4]{0:T(128)}, u32[]{:S(2)}) copy-start(s32[4]{0:T(128)} %get-tuple-element.26.bounds_ref) | copy-start | bytes 52
  45.6 33.3 %copy-start.9 = (f32[1,1536]{1,0:T(1,128)S(1)}, f32[1,1536]{1,0:T(1,128)}, u32[]{:S(2)}) copy-start(f32[1,1536]{1,0:T(1,128)} %get-tuple-element.32) | copy-start | bytes 18436
  62.5 1.4 collective-permute-start
  64.6 4.3 %collective-permute-start.1 = (f32[2,1536]{1,0:T(2,128)S(1)}, f32[2,1536]{1,0:T(2,128)S(1)}, u32[]{:S(2)}, u32[]{:S(2)}) collective-permute-start(f32[2,1536]{1,0:T(2,128)S(1)} %add.93), channel_id=1, source_target_pairs={{0,2},{1,3},{2,0},{3,1},{4,6},{5,7},{6,4},{7,5},{8,10},{9,11},{10,... | collective-permute-start | bytes 36872 | tf_op jit(solution)/shard_map/ppermute | solution.py:354
  68.9 6.9 %collective-permute-start.2 = (f32[2,1536]{1,0:T(2,128)S(1)}, f32[2,1536]{1,0:T(2,128)S(1)}, u32[]{:S(2)}, u32[]{:S(2)}) collective-permute-start(f32[2,1536]{1,0:T(2,128)S(1)} %add.94), channel_id=1, source_target_pairs={{0,4},{1,5},{2,6},{3,7},{4,8},{5,9},{6,10},{7,11},{8,12},{9,13},{1... | collective-permute-start | bytes 36872 | tf_op jit(solution)/shard_map/ppermute | solution.py:354
  69.5 7.6 %collective-permute-start.3 = (f32[2,1536]{1,0:T(2,128)S(1)}, f32[2,1536]{1,0:T(2,128)S(1)}, u32[]{:S(2)}, u32[]{:S(2)}) collective-permute-start(f32[2,1536]{1,0:T(2,128)S(1)} %add.94), channel_id=1, source_target_pairs={{0,8},{1,9},{2,10},{3,11},{4,12},{5,13},{6,14},{7,15},{8,0},{9,1},... | collective-permute-start | bytes 36872 | tf_op jit(solution)/shard_map/ppermute | solution.py:354
  74.4 4.6 %collective-permute-start.4 = (f32[2,1536]{1,0:T(2,128)S(1)}, f32[2,1536]{1,0:T(2,128)S(1)}, u32[]{:S(2)}, u32[]{:S(2)}) collective-permute-start(f32[2,1536]{1,0:T(2,128)S(1)} %add.94), channel_id=1, source_target_pairs={{0,12},{1,13},{2,14},{3,15},{4,0},{5,1},{6,2},{7,3},{8,4},{9,5},{1... | collective-permute-start | bytes 36872 | tf_op jit(solution)/shard_map/ppermute | solution.py:354
  79.0 15.7 %collective-permute-start.5 = (f32[3,1536]{1,0:T(4,128)S(1)}, f32[3,1536]{1,0:T(4,128)S(1)}, u32[]{:S(2)}, u32[]{:S(2)}) collective-permute-start(f32[3,1536]{1,0:T(4,128)S(1)} %pad_maximum_fusion.2), channel_id=1, source_target_pairs={{0,16},{16,32},{32,48},{48,0},{64,80},{80,96},{96,112},{112,64},{1... | collective-permute-start | bytes 55304 | tf_op jit(solution)/shard_map/ppermute | solution.py:354
  80.6 14.1 %collective-permute-start.6 = (f32[3,1536]{1,0:T(4,128)S(1)}, f32[3,1536]{1,0:T(4,128)S(1)}, u32[]{:S(2)}, u32[]{:S(2)}) collective-permute-start(f32[3,1536]{1,0:T(4,128)S(1)} %pad_maximum_fusion.2), channel_id=1, source_target_pairs={{0,32},{16,48},{32,0},{48,16},{64,96},{80,112},{96,64},{112,80},{1... | collective-permute-start | bytes 55304 | tf_op jit(solution)/shard_map/ppermute | solution.py:354
  83.1 11.6 %collective-permute-start.7 = (f32[3,1536]{1,0:T(4,128)S(1)}, f32[3,1536]{1,0:T(4,128)S(1)}, u32[]{:S(2)}, u32[]{:S(2)}) collective-permute-start(f32[3,1536]{1,0:T(4,128)S(1)} %pad_maximum_fusion.2), channel_id=1, source_target_pairs={{0,48},{16,0},{32,16},{48,32},{64,112},{80,64},{96,80},{112,96},{1... | collective-permute-start | bytes 55304 | tf_op jit(solution)/shard_map/ppermute | solution.py:354
  88.3 2.6 %copy-start.3 = (bf16[1,1,768,1536]{3,2,1,0:T(8,128)(2,1)S(1)}, bf16[1,1,768,1536]{3,2,1,0:T(8,128)(2,1)}, u32[]{:S(2)}) copy-start(bf16[1,1,768,1536]{3,2,1,0:T(8,128)(2,1)} %param.7) | copy-start | bytes 7077892
  94.7 10.9 %collective-permute-start.8 = (f32[3,1536]{1,0:T(4,128)S(1)}, f32[3,1536]{1,0:T(4,128)S(1)}, u32[]{:S(2)}, u32[]{:S(2)}) collective-permute-start(f32[3,1536]{1,0:T(4,128)S(1)} %add_add_fusion.1), channel_id=1, source_target_pairs={{0,64},{16,80},{32,96},{48,112},{64,128},{80,144},{96,160},{112,17... | collective-permute-start | bytes 55304 | tf_op jit(solution)/shard_map/ppermute | solution.py:354
  94.9 10.7 %collective-permute-start.9 = (f32[3,1536]{1,0:T(4,128)S(1)}, f32[3,1536]{1,0:T(4,128)S(1)}, u32[]{:S(2)}, u32[]{:S(2)}) collective-permute-start(f32[3,1536]{1,0:T(4,128)S(1)} %add_add_fusion.1), channel_id=1, source_target_pairs={{0,128},{16,144},{32,160},{48,176},{64,192},{80,208},{96,224},{112... | collective-permute-start | bytes 55304 | tf_op jit(solution)/shard_map/ppermute | solution.py:354
  97.6 8.0 %collective-permute-start.10 = (f32[3,1536]{1,0:T(4,128)S(1)}, f32[3,1536]{1,0:T(4,128)S(1)}, u32[]{:S(2)}, u32[]{:S(2)}) collective-permute-start(f32[3,1536]{1,0:T(4,128)S(1)} %add_add_fusion.1), channel_id=1, source_target_pairs={{0,192},{16,208},{32,224},{48,240},{64,0},{80,16},{96,32},{112,48}... | collective-permute-start | bytes 55304 | tf_op jit(solution)/shard_map/ppermute | solution.py:354
  124.1 4.7 %collective-permute-start.11 = (bf16[512,1536]{1,0:T(8,128)(2,1)}, bf16[512,1536]{1,0:T(8,128)(2,1)S(1)}, u32[]{:S(2)}, u32[]{:S(2)}) collective-permute-start(bf16[512,1536]{1,0:T(8,128)(2,1)} %get-tuple-element.44), channel_id=1, source_target_pairs={{0,1},{1,0},{2,3},{3,2},{4,5},{5,4},{6,7},{7,6},{8,9},{9,8},{10,11... | collective-permute-start | bytes 4718600 | tf_op jit(solution)/shard_map/ppermute | solution.py:418
  124.1 4.5 %collective-permute-start.12 = (bf16[512,768]{1,0:T(8,128)(2,1)}, bf16[512,768]{1,0:T(8,128)(2,1)}, u32[]{:S(2)}, u32[]{:S(2)}) collective-permute-start(bf16[512,768]{1,0:T(8,128)(2,1)} %fusion.21), channel_id=1, source_target_pairs={{0,1},{1,0},{2,3},{3,2},{4,5},{5,4},{6,7},{7,6},{8,9},{9,8},{10,11... | collective-permute-start | bytes 2359304 | tf_op jit(solution)/shard_map/ppermute | solution.py:408
  124.6 6.8 %copy-start.5 = (bf16[512,1536]{1,0:T(8,128)(2,1)S(1)}, bf16[512,1536]{1,0:T(8,128)(2,1)}, u32[]{:S(2)}) copy-start(bf16[512,1536]{1,0:T(8,128)(2,1)} %get-tuple-element.44) | copy-start | bytes 4718596
  124.6 6.8 %copy-start.6 = (bf16[512,768]{1,0:T(8,128)(2,1)S(1)}, bf16[512,768]{1,0:T(8,128)(2,1)}, u32[]{:S(2)}) copy-start(bf16[512,768]{1,0:T(8,128)(2,1)} %fusion.18) | copy-start | bytes 2359300
  134.4 45.8 %all-to-all-start.1 = ((bf16[16,96,768]{2,1,0:T(8,128)(2,1)}), bf16[16,96,768]{2,1,0:T(8,128)(2,1)}, u32[]{:S(2)}, u32[]{:S(2)}) async-start(bf16[16,96,768]{2,1,0:T(8,128)(2,1)} %bitcast.57), calls=%async_computation.1 | async-start | bytes 4718592 | tf_op jit(solution)/shard_map/all_to_all | solution.py:423
  147.5 24.3 %copy-start.7 = (f32[32,1536]{1,0:T(8,128)S(1)}, f32[32,1536]{1,0:T(8,128)}, u32[]{:S(2)}) copy-start(f32[32,1536]{1,0:T(8,128)} %fusion.36.rest_1_) | copy-start | bytes 589828
  173.2 3.2 %collective-permute-start.13 = (f32[8,104,96]{1,2,0:T(8,128)S(1)}, f32[8,104,96]{1,2,0:T(8,128)S(1)}, u32[]{:S(2)}, u32[]{:S(2)}) collective-permute-start(f32[8,104,96]{1,2,0:T(8,128)S(1)} %dynamic-slice_bitcast_fusion), channel_id=1, source_target_pairs={{0,1},{1,0},{2,3},{3,2},{4,5},{5,4},{6,7},{7,6},{8,9},{9,8},{10,11... | collective-permute-start | bytes 958472 | tf_op jit(solution)/shard_map/ppermute | solution.py:432
  209.2 33.2 %all-to-all-start.3 = ((f32[16,200,96]{1,2,0:T(8,128)}), f32[16,200,96]{1,2,0:T(8,128)S(1)}, u32[]{:S(2)}, u32[]{:S(2)}) async-start(f32[16,200,96]{1,2,0:T(8,128)} %broadcast_in_dim.8), calls=%async_computation.3 | async-start | bytes 3145728 | tf_op jit(solution)/shard_map/all_to_all | solution.py:448
Sparse Core Ops, SparseCore 0:
  9.8 45.8 all-gather.2

commit v4 on v3

--- a/solution.py
+++ b/solution.py
@@ -12,6 +12,8 @@
 LEFT = 16
 WIN = 96
 LANES = 128
+TILES = 4
+WIDE = TILES * LANES
 EPS = 1e-05
 F32 = jnp.float32
 BF16 = jnp.bfloat16
@@ -28,25 +30,31 @@
     return lax.broadcasted_iota(jnp.int32, (rows, LANES), 0)
 
 
+def tile(g):
+    return pl.ds(LANES * g, LANES)
+
+
 def spread_taps(kern_ref, taps):
-    for k in range(KER):
-        taps[pl.ds(8 * k, 8), :] = jnp.broadcast_to(kern_ref[pl.ds(k, 1), :], (8, LANES))
+    for g in range(TILES):
+        for k in range(KER):
+            row = kern_ref[pl.ds(k, 1), tile(g)]
+            taps[g, pl.ds(8 * k, 8), :] = jnp.broadcast_to(row, (8, LANES))
 
 
 def row_of(v):
     return 8 * row_iota(8) + v
 
 
-def shifted(window, w):
-    return window[pl.ds(w, 8, stride=8), :]
-
-
-def conv_block(window, taps):
-    xs = [shifted(window, w) for w in range(7)]
+def shifted(window, g, w):
+    return window[g, pl.ds(w, 8, stride=8), :]
+
+
+def conv_block(window, taps, g):
+    xs = [shifted(window, g, w) for w in range(7)]
     acc = [None] * 8
     for k in range(KER):
-        xs.append(shifted(window, k + 7))
-        tap = taps[pl.ds(8 * k, 8), :]
+        xs.append(shifted(window, g, k + 7))
+        tap = taps[g, pl.ds(8 * k, 8), :]
         for v in range(8):
             acc[v] = tap * xs[v] if k == 0 else acc[v] + tap * xs[v]
         xs.pop(0)
@@ -154,43 +162,48 @@
             after = jnp.minimum(row + BLOCK, NB * BLOCK - 16)
             for source, place, size in ((before, 0, 16), (row, 16, 64), (after, 80, 16)):
                 rows = row_iota(size) + (row - LEFT + place)
-                x = x_ref[pl.ds(pl.multiple_of(source, 16), size), :].astype(F32)
-                window[pl.ds(place, size), :] = jnp.where((rows >= begin) & (rows < stop), x, 0.0)
-            acc = conv_block(window, taps)
-            total, square = sums[pl.ds(0, 8), :], sums[pl.ds(8, 8), :]
-            for v in range(8):
-                at = row_of(v) + row
-                h = jnp.where((at >= begin) & (at < stop), acc[v], 0.0)
-                total = total + h
-                square = square + h * h
-            sums[pl.ds(0, 8), :] = total
-            sums[pl.ds(8, 8), :] = square
+                keep = (rows >= begin) & (rows < stop)
+                for g in range(TILES):
+                    x = x_ref[pl.ds(pl.multiple_of(source, 16), size), tile(g)].astype(F32)
+                    window[g, pl.ds(place, size), :] = jnp.where(keep, x, 0.0)
+            for g in range(TILES):
+                acc = conv_block(window, taps, g)
+                total, square = sums[g, pl.ds(0, 8), :], sums[g, pl.ds(8, 8), :]
+                for v in range(8):
+                    at = row_of(v) + row
+                    h = jnp.where((at >= begin) & (at < stop), acc[v], 0.0)
+                    total = total + h
+                    square = square + h * h
+                sums[g, pl.ds(0, 8), :] = total
+                sums[g, pl.ds(8, 8), :] = square
             return inner
 
         return lax.fori_loop(*utterances(first, second, row), part, carry)
 
     lax.fori_loop(0, end // BLOCK, block, 0)
-    out_ref[pl.ds(0, 1), :] = jnp.sum(sums[pl.ds(0, 8), :], axis=0, keepdims=True)
-    out_ref[pl.ds(1, 1), :] = jnp.sum(sums[pl.ds(8, 8), :], axis=0, keepdims=True)
+    for g in range(TILES):
+        for i in range(2):
+            part = sums[g, pl.ds(8 * i, 8), :]
+            out_ref[pl.ds(i, 1), tile(g)] = jnp.sum(part, axis=0, keepdims=True)
 
 
 def stats(bounds, x, kern, earlier):
     width = x.shape[1]
     return pl.pallas_call(
         stats_kernel,
-        grid=(width // LANES,),
+        grid=(width // WIDE,),
         out_shape=jax.ShapeDtypeStruct((2, width), F32),
         in_specs=[
             SMEM_SPEC,
-            pl.BlockSpec((NB * BLOCK, LANES), lambda c: (0, c)),
-            pl.BlockSpec((KER, LANES), lambda c: (0, c)),
+            pl.BlockSpec((NB * BLOCK, WIDE), lambda c: (0, c)),
+            pl.BlockSpec((KER, WIDE), lambda c: (0, c)),
             pl.BlockSpec(memory_space=pl.ANY),
         ],
-        out_specs=pl.BlockSpec((2, LANES), lambda c: (0, c)),
+        out_specs=pl.BlockSpec((2, WIDE), lambda c: (0, c)),
         scratch_shapes=[
-            pltpu.VMEM((WIN, LANES), F32),
-            pltpu.VMEM((8 * KER, LANES), F32),
-            pltpu.VMEM((16, LANES), F32),
+            pltpu.VMEM((TILES, WIN, LANES), F32),
+            pltpu.VMEM((TILES, 8 * KER, LANES), F32),
+            pltpu.VMEM((TILES, 16, LANES), F32),
         ],
         cost_estimate=cost(15),
         name="stats",
@@ -206,8 +219,10 @@
             def part(u, carry):
                 begin, stop = info_ref[5 * s + 1 + u], info_ref[5 * s + 2 + u]
                 rows = row_iota(WIN)
-                source = got_ref[s].astype(F32)
-                window[...] = jnp.where((rows >= begin) & (rows < stop), source, 0.0)
+                keep = (rows >= begin) & (rows < stop)
+                for g in range(TILES):
+                    x = got_ref[s, :, tile(g)].astype(F32)
+                    window[g] = jnp.where(keep, x, 0.0)
                 per_part(pl.multiple_of(n * BLOCK, BLOCK), begin - LEFT, stop - LEFT)
                 return carry
 
@@ -225,19 +240,21 @@
 def hidden_kernel(info_ref, got_ref, kern_ref, norm_ref, *rest):
     h_ref, sw_ref, window, taps = rest[-4:]
     spread_taps(kern_ref, taps)
-    mean, inverse = norm_ref[pl.ds(0, 1), :], norm_ref[pl.ds(1, 1), :]
-    scale, shift = norm_ref[pl.ds(2, 1), :], norm_ref[pl.ds(3, 1), :]
 
     def per_part(at, begin, stop):
-        acc = conv_block(window, taps)
-        for v in range(8):
-            place = pl.ds(at + v, 8, stride=8)
-            keep = (row_of(v) >= begin) & (row_of(v) < stop)
-            h_ref[place, :] = jnp.where(keep, acc[v], h_ref[place, :])
+        for g in range(TILES):
+            acc = conv_block(window, taps, g)
+            for v in range(8):
+                place = pl.ds(at + v, 8, stride=8)
+                keep = (row_of(v) >= begin) & (row_of(v) < stop)
+                h_ref[g, place, :] = jnp.where(keep, acc[v], h_ref[g, place, :])
 
     def per_block(at):
-        a = (h_ref[pl.ds(at, BLOCK), :] - mean) * inverse * scale + shift
-        sw_ref[pl.ds(at, BLOCK), :] = (a * jax.nn.sigmoid(a)).astype(BF16)
+        for g in range(TILES):
+            mean, inverse = norm_ref[pl.ds(0, 1), tile(g)], norm_ref[pl.ds(1, 1), tile(g)]
+            scale, shift = norm_ref[pl.ds(2, 1), tile(g)], norm_ref[pl.ds(3, 1), tile(g)]
+            a = (h_ref[g, pl.ds(at, BLOCK), :] - mean) * inverse * scale + shift
+            sw_ref[pl.ds(at, BLOCK), tile(g)] = (a * jax.nn.sigmoid(a)).astype(BF16)
 
     live_parts(info_ref, got_ref, window, per_part, per_block)
 
@@ -247,91 +264,103 @@
     rows = BLOCKS * BLOCK
     return pl.pallas_call(
         hidden_kernel,
-        grid=(width // LANES,),
+        grid=(width // WIDE,),
         out_shape=(
-            jax.ShapeDtypeStruct((rows, width), F32),
+            jax.ShapeDtypeStruct((width // LANES, rows, LANES), F32),
             jax.ShapeDtypeStruct((rows, width), BF16),
         ),
         in_specs=[
             SMEM_SPEC,
-            pl.BlockSpec((16, WIN, LANES), lambda c: (0, 0, c)),
-            pl.BlockSpec((KER, LANES), lambda c: (0, c)),
-            pl.BlockSpec((4, LANES), lambda c: (0, c)),
+            pl.BlockSpec((16, WIN, WIDE), lambda c: (0, 0, c)),
+            pl.BlockSpec((KER, WIDE), lambda c: (0, c)),
+            pl.BlockSpec((4, WIDE), lambda c: (0, c)),
         ]
         + [pl.BlockSpec(memory_space=pl.ANY)] * len(earlier),
         out_specs=(
-            pl.BlockSpec((rows, LANES), lambda c: (0, c)),
-            pl.BlockSpec((rows, LANES), lambda c: (0, c)),
+            pl.BlockSpec((TILES, rows, LANES), lambda c: (c, 0, 0)),
+            pl.BlockSpec((rows, WIDE), lambda c: (0, c)),
         ),
-        scratch_shapes=[pltpu.VMEM((WIN, LANES), F32), pltpu.VMEM((8 * KER, LANES), F32)],
+        scratch_shapes=[pltpu.VMEM((TILES, WIN, LANES), F32), pltpu.VMEM((TILES, 8 * KER, LANES), F32)],
         cost_estimate=cost(16),
         name="hidden",
     )(info, got, kern, norm, *earlier)
 
 
-def terms_kernel(info_ref, got_ref, h_ref, back_ref, norm_ref, out_ref, window, acc_a, acc_x, sums):
+def terms_kernel(
+    info_ref, got_ref, h_ref, wide_ref, norm_ref, out_ref, window, back_ref, acc_a, acc_x, sums
+):
+    for g in range(TILES):
+        back_ref[g] = wide_ref[:, tile(g)]
     acc_a[...] = jnp.zeros_like(acc_a)
     acc_x[...] = jnp.zeros_like(acc_x)
     sums[...] = jnp.zeros_like(sums)
-    mean, inverse = norm_ref[pl.ds(0, 1), :], norm_ref[pl.ds(1, 1), :]
-    scale, shift = norm_ref[pl.ds(2, 1), :], norm_ref[pl.ds(3, 1), :]
-
-    def per_part(at, begin, stop):
+
+    def per_tile(g, at, begin, stop):
+        mean, inverse = norm_ref[pl.ds(0, 1), tile(g)], norm_ref[pl.ds(1, 1), tile(g)]
+        scale, shift = norm_ref[pl.ds(2, 1), tile(g)], norm_ref[pl.ds(3, 1), tile(g)]
         das, hats = [], []
-        sum_x, sum_1 = sums[pl.ds(0, 8), :], sums[pl.ds(8, 8), :]
+        sum_x, sum_1 = sums[g, pl.ds(0, 8), :], sums[g, pl.ds(8, 8), :]
         for v in range(8):
             place = pl.ds(at + v, 8, stride=8)
             keep = (row_of(v) >= begin) & (row_of(v) < stop)
-            hat = (h_ref[place, :] - mean) * inverse
+            hat = (h_ref[g, place, :] - mean) * inverse
             a = hat * scale + shift
             sig = jax.nn.sigmoid(a)
-            da = back_ref[place, :] * (sig * (1.0 + a * (1.0 - sig)))
+            da = back_ref[g, place, :] * (sig * (1.0 + a * (1.0 - sig)))
             da = jnp.where(keep, da, 0.0)
             hat = jnp.where(keep, hat, 0.0)
             sum_x = sum_x + da * hat
             sum_1 = sum_1 + da
             das.append(da)
             hats.append(hat)
-        sums[pl.ds(0, 8), :] = sum_x
-        sums[pl.ds(8, 8), :] = sum_1
-        xs = [shifted(window, w) for w in range(7)]
+        sums[g, pl.ds(0, 8), :] = sum_x
+        sums[g, pl.ds(8, 8), :] = sum_1
+        xs = [shifted(window, g, w) for w in range(7)]
         for k in range(KER):
-            xs.append(shifted(window, k + 7))
+            xs.append(shifted(window, g, k + 7))
             place = pl.ds(8 * k, 8)
             for acc, rows in ((acc_a, das), (acc_x, hats)):
                 terms_k = [rows[v] * xs[v] for v in range(8)]
                 while len(terms_k) > 1:
                     terms_k = [p + q for p, q in zip(terms_k[::2], terms_k[1::2])]
-                acc[place, :] += terms_k[0]
+                acc[g, place, :] += terms_k[0]
             xs.pop(0)
 
+    def per_part(at, begin, stop):
+        for g in range(TILES):
+            per_tile(g, at, begin, stop)
+
     live_parts(info_ref, got_ref, window, per_part)
-    out_ref[pl.ds(0, 32), :] = jnp.sum(acc_a[...].reshape(KER, 8, LANES), axis=1)
-    out_ref[pl.ds(32, 32), :] = jnp.sum(acc_x[...].reshape(KER, 8, LANES), axis=1)
-    out_ref[pl.ds(64, 1), :] = jnp.sum(sums[pl.ds(0, 8), :], axis=0, keepdims=True)
-    out_ref[pl.ds(65, 1), :] = jnp.sum(sums[pl.ds(8, 8), :], axis=0, keepdims=True)
-    out_ref[pl.ds(66, 6), :] = jnp.zeros((6, LANES), F32)
+    for g in range(TILES):
+        for acc, first in ((acc_a, 0), (acc_x, KER)):
+            rows = acc[g].reshape(KER, 8, LANES)
+            out_ref[pl.ds(first, KER), tile(g)] = jnp.sum(rows, axis=1)
+        for i in range(2):
+            part = sums[g, pl.ds(8 * i, 8), :]
+            out_ref[pl.ds(2 * KER + i, 1), tile(g)] = jnp.sum(part, axis=0, keepdims=True)
+    out_ref[pl.ds(66, 6), :] = jnp.zeros((6, WIDE), F32)
 
 
 def terms(info, got, h, back, norm):
     width = got.shape[2]
     return pl.pallas_call(
         terms_kernel,
-        grid=(width // LANES,),
+        grid=(width // WIDE,),
         out_shape=jax.ShapeDtypeStruct((72, width), F32),
         in_specs=[
             SMEM_SPEC,
-            pl.BlockSpec((16, WIN, LANES), lambda c: (0, 0, c)),
-            pl.BlockSpec((BLOCKS * BLOCK, LANES), lambda c: (0, c)),
-            pl.BlockSpec((BLOCKS * BLOCK, LANES), lambda c: (0, c)),
-            pl.BlockSpec((4, LANES), lambda c: (0, c)),
+            pl.BlockSpec((16, WIN, WIDE), lambda c: (0, 0, c)),
+            pl.BlockSpec((TILES, BLOCKS * BLOCK, LANES), lambda c: (c, 0, 0)),
+            pl.BlockSpec((BLOCKS * BLOCK, WIDE), lambda c: (0, c)),
+            pl.BlockSpec((4, WIDE), lambda c: (0, c)),
         ],
-        out_specs=pl.BlockSpec((72, LANES), lambda c: (0, c)),
+        out_specs=pl.BlockSpec((72, WIDE), lambda c: (0, c)),
         scratch_shapes=[
-            pltpu.VMEM((WIN, LANES), F32),
-            pltpu.VMEM((8 * KER, LANES), F32),
-            pltpu.VMEM((8 * KER, LANES), F32),
-            pltpu.VMEM((16, LANES), F32),
+            pltpu.VMEM((TILES, WIN, LANES), F32),
+            pltpu.VMEM((TILES, BLOCKS * BLOCK, LANES), F32),
+            pltpu.VMEM((TILES, 8 * KER, LANES), F32),
+            pltpu.VMEM((TILES, 8 * KER, LANES), F32),
+            pltpu.VMEM((TILES, 16, LANES), F32),
         ],
         cost_estimate=cost(25),
         name="terms",
@@ -354,6 +383,22 @@
     parts = [lax.ppermute(x, axis, step) for step in steps]
     parts, meanwhile = lax.optimization_barrier((parts, meanwhile))
     return sum(parts, x), meanwhile
+
+
+def gather_small(x, zero_id, meanwhile):
+    for step, first in ((1, zero_id % 2 == 0), (2, (zero_id // 2) % 2 == 0)):
+        other = lax.ppermute(x, "zero", zero_step(step))
+        other, meanwhile = lax.optimization_barrier((other, meanwhile))
+        x = jnp.stack([jnp.where(first, x, other), jnp.where(first, other, x)])
+    pairs = [x] + [lax.ppermute(x, "zero", zero_step(step)) for step in (4, 8, 12)]
+    place = zero_id // 4
+    parts = []
+    for q in range(4):
+        part = pairs[0]
+        for s in range(1, 4):
+            part = jnp.where((place - s) % 4 == q, pairs[s], part)
+        parts.append(part)
+    return jnp.stack(parts).reshape((16,) + x.shape[2:])
 
 
 def per_device(frames, segments, targets, cotangent, w_out, kernel, norm_params):
@@ -368,9 +413,8 @@
     )
     send = pack(target_row, x)
     small = jnp.concatenate([kernel, norm_params, jnp.zeros((14, share), BF16)], axis=0)
-    send, small = lax.optimization_barrier((send, small))
     got = lax.all_to_all(send, "dp", 0, 0, tiled=True)
-    small_full = lax.all_gather(small, "zero", axis=0)
+    small_full = gather_small(small, zero_id, send)
     small_full = jnp.transpose(small_full, (1, 0, 2)).reshape(48, width).astype(F32)
     kern_full = small_full[:KER]
 
@@ -414,10 +458,11 @@
     inverse = lax.rsqrt(var + EPS)
     norm = jnp.stack([mean, inverse, small_full[KER], small_full[KER + 1]])
 
-    h, sw = hidden(info, got, kern_full, norm, back, x_sums)
+    h, sw = hidden(info, got, kern_full, norm, back, x_sums, cot_other)
     sw_other = lax.ppermute(sw, "zero", swap)
     contract = (((0,), (0,)), ((), ()))
     term = lax.dot_general(sw, cot_own, contract, preferred_element_type=F32)
+    sw_other, term = lax.optimization_barrier((sw_other, term))
     term = term + lax.dot_general(sw_other, cot_other, contract, preferred_element_type=F32)
     term = term.astype(BF16).reshape(16, share, half)
     term = lax.all_to_all(term, "dp", 0, 0, tiled=True)

time: 254 us -> 233 us (0.917)
  blocking collectives: 45.6 us -> 24.4 us
  Pallas kernels: 61.2 us -> 53.7 us
  waiting for transfers between devices: 29.5 us -> 33.8 us
    all_gather x1 -> x0, blocking collectives: 20.5 us -> none  [per_device(): small_full = lax.all_gather(small, 'zero', axis=0)]
    ppermute x0 -> x5, starting transfers between devices: none -> 12.5 us  [the longest x3 10.5 us: gather_small(): lax.ppermute(x, 'zero', zero_step(step))]
    pallas_call x3, Pallas kernels: 58.4 us -> 50.9 us  [the longest x1 25 us: terms(): pl.pallas_call(terms_kernel, grid=(width // WIDE,), out_shape=jax.ShapeDt...]
    all_to_all x1, starting transfers between devices: 13.1 us -> 6.81 us  [per_device(): term = lax.all_to_all(term, 'dp', 0, 0, tiled=True)]
    ppermute x11, waiting for transfers between devices: 5.55 us -> 9.8 us  [add_from(): parts = [lax.ppermute(x, axis, step) for step in steps]]
    all_to_all x1, starting transfers between devices: 11.9 us -> 7.72 us  [per_device(): lax.all_to_all(jnp.broadcast_to(last[None], (16,) + last.shape), 'dp', 0,...]
    ppermute x1, waiting for transfers between devices: 3.99 us -> 0.01 us  [per_device(): cot_other = lax.ppermute(cot_send, 'zero', swap)]
    ppermute x11, starting transfers between devices: 20.3 us -> 23.1 us  [add_from(): parts = [lax.ppermute(x, axis, step) for step in steps]]
  transfers between devices with their start and end apart: 18 -> 23, of which waited for: 9 -> 9; matrix products, arithmetic and copies ran while one was open for 12% -> 14% of each run, Pallas kernels for 17% -> 17%
where the time goes in v4:
time: 233 us
  starting transfers between devices  57.7 us (25%)
  Pallas kernels  53.7 us (23%)
  waiting for transfers between devices  33.8 us (15%)
  matrix products  26 us (11%)
  blocking collectives  24.4 us (10%)
  between operations  14.5 us (6%)
  local copies, waits for them, and re-layouts  12.9 us (6%)
  other arithmetic  9.68 us (4%)
    pallas_call x1, Pallas kernels, terms(): pl.pallas_call(terms_kernel, grid=(width // WIDE,), out_shape=jax.ShapeDt...  25 us
    all_to_all x1, blocking collectives, per_device(): lax.all_to_all(both, 'zero', 0, 0, axis_index_groups=[[i for i in range(1...  24.4 us
    ppermute x11, starting transfers between devices, add_from(): parts = [lax.ppermute(x, axis, step) for step in steps]  23.1 us
    pallas_call x1, Pallas kernels, hidden(): pl.pallas_call(hidden_kernel, grid=(width // WIDE,), out_shape=(jax.Shape...  14.7 us
    all_to_all x1, waiting for transfers between devices, per_device(): lax.all_to_all(jnp.broadcast_to(last[None], (16,) + last.shape), 'dp', 0,...  14.1 us
    pallas_call x1, Pallas kernels, stats(): pl.pallas_call(stats_kernel, grid=(width // WIDE,), out_shape=jax.ShapeDt...  11.3 us
    ppermute x3, starting transfers between devices, gather_small(): lax.ppermute(x, 'zero', zero_step(step))  10.5 us
    ppermute x11, waiting for transfers between devices, add_from(): parts = [lax.ppermute(x, axis, step) for step in steps]  9.8 us
  transfers between devices with their start and end apart: 23, of which 9 were waited for; matrix products, arithmetic and copies ran while one was open for 14% of the time, Pallas kernels for 17%

profile of v4, /device:TPU:8, one launch (start us, length us, event | category | flops | bytes accessed | tf_op | source)
XLA Modules:
  0.0 232.6 jit_solution(9256349382229391197)
XLA Ops:
  7.2 0.7 all-gather.2.cloned.1.call-update
  8.0 0.8 maximum_maximum_fusion
  8.8 1.7 copy-done.2
  10.5 0.7 copy-done.4
  11.2 1.2 pack.1._
  12.4 2.2 copy-done.1
  14.8 2.0 collective-permute-start.1
  16.8 7.4 %all-to-all-start = ((bf16[16,96,1536]{2,1,0:T(8,128)(2,1)}), bf16[16,96,1536]{2,1,0:T(8,128)(2,1)}, u32[]{:S(2)}, u32[]{:S(2)}) async-start(bf16[16,96,1536]{2,1,0:T(8,128)(2,1)} %copy-done.1), calls=%async_computation | async-start | bytes 9437184 | tf_op jit(solution)/shard_map/all_to_all | solution.py:416
  24.2 0.6 reduce
  24.8 3.4 %collective-permute-start.4 = (bf16[2,2,48,96]{3,2,1,0:T(8,128)(2,1)S(1)}, bf16[2,2,48,96]{3,2,1,0:T(8,128)(2,1)S(1)}, u32[]{:S(2)}, u32[]{:S(2)}) collective-permute-start(bf16[2,2,48,96]{3,2,1,0:T(8,128)(2,1)S(1)} %pad_maximum_fusion.3), channel_id=1, source_target_pairs={{0,4},{1,5},{2,6},{3,7},{4,8},{5,9},{6,10},{7,11},{8,12},{9,13},{1... | collective-permute-start | bytes 110600 | tf_op jit(solution)/shard_map/ppermute | solution.py:393
  28.2 4.5 %collective-permute-start.3 = (bf16[2,2,48,96]{3,2,1,0:T(8,128)(2,1)S(1)}, bf16[2,2,48,96]{3,2,1,0:T(8,128)(2,1)S(1)}, u32[]{:S(2)}, u32[]{:S(2)}) collective-permute-start(bf16[2,2,48,96]{3,2,1,0:T(8,128)(2,1)S(1)} %pad_maximum_fusion.3), channel_id=1, source_target_pairs={{0,8},{1,9},{2,10},{3,11},{4,12},{5,13},{6,14},{7,15},{8,0},{9,1},... | collective-permute-start | bytes 110600 | tf_op jit(solution)/shard_map/ppermute | solution.py:393
  32.6 2.7 %collective-permute-start.2 = (bf16[2,2,48,96]{3,2,1,0:T(8,128)(2,1)S(1)}, bf16[2,2,48,96]{3,2,1,0:T(8,128)(2,1)S(1)}, u32[]{:S(2)}, u32[]{:S(2)}) collective-permute-start(bf16[2,2,48,96]{3,2,1,0:T(8,128)(2,1)S(1)} %pad_maximum_fusion.3), channel_id=1, source_target_pairs={{0,12},{1,13},{2,14},{3,15},{4,0},{5,1},{6,2},{7,3},{8,4},{9,5},{1... | collective-permute-start | bytes 110600 | tf_op jit(solution)/shard_map/ppermute | solution.py:393
  35.3 1.5 places.1
  36.9 2.7 %collective-permute-done.3 = bf16[2,2,48,96]{3,2,1,0:T(8,128)(2,1)S(1)} collective-permute-done((bf16[2,2,48,96]{3,2,1,0:T(8,128)(2,1)S(1)}, bf16[2,2,48,96]{3,2,1,0:T(8,128)(2,1)S(1)}, u32[]{:S(2)}, u32[]{:S(2)}) %collective-permute-start.3) | collective-permute-done | bytes 36896 | tf_op jit(solution)/shard_map/ppermute | solution.py:393
  39.8 0.1 copy.41
  40.0 0.8 slice.66.kern_ref
  40.8 11.3 %stats.1 = f32[2,1536]{1,0:T(2,128)} custom-call(s32[4]{0:T(128)} %get-tuple-element.27.bounds_ref, bf16[768,1536]{1,0:T(8,128)(2,1)} %bitcast.69, f32[32,1536]{1,0:T(8,128)} %slice.66.kern_ref, bf16[16,96,1536]{2,1,0:T(8,128)(2,1)} %copy-done.1), custom_call_target="tpu_custom_call" | custom-call | flops 16499999744 | bytes 1000000 | tf_op jit(solution)/shard_map/stats/pallas_call | solution.py:192
  52.1 0.7 fusion.59
  52.8 0.7 collective-permute-done.5
  53.5 0.7 add.126
  54.2 3.7 %collective-permute-done.6 = f32[2,1536]{1,0:T(2,128)S(1)} collective-permute-done((f32[2,1536]{1,0:T(2,128)S(1)}, f32[2,1536]{1,0:T(2,128)S(1)}, u32[]{:S(2)}, u32[]{:S(2)}) %collective-permute-start.6) | collective-permute-done | bytes 12320 | tf_op jit(solution)/shard_map/ppermute | solution.py:383
  57.9 7.0 %collective-permute-start.9 = (f32[2,1536]{1,0:T(2,128)S(1)}, f32[2,1536]{1,0:T(2,128)S(1)}, u32[]{:S(2)}, u32[]{:S(2)}) collective-permute-start(f32[2,1536]{1,0:T(2,128)S(1)} %add.127), channel_id=1, source_target_pairs={{0,12},{1,13},{2,14},{3,15},{4,0},{5,1},{6,2},{7,3},{8,4},{9,5},{1... | collective-permute-start | bytes 36872 | tf_op jit(solution)/shard_map/ppermute | solution.py:383
  64.9 2.5 %collective-permute-start.7 = (f32[2,1536]{1,0:T(2,128)S(1)}, f32[2,1536]{1,0:T(2,128)S(1)}, u32[]{:S(2)}, u32[]{:S(2)}) collective-permute-start(f32[2,1536]{1,0:T(2,128)S(1)} %add.127), channel_id=1, source_target_pairs={{0,4},{1,5},{2,6},{3,7},{4,8},{5,9},{6,10},{7,11},{8,12},{9,13},{1... | collective-permute-start | bytes 36872 | tf_op jit(solution)/shard_map/ppermute | solution.py:383
  67.5 5.0 %collective-permute-done.8 = f32[2,1536]{1,0:T(2,128)S(1)} collective-permute-done((f32[2,1536]{1,0:T(2,128)S(1)}, f32[2,1536]{1,0:T(2,128)S(1)}, u32[]{:S(2)}, u32[]{:S(2)}) %collective-permute-start.8) | collective-permute-done | bytes 12320 | tf_op jit(solution)/shard_map/ppermute | solution.py:383
  72.7 3.7 %collective-permute-start.11 = (f32[3,1536]{1,0:T(4,128)S(1)}, f32[3,1536]{1,0:T(4,128)S(1)}, u32[]{:S(2)}, u32[]{:S(2)}) collective-permute-start(f32[3,1536]{1,0:T(4,128)S(1)} %pad_maximum_fusion.5), channel_id=1, source_target_pairs={{0,32},{16,48},{32,0},{48,16},{64,96},{80,112},{96,64},{112,80},{1... | collective-permute-start | bytes 55304 | tf_op jit(solution)/shard_map/ppermute | solution.py:383
  76.4 2.0 collective-permute-start.10
  78.4 1.8 fusion.21
  80.2 2.7 %fusion.18 = bf16[512,768]{1,0:T(8,128)(2,1)} fusion(bf16[512,1536]{1,0:T(8,128)(2,1)S(1)} %bitcast.67, s32[768]{0:T(1024)S(1)} %get-tuple-element.74, s32[768]{0:T(1024)S(1)} %get-tuple-element.75, pred[768]{0:T(1024)(128)(4,1)S(1)} %fusion.53, pred[]{:T(512)S(6)} %eq.85), kind=kOutput, calls=%fused_computation.21 | convolution fusion | flops 1216610304 | bytes 2366209 | tf_op jit(solution)/shard_map/dot_general | solution.py:446
  82.9 3.9 %fusion.36.rest_1_ = f32[32,1536]{1,0:T(8,128)} fusion(bf16[768,1536]{1,0:T(8,128)(2,1)S(1)} %bitcast.71, s32[]{:T(128)} %bitcast.17, s32[]{:T(128)} %bitcast.16, s32[]{:T(128)} %bitcast.15, s32[]{:T(128)} %bitcast.14), kind=kOutput, calls=%fused_computation.46 | convolution fusion | flops 75866112 | bytes 2555920 | tf_op jit(solution)/shard_map/dot_general | solution.py:445
  86.7 0.4 collective-permute-done.11
  87.1 2.4 %collective-permute-start.15 = (f32[3,1536]{1,0:T(4,128)S(1)}, f32[3,1536]{1,0:T(4,128)S(1)}, u32[]{:S(2)}, u32[]{:S(2)}) collective-permute-start(f32[3,1536]{1,0:T(4,128)S(1)} %add_add_fusion.1), channel_id=1, source_target_pairs={{0,192},{16,208},{32,224},{48,240},{64,0},{80,16},{96,32},{112,48}... | collective-permute-start | bytes 55304 | tf_op jit(solution)/shard_map/ppermute | solution.py:383
  89.5 4.1 %collective-permute-start.14 = (f32[3,1536]{1,0:T(4,128)S(1)}, f32[3,1536]{1,0:T(4,128)S(1)}, u32[]{:S(2)}, u32[]{:S(2)}) collective-permute-start(f32[3,1536]{1,0:T(4,128)S(1)} %add_add_fusion.1), channel_id=1, source_target_pairs={{0,128},{16,144},{32,160},{48,176},{64,192},{80,208},{96,224},{112... | collective-permute-start | bytes 55304 | tf_op jit(solution)/shard_map/ppermute | solution.py:383
  93.6 1.3 collective-permute-start.13
  95.0 6.6 %fusion.60.rest_0_.wide_ref = f32[512,1536]{1,0:T(8,128)} fusion(bf16[512,1536]{1,0:T(8,128)(2,1)S(1)} %bitcast.66, bf16[1536,1536]{1,0:T(8,128)(2,1)} %all-gather.2.cloned.1.call-done), kind=kOutput, calls=%fused_computation.97 | convolution fusion | flops 2415919104 | bytes 9437184 | tf_op jit(solution)/shard_map/dot_general | solution.py:448
  101.6 0.6 fusion.55.info_ref
  102.2 0.6 pad_maximum_fusion.6.norm_ref
  102.8 0.9 copy-done.6
  103.7 14.7 %hidden.1 = (f32[12,512,128]{2,1,0:T(8,128)}, bf16[512,1536]{1,0:T(8,128)(2,1)}) custom-call(s32[80]{0:T(128)} %fusion.55.info_ref, bf16[16,96,1536]{2,1,0:T(8,128)(2,1)} %all-to-all-done.got_ref, f32[32,1536]{1,0:T(8,128)} %slice.66.kern_ref, f32[4,1536]{1,0:T(4,128)} %pad_maximum_fusion.6.norm_ref, f32[512,1536]{1,0:T(8,128)} %fusion.60.rest_0_.wide_ref, ...), custom_call_target="tpu_custom_call" | custom-call | flops 17600000000 | bytes 1000000 | tf_op jit(solution)/shard_map/hidden/pallas_call | solution.py:265
  118.4 3.1 %fusion.61 = f32[1536,768]{1,0:T(8,128)S(1)} fusion(bf16[512,1536]{1,0:T(8,128)(2,1)} %get-tuple-element.45, bf16[512,768]{1,0:T(8,128)(2,1)} %fusion.18), kind=kOutput, calls=%fused_computation.98 | convolution fusion | flops 1207959552 | bytes 7077888 | tf_op jit(solution)/shard_map/dot_general | solution.py:464
  121.5 0.5 collective-permute-done.17
  122.0 1.4 fusion.62
  123.4 2.0 add_convert_fusion
  125.4 6.8 %all-to-all-start.1 = ((bf16[16,96,768]{2,1,0:T(8,128)(2,1)}), bf16[16,96,768]{2,1,0:T(8,128)(2,1)}, u32[]{:S(2)}, u32[]{:S(2)}) async-start(bf16[16,96,768]{2,1,0:T(8,128)(2,1)} %bitcast.74), calls=%async_computation.1 | async-start | bytes 4718592 | tf_op jit(solution)/shard_map/all_to_all | solution.py:468
  132.2 25.0 %terms.1 = f32[72,1536]{1,0:T(8,128)} custom-call(s32[80]{0:T(128)} %fusion.55.info_ref, bf16[16,96,1536]{2,1,0:T(8,128)(2,1)} %all-to-all-done.got_ref, f32[12,512,128]{2,1,0:T(8,128)} %get-tuple-element.49.h_ref, f32[512,1536]{1,0:T(8,128)} %fusion.60.rest_0_.wide_ref, f32[4,1536]{1,0:T(4,128)} %pad_maximum_fusion.6.norm_ref), custom_call_target="tpu_custom_call" | custom-call | flops 27499999232 | bytes 1000000 | tf_op jit(solution)/shard_map/terms/pallas_call | solution.py:346
  157.2 1.1 pad_maximum_fusion.1
  158.2 0.3 copy.25
  158.6 1.7 collective-permute-done.18
  160.4 4.2 %all-to-all-done.1 = bf16[16,96,768]{2,1,0:T(8,128)(2,1)} async-done(((bf16[16,96,768]{2,1,0:T(8,128)(2,1)}), bf16[16,96,768]{2,1,0:T(8,128)(2,1)}, u32[]{:S(2)}, u32[]{:S(2)}) %all-to-all-start.1) | async-done | bytes 2359328 | tf_op jit(solution)/shard_map/all_to_all | solution.py:468
  164.6 2.0 convert_reduce_fusion
  166.6 0.2 copy.31
  166.8 0.3 pad_maximum_fusion
  167.1 24.4 %all_to_all.20 = f32[8,200,96]{1,2,0:T(8,128)S(1)} all-to-all(f32[8,200,96]{1,2,0:T(8,128)S(1)} %pad_maximum_fusion), channel_id=1, replica_groups={{0,2,4,6,8,10,12,14},{1,3,5,7,9,11,13,15},{16,18,20,22,24,26,28,30},{17..., dimensions={0} | all-to-all | bytes 1228800 | tf_op jit(solution)/shard_map/all_to_all | solution.py:484
  191.5 1.4 broadcast_in_dim.8
  192.9 7.7 %all-to-all-start.3 = ((f32[16,200,96]{1,2,0:T(8,128)}), f32[16,200,96]{1,2,0:T(8,128)S(1)}, u32[]{:S(2)}, u32[]{:S(2)}) async-start(f32[16,200,96]{1,2,0:T(8,128)} %broadcast_in_dim.8), calls=%async_computation.3 | async-start | bytes 3145728 | tf_op jit(solution)/shard_map/all_to_all | solution.py:493
  200.6 0.8 constant_dynamic-slice_fusion
  201.4 6.6 %fusion.5 = bf16[1,1,512,1536]{3,2,1,0:T(8,128)(2,1)} fusion(bf16[512,1536]{1,0:T(8,128)(2,1)} %get-tuple-element.45, bf16[1536,1536]{1,0:T(8,128)(2,1)} %all-gather.2.cloned.1.call-done), kind=kOutput, calls=%fused_computation.10 | convolution fusion | flops 2416705536 | bytes 7864320 | tf_op jit(solution)/shard_map/dot_general | solution.py:471
  208.0 14.1 %all-to-all-done.3 = f32[16,200,96]{1,2,0:T(8,128)S(1)} async-done(((f32[16,200,96]{1,2,0:T(8,128)}), f32[16,200,96]{1,2,0:T(8,128)S(1)}, u32[]{:S(2)}, u32[]{:S(2)}) %all-to-all-start.3) | async-done | bytes 1228832 | tf_op jit(solution)/shard_map/all_to_all | solution.py:493
  222.1 0.3 slice_reduce_fusion
  222.4 0.2 fusion.44
  222.7 0.5 copy.27
  223.2 1.1 reshape.37
  224.3 0.1 fusion.41
  224.5 0.7 copy.29
  225.1 0.6 copy.30
  (72 shorter events, 1.2 us)
Async XLA Ops:
  7.2 65.4 %copy-start = (bf16[1,1,512,1536]{3,2,1,0:T(8,128)(2,1)S(1)}, bf16[1,1,512,1536]{3,2,1,0:T(8,128)(2,1)}, u32[]{:S(2)}) copy-start(bf16[1,1,512,1536]{3,2,1,0:T(8,128)(2,1)} %param.10) | copy-start | bytes 4718596
  7.2 87.8 %all-gather.2.cloned.1.call-start = ((), (), s32[]{:S(2)}) async-start(), calls=%async_computation.4 | async-start | bytes 5013504 | tf_op jit(solution)/shard_map/all_gather | solution.py:421
  8.8 5.9 %collective-permute-start = (bf16[48,96]{1,0:T(8,128)(2,1)S(1)}, bf16[48,96]{1,0:T(8,128)(2,1)S(1)}, u32[]{:S(2)}, u32[]{:S(2)}) collective-permute-start(bf16[48,96]{1,0:T(8,128)(2,1)S(1)} %maximum_maximum_fusion), channel_id=1, source_target_pairs={{0,1},{1,0},{2,3},{3,2},{4,5},{5,4},{6,7},{7,6},{8,9},{9,8},{10,11... | collective-permute-start | bytes 27656 | tf_op jit(solution)/shard_map/ppermute | solution.py:390
  8.8 1.7 copy-start.2
  10.5 0.7 copy-start.4
  11.2 3.5 %copy-start.8 = (bf16[32,96]{1,0:T(8,128)(2,1)S(1)}, bf16[32,96]{1,0:T(8,128)(2,1)}, u32[]{:S(2)}) copy-start(bf16[32,96]{1,0:T(8,128)(2,1)} %param.12) | copy-start | bytes 18436
  11.2 3.5 %copy-start.12 = (bf16[2,96]{1,0:T(2,128)(2,1)S(1)}, bf16[2,96]{1,0:T(2,128)(2,1)}, u32[]{:S(2)}) copy-start(bf16[2,96]{1,0:T(2,128)(2,1)} %param.13) | copy-start | bytes 1156
  12.4 2.2 copy-start.1
  14.7 9.4 %copy-start.11 = (s32[1,1,768]{2,1,0:T(1,128)S(1)}, s32[1,1,768]{2,1,0:T(1,128)}, u32[]{:S(2)}) copy-start(s32[1,1,768]{2,1,0:T(1,128)} %param.8) | copy-start | bytes 9220
  14.8 10.0 %collective-permute-start.1 = (bf16[2,48,96]{2,1,0:T(8,128)(2,1)S(1)}, bf16[2,48,96]{2,1,0:T(8,128)(2,1)S(1)}, u32[]{:S(2)}, u32[]{:S(2)}) collective-permute-start(bf16[2,48,96]{2,1,0:T(8,128)(2,1)S(1)} %pad_maximum_fusion.4), channel_id=1, source_target_pairs={{0,2},{1,3},{2,0},{3,1},{4,6},{5,7},{6,4},{7,5},{8,10},{9,11},{10,... | collective-permute-start | bytes 55304 | tf_op jit(solution)/shard_map/ppermute | solution.py:390
  16.8 86.1 %all-to-all-start = ((bf16[16,96,1536]{2,1,0:T(8,128)(2,1)}), bf16[16,96,1536]{2,1,0:T(8,128)(2,1)}, u32[]{:S(2)}, u32[]{:S(2)}) async-start(bf16[16,96,1536]{2,1,0:T(8,128)(2,1)} %copy-done.1), calls=%async_computation | async-start | bytes 9437184 | tf_op jit(solution)/shard_map/all_to_all | solution.py:416
  24.8 12.1 %collective-permute-start.4 = (bf16[2,2,48,96]{3,2,1,0:T(8,128)(2,1)S(1)}, bf16[2,2,48,96]{3,2,1,0:T(8,128)(2,1)S(1)}, u32[]{:S(2)}, u32[]{:S(2)}) collective-permute-start(bf16[2,2,48,96]{3,2,1,0:T(8,128)(2,1)S(1)} %pad_maximum_fusion.3), channel_id=1, source_target_pairs={{0,4},{1,5},{2,6},{3,7},{4,8},{5,9},{6,10},{7,11},{8,12},{9,13},{1... | collective-permute-start | bytes 110600 | tf_op jit(solution)/shard_map/ppermute | solution.py:393
  28.2 11.5 %collective-permute-start.3 = (bf16[2,2,48,96]{3,2,1,0:T(8,128)(2,1)S(1)}, bf16[2,2,48,96]{3,2,1,0:T(8,128)(2,1)S(1)}, u32[]{:S(2)}, u32[]{:S(2)}) collective-permute-start(bf16[2,2,48,96]{3,2,1,0:T(8,128)(2,1)S(1)} %pad_maximum_fusion.3), channel_id=1, source_target_pairs={{0,8},{1,9},{2,10},{3,11},{4,12},{5,13},{6,14},{7,15},{8,0},{9,1},... | collective-permute-start | bytes 110600 | tf_op jit(solution)/shard_map/ppermute | solution.py:393
  32.6 7.0 %collective-permute-start.2 = (bf16[2,2,48,96]{3,2,1,0:T(8,128)(2,1)S(1)}, bf16[2,2,48,96]{3,2,1,0:T(8,128)(2,1)S(1)}, u32[]{:S(2)}, u32[]{:S(2)}) collective-permute-start(bf16[2,2,48,96]{3,2,1,0:T(8,128)(2,1)S(1)} %pad_maximum_fusion.3), channel_id=1, source_target_pairs={{0,12},{1,13},{2,14},{3,15},{4,0},{5,1},{6,2},{7,3},{8,4},{9,5},{1... | collective-permute-start | bytes 110600 | tf_op jit(solution)/shard_map/ppermute | solution.py:393
  40.8 11.3 %copy-start.9 = (s32[4]{0:T(128)S(1)}, s32[4]{0:T(128)}, u32[]{:S(2)}) copy-start(s32[4]{0:T(128)} %get-tuple-element.27.bounds_ref) | copy-start | bytes 52
  40.8 31.7 %copy-start.10 = (f32[1,1536]{1,0:T(1,128)S(1)}, f32[1,1536]{1,0:T(1,128)}, u32[]{:S(2)}) copy-start(f32[1,1536]{1,0:T(1,128)} %get-tuple-element.32) | copy-start | bytes 18436
  52.1 1.4 collective-permute-start.5
  54.2 3.7 %collective-permute-start.6 = (f32[2,1536]{1,0:T(2,128)S(1)}, f32[2,1536]{1,0:T(2,128)S(1)}, u32[]{:S(2)}, u32[]{:S(2)}) collective-permute-start(f32[2,1536]{1,0:T(2,128)S(1)} %add.126), channel_id=1, source_target_pairs={{0,2},{1,3},{2,0},{3,1},{4,6},{5,7},{6,4},{7,5},{8,10},{9,11},{10,... | collective-permute-start | bytes 36872 | tf_op jit(solution)/shard_map/ppermute | solution.py:383
  57.9 9.6 %collective-permute-start.9 = (f32[2,1536]{1,0:T(2,128)S(1)}, f32[2,1536]{1,0:T(2,128)S(1)}, u32[]{:S(2)}, u32[]{:S(2)}) collective-permute-start(f32[2,1536]{1,0:T(2,128)S(1)} %add.127), channel_id=1, source_target_pairs={{0,12},{1,13},{2,14},{3,15},{4,0},{5,1},{6,2},{7,3},{8,4},{9,5},{1... | collective-permute-start | bytes 36872 | tf_op jit(solution)/shard_map/ppermute | solution.py:383
  64.9 7.6 %collective-permute-start.8 = (f32[2,1536]{1,0:T(2,128)S(1)}, f32[2,1536]{1,0:T(2,128)S(1)}, u32[]{:S(2)}, u32[]{:S(2)}) collective-permute-start(f32[2,1536]{1,0:T(2,128)S(1)} %add.127), channel_id=1, source_target_pairs={{0,8},{1,9},{2,10},{3,11},{4,12},{5,13},{6,14},{7,15},{8,0},{9,1},... | collective-permute-start | bytes 36872 | tf_op jit(solution)/shard_map/ppermute | solution.py:383
  64.9 7.6 %collective-permute-start.7 = (f32[2,1536]{1,0:T(2,128)S(1)}, f32[2,1536]{1,0:T(2,128)S(1)}, u32[]{:S(2)}, u32[]{:S(2)}) collective-permute-start(f32[2,1536]{1,0:T(2,128)S(1)} %add.127), channel_id=1, source_target_pairs={{0,4},{1,5},{2,6},{3,7},{4,8},{5,9},{6,10},{7,11},{8,12},{9,13},{1... | collective-permute-start | bytes 36872 | tf_op jit(solution)/shard_map/ppermute | solution.py:383
  72.6 14.1 %collective-permute-start.12 = (f32[3,1536]{1,0:T(4,128)S(1)}, f32[3,1536]{1,0:T(4,128)S(1)}, u32[]{:S(2)}, u32[]{:S(2)}) collective-permute-start(f32[3,1536]{1,0:T(4,128)S(1)} %pad_maximum_fusion.5), channel_id=1, source_target_pairs={{0,48},{16,0},{32,16},{48,32},{64,112},{80,64},{96,80},{112,96},{1... | collective-permute-start | bytes 55304 | tf_op jit(solution)/shard_map/ppermute | solution.py:383
  72.7 14.4 %collective-permute-start.11 = (f32[3,1536]{1,0:T(4,128)S(1)}, f32[3,1536]{1,0:T(4,128)S(1)}, u32[]{:S(2)}, u32[]{:S(2)}) collective-permute-start(f32[3,1536]{1,0:T(4,128)S(1)} %pad_maximum_fusion.5), channel_id=1, source_target_pairs={{0,32},{16,48},{32,0},{48,16},{64,96},{80,112},{96,64},{112,80},{1... | collective-permute-start | bytes 55304 | tf_op jit(solution)/shard_map/ppermute | solution.py:383
  76.4 10.7 %collective-permute-start.10 = (f32[3,1536]{1,0:T(4,128)S(1)}, f32[3,1536]{1,0:T(4,128)S(1)}, u32[]{:S(2)}, u32[]{:S(2)}) collective-permute-start(f32[3,1536]{1,0:T(4,128)S(1)} %pad_maximum_fusion.5), channel_id=1, source_target_pairs={{0,16},{16,32},{32,48},{48,0},{64,80},{80,96},{96,112},{112,64},{1... | collective-permute-start | bytes 55304 | tf_op jit(solution)/shard_map/ppermute | solution.py:383
  80.2 2.7 %copy-start.3 = (bf16[1,1,768,1536]{3,2,1,0:T(8,128)(2,1)S(1)}, bf16[1,1,768,1536]{3,2,1,0:T(8,128)(2,1)}, u32[]{:S(2)}) copy-start(bf16[1,1,768,1536]{3,2,1,0:T(8,128)(2,1)} %param.7) | copy-start | bytes 7077892
  87.1 14.4 %collective-permute-start.15 = (f32[3,1536]{1,0:T(4,128)S(1)}, f32[3,1536]{1,0:T(4,128)S(1)}, u32[]{:S(2)}, u32[]{:S(2)}) collective-permute-start(f32[3,1536]{1,0:T(4,128)S(1)} %add_add_fusion.1), channel_id=1, source_target_pairs={{0,192},{16,208},{32,224},{48,240},{64,0},{80,16},{96,32},{112,48}... | collective-permute-start | bytes 55304 | tf_op jit(solution)/shard_map/ppermute | solution.py:383
  89.5 12.0 %collective-permute-start.14 = (f32[3,1536]{1,0:T(4,128)S(1)}, f32[3,1536]{1,0:T(4,128)S(1)}, u32[]{:S(2)}, u32[]{:S(2)}) collective-permute-start(f32[3,1536]{1,0:T(4,128)S(1)} %add_add_fusion.1), channel_id=1, source_target_pairs={{0,128},{16,144},{32,160},{48,176},{64,192},{80,208},{96,224},{112... | collective-permute-start | bytes 55304 | tf_op jit(solution)/shard_map/ppermute | solution.py:383
  93.6 7.9 %collective-permute-start.13 = (f32[3,1536]{1,0:T(4,128)S(1)}, f32[3,1536]{1,0:T(4,128)S(1)}, u32[]{:S(2)}, u32[]{:S(2)}) collective-permute-start(f32[3,1536]{1,0:T(4,128)S(1)} %add_add_fusion.1), channel_id=1, source_target_pairs={{0,64},{16,80},{32,96},{48,112},{64,128},{80,144},{96,160},{112,17... | collective-permute-start | bytes 55304 | tf_op jit(solution)/shard_map/ppermute | solution.py:383
  95.0 7.8 %collective-permute-start.16 = (bf16[512,768]{1,0:T(8,128)(2,1)S(1)}, bf16[512,768]{1,0:T(8,128)(2,1)S(1)}, u32[]{:S(2)}, u32[]{:S(2)}) collective-permute-start(bf16[512,768]{1,0:T(8,128)(2,1)S(1)} %fusion.21), channel_id=1, source_target_pairs={{0,1},{1,0},{2,3},{3,2},{4,5},{5,4},{6,7},{7,6},{8,9},{9,8},{10,11... | collective-permute-start | bytes 2359304 | tf_op jit(solution)/shard_map/ppermute | solution.py:452
  102.8 0.9 copy-start.6
  118.4 3.6 %collective-permute-start.17 = (bf16[512,1536]{1,0:T(8,128)(2,1)}, bf16[512,1536]{1,0:T(8,128)(2,1)S(1)}, u32[]{:S(2)}, u32[]{:S(2)}) collective-permute-start(bf16[512,1536]{1,0:T(8,128)(2,1)} %get-tuple-element.45), channel_id=1, source_target_pairs={{0,1},{1,0},{2,3},{3,2},{4,5},{5,4},{6,7},{7,6},{8,9},{9,8},{10,11... | collective-permute-start | bytes 4718600 | tf_op jit(solution)/shard_map/ppermute | solution.py:462
  118.4 3.6 %copy-start.7 = (bf16[512,768]{1,0:T(8,128)(2,1)S(1)}, bf16[512,768]{1,0:T(8,128)(2,1)}, u32[]{:S(2)}) copy-start(bf16[512,768]{1,0:T(8,128)(2,1)} %copy-done.6) | copy-start | bytes 2359300
  125.4 39.2 %all-to-all-start.1 = ((bf16[16,96,768]{2,1,0:T(8,128)(2,1)}), bf16[16,96,768]{2,1,0:T(8,128)(2,1)}, u32[]{:S(2)}, u32[]{:S(2)}) async-start(bf16[16,96,768]{2,1,0:T(8,128)(2,1)} %bitcast.74), calls=%async_computation.1 | async-start | bytes 4718592 | tf_op jit(solution)/shard_map/all_to_all | solution.py:468
  132.2 25.0 %copy-start.5 = (f32[32,1536]{1,0:T(8,128)S(1)}, f32[32,1536]{1,0:T(8,128)}, u32[]{:S(2)}) copy-start(f32[32,1536]{1,0:T(8,128)} %fusion.36.rest_1_) | copy-start | bytes 589828
  158.5 1.8 collective-permute-start.18
  192.9 29.2 %all-to-all-start.3 = ((f32[16,200,96]{1,2,0:T(8,128)}), f32[16,200,96]{1,2,0:T(8,128)S(1)}, u32[]{:S(2)}, u32[]{:S(2)}) async-start(f32[16,200,96]{1,2,0:T(8,128)} %broadcast_in_dim.8), calls=%async_computation.3 | async-start | bytes 3145728 | tf_op jit(solution)/shard_map/all_to_all | solution.py:493
Sparse Core Ops, SparseCore 0:
  9.8 49.2 all-gather.1

commit v5 on v4

--- a/solution.py
+++ b/solution.py
@@ -68,52 +68,22 @@
     return low, high + 1
 
 
-def places_kernel(target_ref, group_ref, segment_ref, bounds_ref, row_ref):
-    live = jnp.int32(0)
-    for slot in range(NB):
-        live = live + (target_ref[slot] >= 0).astype(jnp.int32)
-    segment = segment_ref[...]
-    bounds = [jnp.int32(0)]
-    for u in (1, 2):
-        bounds.append(jnp.minimum(jnp.sum((segment < u).astype(jnp.int32)), BLOCK * live))
-    bounds.append(BLOCK * live)
-    for u in range(4):
-        bounds_ref[u] = bounds[u]
-
-    lane = lax.broadcasted_iota(jnp.int32, row_ref.shape, 1)
-    group = sum((lane >= 96 * m).astype(jnp.int32) for m in range(1, 16))
-    lane = lane - 96 * group
-    source = sum((lane >= 5 * m).astype(jnp.int32) for m in range(1, 17))
-    field = lane - 5 * source
-    valid = jnp.zeros(row_ref.shape, jnp.int32)
-    block = jnp.zeros(row_ref.shape, jnp.int32)
-    for slot in range(NB):
-        here = group == target_ref[slot]
-        valid = jnp.where(here, 1, valid)
-        block = jnp.where(here, slot, block)
-    bound = jnp.zeros(row_ref.shape, jnp.int32)
-    for u in range(4):
-        bound = jnp.where(field == u + 1, bounds[u], bound)
-    bound = jnp.clip(bound - (BLOCK * block - LEFT), 0, WIN)
-    value = jnp.where(field == 0, valid, bound)
-    row_ref[...] = jnp.where(source == group_ref[0], value, 0).astype(F32)
-
-
-def places(target_row, group, segment, width):
-    return pl.pallas_call(
-        places_kernel,
-        out_shape=(
-            jax.ShapeDtypeStruct((4,), jnp.int32),
-            jax.ShapeDtypeStruct((1, width), F32),
-        ),
-        in_specs=[SMEM_SPEC, SMEM_SPEC, pl.BlockSpec(memory_space=pltpu.VMEM)],
-        out_specs=(SMEM_SPEC, pl.BlockSpec(memory_space=pltpu.VMEM)),
-        cost_estimate=cost(1),
-        name="places",
-    )(target_row, group, segment)
-
-
-def pack_kernel(target_ref, x_ref, out_ref):
+def pack_kernel(target_ref, segment_ref, x_ref, out_ref, bounds_ref):
+    @pl.when(pl.program_id(0) == 0)
+    def _():
+        live = jnp.int32(0)
+        for slot in range(NB):
+            live = live + (target_ref[slot] >= 0).astype(jnp.int32)
+        segment = segment_ref[...]
+        bounds_ref[0] = jnp.int32(0)
+        for u in (1, 2):
+            ended = jnp.sum((segment < u).astype(jnp.int32))
+            bounds_ref[u] = jnp.minimum(ended, BLOCK * live)
+        bounds_ref[3] = BLOCK * live
+
+    row = lax.broadcasted_iota(jnp.int32, (16, LANES), 0)
+    lane = lax.broadcasted_iota(jnp.int32, (16, LANES), 1)
+    width = x_ref.shape[1]
     for i in range(4):
         group = 4 * pl.program_id(0) + i
         b = jnp.int32(-1)
@@ -127,25 +97,40 @@
             after = pl.multiple_of(jnp.minimum((b + 1) * BLOCK, NB * BLOCK - 16), 16)
             out_ref[i, pl.ds(0, 16), :] = x_ref[pl.ds(before, 16), :]
             out_ref[i, pl.ds(16, 64), :] = x_ref[pl.ds(start, 64), :]
-            out_ref[i, pl.ds(80, 16), :] = x_ref[pl.ds(after, 16), :]
+            rest = pl.ds(LANES, width - LANES)
+            out_ref[i, pl.ds(80, 16), rest] = x_ref[pl.ds(after, 16), rest]
+            info = jnp.ones((16, LANES), jnp.int32)
+            for u in range(4):
+                end = jnp.clip(bounds_ref[u] - (b * BLOCK - LEFT), 0, WIN)
+                info = jnp.where(lane == u + 1, end, info)
+            tail = x_ref[pl.ds(after, 16), pl.ds(0, LANES)].astype(F32)
+            tail = jnp.where(row == 15, info.astype(F32), tail)
+            out_ref[i, pl.ds(80, 16), pl.ds(0, LANES)] = tail.astype(BF16)
 
         @pl.when(b < 0)
         def _():
             out_ref[i] = jnp.zeros_like(out_ref[i])
 
 
-def pack(target_row, x):
+def pack(target_row, segment, x):
     rows, width = x.shape
     return pl.pallas_call(
         pack_kernel,
         grid=(4,),
-        out_shape=jax.ShapeDtypeStruct((16, WIN, width), BF16),
-        in_specs=[SMEM_SPEC, pl.BlockSpec((rows, width), lambda r: (0, 0))],
-        out_specs=pl.BlockSpec((4, WIN, width), lambda r: (r, 0, 0)),
+        out_shape=(
+            jax.ShapeDtypeStruct((16, WIN, width), BF16),
+            jax.ShapeDtypeStruct((4,), jnp.int32),
+        ),
+        in_specs=[
+            SMEM_SPEC,
+            pl.BlockSpec((NB // 2, 2 * BLOCK), lambda r: (0, 0)),
+            pl.BlockSpec((rows, width), lambda r: (0, 0)),
+        ],
+        out_specs=(pl.BlockSpec((4, WIN, width), lambda r: (r, 0, 0)), SMEM_SPEC),
         cost_estimate=cost(4),
         compiler_params=pltpu.CompilerParams(vmem_limit_bytes=32 * 1024 * 1024),
         name="pack",
-    )(target_row, x)
+    )(target_row, segment.reshape(NB // 2, 2 * BLOCK), x)
 
 
 def stats_kernel(bounds_ref, x_ref, kern_ref, _, out_ref, window, taps, sums):
@@ -210,7 +195,7 @@
     )(bounds, x, kern, earlier)
 
 
-def live_parts(info_ref, got_ref, window, per_part, per_block=None):
+def live_parts(info_ref, got_ref, window, per_part):
     def slot(s, n):
         valid = info_ref[5 * s] > 0
 
@@ -229,16 +214,14 @@
             lax.fori_loop(
                 *utterances(info_ref[5 * s + 2], info_ref[5 * s + 3], LEFT), part, 0
             )
-            if per_block is not None:
-                per_block(pl.multiple_of(n * BLOCK, BLOCK))
 
         return n + valid.astype(jnp.int32)
 
     lax.fori_loop(0, 16, slot, 0)
 
 
-def hidden_kernel(info_ref, got_ref, kern_ref, norm_ref, *rest):
-    h_ref, sw_ref, window, taps = rest[-4:]
+def hidden_kernel(info_ref, got_ref, kern_ref, *rest):
+    h_ref, window, taps = rest[-3:]
     spread_taps(kern_ref, taps)
 
     def per_part(at, begin, stop):
@@ -249,41 +232,54 @@
                 keep = (row_of(v) >= begin) & (row_of(v) < stop)
                 h_ref[g, place, :] = jnp.where(keep, acc[v], h_ref[g, place, :])
 
-    def per_block(at):
-        for g in range(TILES):
-            mean, inverse = norm_ref[pl.ds(0, 1), tile(g)], norm_ref[pl.ds(1, 1), tile(g)]
-            scale, shift = norm_ref[pl.ds(2, 1), tile(g)], norm_ref[pl.ds(3, 1), tile(g)]
-            a = (h_ref[g, pl.ds(at, BLOCK), :] - mean) * inverse * scale + shift
-            sw_ref[pl.ds(at, BLOCK), tile(g)] = (a * jax.nn.sigmoid(a)).astype(BF16)
-
-    live_parts(info_ref, got_ref, window, per_part, per_block)
-
-
-def hidden(info, got, kern, norm, *earlier):
+    live_parts(info_ref, got_ref, window, per_part)
+
+
+def hidden(info, got, kern, *earlier):
     width = got.shape[2]
     rows = BLOCKS * BLOCK
     return pl.pallas_call(
         hidden_kernel,
         grid=(width // WIDE,),
-        out_shape=(
-            jax.ShapeDtypeStruct((width // LANES, rows, LANES), F32),
-            jax.ShapeDtypeStruct((rows, width), BF16),
-        ),
+        out_shape=jax.ShapeDtypeStruct((width // LANES, rows, LANES), F32),
         in_specs=[
             SMEM_SPEC,
             pl.BlockSpec((16, WIN, WIDE), lambda c: (0, 0, c)),
             pl.BlockSpec((KER, WIDE), lambda c: (0, c)),
-            pl.BlockSpec((4, WIDE), lambda c: (0, c)),
         ]
         + [pl.BlockSpec(memory_space=pl.ANY)] * len(earlier),
-        out_specs=(
+        out_specs=pl.BlockSpec((TILES, rows, LANES), lambda c: (c, 0, 0)),
+        scratch_shapes=[
+            pltpu.VMEM((TILES, WIN, LANES), F32),
+            pltpu.VMEM((TILES, 8 * KER, LANES), F32),
+        ],
+        cost_estimate=cost(12),
+        name="hidden",
+    )(info, got, kern, *earlier)
+
+
+def swish_kernel(h_ref, norm_ref, sw_ref):
+    for g in range(TILES):
+        mean, inverse = norm_ref[pl.ds(0, 1), tile(g)], norm_ref[pl.ds(1, 1), tile(g)]
+        scale, shift = norm_ref[pl.ds(2, 1), tile(g)], norm_ref[pl.ds(3, 1), tile(g)]
+        a = (h_ref[g] - mean) * inverse * scale + shift
+        sw_ref[:, tile(g)] = (a * jax.nn.sigmoid(a)).astype(BF16)
+
+
+def swish(h, norm):
+    tiles, rows, _ = h.shape
+    return pl.pallas_call(
+        swish_kernel,
+        grid=(tiles // TILES,),
+        out_shape=jax.ShapeDtypeStruct((rows, tiles * LANES), BF16),
+        in_specs=[
             pl.BlockSpec((TILES, rows, LANES), lambda c: (c, 0, 0)),
-            pl.BlockSpec((rows, WIDE), lambda c: (0, c)),
-        ),
-        scratch_shapes=[pltpu.VMEM((TILES, WIN, LANES), F32), pltpu.VMEM((TILES, 8 * KER, LANES), F32)],
-        cost_estimate=cost(16),
-        name="hidden",
-    )(info, got, kern, norm, *earlier)
+            pl.BlockSpec((4, WIDE), lambda c: (0, c)),
+        ],
+        out_specs=pl.BlockSpec((rows, WIDE), lambda c: (0, c)),
+        cost_estimate=cost(3),
+        name="swish",
+    )(h, norm)
 
 
 def terms_kernel(
@@ -338,7 +334,7 @@
         for i in range(2):
             part = sums[g, pl.ds(8 * i, 8), :]
             out_ref[pl.ds(2 * KER + i, 1), tile(g)] = jnp.sum(part, axis=0, keepdims=True)
-    out_ref[pl.ds(66, 6), :] = jnp.zeros((6, WIDE), F32)
+    out_ref[pl.ds(66, 14), :] = jnp.zeros((14, WIDE), F32)
 
 
 def terms(info, got, h, back, norm):
@@ -346,7 +342,7 @@
     return pl.pallas_call(
         terms_kernel,
         grid=(width // WIDE,),
-        out_shape=jax.ShapeDtypeStruct((72, width), F32),
+        out_shape=jax.ShapeDtypeStruct((80, width), F32),
         in_specs=[
             SMEM_SPEC,
             pl.BlockSpec((16, WIN, WIDE), lambda c: (0, 0, c)),
@@ -354,7 +350,7 @@
             pl.BlockSpec((BLOCKS * BLOCK, WIDE), lambda c: (0, c)),
             pl.BlockSpec((4, WIDE), lambda c: (0, c)),
         ],
-        out_specs=pl.BlockSpec((72, WIDE), lambda c: (0, c)),
+        out_specs=pl.BlockSpec((80, WIDE), lambda c: (0, c)),
         scratch_shapes=[
             pltpu.VMEM((TILES, WIN, LANES), F32),
             pltpu.VMEM((TILES, BLOCKS * BLOCK, LANES), F32),
@@ -385,39 +381,38 @@
     return sum(parts, x), meanwhile
 
 
-def gather_small(x, zero_id, meanwhile):
+def gather_small(x, zero_id, send):
     for step, first in ((1, zero_id % 2 == 0), (2, (zero_id // 2) % 2 == 0)):
         other = lax.ppermute(x, "zero", zero_step(step))
-        other, meanwhile = lax.optimization_barrier((other, meanwhile))
+        other, send = lax.optimization_barrier((other, send))
         x = jnp.stack([jnp.where(first, x, other), jnp.where(first, other, x)])
     pairs = [x] + [lax.ppermute(x, "zero", zero_step(step)) for step in (4, 8, 12)]
     place = zero_id // 4
-    parts = []
-    for q in range(4):
-        part = pairs[0]
-        for s in range(1, 4):
-            part = jnp.where((place - s) % 4 == q, pairs[s], part)
-        parts.append(part)
-    return jnp.stack(parts).reshape((16,) + x.shape[2:])
+
+    def join(pairs):
+        parts = []
+        for q in range(4):
+            part = pairs[0]
+            for s in range(1, 4):
+                part = jnp.where((place - s) % 4 == q, pairs[s], part)
+            parts.append(part)
+        return jnp.stack(parts).reshape((16,) + x.shape[2:])
+
+    return pairs, join
 
 
 def per_device(frames, segments, targets, cotangent, w_out, kernel, norm_params):
     x, seg, target_row, cot = frames[0, 0], segments[0, 0], targets[0, 0], cotangent[0, 0]
     width = x.shape[1]
-    share = width // 16
+    share, half = width // 16, width // 2
     zero_id = lax.axis_index("zero")
     core = lax.rem(zero_id, 2)
-
-    bounds, info = places(
-        target_row, lax.axis_index("dp").reshape(1), seg.reshape(NB // 2, 2 * BLOCK), width
-    )
-    send = pack(target_row, x)
+    swap = zero_step(1)
+
     small = jnp.concatenate([kernel, norm_params, jnp.zeros((14, share), BF16)], axis=0)
+    small, target_row = lax.optimization_barrier((small, target_row))
+    send, bounds = pack(target_row, seg, x)
     got = lax.all_to_all(send, "dp", 0, 0, tiled=True)
-    small_full = gather_small(small, zero_id, send)
-    small_full = jnp.transpose(small_full, (1, 0, 2)).reshape(48, width).astype(F32)
-    kern_full = small_full[:KER]
-
     w_t = lax.all_gather(w_out.T, "zero", axis=0, tiled=True)
 
     frame = lax.broadcasted_iota(jnp.int32, (KER, NB * BLOCK), 1)
@@ -427,44 +422,41 @@
         begin, stop = bounds[u], bounds[u + 1]
         within = (jnp.minimum(frame, centre) >= begin) & (jnp.maximum(frame, centre) < stop)
         meets = meets | within
-
-    half = width // 2
-    column = lax.broadcasted_iota(jnp.int32, (width, half), 0)
-    place = lax.broadcasted_iota(jnp.int32, (width, half), 1)
-    even = column == place + share * (place // share)
-    odd = column == place + share * (place // share) + share
-    own_columns = jnp.where(core == 0, even, odd).astype(BF16)
-    other_columns = jnp.where(core == 0, odd, even).astype(BF16)
-    swap = [(i, i ^ 1) for i in range(16)]
+    x_sums = jnp.dot(meets.astype(BF16), x, preferred_element_type=F32)
+
+    pairs, join = gather_small(small, zero_id, send)
+    pairs, x_sums = lax.optimization_barrier((pairs, x_sums))
+    small_full = jnp.transpose(join(pairs), (1, 0, 2)).reshape(48, width).astype(F32)
+    kern_full = small_full[:KER]
 
     sums = stats(bounds, x, kern_full, send)
     for steps in ((1,), (2,), (4, 8, 12)):
         sums, _ = add_from(sums, "zero", [zero_step(step) for step in steps])
-    sums = jnp.concatenate([sums, info], axis=0)
-    sums, cot, x = lax.optimization_barrier((sums, cot, x))
-    x_sums = jnp.dot(meets.astype(BF16), x, preferred_element_type=F32)
-    cot_own = jnp.dot(cot, own_columns, preferred_element_type=F32).astype(BF16)
-    cot_send = jnp.dot(cot, other_columns, preferred_element_type=F32).astype(BF16)
-    back = jnp.dot(cot, w_t, preferred_element_type=F32)
-    sums, (x_sums, cot_own, cot_send) = add_from(
-        sums, "dp", [dp_step(step, True) for step in (1, 2, 3)], x_sums, cot_own, cot_send
-    )
-    cot_other = lax.ppermute(cot_send, "zero", swap)
-    sums, (back,) = add_from(sums, "dp", [dp_step(step, False) for step in (1, 2, 3)], back)
-    info = lax.dynamic_slice_in_dim(sums[2], lax.axis_index("dp") * 96, 80, 0).astype(jnp.int32)
+    sums, cot_now = lax.optimization_barrier((sums, cot))
+    back = jnp.dot(cot_now, w_t, preferred_element_type=F32)
+    sums, (back,) = add_from(sums, "dp", [dp_step(step, True) for step in (1, 2, 3)], back)
+
+    got, back = lax.optimization_barrier((got, back))
+    info = got[:, WIN - 1, :5].astype(jnp.int32).reshape(80)
+    cot_other = lax.ppermute(cot, "zero", swap)
+    h = hidden(info, got, kern_full, cot_other)
+    sums, (h,) = add_from(sums, "dp", [dp_step(step, False) for step in (1, 2, 3)], h)
     frame_count = jnp.float32(BLOCKS * BLOCK * 256)
     mean = sums[0] / frame_count
     var = sums[1] / frame_count - mean * mean
     inverse = lax.rsqrt(var + EPS)
     norm = jnp.stack([mean, inverse, small_full[KER], small_full[KER + 1]])
-
-    h, sw = hidden(info, got, kern_full, norm, back, x_sums, cot_other)
-    sw_other = lax.ppermute(sw, "zero", swap)
+    sw = swish(h, norm)
+
+    sw_other = lax.ppermute(
+        lax.dynamic_slice_in_dim(sw, (1 - core) * half, half, 1), "zero", swap
+    )
     contract = (((0,), (0,)), ((), ()))
-    term = lax.dot_general(sw, cot_own, contract, preferred_element_type=F32)
+    sw_own = lax.dynamic_slice_in_dim(sw, core * half, half, 1)
+    term = lax.dot_general(sw_own, cot, contract, preferred_element_type=F32)
     sw_other, term = lax.optimization_barrier((sw_other, term))
     term = term + lax.dot_general(sw_other, cot_other, contract, preferred_element_type=F32)
-    term = term.astype(BF16).reshape(16, share, half)
+    term = term.astype(BF16).reshape(16, share // 2, width)
     term = lax.all_to_all(term, "dp", 0, 0, tiled=True)
 
     grads = terms(info, got, h, back, norm)
@@ -472,32 +464,24 @@
         sw, w_t, (((1,), (1,)), ((), ())), preferred_element_type=F32
     ).astype(BF16)
 
-    grads = jnp.concatenate([grads, x_sums], axis=0).reshape(104, 8, 2, share)
-    grads = jnp.transpose(grads, (2, 1, 0, 3))
+    grads = jnp.concatenate([grads, x_sums], axis=0)
     grads_other = lax.ppermute(
-        lax.dynamic_index_in_dim(grads, 1 - core, 0, False), "zero", swap
+        lax.dynamic_slice_in_dim(grads, (1 - core) * 56, 56, 0), "zero", swap
     )
-    grads = lax.dynamic_index_in_dim(grads, core, 0, False) + grads_other
-
-    term = jnp.sum(term.astype(F32), axis=0).reshape(share, 8, share)
-    both = jnp.concatenate([jnp.transpose(term, (1, 0, 2)), grads], axis=1)
-    both = lax.all_to_all(
-        both,
-        "zero",
-        0,
-        0,
-        axis_index_groups=[[i for i in range(16) if i % 2 == c] for c in range(2)],
-        tiled=True,
-    )
-    last = jnp.sum(both, axis=0)
+    grads = lax.dynamic_slice_in_dim(grads, core * 56, 56, 0) + grads_other
+
+    term = jnp.sum(term.astype(F32), axis=0)
+    both = jnp.concatenate([term, grads], axis=0).reshape(-1, 16, share)
+    both = lax.all_to_all(jnp.transpose(both, (1, 0, 2)), "zero", 0, 0, tiled=True)
+    last = jnp.sum(both.reshape((8, 2) + both.shape[1:]), axis=0)
     last = lax.all_to_all(
         jnp.broadcast_to(last[None], (16,) + last.shape), "dp", 0, 0, tiled=True
     )
-    part_w = last[:, :share].reshape(width, share)
-    grads = jnp.sum(last[:, share:], axis=0)
+    part_w = jnp.transpose(last[:, :, : share // 2], (1, 0, 2, 3)).reshape(width, share)
+    grads = jnp.sum(last[:, :, share // 2 :], axis=0).reshape(112, share)
 
     own = lax.dynamic_slice_in_dim(norm, zero_id * share, share, 1)
-    da_x, hat_x, x_k = grads[:KER], grads[KER : 2 * KER], grads[72 : 72 + KER]
+    da_x, hat_x, x_k = grads[:KER], grads[KER : 2 * KER], grads[80 : 80 + KER]
     sum_x, sum_1 = grads[64], grads[65]
     part_k = (own[2] * own[1]) * (da_x - (sum_1 / frame_count) * x_k - (sum_x / frame_count) * hat_x)
     return out[None, None], part_w, part_k, jnp.stack([sum_x, sum_1])

time: 233 us -> 240 us (1.030)
  starting transfers between devices: 57.7 us -> 63.2 us
  matrix products: 26 us -> 21 us
  waiting for transfers between devices: 33.8 us -> 38.2 us
  Pallas kernels: 53.7 us -> 49.9 us
  blocking collectives: 24.4 us -> 28.1 us
    all_to_all x1, starting transfers between devices: 6.81 us -> 13.3 us  [per_device(): term = lax.all_to_all(term, 'dp', 0, 0, tiled=True)]
    dot_general x4 -> x2, matrix products: 14.1 us -> 9.15 us  [the longest x1 6.6 us: per_device(): back = jnp.dot(cot_now, w_t, preferred_element_type=F32)]
    pallas_call x1, Pallas kernels: 25 us -> 20.9 us  [terms(): pl.pallas_call(terms_kernel, grid=(width // WIDE,), out_shape=jax.ShapeDt...]
    all_to_all x1, blocking collectives: 24.4 us -> 28.1 us  [per_device(): lax.all_to_all(jnp.transpose(both, (1, 0, 2)), 'zero', 0, 0, tiled=True)]
    ppermute x11, waiting for transfers between devices: 9.8 us -> 6.31 us  [add_from(): parts = [lax.ppermute(x, axis, step) for step in steps]]
    all_to_all x1, waiting for transfers between devices: 4.23 us -> 7.71 us  [per_device(): term = lax.all_to_all(term, 'dp', 0, 0, tiled=True)]
    all_to_all x1, waiting for transfers between devices: 14.1 us -> 16.8 us  [per_device(): lax.all_to_all(jnp.broadcast_to(last[None], (16,) + last.shape), 'dp', 0,...]
    unnamed x28 -> x15, local copies, waits for them, and re-layouts: 6.78 us -> 5.49 us
  transfers between devices with their start and end apart: 23 -> 23, of which waited for: 9 -> 8; matrix products, arithmetic and copies ran while one was open for 14% -> 11% of each run, Pallas kernels for 17% -> 19%
where the time goes in v5:
time: 240 us; the launch traced here: 237 us
  starting transfers between devices  63.2 us (26%)
  Pallas kernels  49.9 us (21%)
  waiting for transfers between devices  38.2 us (16%)
  blocking collectives  28.1 us (12%)
  matrix products  21 us (9%)
  between operations  14.3 us (6%)
  local copies, waits for them, and re-layouts  13 us (5%)
  other arithmetic  9.52 us (4%)
    all_to_all x1, blocking collectives, per_device(): lax.all_to_all(jnp.transpose(both, (1, 0, 2)), 'zero', 0, 0, tiled=True)  28.1 us
    ppermute x11, starting transfers between devices, add_from(): parts = [lax.ppermute(x, axis, step) for step in steps]  22.8 us
    pallas_call x1, Pallas kernels, terms(): pl.pallas_call(terms_kernel, grid=(width // WIDE,), out_shape=jax.ShapeDt...  20.9 us
    all_to_all x1, waiting for transfers between devices, per_device(): lax.all_to_all(jnp.broadcast_to(last[None], (16,) + last.shape), 'dp', 0,...  16.8 us
    all_to_all x1, starting transfers between devices, per_device(): term = lax.all_to_all(term, 'dp', 0, 0, tiled=True)  13.3 us
    pallas_call x1, Pallas kernels, hidden(): pl.pallas_call(hidden_kernel, grid=(width // WIDE,), out_shape=jax.ShapeD...  11.4 us
    pallas_call x1, Pallas kernels, stats(): pl.pallas_call(stats_kernel, grid=(width // WIDE,), out_shape=jax.ShapeDt...  11.4 us
    ppermute x3, starting transfers between devices, gather_small(): lax.ppermute(x, 'zero', zero_step(step))  10 us
  transfers between devices with their start and end apart: 23, of which 8 were waited for; matrix products, arithmetic and copies ran while one was open for 11% of the time, Pallas kernels for 19%

profile of v5, /device:TPU:8, one launch (start us, length us, event | category | flops | bytes accessed | tf_op | source)
XLA Modules:
  0.0 237.4 jit_solution(13773920817647339095)
XLA Ops:
  7.2 0.7 all-gather.2.cloned.1.call-update
  8.0 0.8 maximum_maximum_fusion
  8.8 0.7 reduce
  9.5 1.7 copy-done.1
  11.2 0.7 copy-done.4
  11.8 2.0 pack.1
  13.9 2.1 copy-done
  15.9 7.5 %all-to-all-start = ((bf16[16,96,1536]{2,1,0:T(8,128)(2,1)}), bf16[16,96,1536]{2,1,0:T(8,128)(2,1)}, u32[]{:S(2)}, u32[]{:S(2)}) async-start(bf16[16,96,1536]{2,1,0:T(8,128)(2,1)} %copy-done), calls=%async_computation | async-start | bytes 9437184 | tf_op jit(solution)/shard_map/all_to_all | solution.py:415
  23.5 2.0 collective-permute-start.1
  25.5 0.6 fusion.37
  26.1 1.6 collective-permute-done.1
  27.7 6.4 %collective-permute-start.4 = (bf16[2,2,48,96]{3,2,1,0:T(8,128)(2,1)S(1)}, bf16[2,2,48,96]{3,2,1,0:T(8,128)(2,1)S(1)}, u32[]{:S(2)}, u32[]{:S(2)}) collective-permute-start(bf16[2,2,48,96]{3,2,1,0:T(8,128)(2,1)S(1)} %pad_maximum_fusion.2), channel_id=1, source_target_pairs={{0,12},{1,13},{2,14},{3,15},{4,0},{5,1},{6,2},{7,3},{8,4},{9,5},{1... | collective-permute-start | bytes 110600 | tf_op jit(solution)/shard_map/ppermute | solution.py:389
  34.1 0.8 collective-permute-start.3
  34.9 2.8 %collective-permute-start.2 = (bf16[2,2,48,96]{3,2,1,0:T(8,128)(2,1)S(1)}, bf16[2,2,48,96]{3,2,1,0:T(8,128)(2,1)S(1)}, u32[]{:S(2)}, u32[]{:S(2)}) collective-permute-start(bf16[2,2,48,96]{3,2,1,0:T(8,128)(2,1)S(1)} %pad_maximum_fusion.2), channel_id=1, source_target_pairs={{0,4},{1,5},{2,6},{3,7},{4,8},{5,9},{6,10},{7,11},{8,12},{9,13},{1... | collective-permute-start | bytes 110600 | tf_op jit(solution)/shard_map/ppermute | solution.py:389
  37.8 3.0 %fusion.18 = f32[32,1536]{1,0:T(8,128)S(1)} fusion(s32[]{:T(128)} %bitcast.9, s32[]{:T(128)} %bitcast.8, s32[]{:T(128)} %bitcast.7, s32[]{:T(128)} %bitcast.6, bf16[1,1,768,1536]{3,2,1,0:T(8,128)(2,1)S(1)} %copy-done.2), kind=kOutput, calls=%fused_computation.34 | convolution fusion | flops 75866112 | bytes 2555920 | tf_op jit(solution)/shard_map/dot_general | solution.py:425
  40.7 3.4 %collective-permute-done.3 = bf16[2,2,48,96]{3,2,1,0:T(8,128)(2,1)S(1)} collective-permute-done((bf16[2,2,48,96]{3,2,1,0:T(8,128)(2,1)S(1)}, bf16[2,2,48,96]{3,2,1,0:T(8,128)(2,1)S(1)}, u32[]{:S(2)}, u32[]{:S(2)}) %collective-permute-start.3) | collective-permute-done | bytes 36896 | tf_op jit(solution)/shard_map/ppermute | solution.py:389
  44.3 0.1 copy.35
  44.5 0.8 slice.70.kern_ref
  45.3 11.4 %stats.1 = f32[2,1536]{1,0:T(2,128)} custom-call(s32[4]{0:T(128)} %copy-done.3, bf16[768,1536]{1,0:T(8,128)(2,1)} %bitcast.56, f32[32,1536]{1,0:T(8,128)} %slice.70.kern_ref, bf16[16,96,1536]{2,1,0:T(8,128)(2,1)} %copy-done), custom_call_target="tpu_custom_call" | custom-call | flops 16499999744 | bytes 1000000 | tf_op jit(solution)/shard_map/stats/pallas_call | solution.py:177
  56.7 3.3 %collective-permute-start.5 = (f32[2,1536]{1,0:T(2,128)}, f32[2,1536]{1,0:T(2,128)S(1)}, u32[]{:S(2)}, u32[]{:S(2)}) collective-permute-start(f32[2,1536]{1,0:T(2,128)} %stats.1), channel_id=1, source_target_pairs={{0,1},{1,0},{2,3},{3,2},{4,5},{5,4},{6,7},{7,6},{8,9},{9,8},{10,11... | collective-permute-start | bytes 36872 | tf_op jit(solution)/shard_map/ppermute | solution.py:379
  60.0 1.0 collective-permute-done.5
  61.1 0.7 add.114
  61.8 2.2 collective-permute-start.6
  63.9 1.7 collective-permute-done.6
  65.6 2.9 %collective-permute-start.9 = (f32[2,1536]{1,0:T(2,128)S(1)}, f32[2,1536]{1,0:T(2,128)S(1)}, u32[]{:S(2)}, u32[]{:S(2)}) collective-permute-start(f32[2,1536]{1,0:T(2,128)S(1)} %add.115), channel_id=1, source_target_pairs={{0,12},{1,13},{2,14},{3,15},{4,0},{5,1},{6,2},{7,3},{8,4},{9,5},{1... | collective-permute-start | bytes 36872 | tf_op jit(solution)/shard_map/ppermute | solution.py:379
  68.5 1.1 collective-permute-start.8
  69.6 2.8 %collective-permute-start.7 = (f32[2,1536]{1,0:T(2,128)S(1)}, f32[2,1536]{1,0:T(2,128)S(1)}, u32[]{:S(2)}, u32[]{:S(2)}) collective-permute-start(f32[2,1536]{1,0:T(2,128)S(1)} %add.115), channel_id=1, source_target_pairs={{0,4},{1,5},{2,6},{3,7},{4,8},{5,9},{6,10},{7,11},{8,12},{9,13},{1... | collective-permute-start | bytes 36872 | tf_op jit(solution)/shard_map/ppermute | solution.py:379
  72.6 3.6 %collective-permute-done.8 = f32[2,1536]{1,0:T(2,128)S(1)} collective-permute-done((f32[2,1536]{1,0:T(2,128)S(1)}, f32[2,1536]{1,0:T(2,128)S(1)}, u32[]{:S(2)}, u32[]{:S(2)}) %collective-permute-start.8) | collective-permute-done | bytes 12320 | tf_op jit(solution)/shard_map/ppermute | solution.py:379
  76.2 1.9 collective-permute-start.12
  78.1 1.8 collective-permute-start.10
  79.9 6.6 %fusion.38.wide_ref = f32[512,1536]{1,0:T(8,128)} fusion(bf16[512,1536]{1,0:T(8,128)(2,1)S(1)} %bitcast.65, bf16[1536,1536]{1,0:T(8,128)(2,1)} %all-gather.2.cloned.1.call-done), kind=kOutput, calls=%fused_computation.77 | convolution fusion | flops 2415919104 | bytes 9437184 | tf_op jit(solution)/shard_map/dot_general | solution.py:436
  86.5 3.1 %collective-permute-start.15 = (f32[2,1536]{1,0:T(2,128)S(1)}, f32[2,1536]{1,0:T(2,128)S(1)}, u32[]{:S(2)}, u32[]{:S(2)}) collective-permute-start(f32[2,1536]{1,0:T(2,128)S(1)} %add_add_fusion.1), channel_id=1, source_target_pairs={{0,192},{16,208},{32,224},{48,240},{64,0},{80,16},{96,32},{112,48}... | collective-permute-start | bytes 36872 | tf_op jit(solution)/shard_map/ppermute | solution.py:379
  89.7 2.3 collective-permute-start.14
  92.0 1.3 collective-permute-start.13
  93.3 0.8 convert_reduce_fusion.1
  94.1 0.6 reshape.40.info_ref
  94.7 11.4 %hidden.1.h_ref = f32[12,512,128]{2,1,0:T(8,128)} custom-call(s32[80]{0:T(128)} %reshape.40.info_ref, bf16[16,96,1536]{2,1,0:T(8,128)(2,1)} %all-to-all-done.got_ref, f32[32,1536]{1,0:T(8,128)} %slice.70.kern_ref, bf16[512,1536]{1,0:T(8,128)(2,1)} %collective-permute-done.16.rest_0_), custom_call_target="tpu_custom_call" | custom-call | flops 13200000000 | bytes 1000000 | tf_op jit(solution)/shard_map/hidden/pallas_call | solution.py:241
  106.2 0.6 pad_maximum_fusion.4.norm_ref
  106.8 4.2 %swish.1 = bf16[512,1536]{1,0:T(8,128)(2,1)} custom-call(f32[12,512,128]{2,1,0:T(8,128)} %hidden.1.h_ref, f32[4,1536]{1,0:T(4,128)} %pad_maximum_fusion.4.norm_ref), custom_call_target="tpu_custom_call" | custom-call | flops 3300000000 | bytes 1000000 | tf_op jit(solution)/shard_map/swish/pallas_call | solution.py:271
  111.0 1.2 constant_dynamic-slice_fusion.1
  112.3 2.5 %fusion.1 = f32[768,1536]{1,0:T(8,128)S(1)} fusion(bf16[512,1536]{1,0:T(8,128)(2,1)} %swish.1, s32[]{:T(128)S(6)} %select_n.199, bf16[1,1,512,1536]{3,2,1,0:T(8,128)(2,1)S(1)} %copy-done.5), kind=kOutput, calls=%fused_computation.8 | convolution fusion | flops 1207959552 | bytes 7077892 | tf_op jit(solution)/shard_map/dot_general | solution.py:456
  114.9 2.8 %fusion.39 = f32[768,1536]{1,0:T(8,128)S(1)} fusion(bf16[512,768]{1,0:T(8,128)(2,1)S(1)} %collective-permute-done.17, bf16[512,1536]{1,0:T(8,128)(2,1)} %collective-permute-done.16.rest_0_), kind=kOutput, calls=%fused_computation.78 | convolution fusion | flops 1207959552 | bytes 7077888 | tf_op jit(solution)/shard_map/dot_general | solution.py:458
  117.7 2.1 add_convert_fusion
  119.8 13.3 %all-to-all-start.1 = ((bf16[16,48,1536]{2,1,0:T(8,128)(2,1)}), bf16[16,48,1536]{2,1,0:T(8,128)(2,1)S(1)}, u32[]{:S(2)}, u32[]{:S(2)}) async-start(bf16[16,48,1536]{2,1,0:T(8,128)(2,1)} %bitcast.60), calls=%async_computation.1 | async-start | bytes 4718592 | tf_op jit(solution)/shard_map/all_to_all | solution.py:460
  133.1 20.9 %terms.1 = f32[80,1536]{1,0:T(8,128)} custom-call(s32[80]{0:T(128)} %reshape.40.info_ref, bf16[16,96,1536]{2,1,0:T(8,128)(2,1)} %all-to-all-done.got_ref, f32[12,512,128]{2,1,0:T(8,128)} %hidden.1.h_ref, f32[512,1536]{1,0:T(8,128)} %fusion.38.wide_ref, f32[4,1536]{1,0:T(4,128)} %pad_maximum_fusion.4.norm_ref), custom_call_target="tpu_custom_call" | custom-call | flops 27499999232 | bytes 1000000 | tf_op jit(solution)/shard_map/terms/pallas_call | solution.py:342
  154.1 1.0 fusion.3
  155.1 1.6 collective-permute-done.18
  156.8 1.0 fusion.5
  157.8 7.7 %all-to-all-done.1 = bf16[16,48,1536]{2,1,0:T(8,128)(2,1)S(1)} async-done(((bf16[16,48,1536]{2,1,0:T(8,128)(2,1)}), bf16[16,48,1536]{2,1,0:T(8,128)(2,1)S(1)}, u32[]{:S(2)}, u32[]{:S(2)}) %all-to-all-start.1) | async-done | bytes 2359328 | tf_op jit(solution)/shard_map/all_to_all | solution.py:460
  165.5 0.3 convert_reduce_fusion
  165.9 0.3 reshape.36
  166.2 0.4 copy.27
  166.5 28.1 %all_to_all.20 = f32[16,104,96]{1,2,0:T(8,128)S(1)} all-to-all(f32[16,104,96]{1,2,0:T(8,128)S(1)} %copy.27), channel_id=1, replica_groups=mesh['dp'=16,'zero'=16] {'zero'}, dimensions={0} | all-to-all | bytes 1277952 | tf_op jit(solution)/shard_map/all_to_all | solution.py:475
  194.8 1.4 broadcast_in_dim.8
  196.1 7.3 %all-to-all-start.3 = ((f32[16,2,104,96]{2,3,1,0:T(8,128)}), f32[16,2,104,96]{2,3,1,0:T(8,128)S(1)}, u32[]{:S(2)}, u32[]{:S(2)}) async-start(f32[16,2,104,96]{2,3,1,0:T(8,128)} %broadcast_in_dim.8), calls=%async_computation.3 | async-start | bytes 3145728 | tf_op jit(solution)/shard_map/all_to_all | solution.py:477
  203.4 0.7 constant_dynamic-slice_fusion
  204.2 6.1 %fusion = bf16[1,1,512,1536]{3,2,1,0:T(8,128)(2,1)} fusion(bf16[512,1536]{1,0:T(8,128)(2,1)S(1)} %copy-done.6, bf16[1536,1536]{1,0:T(8,128)(2,1)} %all-gather.2.cloned.1.call-done), kind=kOutput, calls=%fused_computation.3 | convolution fusion | flops 2416705536 | bytes 7864320 | tf_op jit(solution)/shard_map/dot_general | solution.py:463
  210.2 16.8 %all-to-all-done.3 = f32[16,2,104,96]{2,3,1,0:T(8,128)S(1)} async-done(((f32[16,2,104,96]{2,3,1,0:T(8,128)}), f32[16,2,104,96]{2,3,1,0:T(8,128)S(1)}, u32[]{:S(2)}, u32[]{:S(2)}) %all-to-all-start.3) | async-done | bytes 1277984 | tf_op jit(solution)/shard_map/all_to_all | solution.py:477
  227.1 0.5 slice_reduce_fusion
  227.7 0.6 stack.54
  228.2 0.1 slice_bitcast_fusion
  228.4 0.5 copy.30
  228.8 1.1 copy.32
  229.9 0.6 fusion.28
  (54 shorter events, 0.9 us)
Async XLA Ops:
  7.2 72.7 %all-gather.2.cloned.1.call-start = ((), (), s32[]{:S(2)}) async-start(), calls=%async_computation.4 | async-start | bytes 5013504 | tf_op jit(solution)/shard_map/all_gather | solution.py:416
  8.8 14.7 %collective-permute-start = (bf16[48,96]{1,0:T(8,128)(2,1)S(1)}, bf16[48,96]{1,0:T(8,128)(2,1)S(1)}, u32[]{:S(2)}, u32[]{:S(2)}) collective-permute-start(bf16[48,96]{1,0:T(8,128)(2,1)S(1)} %maximum_maximum_fusion), channel_id=1, source_target_pairs={{0,1},{1,0},{2,3},{3,2},{4,5},{5,4},{6,7},{7,6},{8,9},{9,8},{10,11... | collective-permute-start | bytes 27656 | tf_op jit(solution)/shard_map/ppermute | solution.py:386
  9.5 1.7 copy-start.1
  11.2 0.7 copy-start.4
  13.9 2.1 copy-start
  15.9 9.5 %copy-start.3 = (s32[4]{0:T(128)}, s32[4]{0:T(128)S(1)}, u32[]{:S(2)}) copy-start(s32[4]{0:T(128)S(1)} %get-tuple-element.32.bounds_ref) | copy-start | bytes 52
  15.9 21.8 %copy-start.2 = (bf16[1,1,768,1536]{3,2,1,0:T(8,128)(2,1)S(1)}, bf16[1,1,768,1536]{3,2,1,0:T(8,128)(2,1)}, u32[]{:S(2)}) copy-start(bf16[1,1,768,1536]{3,2,1,0:T(8,128)(2,1)} %param.7) | copy-start | bytes 7077892
  15.9 77.3 %all-to-all-start = ((bf16[16,96,1536]{2,1,0:T(8,128)(2,1)}), bf16[16,96,1536]{2,1,0:T(8,128)(2,1)}, u32[]{:S(2)}, u32[]{:S(2)}) async-start(bf16[16,96,1536]{2,1,0:T(8,128)(2,1)} %copy-done), calls=%async_computation | async-start | bytes 9437184 | tf_op jit(solution)/shard_map/all_to_all | solution.py:415
  23.5 4.2 %collective-permute-start.1 = (bf16[2,48,96]{2,1,0:T(8,128)(2,1)S(1)}, bf16[2,48,96]{2,1,0:T(8,128)(2,1)S(1)}, u32[]{:S(2)}, u32[]{:S(2)}) collective-permute-start(bf16[2,48,96]{2,1,0:T(8,128)(2,1)S(1)} %pad_maximum_fusion.3), channel_id=1, source_target_pairs={{0,2},{1,3},{2,0},{3,1},{4,6},{5,7},{6,4},{7,5},{8,10},{9,11},{10,... | collective-permute-start | bytes 55304 | tf_op jit(solution)/shard_map/ppermute | solution.py:386
  27.7 13.0 %collective-permute-start.4 = (bf16[2,2,48,96]{3,2,1,0:T(8,128)(2,1)S(1)}, bf16[2,2,48,96]{3,2,1,0:T(8,128)(2,1)S(1)}, u32[]{:S(2)}, u32[]{:S(2)}) collective-permute-start(bf16[2,2,48,96]{3,2,1,0:T(8,128)(2,1)S(1)} %pad_maximum_fusion.2), channel_id=1, source_target_pairs={{0,12},{1,13},{2,14},{3,15},{4,0},{5,1},{6,2},{7,3},{8,4},{9,5},{1... | collective-permute-start | bytes 110600 | tf_op jit(solution)/shard_map/ppermute | solution.py:389
  34.1 10.1 %collective-permute-start.3 = (bf16[2,2,48,96]{3,2,1,0:T(8,128)(2,1)S(1)}, bf16[2,2,48,96]{3,2,1,0:T(8,128)(2,1)S(1)}, u32[]{:S(2)}, u32[]{:S(2)}) collective-permute-start(bf16[2,2,48,96]{3,2,1,0:T(8,128)(2,1)S(1)} %pad_maximum_fusion.2), channel_id=1, source_target_pairs={{0,8},{1,9},{2,10},{3,11},{4,12},{5,13},{6,14},{7,15},{8,0},{9,1},... | collective-permute-start | bytes 110600 | tf_op jit(solution)/shard_map/ppermute | solution.py:389
  34.9 9.2 %collective-permute-start.2 = (bf16[2,2,48,96]{3,2,1,0:T(8,128)(2,1)S(1)}, bf16[2,2,48,96]{3,2,1,0:T(8,128)(2,1)S(1)}, u32[]{:S(2)}, u32[]{:S(2)}) collective-permute-start(bf16[2,2,48,96]{3,2,1,0:T(8,128)(2,1)S(1)} %pad_maximum_fusion.2), channel_id=1, source_target_pairs={{0,4},{1,5},{2,6},{3,7},{4,8},{5,9},{6,10},{7,11},{8,12},{9,13},{1... | collective-permute-start | bytes 110600 | tf_op jit(solution)/shard_map/ppermute | solution.py:389
  45.3 27.2 %copy-start.5 = (bf16[1,1,512,1536]{3,2,1,0:T(8,128)(2,1)S(1)}, bf16[1,1,512,1536]{3,2,1,0:T(8,128)(2,1)}, u32[]{:S(2)}) copy-start(bf16[1,1,512,1536]{3,2,1,0:T(8,128)(2,1)} %param.10) | copy-start | bytes 4718596
  56.7 4.4 %collective-permute-start.5 = (f32[2,1536]{1,0:T(2,128)}, f32[2,1536]{1,0:T(2,128)S(1)}, u32[]{:S(2)}, u32[]{:S(2)}) collective-permute-start(f32[2,1536]{1,0:T(2,128)} %stats.1), channel_id=1, source_target_pairs={{0,1},{1,0},{2,3},{3,2},{4,5},{5,4},{6,7},{7,6},{8,9},{9,8},{10,11... | collective-permute-start | bytes 36872 | tf_op jit(solution)/shard_map/ppermute | solution.py:379
  61.8 3.8 %collective-permute-start.6 = (f32[2,1536]{1,0:T(2,128)S(1)}, f32[2,1536]{1,0:T(2,128)S(1)}, u32[]{:S(2)}, u32[]{:S(2)}) collective-permute-start(f32[2,1536]{1,0:T(2,128)S(1)} %add.114), channel_id=1, source_target_pairs={{0,2},{1,3},{2,0},{3,1},{4,6},{5,7},{6,4},{7,5},{8,10},{9,11},{10,... | collective-permute-start | bytes 36872 | tf_op jit(solution)/shard_map/ppermute | solution.py:379
  65.6 6.9 %collective-permute-start.9 = (f32[2,1536]{1,0:T(2,128)S(1)}, f32[2,1536]{1,0:T(2,128)S(1)}, u32[]{:S(2)}, u32[]{:S(2)}) collective-permute-start(f32[2,1536]{1,0:T(2,128)S(1)} %add.115), channel_id=1, source_target_pairs={{0,12},{1,13},{2,14},{3,15},{4,0},{5,1},{6,2},{7,3},{8,4},{9,5},{1... | collective-permute-start | bytes 36872 | tf_op jit(solution)/shard_map/ppermute | solution.py:379
  68.5 7.6 %collective-permute-start.8 = (f32[2,1536]{1,0:T(2,128)S(1)}, f32[2,1536]{1,0:T(2,128)S(1)}, u32[]{:S(2)}, u32[]{:S(2)}) collective-permute-start(f32[2,1536]{1,0:T(2,128)S(1)} %add.115), channel_id=1, source_target_pairs={{0,8},{1,9},{2,10},{3,11},{4,12},{5,13},{6,14},{7,15},{8,0},{9,1},... | collective-permute-start | bytes 36872 | tf_op jit(solution)/shard_map/ppermute | solution.py:379
  69.6 6.5 %collective-permute-start.7 = (f32[2,1536]{1,0:T(2,128)S(1)}, f32[2,1536]{1,0:T(2,128)S(1)}, u32[]{:S(2)}, u32[]{:S(2)}) collective-permute-start(f32[2,1536]{1,0:T(2,128)S(1)} %add.115), channel_id=1, source_target_pairs={{0,4},{1,5},{2,6},{3,7},{4,8},{5,9},{6,10},{7,11},{8,12},{9,13},{1... | collective-permute-start | bytes 36872 | tf_op jit(solution)/shard_map/ppermute | solution.py:379
  72.5 22.2 %collective-permute-start.16 = (bf16[512,1536]{1,0:T(8,128)(2,1)S(1)}, bf16[512,1536]{1,0:T(8,128)(2,1)}, u32[]{:S(2)}, u32[]{:S(2)}) collective-permute-start(bf16[512,1536]{1,0:T(8,128)(2,1)S(1)} %bitcast.64), channel_id=1, source_target_pairs={{0,1},{1,0},{2,3},{3,2},{4,5},{5,4},{6,7},{7,6},{8,9},{9,8},{10,11... | collective-permute-start | bytes 4718600 | tf_op jit(solution)/shard_map/ppermute | solution.py:441
  76.2 10.3 %collective-permute-start.12 = (f32[2,1536]{1,0:T(2,128)S(1)}, f32[2,1536]{1,0:T(2,128)S(1)}, u32[]{:S(2)}, u32[]{:S(2)}) collective-permute-start(f32[2,1536]{1,0:T(2,128)S(1)} %add_add_fusion.2), channel_id=1, source_target_pairs={{0,48},{16,0},{32,16},{48,32},{64,112},{80,64},{96,80},{112,96},{1... | collective-permute-start | bytes 36872 | tf_op jit(solution)/shard_map/ppermute | solution.py:379
  78.1 8.4 %collective-permute-start.11 = (f32[2,1536]{1,0:T(2,128)S(1)}, f32[2,1536]{1,0:T(2,128)S(1)}, u32[]{:S(2)}, u32[]{:S(2)}) collective-permute-start(f32[2,1536]{1,0:T(2,128)S(1)} %add_add_fusion.2), channel_id=1, source_target_pairs={{0,32},{16,48},{32,0},{48,16},{64,96},{80,112},{96,64},{112,80},{1... | collective-permute-start | bytes 36872 | tf_op jit(solution)/shard_map/ppermute | solution.py:379
  78.1 8.4 %collective-permute-start.10 = (f32[2,1536]{1,0:T(2,128)S(1)}, f32[2,1536]{1,0:T(2,128)S(1)}, u32[]{:S(2)}, u32[]{:S(2)}) collective-permute-start(f32[2,1536]{1,0:T(2,128)S(1)} %add_add_fusion.2), channel_id=1, source_target_pairs={{0,16},{16,32},{32,48},{48,0},{64,80},{80,96},{96,112},{112,64},{1... | collective-permute-start | bytes 36872 | tf_op jit(solution)/shard_map/ppermute | solution.py:379
  86.5 19.6 %collective-permute-start.15 = (f32[2,1536]{1,0:T(2,128)S(1)}, f32[2,1536]{1,0:T(2,128)S(1)}, u32[]{:S(2)}, u32[]{:S(2)}) collective-permute-start(f32[2,1536]{1,0:T(2,128)S(1)} %add_add_fusion.1), channel_id=1, source_target_pairs={{0,192},{16,208},{32,224},{48,240},{64,0},{80,16},{96,32},{112,48}... | collective-permute-start | bytes 36872 | tf_op jit(solution)/shard_map/ppermute | solution.py:379
  89.7 16.5 %collective-permute-start.14 = (f32[2,1536]{1,0:T(2,128)S(1)}, f32[2,1536]{1,0:T(2,128)S(1)}, u32[]{:S(2)}, u32[]{:S(2)}) collective-permute-start(f32[2,1536]{1,0:T(2,128)S(1)} %add_add_fusion.1), channel_id=1, source_target_pairs={{0,128},{16,144},{32,160},{48,176},{64,192},{80,208},{96,224},{112... | collective-permute-start | bytes 36872 | tf_op jit(solution)/shard_map/ppermute | solution.py:379
  92.0 14.2 %collective-permute-start.13 = (f32[2,1536]{1,0:T(2,128)S(1)}, f32[2,1536]{1,0:T(2,128)S(1)}, u32[]{:S(2)}, u32[]{:S(2)}) collective-permute-start(f32[2,1536]{1,0:T(2,128)S(1)} %add_add_fusion.1), channel_id=1, source_target_pairs={{0,64},{16,80},{32,96},{48,112},{64,128},{80,144},{96,160},{112,17... | collective-permute-start | bytes 36872 | tf_op jit(solution)/shard_map/ppermute | solution.py:379
  112.2 2.7 %collective-permute-start.17 = (bf16[512,768]{1,0:T(8,128)(2,1)S(1)}, bf16[512,768]{1,0:T(8,128)(2,1)S(1)}, u32[]{:S(2)}, u32[]{:S(2)}) collective-permute-start(bf16[512,768]{1,0:T(8,128)(2,1)S(1)} %constant_dynamic-slice_fusion.1), channel_id=1, source_target_pairs={{0,1},{1,0},{2,3},{3,2},{4,5},{5,4},{6,7},{7,6},{8,9},{9,8},{10,11... | collective-permute-start | bytes 2359304 | tf_op jit(solution)/shard_map/ppermute | solution.py:451
  119.8 45.7 %all-to-all-start.1 = ((bf16[16,48,1536]{2,1,0:T(8,128)(2,1)}), bf16[16,48,1536]{2,1,0:T(8,128)(2,1)S(1)}, u32[]{:S(2)}, u32[]{:S(2)}) async-start(bf16[16,48,1536]{2,1,0:T(8,128)(2,1)} %bitcast.60), calls=%async_computation.1 | async-start | bytes 4718592 | tf_op jit(solution)/shard_map/all_to_all | solution.py:460
  155.0 1.7 collective-permute-start.18
  194.7 9.4 %copy-start.6 = (bf16[512,1536]{1,0:T(8,128)(2,1)S(1)}, bf16[512,1536]{1,0:T(8,128)(2,1)}, u32[]{:S(2)}) copy-start(bf16[512,1536]{1,0:T(8,128)(2,1)} %swish.1) | copy-start | bytes 4718596
  196.1 31.0 %all-to-all-start.3 = ((f32[16,2,104,96]{2,3,1,0:T(8,128)}), f32[16,2,104,96]{2,3,1,0:T(8,128)S(1)}, u32[]{:S(2)}, u32[]{:S(2)}) async-start(f32[16,2,104,96]{2,3,1,0:T(8,128)} %broadcast_in_dim.8), calls=%async_computation.3 | async-start | bytes 3145728 | tf_op jit(solution)/shard_map/all_to_all | solution.py:477
Sparse Core Ops, SparseCore 0:
  9.8 48.9 all-gather.1

commit v6 on v5

--- a/solution.py
+++ b/solution.py
@@ -41,24 +41,37 @@
             taps[g, pl.ds(8 * k, 8), :] = jnp.broadcast_to(row, (8, LANES))
 
 
-def row_of(v):
-    return 8 * row_iota(8) + v
-
-
-def shifted(window, g, w):
-    return window[g, pl.ds(w, 8, stride=8), :]
-
-
-def conv_block(window, taps, g):
-    xs = [shifted(window, g, w) for w in range(7)]
-    acc = [None] * 8
+def row_of(v, n):
+    return n * row_iota(8) + v
+
+
+def shifted(window, g, w, n):
+    return window[g, pl.ds(w, 8, stride=n), :]
+
+
+def conv_rows(window, taps, g, base, n):
+    xs = [shifted(window, g, base + w, n) for w in range(n - 1)]
+    acc = [None] * n
     for k in range(KER):
-        xs.append(shifted(window, g, k + 7))
+        xs.append(shifted(window, g, base + k + n - 1, n))
         tap = taps[g, pl.ds(8 * k, 8), :]
-        for v in range(8):
+        for v in range(n):
             acc[v] = tap * xs[v] if k == 0 else acc[v] + tap * xs[v]
         xs.pop(0)
     return acc
+
+
+def in_rows(alone, begin, stop, per_rows):
+    @pl.when(alone)
+    def _():
+        per_rows(0, 8)
+
+    for base in (0, BLOCK // 2):
+        meets = (begin < base + BLOCK // 2) & (stop > base)
+
+        @pl.when(jnp.logical_not(alone) & meets)
+        def _():
+            per_rows(base, 4)
 
 
 def utterances(first, second, row):
@@ -133,13 +146,22 @@
     )(target_row, segment.reshape(NB // 2, 2 * BLOCK), x)
 
 
-def stats_kernel(bounds_ref, x_ref, kern_ref, _, out_ref, window, taps, sums):
+def stats_kernel(bounds_ref, x_ref, kern_ref, _, out_ref, x_sums_ref, window, taps, sums):
     spread_taps(kern_ref, taps)
     sums[...] = jnp.zeros_like(sums)
     first, second, end = bounds_ref[1], bounds_ref[2], bounds_ref[3]
 
+    frame = lax.broadcasted_iota(jnp.int32, (KER, NB * BLOCK), 1)
+    centre = frame - lax.broadcasted_iota(jnp.int32, (KER, NB * BLOCK), 0) + LEFT
+    low, high = jnp.minimum(frame, centre), jnp.maximum(frame, centre)
+    meets = jnp.zeros((KER, NB * BLOCK), F32)
+    for u in range(3):
+        meets = jnp.where((low >= bounds_ref[u]) & (high < bounds_ref[u + 1]), 1.0, meets)
+    x_sums_ref[...] = jnp.dot(meets.astype(BF16), x_ref[...], preferred_element_type=F32)
+
     def block(n, carry):
         row = n * BLOCK
+        low, high = utterances(first, second, row)
 
         def part(u, inner):
             begin, stop = bounds_ref[u], bounds_ref[u + 1]
@@ -151,19 +173,23 @@
                 for g in range(TILES):
                     x = x_ref[pl.ds(pl.multiple_of(source, 16), size), tile(g)].astype(F32)
                     window[g, pl.ds(place, size), :] = jnp.where(keep, x, 0.0)
-            for g in range(TILES):
-                acc = conv_block(window, taps, g)
-                total, square = sums[g, pl.ds(0, 8), :], sums[g, pl.ds(8, 8), :]
-                for v in range(8):
-                    at = row_of(v) + row
-                    h = jnp.where((at >= begin) & (at < stop), acc[v], 0.0)
-                    total = total + h
-                    square = square + h * h
-                sums[g, pl.ds(0, 8), :] = total
-                sums[g, pl.ds(8, 8), :] = square
+
+            def per_rows(base, n):
+                for g in range(TILES):
+                    acc = conv_rows(window, taps, g, base, n)
+                    total, square = sums[g, pl.ds(0, 8), :], sums[g, pl.ds(8, 8), :]
+                    for v in range(n):
+                        at = row_of(v, n) + (row + base)
+                        h = jnp.where((at >= begin) & (at < stop), acc[v], 0.0)
+                        total = total + h
+                        square = square + h * h
+                    sums[g, pl.ds(0, 8), :] = total
+                    sums[g, pl.ds(8, 8), :] = square
+
+            in_rows(low + 1 == high, begin - row, stop - row, per_rows)
             return inner
 
-        return lax.fori_loop(*utterances(first, second, row), part, carry)
+        return lax.fori_loop(low, high, part, carry)
 
     lax.fori_loop(0, end // BLOCK, block, 0)
     for g in range(TILES):
@@ -177,14 +203,20 @@
     return pl.pallas_call(
         stats_kernel,
         grid=(width // WIDE,),
-        out_shape=jax.ShapeDtypeStruct((2, width), F32),
+        out_shape=(
+            jax.ShapeDtypeStruct((2, width), F32),
+            jax.ShapeDtypeStruct((KER, width), F32),
+        ),
         in_specs=[
             SMEM_SPEC,
             pl.BlockSpec((NB * BLOCK, WIDE), lambda c: (0, c)),
             pl.BlockSpec((KER, WIDE), lambda c: (0, c)),
             pl.BlockSpec(memory_space=pl.ANY),
         ],
-        out_specs=pl.BlockSpec((2, WIDE), lambda c: (0, c)),
+        out_specs=(
+            pl.BlockSpec((2, WIDE), lambda c: (0, c)),
+            pl.BlockSpec((KER, WIDE), lambda c: (0, c)),
+        ),
         scratch_shapes=[
             pltpu.VMEM((TILES, WIN, LANES), F32),
             pltpu.VMEM((TILES, 8 * KER, LANES), F32),
@@ -195,12 +227,15 @@
     )(bounds, x, kern, earlier)
 
 
-def live_parts(info_ref, got_ref, window, per_part):
+def live_parts(info_ref, got_ref, window, per_part, per_block=None):
     def slot(s, n):
         valid = info_ref[5 * s] > 0
 
         @pl.when(valid)
         def _():
+            at = pl.multiple_of(n * BLOCK, BLOCK)
+            low, high = utterances(info_ref[5 * s + 2], info_ref[5 * s + 3], LEFT)
+
             def part(u, carry):
                 begin, stop = info_ref[5 * s + 1 + u], info_ref[5 * s + 2 + u]
                 rows = row_iota(WIN)
@@ -208,12 +243,17 @@
                 for g in range(TILES):
                     x = got_ref[s, :, tile(g)].astype(F32)
                     window[g] = jnp.where(keep, x, 0.0)
-                per_part(pl.multiple_of(n * BLOCK, BLOCK), begin - LEFT, stop - LEFT)
+                begin, stop = begin - LEFT, stop - LEFT
+
+                def per_rows(base, groups):
+                    per_part(at + base, begin - base, stop - base, base, groups)
+
+                in_rows(low + 1 == high, begin, stop, per_rows)
                 return carry
 
-            lax.fori_loop(
-                *utterances(info_ref[5 * s + 2], info_ref[5 * s + 3], LEFT), part, 0
-            )
+            lax.fori_loop(low, high, part, 0)
+            if per_block is not None:
+                per_block(at)
 
         return n + valid.astype(jnp.int32)
 
@@ -221,18 +261,22 @@
 
 
 def hidden_kernel(info_ref, got_ref, kern_ref, *rest):
-    h_ref, window, taps = rest[-3:]
+    h_ref, window, rows, taps = rest[-4:]
     spread_taps(kern_ref, taps)
 
-    def per_part(at, begin, stop):
+    def per_part(at, begin, stop, base, n):
         for g in range(TILES):
-            acc = conv_block(window, taps, g)
-            for v in range(8):
-                place = pl.ds(at + v, 8, stride=8)
-                keep = (row_of(v) >= begin) & (row_of(v) < stop)
-                h_ref[g, place, :] = jnp.where(keep, acc[v], h_ref[g, place, :])
-
-    live_parts(info_ref, got_ref, window, per_part)
+            acc = conv_rows(window, taps, g, base, n)
+            for v in range(n):
+                place = pl.ds(base + v, 8, stride=n)
+                keep = (row_of(v, n) >= begin) & (row_of(v, n) < stop)
+                rows[g, place, :] = jnp.where(keep, acc[v], rows[g, place, :])
+
+    def per_block(at):
+        for g in range(TILES):
+            h_ref[pl.ds(at, BLOCK), tile(g)] = rows[g]
+
+    live_parts(info_ref, got_ref, window, per_part, per_block)
 
 
 def hidden(info, got, kern, *earlier):
@@ -241,16 +285,17 @@
     return pl.pallas_call(
         hidden_kernel,
         grid=(width // WIDE,),
-        out_shape=jax.ShapeDtypeStruct((width // LANES, rows, LANES), F32),
+        out_shape=jax.ShapeDtypeStruct((rows, width), F32),
         in_specs=[
             SMEM_SPEC,
             pl.BlockSpec((16, WIN, WIDE), lambda c: (0, 0, c)),
             pl.BlockSpec((KER, WIDE), lambda c: (0, c)),
         ]
         + [pl.BlockSpec(memory_space=pl.ANY)] * len(earlier),
-        out_specs=pl.BlockSpec((TILES, rows, LANES), lambda c: (c, 0, 0)),
+        out_specs=pl.BlockSpec((rows, WIDE), lambda c: (0, c)),
         scratch_shapes=[
             pltpu.VMEM((TILES, WIN, LANES), F32),
+            pltpu.VMEM((TILES, BLOCK, LANES), F32),
             pltpu.VMEM((TILES, 8 * KER, LANES), F32),
         ],
         cost_estimate=cost(12),
@@ -258,47 +303,24 @@
     )(info, got, kern, *earlier)
 
 
-def swish_kernel(h_ref, norm_ref, sw_ref):
-    for g in range(TILES):
-        mean, inverse = norm_ref[pl.ds(0, 1), tile(g)], norm_ref[pl.ds(1, 1), tile(g)]
-        scale, shift = norm_ref[pl.ds(2, 1), tile(g)], norm_ref[pl.ds(3, 1), tile(g)]
-        a = (h_ref[g] - mean) * inverse * scale + shift
-        sw_ref[:, tile(g)] = (a * jax.nn.sigmoid(a)).astype(BF16)
-
-
-def swish(h, norm):
-    tiles, rows, _ = h.shape
-    return pl.pallas_call(
-        swish_kernel,
-        grid=(tiles // TILES,),
-        out_shape=jax.ShapeDtypeStruct((rows, tiles * LANES), BF16),
-        in_specs=[
-            pl.BlockSpec((TILES, rows, LANES), lambda c: (c, 0, 0)),
-            pl.BlockSpec((4, WIDE), lambda c: (0, c)),
-        ],
-        out_specs=pl.BlockSpec((rows, WIDE), lambda c: (0, c)),
-        cost_estimate=cost(3),
-        name="swish",
-    )(h, norm)
-
-
 def terms_kernel(
-    info_ref, got_ref, h_ref, wide_ref, norm_ref, out_ref, window, back_ref, acc_a, acc_x, sums
+    info_ref, got_ref, wide_h, wide_back, norm_ref, out_ref, window, h_ref, back_ref, acc_a, acc_x, sums
 ):
     for g in range(TILES):
-        back_ref[g] = wide_ref[:, tile(g)]
+        h_ref[g] = wide_h[:, tile(g)]
+        back_ref[g] = wide_back[:, tile(g)]
     acc_a[...] = jnp.zeros_like(acc_a)
     acc_x[...] = jnp.zeros_like(acc_x)
     sums[...] = jnp.zeros_like(sums)
 
-    def per_tile(g, at, begin, stop):
+    def per_tile(g, at, begin, stop, base, n):
         mean, inverse = norm_ref[pl.ds(0, 1), tile(g)], norm_ref[pl.ds(1, 1), tile(g)]
         scale, shift = norm_ref[pl.ds(2, 1), tile(g)], norm_ref[pl.ds(3, 1), tile(g)]
         das, hats = [], []
         sum_x, sum_1 = sums[g, pl.ds(0, 8), :], sums[g, pl.ds(8, 8), :]
-        for v in range(8):
-            place = pl.ds(at + v, 8, stride=8)
-            keep = (row_of(v) >= begin) & (row_of(v) < stop)
+        for v in range(n):
+            place = pl.ds(at + v, 8, stride=n)
+            keep = (row_of(v, n) >= begin) & (row_of(v, n) < stop)
             hat = (h_ref[g, place, :] - mean) * inverse
             a = hat * scale + shift
             sig = jax.nn.sigmoid(a)
@@ -311,20 +333,20 @@
             hats.append(hat)
         sums[g, pl.ds(0, 8), :] = sum_x
         sums[g, pl.ds(8, 8), :] = sum_1
-        xs = [shifted(window, g, w) for w in range(7)]
+        xs = [shifted(window, g, base + w, n) for w in range(n - 1)]
         for k in range(KER):
-            xs.append(shifted(window, g, k + 7))
+            xs.append(shifted(window, g, base + k + n - 1, n))
             place = pl.ds(8 * k, 8)
             for acc, rows in ((acc_a, das), (acc_x, hats)):
-                terms_k = [rows[v] * xs[v] for v in range(8)]
+                terms_k = [rows[v] * xs[v] for v in range(n)]
                 while len(terms_k) > 1:
                     terms_k = [p + q for p, q in zip(terms_k[::2], terms_k[1::2])]
                 acc[g, place, :] += terms_k[0]
             xs.pop(0)
 
-    def per_part(at, begin, stop):
+    def per_part(at, begin, stop, base, n):
         for g in range(TILES):
-            per_tile(g, at, begin, stop)
+            per_tile(g, at, begin, stop, base, n)
 
     live_parts(info_ref, got_ref, window, per_part)
     for g in range(TILES):
@@ -334,7 +356,7 @@
         for i in range(2):
             part = sums[g, pl.ds(8 * i, 8), :]
             out_ref[pl.ds(2 * KER + i, 1), tile(g)] = jnp.sum(part, axis=0, keepdims=True)
-    out_ref[pl.ds(66, 14), :] = jnp.zeros((14, WIDE), F32)
+    out_ref[pl.ds(66, 6), :] = jnp.zeros((6, WIDE), F32)
 
 
 def terms(info, got, h, back, norm):
@@ -342,17 +364,18 @@
     return pl.pallas_call(
         terms_kernel,
         grid=(width // WIDE,),
-        out_shape=jax.ShapeDtypeStruct((80, width), F32),
+        out_shape=jax.ShapeDtypeStruct((72, width), F32),
         in_specs=[
             SMEM_SPEC,
             pl.BlockSpec((16, WIN, WIDE), lambda c: (0, 0, c)),
-            pl.BlockSpec((TILES, BLOCKS * BLOCK, LANES), lambda c: (c, 0, 0)),
+            pl.BlockSpec((BLOCKS * BLOCK, WIDE), lambda c: (0, c)),
             pl.BlockSpec((BLOCKS * BLOCK, WIDE), lambda c: (0, c)),
             pl.BlockSpec((4, WIDE), lambda c: (0, c)),
         ],
-        out_specs=pl.BlockSpec((80, WIDE), lambda c: (0, c)),
+        out_specs=pl.BlockSpec((72, WIDE), lambda c: (0, c)),
         scratch_shapes=[
             pltpu.VMEM((TILES, WIN, LANES), F32),
+            pltpu.VMEM((TILES, BLOCKS * BLOCK, LANES), F32),
             pltpu.VMEM((TILES, BLOCKS * BLOCK, LANES), F32),
             pltpu.VMEM((TILES, 8 * KER, LANES), F32),
             pltpu.VMEM((TILES, 8 * KER, LANES), F32),
@@ -415,21 +438,21 @@
     got = lax.all_to_all(send, "dp", 0, 0, tiled=True)
     w_t = lax.all_gather(w_out.T, "zero", axis=0, tiled=True)
 
-    frame = lax.broadcasted_iota(jnp.int32, (KER, NB * BLOCK), 1)
-    centre = frame - lax.broadcasted_iota(jnp.int32, (KER, NB * BLOCK), 0) + LEFT
-    meets = jnp.zeros((KER, NB * BLOCK), jnp.bool_)
-    for u in range(3):
-        begin, stop = bounds[u], bounds[u + 1]
-        within = (jnp.minimum(frame, centre) >= begin) & (jnp.maximum(frame, centre) < stop)
-        meets = meets | within
-    x_sums = jnp.dot(meets.astype(BF16), x, preferred_element_type=F32)
+    column = lax.broadcasted_iota(jnp.int32, (width, half), 0)
+    place = lax.broadcasted_iota(jnp.int32, (width, half), 1)
+    even = column == place + share * (place // share)
+    odd = column == place + share * (place // share) + share
+    own_columns = jnp.where(core == 0, even, odd).astype(BF16)
+    other_columns = jnp.where(core == 0, odd, even).astype(BF16)
 
     pairs, join = gather_small(small, zero_id, send)
-    pairs, x_sums = lax.optimization_barrier((pairs, x_sums))
+    cot_own = jnp.dot(cot, own_columns, preferred_element_type=F32).astype(BF16)
+    cot_send = jnp.dot(cot, other_columns, preferred_element_type=F32).astype(BF16)
+    pairs, cot_own, cot_send = lax.optimization_barrier((pairs, cot_own, cot_send))
     small_full = jnp.transpose(join(pairs), (1, 0, 2)).reshape(48, width).astype(F32)
     kern_full = small_full[:KER]
 
-    sums = stats(bounds, x, kern_full, send)
+    sums, x_sums = stats(bounds, x, kern_full, send)
     for steps in ((1,), (2,), (4, 8, 12)):
         sums, _ = add_from(sums, "zero", [zero_step(step) for step in steps])
     sums, cot_now = lax.optimization_barrier((sums, cot))
@@ -438,7 +461,7 @@
 
     got, back = lax.optimization_barrier((got, back))
     info = got[:, WIN - 1, :5].astype(jnp.int32).reshape(80)
-    cot_other = lax.ppermute(cot, "zero", swap)
+    cot_other = lax.ppermute(cot_send, "zero", swap)
     h = hidden(info, got, kern_full, cot_other)
     sums, (h,) = add_from(sums, "dp", [dp_step(step, False) for step in (1, 2, 3)], h)
     frame_count = jnp.float32(BLOCKS * BLOCK * 256)
@@ -446,17 +469,14 @@
     var = sums[1] / frame_count - mean * mean
     inverse = lax.rsqrt(var + EPS)
     norm = jnp.stack([mean, inverse, small_full[KER], small_full[KER + 1]])
-    sw = swish(h, norm)
-
-    sw_other = lax.ppermute(
-        lax.dynamic_slice_in_dim(sw, (1 - core) * half, half, 1), "zero", swap
-    )
+    a = (h - mean) * inverse * norm[2] + norm[3]
+    sw = (a * jax.nn.sigmoid(a)).astype(BF16)
+    sw_other = lax.ppermute(sw, "zero", swap)
     contract = (((0,), (0,)), ((), ()))
-    sw_own = lax.dynamic_slice_in_dim(sw, core * half, half, 1)
-    term = lax.dot_general(sw_own, cot, contract, preferred_element_type=F32)
+    term = lax.dot_general(sw, cot_own, contract, preferred_element_type=F32)
     sw_other, term = lax.optimization_barrier((sw_other, term))
     term = term + lax.dot_general(sw_other, cot_other, contract, preferred_element_type=F32)
-    term = term.astype(BF16).reshape(16, share // 2, width)
+    term = term.astype(BF16).reshape(16, share, half)
     term = lax.all_to_all(term, "dp", 0, 0, tiled=True)
 
     grads = terms(info, got, h, back, norm)
@@ -464,24 +484,32 @@
         sw, w_t, (((1,), (1,)), ((), ())), preferred_element_type=F32
     ).astype(BF16)
 
-    grads = jnp.concatenate([grads, x_sums], axis=0)
+    grads = jnp.concatenate([grads, x_sums], axis=0).reshape(104, 8, 2, share)
+    grads = jnp.transpose(grads, (2, 1, 0, 3))
     grads_other = lax.ppermute(
-        lax.dynamic_slice_in_dim(grads, (1 - core) * 56, 56, 0), "zero", swap
+        lax.dynamic_index_in_dim(grads, 1 - core, 0, False), "zero", swap
     )
-    grads = lax.dynamic_slice_in_dim(grads, core * 56, 56, 0) + grads_other
-
-    term = jnp.sum(term.astype(F32), axis=0)
-    both = jnp.concatenate([term, grads], axis=0).reshape(-1, 16, share)
-    both = lax.all_to_all(jnp.transpose(both, (1, 0, 2)), "zero", 0, 0, tiled=True)
-    last = jnp.sum(both.reshape((8, 2) + both.shape[1:]), axis=0)
+    grads = lax.dynamic_index_in_dim(grads, core, 0, False) + grads_other
+
+    term = jnp.sum(term.astype(F32), axis=0).reshape(share, 8, share)
+    both = jnp.concatenate([jnp.transpose(term, (1, 0, 2)), grads], axis=1)
+    both = lax.all_to_all(
+        both,
+        "zero",
+        0,
+        0,
+        axis_index_groups=[[i for i in range(16) if i % 2 == c] for c in range(2)],
+        tiled=True,
+    )
+    last = jnp.sum(both, axis=0)
     last = lax.all_to_all(
         jnp.broadcast_to(last[None], (16,) + last.shape), "dp", 0, 0, tiled=True
     )
-    part_w = jnp.transpose(last[:, :, : share // 2], (1, 0, 2, 3)).reshape(width, share)
-    grads = jnp.sum(last[:, :, share // 2 :], axis=0).reshape(112, share)
+    part_w = last[:, :share].reshape(width, share)
+    grads = jnp.sum(last[:, share:], axis=0)
 
     own = lax.dynamic_slice_in_dim(norm, zero_id * share, share, 1)
-    da_x, hat_x, x_k = grads[:KER], grads[KER : 2 * KER], grads[80 : 80 + KER]
+    da_x, hat_x, x_k = grads[:KER], grads[KER : 2 * KER], grads[72 : 72 + KER]
     sum_x, sum_1 = grads[64], grads[65]
     part_k = (own[2] * own[1]) * (da_x - (sum_1 / frame_count) * x_k - (sum_x / frame_count) * hat_x)
     return out[None, None], part_w, part_k, jnp.stack([sum_x, sum_1])

time: 240 us -> 245 us (1.021); the launches traced: 237 us -> 246 us
  other arithmetic: 9.52 us -> 20.2 us
  waiting for transfers between devices: 38.2 us -> 28.3 us
  local copies, waits for them, and re-layouts: 13 us -> 19.1 us
  Pallas kernels: 49.9 us -> 43.9 us
  starting transfers between devices: 63.2 us -> 67.6 us
    pallas_call x2 -> x1, Pallas kernels: 15.6 us -> 7.52 us  [stats(): pl.pallas_call(stats_kernel, grid=(width // WIDE,), out_shape=(jax.ShapeD...]
    all_to_all x1, waiting for transfers between devices: 7.71 us -> 1.09 us  [per_device(): term = lax.all_to_all(term, 'dp', 0, 0, tiled=True)]
    reduce_sum x3, other arithmetic: 0.85 us -> 5.59 us  [the longest x1 2.72 us: per_device(): term = jnp.sum(term.astype(F32), axis=0).reshape(share, 8, share)]
    ppermute x11, starting transfers between devices: 22.8 us -> 26.7 us  [add_from(): parts = [lax.ppermute(x, axis, step) for step in steps]]
    reshape x1 -> x2, local copies, waits for them, and re-layouts: 0.28 us -> 3.02 us  [the longest x1 1.88 us: per_device(): term = jnp.sum(term.astype(F32), axis=0).reshape(share, 8, share)]
    convert_element_type x1 -> x2, other arithmetic: 2.14 us -> 4.74 us  [the longest x1 2.87 us: per_device(): sw = (a * jax.nn.sigmoid(a)).astype(BF16)]
    dot_general x2 -> x3, matrix products: 5.52 us -> 7.89 us  [the longest x1 2.84 us: per_device(): jnp.dot(cot, other_columns, preferred_element_type=F32).astype(BF16)]
    unnamed x15 -> x18, local copies, waits for them, and re-layouts: 5.49 us -> 7.17 us
  transfers between devices with their start and end apart: 23 -> 23, of which waited for: 8 -> 8; matrix products, arithmetic and copies ran while one was open for 11% -> 14% of each run, Pallas kernels for 19% -> 18%
where the time goes in v6:
time: 245 us; the launch traced here: 246 us
  starting transfers between devices  67.6 us (28%)
  Pallas kernels  43.9 us (18%)
  blocking collectives  29 us (12%)
  waiting for transfers between devices  28.3 us (12%)
  matrix products  23.4 us (10%)
  other arithmetic  20.2 us (8%)
  local copies, waits for them, and re-layouts  19.1 us (8%)
  between operations  14.4 us (6%)
    all_to_all x1, blocking collectives, per_device(): lax.all_to_all(both, 'zero', 0, 0, axis_index_groups=[[i for i in range(1...  29 us
    ppermute x11, starting transfers between devices, add_from(): parts = [lax.ppermute(x, axis, step) for step in steps]  26.7 us
    pallas_call x1, Pallas kernels, terms(): pl.pallas_call(terms_kernel, grid=(width // WIDE,), out_shape=jax.ShapeDt...  21.7 us
    all_to_all x1, waiting for transfers between devices, per_device(): lax.all_to_all(jnp.broadcast_to(last[None], (16,) + last.shape), 'dp', 0,...  15.9 us
    pallas_call x1, Pallas kernels, hidden(): pl.pallas_call(hidden_kernel, grid=(width // WIDE,), out_shape=jax.ShapeD...  12.8 us
    all_to_all x1, starting transfers between devices, per_device(): term = lax.all_to_all(term, 'dp', 0, 0, tiled=True)  11.8 us
    ppermute x3, starting transfers between devices, gather_small(): lax.ppermute(x, 'zero', zero_step(step))  10.2 us
    pallas_call x1, Pallas kernels, stats(): pl.pallas_call(stats_kernel, grid=(width // WIDE,), out_shape=(jax.ShapeD...  7.52 us
  transfers between devices with their start and end apart: 23, of which 8 were waited for; matrix products, arithmetic and copies ran while one was open for 14% of the time, Pallas kernels for 18%

profile of v6, /device:TPU:8, one launch (start us, length us, event | category | flops | bytes accessed | tf_op | source)
XLA Modules:
  0.0 245.9 jit_solution(3708903514417607047)
XLA Ops:
  7.2 0.7 all-gather.2.cloned.1.call-update
  8.0 0.8 maximum_maximum_fusion
  8.8 0.7 reduce
  9.5 1.7 copy-done.2
  11.2 0.7 copy-done.3
  11.9 2.0 pack.1
  13.9 2.1 copy-done.1
  16.0 0.5 copy-done.4
  16.5 7.4 %all-to-all-start = ((bf16[16,96,1536]{2,1,0:T(8,128)(2,1)}), bf16[16,96,1536]{2,1,0:T(8,128)(2,1)}, u32[]{:S(2)}, u32[]{:S(2)}) async-start(bf16[16,96,1536]{2,1,0:T(8,128)(2,1)} %copy-done.1), calls=%async_computation | async-start | bytes 9437184 | tf_op jit(solution)/shard_map/all_to_all | solution.py:438
  24.0 2.0 collective-permute-start.1
  26.0 2.4 fusion.23
  28.4 6.2 %collective-permute-start.4 = (bf16[2,2,48,96]{3,2,1,0:T(8,128)(2,1)S(1)}, bf16[2,2,48,96]{3,2,1,0:T(8,128)(2,1)S(1)}, u32[]{:S(2)}, u32[]{:S(2)}) collective-permute-start(bf16[2,2,48,96]{3,2,1,0:T(8,128)(2,1)S(1)} %pad_maximum_fusion.3), channel_id=1, source_target_pairs={{0,12},{1,13},{2,14},{3,15},{4,0},{5,1},{6,2},{7,3},{8,4},{9,5},{1... | collective-permute-start | bytes 110600 | tf_op jit(solution)/shard_map/ppermute | solution.py:412
  34.7 1.2 collective-permute-start.3
  35.8 2.8 %collective-permute-start.2 = (bf16[2,2,48,96]{3,2,1,0:T(8,128)(2,1)S(1)}, bf16[2,2,48,96]{3,2,1,0:T(8,128)(2,1)S(1)}, u32[]{:S(2)}, u32[]{:S(2)}) collective-permute-start(bf16[2,2,48,96]{3,2,1,0:T(8,128)(2,1)S(1)} %pad_maximum_fusion.3), channel_id=1, source_target_pairs={{0,4},{1,5},{2,6},{3,7},{4,8},{5,9},{6,10},{7,11},{8,12},{9,13},{1... | collective-permute-start | bytes 110600 | tf_op jit(solution)/shard_map/ppermute | solution.py:412
  38.6 2.8 %fusion.20 = bf16[512,768]{1,0:T(8,128)(2,1)} fusion(s32[768]{0:T(1024)S(1)} %get-tuple-element.90, s32[768]{0:T(1024)S(1)} %get-tuple-element.91, pred[768]{0:T(1024)(128)(4,1)S(1)} %fusion.32, pred[]{:T(512)S(6)} %eq.74, bf16[1,1,512,1536]{3,2,1,0:T(8,128)(2,1)S(1)} %copy-done), kind=kOutput, calls=%fused_computation.24 | convolution fusion | flops 1216610304 | bytes 2366209 | tf_op jit(solution)/shard_map/dot_general | solution.py:450
  41.5 3.4 %collective-permute-done.3 = bf16[2,2,48,96]{3,2,1,0:T(8,128)(2,1)S(1)} collective-permute-done((bf16[2,2,48,96]{3,2,1,0:T(8,128)(2,1)S(1)}, bf16[2,2,48,96]{3,2,1,0:T(8,128)(2,1)S(1)}, u32[]{:S(2)}, u32[]{:S(2)}) %collective-permute-start.3) | collective-permute-done | bytes 36896 | tf_op jit(solution)/shard_map/ppermute | solution.py:412
  45.2 0.8 slice.58.kern_ref
  46.0 7.5 %stats.1 = (f32[2,1536]{1,0:T(2,128)}, f32[32,1536]{1,0:T(8,128)}) custom-call(s32[4]{0:T(128)} %copy-done.4, bf16[768,1536]{1,0:T(8,128)(2,1)} %bitcast.66, f32[32,1536]{1,0:T(8,128)} %slice.58.kern_ref, bf16[16,96,1536]{2,1,0:T(8,128)(2,1)} %copy-done.1), custom_call_target="tpu_custom_call" | custom-call | flops 16499999744 | bytes 1000000 | tf_op jit(solution)/shard_map/stats/pallas_call | solution.py:203
  53.5 1.7 collective-permute-start.5
  55.2 1.0 collective-permute-done.5
  56.3 0.7 add.122
  57.0 8.5 %collective-permute-start.6 = (f32[2,1536]{1,0:T(2,128)S(1)}, f32[2,1536]{1,0:T(2,128)S(1)}, u32[]{:S(2)}, u32[]{:S(2)}) collective-permute-start(f32[2,1536]{1,0:T(2,128)S(1)} %add.122), channel_id=1, source_target_pairs={{0,2},{1,3},{2,0},{3,1},{4,6},{5,7},{6,4},{7,5},{8,10},{9,11},{10,... | collective-permute-start | bytes 36872 | tf_op jit(solution)/shard_map/ppermute | solution.py:402
  65.4 1.7 collective-permute-done.6
  67.2 4.8 %collective-permute-start.8 = (f32[2,1536]{1,0:T(2,128)S(1)}, f32[2,1536]{1,0:T(2,128)S(1)}, u32[]{:S(2)}, u32[]{:S(2)}) collective-permute-start(f32[2,1536]{1,0:T(2,128)S(1)} %add.123), channel_id=1, source_target_pairs={{0,8},{1,9},{2,10},{3,11},{4,12},{5,13},{6,14},{7,15},{8,0},{9,1},... | collective-permute-start | bytes 36872 | tf_op jit(solution)/shard_map/ppermute | solution.py:402
  72.0 2.6 %collective-permute-start.7 = (f32[2,1536]{1,0:T(2,128)S(1)}, f32[2,1536]{1,0:T(2,128)S(1)}, u32[]{:S(2)}, u32[]{:S(2)}) collective-permute-start(f32[2,1536]{1,0:T(2,128)S(1)} %add.123), channel_id=1, source_target_pairs={{0,4},{1,5},{2,6},{3,7},{4,8},{5,9},{6,10},{7,11},{8,12},{9,13},{1... | collective-permute-start | bytes 36872 | tf_op jit(solution)/shard_map/ppermute | solution.py:402
  75.0 2.8 %collective-permute-done.7 = f32[2,1536]{1,0:T(2,128)S(1)} collective-permute-done((f32[2,1536]{1,0:T(2,128)S(1)}, f32[2,1536]{1,0:T(2,128)S(1)}, u32[]{:S(2)}, u32[]{:S(2)}) %collective-permute-start.7) | collective-permute-done | bytes 12320 | tf_op jit(solution)/shard_map/ppermute | solution.py:402
  78.0 4.0 %collective-permute-start.11 = (f32[2,1536]{1,0:T(2,128)S(1)}, f32[2,1536]{1,0:T(2,128)S(1)}, u32[]{:S(2)}, u32[]{:S(2)}) collective-permute-start(f32[2,1536]{1,0:T(2,128)S(1)} %add_add_fusion.2), channel_id=1, source_target_pairs={{0,32},{16,48},{32,0},{48,16},{64,96},{80,112},{96,64},{112,80},{1... | collective-permute-start | bytes 36872 | tf_op jit(solution)/shard_map/ppermute | solution.py:402
  82.5 6.6 %fusion.40.wide_back = f32[512,1536]{1,0:T(8,128)} fusion(bf16[512,1536]{1,0:T(8,128)(2,1)S(1)} %bitcast.64, bf16[1536,1536]{1,0:T(8,128)(2,1)} %all-gather.2.cloned.1.call-done), kind=kOutput, calls=%fused_computation.79 | convolution fusion | flops 2415919104 | bytes 9437184 | tf_op jit(solution)/shard_map/dot_general | solution.py:459
  89.2 3.4 %collective-permute-start.15 = (f32[2,1536]{1,0:T(2,128)S(1)}, f32[2,1536]{1,0:T(2,128)S(1)}, u32[]{:S(2)}, u32[]{:S(2)}) collective-permute-start(f32[2,1536]{1,0:T(2,128)S(1)} %add_add_fusion.1), channel_id=1, source_target_pairs={{0,192},{16,208},{32,224},{48,240},{64,0},{80,16},{96,32},{112,48}... | collective-permute-start | bytes 36872 | tf_op jit(solution)/shard_map/ppermute | solution.py:402
  92.7 0.9 collective-permute-start.13
  93.6 0.8 convert_reduce_fusion.1
  94.4 0.6 reshape.40.info_ref
  95.0 0.9 copy-done.5
  95.9 12.8 %hidden.1.wide_h = f32[512,1536]{1,0:T(8,128)} custom-call(s32[80]{0:T(128)} %reshape.40.info_ref, bf16[16,96,1536]{2,1,0:T(8,128)(2,1)} %all-to-all-done.got_ref, f32[32,1536]{1,0:T(8,128)} %slice.58.kern_ref, bf16[512,768]{1,0:T(8,128)(2,1)} %copy-done.5), custom_call_target="tpu_custom_call" | custom-call | flops 13200000000 | bytes 1000000 | tf_op jit(solution)/shard_map/hidden/pallas_call | solution.py:285
  108.7 0.6 slice_multiply_fusion.5
  109.3 2.9 %multiply_convert_fusion = bf16[512,1536]{1,0:T(8,128)(2,1)S(1)} fusion(f32[512,1536]{1,0:T(8,128)} %hidden.1.wide_h, f32[1536]{0:T(1024)S(1)} %add.135, f32[1536]{0:T(1024)S(1)} %mul.79, f32[1536]{0:T(1024)S(1)} %get-tuple-element.88, f32[1536]{0:T(1024)S(1)} %get-tuple-element.87), kind=kLoop, calls=%fused_computation.8 | loop fusion | flops 7077888 | bytes 4743168 | tf_op jit(solution)/shard_map/convert_element_type | solution.py:473
  112.4 1.3 pad_maximum_fusion.5.norm_ref
  113.7 2.6 %fusion.41 = f32[1536,768]{1,0:T(8,128)S(1)} fusion(bf16[512,1536]{1,0:T(8,128)(2,1)S(1)} %multiply_convert_fusion, bf16[512,768]{0,1:T(8,128)(2,1)} %fusion.23), kind=kOutput, calls=%fused_computation.80 | convolution fusion | flops 1207959552 | bytes 7077888 | tf_op jit(solution)/shard_map/dot_general | solution.py:476
  116.4 2.8 %fusion.42 = f32[1536,768]{1,0:T(8,128)S(1)} fusion(bf16[512,1536]{1,0:T(8,128)(2,1)} %collective-permute-done.17, bf16[512,768]{1,0:T(8,128)(2,1)S(1)} %copy-done.6), kind=kOutput, calls=%fused_computation.81 | convolution fusion | flops 1207959552 | bytes 7077888 | tf_op jit(solution)/shard_map/dot_general | solution.py:478
  119.2 1.9 add_convert_fusion
  121.1 11.8 %all-to-all-start.1 = ((bf16[16,96,768]{2,1,0:T(8,128)(2,1)}), bf16[16,96,768]{2,1,0:T(8,128)(2,1)}, u32[]{:S(2)}, u32[]{:S(2)}) async-start(bf16[16,96,768]{2,1,0:T(8,128)(2,1)} %bitcast.69), calls=%async_computation.1 | async-start | bytes 4718592 | tf_op jit(solution)/shard_map/all_to_all | solution.py:480
  132.9 21.7 %terms.1 = f32[72,1536]{1,0:T(8,128)} custom-call(s32[80]{0:T(128)} %reshape.40.info_ref, bf16[16,96,1536]{2,1,0:T(8,128)(2,1)} %all-to-all-done.got_ref, f32[512,1536]{1,0:T(8,128)} %hidden.1.wide_h, f32[512,1536]{1,0:T(8,128)} %fusion.40.wide_back, f32[4,1536]{1,0:T(4,128)} %pad_maximum_fusion.5.norm_ref), custom_call_target="tpu_custom_call" | custom-call | flops 27499999232 | bytes 1000000 | tf_op jit(solution)/shard_map/terms/pallas_call | solution.py:364
  154.5 1.9 pad_maximum_fusion.1
  156.4 2.2 copy.29
  158.7 1.0 dynamic-slice_bitcast_fusion
  159.7 1.9 collective-permute-start.18
  161.6 1.5 collective-permute-done.18
  163.1 1.2 bitcast_add_fusion
  164.2 1.1 all-to-all-done.1
  165.3 2.7 %convert_reduce_fusion = f32[96,768]{1,0:T(8,128)} fusion(bf16[16,96,768]{2,1,0:T(8,128)(2,1)} %all-to-all-done.1), kind=kLoop, calls=%fused_computation | loop fusion | flops 2285568 | bytes 2654208 | tf_op jit(solution)/shard_map/reduce_sum | solution.py:494
  168.1 1.9 copy.36
  169.9 1.3 pad_maximum_fusion
  171.2 29.0 %all_to_all.20 = f32[8,200,96]{1,2,0:T(8,128)} all-to-all(f32[8,200,96]{1,2,0:T(8,128)S(1)} %pad_maximum_fusion), channel_id=1, replica_groups={{0,2,4,6,8,10,12,14},{1,3,5,7,9,11,13,15},{16,18,20,22,24,26,28,30},{17..., dimensions={0} | all-to-all | bytes 1228800 | tf_op jit(solution)/shard_map/all_to_all | solution.py:496
  200.2 1.2 reduce_sum.28
  201.4 1.3 broadcast_in_dim.8
  202.7 7.4 %all-to-all-start.3 = ((f32[16,200,96]{1,2,0:T(8,128)}), f32[16,200,96]{1,2,0:T(8,128)}, u32[]{:S(2)}, u32[]{:S(2)}) async-start(f32[16,200,96]{1,2,0:T(8,128)} %broadcast_in_dim.8), calls=%async_computation.3 | async-start | bytes 3145728 | tf_op jit(solution)/shard_map/all_to_all | solution.py:505
  210.1 0.7 constant_dynamic-slice_fusion
  210.8 6.1 %fusion.3 = bf16[1,1,512,1536]{3,2,1,0:T(8,128)(2,1)} fusion(bf16[512,1536]{1,0:T(8,128)(2,1)S(1)} %multiply_convert_fusion, bf16[1536,1536]{1,0:T(8,128)(2,1)} %all-gather.2.cloned.1.call-done), kind=kOutput, calls=%fused_computation.10 | convolution fusion | flops 2416705536 | bytes 7864320 | tf_op jit(solution)/shard_map/dot_general | solution.py:483
  216.9 15.9 %all-to-all-done.3 = f32[16,200,96]{1,2,0:T(8,128)} async-done(((f32[16,200,96]{1,2,0:T(8,128)}), f32[16,200,96]{1,2,0:T(8,128)}, u32[]{:S(2)}, u32[]{:S(2)}) %all-to-all-start.3) | async-done | bytes 1228832 | tf_op jit(solution)/shard_map/all_to_all | solution.py:505
  232.8 1.7 slice_reduce_fusion
  234.8 1.2 slice.81
  236.4 1.1 reshape.39
  237.7 0.7 copy.33
  238.4 0.6 copy.34
  (62 shorter events, 2.7 us)
Async XLA Ops:
  7.2 18.8 %copy-start = (bf16[1,1,512,1536]{3,2,1,0:T(8,128)(2,1)S(1)}, bf16[1,1,512,1536]{3,2,1,0:T(8,128)(2,1)}, u32[]{:S(2)}) copy-start(bf16[1,1,512,1536]{3,2,1,0:T(8,128)(2,1)} %param.10) | copy-start | bytes 4718596
  7.2 75.3 %all-gather.2.cloned.1.call-start = ((), (), s32[]{:S(2)}) async-start(), calls=%async_computation.4 | async-start | bytes 5013504 | tf_op jit(solution)/shard_map/all_gather | solution.py:439
  8.8 15.2 %collective-permute-start = (bf16[48,96]{1,0:T(8,128)(2,1)S(1)}, bf16[48,96]{1,0:T(8,128)(2,1)S(1)}, u32[]{:S(2)}, u32[]{:S(2)}) collective-permute-start(bf16[48,96]{1,0:T(8,128)(2,1)S(1)} %maximum_maximum_fusion), channel_id=1, source_target_pairs={{0,1},{1,0},{2,3},{3,2},{4,5},{5,4},{6,7},{7,6},{8,9},{9,8},{10,11... | collective-permute-start | bytes 27656 | tf_op jit(solution)/shard_map/ppermute | solution.py:409
  9.5 1.7 copy-start.2
  11.2 0.7 copy-start.3
  13.8 2.1 copy-start.1
  16.0 0.5 copy-start.4
  16.5 77.1 %all-to-all-start = ((bf16[16,96,1536]{2,1,0:T(8,128)(2,1)}), bf16[16,96,1536]{2,1,0:T(8,128)(2,1)}, u32[]{:S(2)}, u32[]{:S(2)}) async-start(bf16[16,96,1536]{2,1,0:T(8,128)(2,1)} %copy-done.1), calls=%async_computation | async-start | bytes 9437184 | tf_op jit(solution)/shard_map/all_to_all | solution.py:438
  24.0 4.4 %collective-permute-start.1 = (bf16[2,48,96]{2,1,0:T(8,128)(2,1)S(1)}, bf16[2,48,96]{2,1,0:T(8,128)(2,1)S(1)}, u32[]{:S(2)}, u32[]{:S(2)}) collective-permute-start(bf16[2,48,96]{2,1,0:T(8,128)(2,1)S(1)} %pad_maximum_fusion.4), channel_id=1, source_target_pairs={{0,2},{1,3},{2,0},{3,1},{4,6},{5,7},{6,4},{7,5},{8,10},{9,11},{10,... | collective-permute-start | bytes 55304 | tf_op jit(solution)/shard_map/ppermute | solution.py:409
  28.4 13.0 %collective-permute-start.4 = (bf16[2,2,48,96]{3,2,1,0:T(8,128)(2,1)S(1)}, bf16[2,2,48,96]{3,2,1,0:T(8,128)(2,1)S(1)}, u32[]{:S(2)}, u32[]{:S(2)}) collective-permute-start(bf16[2,2,48,96]{3,2,1,0:T(8,128)(2,1)S(1)} %pad_maximum_fusion.3), channel_id=1, source_target_pairs={{0,12},{1,13},{2,14},{3,15},{4,0},{5,1},{6,2},{7,3},{8,4},{9,5},{1... | collective-permute-start | bytes 110600 | tf_op jit(solution)/shard_map/ppermute | solution.py:412
  34.7 10.2 %collective-permute-start.3 = (bf16[2,2,48,96]{3,2,1,0:T(8,128)(2,1)S(1)}, bf16[2,2,48,96]{3,2,1,0:T(8,128)(2,1)S(1)}, u32[]{:S(2)}, u32[]{:S(2)}) collective-permute-start(bf16[2,2,48,96]{3,2,1,0:T(8,128)(2,1)S(1)} %pad_maximum_fusion.3), channel_id=1, source_target_pairs={{0,8},{1,9},{2,10},{3,11},{4,12},{5,13},{6,14},{7,15},{8,0},{9,1},... | collective-permute-start | bytes 110600 | tf_op jit(solution)/shard_map/ppermute | solution.py:412
  35.8 9.0 %collective-permute-start.2 = (bf16[2,2,48,96]{3,2,1,0:T(8,128)(2,1)S(1)}, bf16[2,2,48,96]{3,2,1,0:T(8,128)(2,1)S(1)}, u32[]{:S(2)}, u32[]{:S(2)}) collective-permute-start(bf16[2,2,48,96]{3,2,1,0:T(8,128)(2,1)S(1)} %pad_maximum_fusion.3), channel_id=1, source_target_pairs={{0,4},{1,5},{2,6},{3,7},{4,8},{5,9},{6,10},{7,11},{8,12},{9,13},{1... | collective-permute-start | bytes 110600 | tf_op jit(solution)/shard_map/ppermute | solution.py:412
  53.5 2.8 %collective-permute-start.5 = (f32[2,1536]{1,0:T(2,128)}, f32[2,1536]{1,0:T(2,128)S(1)}, u32[]{:S(2)}, u32[]{:S(2)}) collective-permute-start(f32[2,1536]{1,0:T(2,128)} %get-tuple-element.43), channel_id=1, source_target_pairs={{0,1},{1,0},{2,3},{3,2},{4,5},{5,4},{6,7},{7,6},{8,9},{9,8},{10,11... | collective-permute-start | bytes 36872 | tf_op jit(solution)/shard_map/ppermute | solution.py:402
  57.0 10.1 %collective-permute-start.6 = (f32[2,1536]{1,0:T(2,128)S(1)}, f32[2,1536]{1,0:T(2,128)S(1)}, u32[]{:S(2)}, u32[]{:S(2)}) collective-permute-start(f32[2,1536]{1,0:T(2,128)S(1)} %add.122), channel_id=1, source_target_pairs={{0,2},{1,3},{2,0},{3,1},{4,6},{5,7},{6,4},{7,5},{8,10},{9,11},{10,... | collective-permute-start | bytes 36872 | tf_op jit(solution)/shard_map/ppermute | solution.py:402
  67.1 7.7 %collective-permute-start.9 = (f32[2,1536]{1,0:T(2,128)S(1)}, f32[2,1536]{1,0:T(2,128)S(1)}, u32[]{:S(2)}, u32[]{:S(2)}) collective-permute-start(f32[2,1536]{1,0:T(2,128)S(1)} %add.123), channel_id=1, source_target_pairs={{0,12},{1,13},{2,14},{3,15},{4,0},{5,1},{6,2},{7,3},{8,4},{9,5},{1... | collective-permute-start | bytes 36872 | tf_op jit(solution)/shard_map/ppermute | solution.py:402
  67.2 7.8 %collective-permute-start.8 = (f32[2,1536]{1,0:T(2,128)S(1)}, f32[2,1536]{1,0:T(2,128)S(1)}, u32[]{:S(2)}, u32[]{:S(2)}) collective-permute-start(f32[2,1536]{1,0:T(2,128)S(1)} %add.123), channel_id=1, source_target_pairs={{0,8},{1,9},{2,10},{3,11},{4,12},{5,13},{6,14},{7,15},{8,0},{9,1},... | collective-permute-start | bytes 36872 | tf_op jit(solution)/shard_map/ppermute | solution.py:402
  72.0 5.8 %collective-permute-start.7 = (f32[2,1536]{1,0:T(2,128)S(1)}, f32[2,1536]{1,0:T(2,128)S(1)}, u32[]{:S(2)}, u32[]{:S(2)}) collective-permute-start(f32[2,1536]{1,0:T(2,128)S(1)} %add.123), channel_id=1, source_target_pairs={{0,4},{1,5},{2,6},{3,7},{4,8},{5,9},{6,10},{7,11},{8,12},{9,13},{1... | collective-permute-start | bytes 36872 | tf_op jit(solution)/shard_map/ppermute | solution.py:402
  74.8 20.2 %collective-permute-start.16 = (bf16[512,768]{1,0:T(8,128)(2,1)}, bf16[512,768]{1,0:T(8,128)(2,1)S(1)}, u32[]{:S(2)}, u32[]{:S(2)}) collective-permute-start(bf16[512,768]{1,0:T(8,128)(2,1)} %fusion.20), channel_id=1, source_target_pairs={{0,1},{1,0},{2,3},{3,2},{4,5},{5,4},{6,7},{7,6},{8,9},{9,8},{10,11... | collective-permute-start | bytes 2359304 | tf_op jit(solution)/shard_map/ppermute | solution.py:464
  77.9 11.3 %collective-permute-start.12 = (f32[2,1536]{1,0:T(2,128)S(1)}, f32[2,1536]{1,0:T(2,128)S(1)}, u32[]{:S(2)}, u32[]{:S(2)}) collective-permute-start(f32[2,1536]{1,0:T(2,128)S(1)} %add_add_fusion.2), channel_id=1, source_target_pairs={{0,48},{16,0},{32,16},{48,32},{64,112},{80,64},{96,80},{112,96},{1... | collective-permute-start | bytes 36872 | tf_op jit(solution)/shard_map/ppermute | solution.py:402
  78.0 11.2 %collective-permute-start.11 = (f32[2,1536]{1,0:T(2,128)S(1)}, f32[2,1536]{1,0:T(2,128)S(1)}, u32[]{:S(2)}, u32[]{:S(2)}) collective-permute-start(f32[2,1536]{1,0:T(2,128)S(1)} %add_add_fusion.2), channel_id=1, source_target_pairs={{0,32},{16,48},{32,0},{48,16},{64,96},{80,112},{96,64},{112,80},{1... | collective-permute-start | bytes 36872 | tf_op jit(solution)/shard_map/ppermute | solution.py:402
  82.0 7.1 %collective-permute-start.10 = (f32[2,1536]{1,0:T(2,128)S(1)}, f32[2,1536]{1,0:T(2,128)S(1)}, u32[]{:S(2)}, u32[]{:S(2)}) collective-permute-start(f32[2,1536]{1,0:T(2,128)S(1)} %add_add_fusion.2), channel_id=1, source_target_pairs={{0,16},{16,32},{32,48},{48,0},{64,80},{80,96},{96,112},{112,64},{1... | collective-permute-start | bytes 36872 | tf_op jit(solution)/shard_map/ppermute | solution.py:402
  89.2 19.5 %collective-permute-start.15 = (f32[2,1536]{1,0:T(2,128)S(1)}, f32[2,1536]{1,0:T(2,128)S(1)}, u32[]{:S(2)}, u32[]{:S(2)}) collective-permute-start(f32[2,1536]{1,0:T(2,128)S(1)} %add_add_fusion.1), channel_id=1, source_target_pairs={{0,192},{16,208},{32,224},{48,240},{64,0},{80,16},{96,32},{112,48}... | collective-permute-start | bytes 36872 | tf_op jit(solution)/shard_map/ppermute | solution.py:402
  92.6 16.0 %collective-permute-start.14 = (f32[2,1536]{1,0:T(2,128)S(1)}, f32[2,1536]{1,0:T(2,128)S(1)}, u32[]{:S(2)}, u32[]{:S(2)}) collective-permute-start(f32[2,1536]{1,0:T(2,128)S(1)} %add_add_fusion.1), channel_id=1, source_target_pairs={{0,128},{16,144},{32,160},{48,176},{64,192},{80,208},{96,224},{112... | collective-permute-start | bytes 36872 | tf_op jit(solution)/shard_map/ppermute | solution.py:402
  92.7 15.9 %collective-permute-start.13 = (f32[2,1536]{1,0:T(2,128)S(1)}, f32[2,1536]{1,0:T(2,128)S(1)}, u32[]{:S(2)}, u32[]{:S(2)}) collective-permute-start(f32[2,1536]{1,0:T(2,128)S(1)} %add_add_fusion.1), channel_id=1, source_target_pairs={{0,64},{16,80},{32,96},{48,112},{64,128},{80,144},{96,160},{112,17... | collective-permute-start | bytes 36872 | tf_op jit(solution)/shard_map/ppermute | solution.py:402
  95.0 0.9 copy-start.5
  112.2 4.2 %collective-permute-start.17 = (bf16[512,1536]{1,0:T(8,128)(2,1)S(1)}, bf16[512,1536]{1,0:T(8,128)(2,1)}, u32[]{:S(2)}, u32[]{:S(2)}) collective-permute-start(bf16[512,1536]{1,0:T(8,128)(2,1)S(1)} %multiply_convert_fusion), channel_id=1, source_target_pairs={{0,1},{1,0},{2,3},{3,2},{4,5},{5,4},{6,7},{7,6},{8,9},{9,8},{10,11... | collective-permute-start | bytes 4718600 | tf_op jit(solution)/shard_map/ppermute | solution.py:474
  113.7 2.7 %copy-start.6 = (bf16[512,768]{1,0:T(8,128)(2,1)S(1)}, bf16[512,768]{1,0:T(8,128)(2,1)}, u32[]{:S(2)}) copy-start(bf16[512,768]{1,0:T(8,128)(2,1)} %copy-done.5) | copy-start | bytes 2359300
  121.1 44.2 %all-to-all-start.1 = ((bf16[16,96,768]{2,1,0:T(8,128)(2,1)}), bf16[16,96,768]{2,1,0:T(8,128)(2,1)}, u32[]{:S(2)}, u32[]{:S(2)}) async-start(bf16[16,96,768]{2,1,0:T(8,128)(2,1)} %bitcast.69), calls=%async_computation.1 | async-start | bytes 4718592 | tf_op jit(solution)/shard_map/all_to_all | solution.py:480
  132.9 21.7 %copy-start.7 = (f32[32,1536]{1,0:T(8,128)S(1)}, f32[32,1536]{1,0:T(8,128)}, u32[]{:S(2)}) copy-start(f32[32,1536]{1,0:T(8,128)} %get-tuple-element.63) | copy-start | bytes 589828
  159.7 3.4 %collective-permute-start.18 = (f32[8,104,96]{1,2,0:T(8,128)S(1)}, f32[8,104,96]{1,2,0:T(8,128)}, u32[]{:S(2)}, u32[]{:S(2)}) collective-permute-start(f32[8,104,96]{1,2,0:T(8,128)S(1)} %dynamic-slice_bitcast_fusion), channel_id=1, source_target_pairs={{0,1},{1,0},{2,3},{3,2},{4,5},{5,4},{6,7},{7,6},{8,9},{9,8},{10,11... | collective-permute-start | bytes 958472 | tf_op jit(solution)/shard_map/ppermute | solution.py:489
  202.7 30.1 %all-to-all-start.3 = ((f32[16,200,96]{1,2,0:T(8,128)}), f32[16,200,96]{1,2,0:T(8,128)}, u32[]{:S(2)}, u32[]{:S(2)}) async-start(f32[16,200,96]{1,2,0:T(8,128)} %broadcast_in_dim.8), calls=%async_computation.3 | async-start | bytes 3145728 | tf_op jit(solution)/shard_map/all_to_all | solution.py:505
Sparse Core Ops, SparseCore 0:
  9.8 49.0 all-gather.1

commit v7 on v4

--- a/solution.py
+++ b/solution.py
@@ -41,24 +41,37 @@
             taps[g, pl.ds(8 * k, 8), :] = jnp.broadcast_to(row, (8, LANES))
 
 
-def row_of(v):
-    return 8 * row_iota(8) + v
-
-
-def shifted(window, g, w):
-    return window[g, pl.ds(w, 8, stride=8), :]
-
-
-def conv_block(window, taps, g):
-    xs = [shifted(window, g, w) for w in range(7)]
-    acc = [None] * 8
+def row_of(v, n):
+    return n * row_iota(8) + v
+
+
+def shifted(window, g, w, n):
+    return window[g, pl.ds(w, 8, stride=n), :]
+
+
+def conv_rows(window, taps, g, base, n):
+    xs = [shifted(window, g, base + w, n) for w in range(n - 1)]
+    acc = [None] * n
     for k in range(KER):
-        xs.append(shifted(window, g, k + 7))
+        xs.append(shifted(window, g, base + k + n - 1, n))
         tap = taps[g, pl.ds(8 * k, 8), :]
-        for v in range(8):
+        for v in range(n):
             acc[v] = tap * xs[v] if k == 0 else acc[v] + tap * xs[v]
         xs.pop(0)
     return acc
+
+
+def in_rows(alone, begin, stop, per_rows):
+    @pl.when(alone)
+    def _():
+        per_rows(0, 8)
+
+    for base in (0, BLOCK // 2):
+        meets = (begin < base + BLOCK // 2) & (stop > base)
+
+        @pl.when(jnp.logical_not(alone) & meets)
+        def _():
+            per_rows(base, 4)
 
 
 def utterances(first, second, row):
@@ -148,13 +161,22 @@
     )(target_row, x)
 
 
-def stats_kernel(bounds_ref, x_ref, kern_ref, _, out_ref, window, taps, sums):
+def stats_kernel(bounds_ref, x_ref, kern_ref, _, out_ref, x_sums_ref, window, taps, sums):
     spread_taps(kern_ref, taps)
     sums[...] = jnp.zeros_like(sums)
     first, second, end = bounds_ref[1], bounds_ref[2], bounds_ref[3]
 
+    frame = lax.broadcasted_iota(jnp.int32, (KER, NB * BLOCK), 1)
+    centre = frame - lax.broadcasted_iota(jnp.int32, (KER, NB * BLOCK), 0) + LEFT
+    low, high = jnp.minimum(frame, centre), jnp.maximum(frame, centre)
+    meets = jnp.zeros((KER, NB * BLOCK), F32)
+    for u in range(3):
+        meets = jnp.where((low >= bounds_ref[u]) & (high < bounds_ref[u + 1]), 1.0, meets)
+    x_sums_ref[...] = jnp.dot(meets.astype(BF16), x_ref[...], preferred_element_type=F32)
+
     def block(n, carry):
         row = n * BLOCK
+        low, high = utterances(first, second, row)
 
         def part(u, inner):
             begin, stop = bounds_ref[u], bounds_ref[u + 1]
@@ -166,19 +188,23 @@
                 for g in range(TILES):
                     x = x_ref[pl.ds(pl.multiple_of(source, 16), size), tile(g)].astype(F32)
                     window[g, pl.ds(place, size), :] = jnp.where(keep, x, 0.0)
-            for g in range(TILES):
-                acc = conv_block(window, taps, g)
-                total, square = sums[g, pl.ds(0, 8), :], sums[g, pl.ds(8, 8), :]
-                for v in range(8):
-                    at = row_of(v) + row
-                    h = jnp.where((at >= begin) & (at < stop), acc[v], 0.0)
-                    total = total + h
-                    square = square + h * h
-                sums[g, pl.ds(0, 8), :] = total
-                sums[g, pl.ds(8, 8), :] = square
+
+            def per_rows(base, n):
+                for g in range(TILES):
+                    acc = conv_rows(window, taps, g, base, n)
+                    total, square = sums[g, pl.ds(0, 8), :], sums[g, pl.ds(8, 8), :]
+                    for v in range(n):
+                        at = row_of(v, n) + (row + base)
+                        h = jnp.where((at >= begin) & (at < stop), acc[v], 0.0)
+                        total = total + h
+                        square = square + h * h
+                    sums[g, pl.ds(0, 8), :] = total
+                    sums[g, pl.ds(8, 8), :] = square
+
+            in_rows(low + 1 == high, begin - row, stop - row, per_rows)
             return inner
 
-        return lax.fori_loop(*utterances(first, second, row), part, carry)
+        return lax.fori_loop(low, high, part, carry)
 
     lax.fori_loop(0, end // BLOCK, block, 0)
     for g in range(TILES):
@@ -192,14 +218,20 @@
     return pl.pallas_call(
         stats_kernel,
         grid=(width // WIDE,),
-        out_shape=jax.ShapeDtypeStruct((2, width), F32),
+        out_shape=(
+            jax.ShapeDtypeStruct((2, width), F32),
+            jax.ShapeDtypeStruct((KER, width), F32),
+        ),
         in_specs=[
             SMEM_SPEC,
             pl.BlockSpec((NB * BLOCK, WIDE), lambda c: (0, c)),
             pl.BlockSpec((KER, WIDE), lambda c: (0, c)),
             pl.BlockSpec(memory_space=pl.ANY),
         ],
-        out_specs=pl.BlockSpec((2, WIDE), lambda c: (0, c)),
+        out_specs=(
+            pl.BlockSpec((2, WIDE), lambda c: (0, c)),
+            pl.BlockSpec((KER, WIDE), lambda c: (0, c)),
+        ),
         scratch_shapes=[
             pltpu.VMEM((TILES, WIN, LANES), F32),
             pltpu.VMEM((TILES, 8 * KER, LANES), F32),
@@ -216,6 +248,9 @@
 
         @pl.when(valid)
         def _():
+            at = pl.multiple_of(n * BLOCK, BLOCK)
+            low, high = utterances(info_ref[5 * s + 2], info_ref[5 * s + 3], LEFT)
+
             def part(u, carry):
                 begin, stop = info_ref[5 * s + 1 + u], info_ref[5 * s + 2 + u]
                 rows = row_iota(WIN)
@@ -223,14 +258,17 @@
                 for g in range(TILES):
                     x = got_ref[s, :, tile(g)].astype(F32)
                     window[g] = jnp.where(keep, x, 0.0)
-                per_part(pl.multiple_of(n * BLOCK, BLOCK), begin - LEFT, stop - LEFT)
+                begin, stop = begin - LEFT, stop - LEFT
+
+                def per_rows(base, groups):
+                    per_part(at + base, begin - base, stop - base, base, groups)
+
+                in_rows(low + 1 == high, begin, stop, per_rows)
                 return carry
 
-            lax.fori_loop(
-                *utterances(info_ref[5 * s + 2], info_ref[5 * s + 3], LEFT), part, 0
-            )
+            lax.fori_loop(low, high, part, 0)
             if per_block is not None:
-                per_block(pl.multiple_of(n * BLOCK, BLOCK))
+                per_block(at)
 
         return n + valid.astype(jnp.int32)
 
@@ -241,12 +279,12 @@
     h_ref, sw_ref, window, taps = rest[-4:]
     spread_taps(kern_ref, taps)
 
-    def per_part(at, begin, stop):
+    def per_part(at, begin, stop, base, n):
         for g in range(TILES):
-            acc = conv_block(window, taps, g)
-            for v in range(8):
-                place = pl.ds(at + v, 8, stride=8)
-                keep = (row_of(v) >= begin) & (row_of(v) < stop)
+            acc = conv_rows(window, taps, g, base, n)
+            for v in range(n):
+                place = pl.ds(at + v, 8, stride=n)
+                keep = (row_of(v, n) >= begin) & (row_of(v, n) < stop)
                 h_ref[g, place, :] = jnp.where(keep, acc[v], h_ref[g, place, :])
 
     def per_block(at):
@@ -287,22 +325,22 @@
 
 
 def terms_kernel(
-    info_ref, got_ref, h_ref, wide_ref, norm_ref, out_ref, window, back_ref, acc_a, acc_x, sums
+    info_ref, got_ref, h_ref, wide_back, norm_ref, out_ref, window, back_ref, acc_a, acc_x, sums
 ):
     for g in range(TILES):
-        back_ref[g] = wide_ref[:, tile(g)]
+        back_ref[g] = wide_back[:, tile(g)]
     acc_a[...] = jnp.zeros_like(acc_a)
     acc_x[...] = jnp.zeros_like(acc_x)
     sums[...] = jnp.zeros_like(sums)
 
-    def per_tile(g, at, begin, stop):
+    def per_tile(g, at, begin, stop, base, n):
         mean, inverse = norm_ref[pl.ds(0, 1), tile(g)], norm_ref[pl.ds(1, 1), tile(g)]
         scale, shift = norm_ref[pl.ds(2, 1), tile(g)], norm_ref[pl.ds(3, 1), tile(g)]
         das, hats = [], []
         sum_x, sum_1 = sums[g, pl.ds(0, 8), :], sums[g, pl.ds(8, 8), :]
-        for v in range(8):
-            place = pl.ds(at + v, 8, stride=8)
-            keep = (row_of(v) >= begin) & (row_of(v) < stop)
+        for v in range(n):
+            place = pl.ds(at + v, 8, stride=n)
+            keep = (row_of(v, n) >= begin) & (row_of(v, n) < stop)
             hat = (h_ref[g, place, :] - mean) * inverse
             a = hat * scale + shift
             sig = jax.nn.sigmoid(a)
@@ -315,20 +353,20 @@
             hats.append(hat)
         sums[g, pl.ds(0, 8), :] = sum_x
         sums[g, pl.ds(8, 8), :] = sum_1
-        xs = [shifted(window, g, w) for w in range(7)]
+        xs = [shifted(window, g, base + w, n) for w in range(n - 1)]
         for k in range(KER):
-            xs.append(shifted(window, g, k + 7))
+            xs.append(shifted(window, g, base + k + n - 1, n))
             place = pl.ds(8 * k, 8)
             for acc, rows in ((acc_a, das), (acc_x, hats)):
-                terms_k = [rows[v] * xs[v] for v in range(8)]
+                terms_k = [rows[v] * xs[v] for v in range(n)]
                 while len(terms_k) > 1:
                     terms_k = [p + q for p, q in zip(terms_k[::2], terms_k[1::2])]
                 acc[g, place, :] += terms_k[0]
             xs.pop(0)
 
-    def per_part(at, begin, stop):
+    def per_part(at, begin, stop, base, n):
         for g in range(TILES):
-            per_tile(g, at, begin, stop)
+            per_tile(g, at, begin, stop, base, n)
 
     live_parts(info_ref, got_ref, window, per_part)
     for g in range(TILES):
@@ -420,14 +458,6 @@
 
     w_t = lax.all_gather(w_out.T, "zero", axis=0, tiled=True)
 
-    frame = lax.broadcasted_iota(jnp.int32, (KER, NB * BLOCK), 1)
-    centre = frame - lax.broadcasted_iota(jnp.int32, (KER, NB * BLOCK), 0) + LEFT
-    meets = jnp.zeros((KER, NB * BLOCK), jnp.bool_)
-    for u in range(3):
-        begin, stop = bounds[u], bounds[u + 1]
-        within = (jnp.minimum(frame, centre) >= begin) & (jnp.maximum(frame, centre) < stop)
-        meets = meets | within
-
     half = width // 2
     column = lax.broadcasted_iota(jnp.int32, (width, half), 0)
     place = lax.broadcasted_iota(jnp.int32, (width, half), 1)
@@ -437,20 +467,19 @@
     other_columns = jnp.where(core == 0, odd, even).astype(BF16)
     swap = [(i, i ^ 1) for i in range(16)]
 
-    sums = stats(bounds, x, kern_full, send)
+    sums, x_sums = stats(bounds, x, kern_full, send)
     for steps in ((1,), (2,), (4, 8, 12)):
         sums, _ = add_from(sums, "zero", [zero_step(step) for step in steps])
     sums = jnp.concatenate([sums, info], axis=0)
-    sums, cot, x = lax.optimization_barrier((sums, cot, x))
-    x_sums = jnp.dot(meets.astype(BF16), x, preferred_element_type=F32)
+    sums, cot = lax.optimization_barrier((sums, cot))
     cot_own = jnp.dot(cot, own_columns, preferred_element_type=F32).astype(BF16)
     cot_send = jnp.dot(cot, other_columns, preferred_element_type=F32).astype(BF16)
     back = jnp.dot(cot, w_t, preferred_element_type=F32)
-    sums, (x_sums, cot_own, cot_send) = add_from(
-        sums, "dp", [dp_step(step, True) for step in (1, 2, 3)], x_sums, cot_own, cot_send
+    sums, (back, cot_own, cot_send) = add_from(
+        sums, "dp", [dp_step(step, True) for step in (1, 2, 3)], back, cot_own, cot_send
     )
     cot_other = lax.ppermute(cot_send, "zero", swap)
-    sums, (back,) = add_from(sums, "dp", [dp_step(step, False) for step in (1, 2, 3)], back)
+    sums, _ = add_from(sums, "dp", [dp_step(step, False) for step in (1, 2, 3)])
     info = lax.dynamic_slice_in_dim(sums[2], lax.axis_index("dp") * 96, 80, 0).astype(jnp.int32)
     frame_count = jnp.float32(BLOCKS * BLOCK * 256)
     mean = sums[0] / frame_count
@@ -458,7 +487,7 @@
     inverse = lax.rsqrt(var + EPS)
     norm = jnp.stack([mean, inverse, small_full[KER], small_full[KER + 1]])
 
-    h, sw = hidden(info, got, kern_full, norm, back, x_sums, cot_other)
+    h, sw = hidden(info, got, kern_full, norm, back, cot_other)
     sw_other = lax.ppermute(sw, "zero", swap)
     contract = (((0,), (0,)), ((), ()))
     term = lax.dot_general(sw, cot_own, contract, preferred_element_type=F32)

time: 233 us -> 232 us (level)
  blocking collectives: 24.4 us -> 29.1 us
  matrix products: 26 us -> 22.1 us
  waiting for transfers between devices: 33.8 us -> 37.5 us
  Pallas kernels: 53.7 us -> 50.7 us
  starting transfers between devices: 57.7 us -> 54.7 us
    all_to_all x1, blocking collectives: 24.4 us -> 29.1 us  [per_device(): lax.all_to_all(both, 'zero', 0, 0, axis_index_groups=[[i for i in range(1...]
    dot_general x1 -> x0, matrix products: 3.86 us -> none  [per_device(): x_sums = jnp.dot(meets.astype(BF16), x, preferred_element_type=F32)]
    ppermute x11, waiting for transfers between devices: 9.8 us -> 12.8 us  [add_from(): parts = [lax.ppermute(x, axis, step) for step in steps]]
    all_to_all x1, waiting for transfers between devices: 4.23 us -> 7.17 us  [per_device(): term = lax.all_to_all(term, 'dp', 0, 0, tiled=True)]
    pallas_call x1, Pallas kernels: 25 us -> 22.3 us  [terms(): pl.pallas_call(terms_kernel, grid=(width // WIDE,), out_shape=jax.ShapeDt...]
    unnamed x28 -> x24, local copies, waits for them, and re-layouts: 6.78 us -> 6.78 us
  transfers between devices with their start and end apart: 23 -> 23, of which waited for: 9 -> 11; matrix products, arithmetic and copies ran while one was open for 14% -> 12% of each run, Pallas kernels for 17% -> 16%
where the time goes in v7:
time: 232 us; the launch traced here: 230 us
  starting transfers between devices  54.7 us (24%)
  Pallas kernels  50.7 us (22%)
  waiting for transfers between devices  37.5 us (16%)
  blocking collectives  29.1 us (13%)
  matrix products  22.1 us (10%)
  between operations  14.5 us (6%)
  local copies, waits for them, and re-layouts  12.2 us (5%)
  other arithmetic  9.68 us (4%)
    all_to_all x1, blocking collectives, per_device(): lax.all_to_all(both, 'zero', 0, 0, axis_index_groups=[[i for i in range(1...  29.1 us
    pallas_call x1, Pallas kernels, terms(): pl.pallas_call(terms_kernel, grid=(width // WIDE,), out_shape=jax.ShapeDt...  22.3 us
    ppermute x11, starting transfers between devices, add_from(): parts = [lax.ppermute(x, axis, step) for step in steps]  21.8 us
    pallas_call x1, Pallas kernels, hidden(): pl.pallas_call(hidden_kernel, grid=(width // WIDE,), out_shape=(jax.Shape...  14.3 us
    ppermute x11, waiting for transfers between devices, add_from(): parts = [lax.ppermute(x, axis, step) for step in steps]  12.8 us
    all_to_all x1, waiting for transfers between devices, per_device(): lax.all_to_all(jnp.broadcast_to(last[None], (16,) + last.shape), 'dp', 0,...  11.9 us
    pallas_call x1, Pallas kernels, stats(): pl.pallas_call(stats_kernel, grid=(width // WIDE,), out_shape=(jax.ShapeD...  11.4 us
    ppermute x3, starting transfers between devices, gather_small(): lax.ppermute(x, 'zero', zero_step(step))  10.5 us
  transfers between devices with their start and end apart: 23, of which 11 were waited for; matrix products, arithmetic and copies ran while one was open for 12% of the time, Pallas kernels for 16%

profile of v7, /device:TPU:8, one launch (start us, length us, event | category | flops | bytes accessed | tf_op | source)
XLA Modules:
  0.0 230.4 jit_solution(1843279174029550319)
XLA Ops:
  7.2 0.7 all-gather.2.cloned.1.call-update
  8.0 0.8 maximum_maximum_fusion
  8.8 1.7 copy-done.2
  10.5 0.7 copy-done.3
  11.2 1.2 pack.1._
  12.4 2.2 copy-done.1
  14.8 2.0 collective-permute-start.1
  16.8 7.4 %all-to-all-start = ((bf16[16,96,1536]{2,1,0:T(8,128)(2,1)}), bf16[16,96,1536]{2,1,0:T(8,128)(2,1)}, u32[]{:S(2)}, u32[]{:S(2)}) async-start(bf16[16,96,1536]{2,1,0:T(8,128)(2,1)} %copy-done.1), calls=%async_computation | async-start | bytes 9437184 | tf_op jit(solution)/shard_map/all_to_all | solution.py:454
  24.2 0.6 reduce
  24.8 3.4 %collective-permute-start.4 = (bf16[2,2,48,96]{3,2,1,0:T(8,128)(2,1)S(1)}, bf16[2,2,48,96]{3,2,1,0:T(8,128)(2,1)S(1)}, u32[]{:S(2)}, u32[]{:S(2)}) collective-permute-start(bf16[2,2,48,96]{3,2,1,0:T(8,128)(2,1)S(1)} %pad_maximum_fusion.3), channel_id=1, source_target_pairs={{0,4},{1,5},{2,6},{3,7},{4,8},{5,9},{6,10},{7,11},{8,12},{9,13},{1... | collective-permute-start | bytes 110600 | tf_op jit(solution)/shard_map/ppermute | solution.py:431
  28.2 4.5 %collective-permute-start.3 = (bf16[2,2,48,96]{3,2,1,0:T(8,128)(2,1)S(1)}, bf16[2,2,48,96]{3,2,1,0:T(8,128)(2,1)S(1)}, u32[]{:S(2)}, u32[]{:S(2)}) collective-permute-start(bf16[2,2,48,96]{3,2,1,0:T(8,128)(2,1)S(1)} %pad_maximum_fusion.3), channel_id=1, source_target_pairs={{0,8},{1,9},{2,10},{3,11},{4,12},{5,13},{6,14},{7,15},{8,0},{9,1},... | collective-permute-start | bytes 110600 | tf_op jit(solution)/shard_map/ppermute | solution.py:431
  32.7 2.6 %collective-permute-start.2 = (bf16[2,2,48,96]{3,2,1,0:T(8,128)(2,1)S(1)}, bf16[2,2,48,96]{3,2,1,0:T(8,128)(2,1)S(1)}, u32[]{:S(2)}, u32[]{:S(2)}) collective-permute-start(bf16[2,2,48,96]{3,2,1,0:T(8,128)(2,1)S(1)} %pad_maximum_fusion.3), channel_id=1, source_target_pairs={{0,12},{1,13},{2,14},{3,15},{4,0},{5,1},{6,2},{7,3},{8,4},{9,5},{1... | collective-permute-start | bytes 110600 | tf_op jit(solution)/shard_map/ppermute | solution.py:431
  35.3 1.5 places.1
  36.9 2.7 %collective-permute-done.3 = bf16[2,2,48,96]{3,2,1,0:T(8,128)(2,1)S(1)} collective-permute-done((bf16[2,2,48,96]{3,2,1,0:T(8,128)(2,1)S(1)}, bf16[2,2,48,96]{3,2,1,0:T(8,128)(2,1)S(1)}, u32[]{:S(2)}, u32[]{:S(2)}) %collective-permute-start.3) | collective-permute-done | bytes 36896 | tf_op jit(solution)/shard_map/ppermute | solution.py:431
  40.0 0.8 slice.52.kern_ref
  40.8 11.4 %stats.1 = (f32[2,1536]{1,0:T(2,128)}, f32[32,1536]{1,0:T(8,128)}) custom-call(s32[4]{0:T(128)} %get-tuple-element.27.bounds_ref, bf16[768,1536]{1,0:T(8,128)(2,1)} %bitcast.64, f32[32,1536]{1,0:T(8,128)} %slice.52.kern_ref, bf16[16,96,1536]{2,1,0:T(8,128)(2,1)} %copy-done.1), custom_call_target="tpu_custom_call" | custom-call | flops 16499999744 | bytes 1000000 | tf_op jit(solution)/shard_map/stats/pallas_call | solution.py:218
  52.2 1.4 collective-permute-done.5
  53.6 0.7 add.110
  54.3 1.2 collective-permute-start.6
  55.5 2.5 %collective-permute-done.6 = f32[2,1536]{1,0:T(2,128)S(1)} collective-permute-done((f32[2,1536]{1,0:T(2,128)S(1)}, f32[2,1536]{1,0:T(2,128)S(1)}, u32[]{:S(2)}, u32[]{:S(2)}) %collective-permute-start.6) | collective-permute-done | bytes 12320 | tf_op jit(solution)/shard_map/ppermute | solution.py:421
  58.0 5.6 %collective-permute-start.9 = (f32[2,1536]{1,0:T(2,128)S(1)}, f32[2,1536]{1,0:T(2,128)S(1)}, u32[]{:S(2)}, u32[]{:S(2)}) collective-permute-start(f32[2,1536]{1,0:T(2,128)S(1)} %add.111), channel_id=1, source_target_pairs={{0,12},{1,13},{2,14},{3,15},{4,0},{5,1},{6,2},{7,3},{8,4},{9,5},{1... | collective-permute-start | bytes 36872 | tf_op jit(solution)/shard_map/ppermute | solution.py:421
  63.6 5.0 %collective-permute-start.8 = (f32[2,1536]{1,0:T(2,128)S(1)}, f32[2,1536]{1,0:T(2,128)S(1)}, u32[]{:S(2)}, u32[]{:S(2)}) collective-permute-start(f32[2,1536]{1,0:T(2,128)S(1)} %add.111), channel_id=1, source_target_pairs={{0,8},{1,9},{2,10},{3,11},{4,12},{5,13},{6,14},{7,15},{8,0},{9,1},... | collective-permute-start | bytes 36872 | tf_op jit(solution)/shard_map/ppermute | solution.py:421
  68.6 0.7 collective-permute-start.7
  69.3 1.9 collective-permute-done.8
  71.2 3.2 %collective-permute-done.7 = f32[2,1536]{1,0:T(2,128)S(1)} collective-permute-done((f32[2,1536]{1,0:T(2,128)S(1)}, f32[2,1536]{1,0:T(2,128)S(1)}, u32[]{:S(2)}, u32[]{:S(2)}) %collective-permute-start.7) | collective-permute-done | bytes 12320 | tf_op jit(solution)/shard_map/ppermute | solution.py:421
  74.4 0.3 collective-permute-start.12
  74.7 2.4 %collective-permute-start.11 = (f32[3,1536]{1,0:T(4,128)S(1)}, f32[3,1536]{1,0:T(4,128)S(1)}, u32[]{:S(2)}, u32[]{:S(2)}) collective-permute-start(f32[3,1536]{1,0:T(4,128)S(1)} %pad_maximum_fusion.5), channel_id=1, source_target_pairs={{0,32},{16,48},{32,0},{48,16},{64,96},{80,112},{96,64},{112,80},{1... | collective-permute-start | bytes 55304 | tf_op jit(solution)/shard_map/ppermute | solution.py:421
  77.1 2.5 %collective-permute-start.10 = (f32[3,1536]{1,0:T(4,128)S(1)}, f32[3,1536]{1,0:T(4,128)S(1)}, u32[]{:S(2)}, u32[]{:S(2)}) collective-permute-start(f32[3,1536]{1,0:T(4,128)S(1)} %pad_maximum_fusion.5), channel_id=1, source_target_pairs={{0,16},{16,32},{32,48},{48,0},{64,80},{80,96},{96,112},{112,64},{1... | collective-permute-start | bytes 55304 | tf_op jit(solution)/shard_map/ppermute | solution.py:421
  79.6 1.8 fusion.21
  81.4 2.7 %fusion.18 = bf16[512,768]{1,0:T(8,128)(2,1)} fusion(bf16[512,1536]{1,0:T(8,128)(2,1)S(1)} %bitcast.63, s32[768]{0:T(1024)S(1)} %get-tuple-element.70, s32[768]{0:T(1024)S(1)} %get-tuple-element.71, pred[768]{0:T(1024)(128)(4,1)S(1)} %fusion.32, pred[]{:T(512)S(6)} %eq.85), kind=kOutput, calls=%fused_computation.21 | convolution fusion | flops 1216610304 | bytes 2366209 | tf_op jit(solution)/shard_map/dot_general | solution.py:475
  84.1 6.6 %fusion.37.rest_0_.wide_back = f32[512,1536]{1,0:T(8,128)} fusion(bf16[512,1536]{1,0:T(8,128)(2,1)S(1)} %bitcast.62, bf16[1536,1536]{1,0:T(8,128)(2,1)} %all-gather.2.cloned.1.call-done), kind=kOutput, calls=%fused_computation.74 | convolution fusion | flops 2415919104 | bytes 9437184 | tf_op jit(solution)/shard_map/dot_general | solution.py:477
  90.8 3.1 %collective-permute-start.14 = (f32[3,1536]{1,0:T(4,128)S(1)}, f32[3,1536]{1,0:T(4,128)S(1)}, u32[]{:S(2)}, u32[]{:S(2)}) collective-permute-start(f32[3,1536]{1,0:T(4,128)S(1)} %add_add_fusion.1), channel_id=1, source_target_pairs={{0,128},{16,144},{32,160},{48,176},{64,192},{80,208},{96,224},{112... | collective-permute-start | bytes 55304 | tf_op jit(solution)/shard_map/ppermute | solution.py:421
  93.8 1.0 collective-permute-start.13
  95.0 1.2 collective-permute-done.14
  96.2 2.7 %collective-permute-done.13 = f32[3,1536]{1,0:T(4,128)S(1)} collective-permute-done((f32[3,1536]{1,0:T(4,128)S(1)}, f32[3,1536]{1,0:T(4,128)S(1)}, u32[]{:S(2)}, u32[]{:S(2)}) %collective-permute-start.13) | collective-permute-done | bytes 18464 | tf_op jit(solution)/shard_map/ppermute | solution.py:421
  98.9 0.6 fusion.34.info_ref
  99.5 0.6 pad_maximum_fusion.6.norm_ref
  100.1 0.9 copy-done.4
  101.0 14.3 %hidden.1 = (f32[12,512,128]{2,1,0:T(8,128)}, bf16[512,1536]{1,0:T(8,128)(2,1)}) custom-call(s32[80]{0:T(128)} %fusion.34.info_ref, bf16[16,96,1536]{2,1,0:T(8,128)(2,1)} %all-to-all-done.got_ref, f32[32,1536]{1,0:T(8,128)} %slice.52.kern_ref, f32[4,1536]{1,0:T(4,128)} %pad_maximum_fusion.6.norm_ref, f32[512,1536]{1,0:T(8,128)} %fusion.37.rest_0_.wide_back, ...), custom_call_target="tpu_custom_call" | custom-call | flops 17600000000 | bytes 1000000 | tf_op jit(solution)/shard_map/hidden/pallas_call | solution.py:303
  115.3 3.1 %fusion.38 = f32[1536,768]{1,0:T(8,128)S(1)} fusion(bf16[512,1536]{1,0:T(8,128)(2,1)} %get-tuple-element.44, bf16[512,768]{1,0:T(8,128)(2,1)} %fusion.18), kind=kOutput, calls=%fused_computation.75 | convolution fusion | flops 1207959552 | bytes 7077888 | tf_op jit(solution)/shard_map/dot_general | solution.py:493
  118.4 0.5 collective-permute-done.17
  118.9 1.4 fusion.39
  120.4 1.9 add_convert_fusion
  122.3 4.8 %all-to-all-start.1 = ((bf16[16,96,768]{2,1,0:T(8,128)(2,1)}), bf16[16,96,768]{2,1,0:T(8,128)(2,1)}, u32[]{:S(2)}, u32[]{:S(2)}) async-start(bf16[16,96,768]{2,1,0:T(8,128)(2,1)} %bitcast.68), calls=%async_computation.1 | async-start | bytes 4718592 | tf_op jit(solution)/shard_map/all_to_all | solution.py:497
  127.2 22.3 %terms.1 = f32[72,1536]{1,0:T(8,128)} custom-call(s32[80]{0:T(128)} %fusion.34.info_ref, bf16[16,96,1536]{2,1,0:T(8,128)(2,1)} %all-to-all-done.got_ref, f32[12,512,128]{2,1,0:T(8,128)} %get-tuple-element.48.h_ref, f32[512,1536]{1,0:T(8,128)} %fusion.37.rest_0_.wide_back, f32[4,1536]{1,0:T(4,128)} %pad_maximum_fusion.6.norm_ref), custom_call_target="tpu_custom_call" | custom-call | flops 27499999232 | bytes 1000000 | tf_op jit(solution)/shard_map/terms/pallas_call | solution.py:384
  149.4 1.1 pad_maximum_fusion.1
  150.5 0.3 copy.25
  150.9 1.7 collective-permute-done.18
  152.7 7.2 %all-to-all-done.1 = bf16[16,96,768]{2,1,0:T(8,128)(2,1)} async-done(((bf16[16,96,768]{2,1,0:T(8,128)(2,1)}), bf16[16,96,768]{2,1,0:T(8,128)(2,1)}, u32[]{:S(2)}, u32[]{:S(2)}) %all-to-all-start.1) | async-done | bytes 2359328 | tf_op jit(solution)/shard_map/all_to_all | solution.py:497
  159.8 2.0 convert_reduce_fusion
  161.9 0.2 copy.31
  162.0 0.3 pad_maximum_fusion
  162.3 29.1 %all_to_all.20 = f32[8,200,96]{1,2,0:T(8,128)S(1)} all-to-all(f32[8,200,96]{1,2,0:T(8,128)S(1)} %pad_maximum_fusion), channel_id=1, replica_groups={{0,2,4,6,8,10,12,14},{1,3,5,7,9,11,13,15},{16,18,20,22,24,26,28,30},{17..., dimensions={0} | all-to-all | bytes 1228800 | tf_op jit(solution)/shard_map/all_to_all | solution.py:513
  191.4 1.4 broadcast_in_dim.8
  192.8 7.9 %all-to-all-start.3 = ((f32[16,200,96]{1,2,0:T(8,128)}), f32[16,200,96]{1,2,0:T(8,128)S(1)}, u32[]{:S(2)}, u32[]{:S(2)}) async-start(f32[16,200,96]{1,2,0:T(8,128)} %broadcast_in_dim.8), calls=%async_computation.3 | async-start | bytes 3145728 | tf_op jit(solution)/shard_map/all_to_all | solution.py:522
  200.7 0.8 constant_dynamic-slice_fusion
  201.4 6.6 %fusion.5 = bf16[1,1,512,1536]{3,2,1,0:T(8,128)(2,1)} fusion(bf16[512,1536]{1,0:T(8,128)(2,1)} %get-tuple-element.44, bf16[1536,1536]{1,0:T(8,128)(2,1)} %all-gather.2.cloned.1.call-done), kind=kOutput, calls=%fused_computation.10 | convolution fusion | flops 2416705536 | bytes 7864320 | tf_op jit(solution)/shard_map/dot_general | solution.py:500
  208.0 11.9 %all-to-all-done.3 = f32[16,200,96]{1,2,0:T(8,128)S(1)} async-done(((f32[16,200,96]{1,2,0:T(8,128)}), f32[16,200,96]{1,2,0:T(8,128)S(1)}, u32[]{:S(2)}, u32[]{:S(2)}) %all-to-all-start.3) | async-done | bytes 1228832 | tf_op jit(solution)/shard_map/all_to_all | solution.py:522
  219.9 0.3 slice_reduce_fusion
  220.2 0.2 fusion.28
  220.5 0.5 copy.27
  221.0 1.1 reshape.37
  222.3 0.7 copy.29
  222.9 0.6 copy.30
  (66 shorter events, 1.6 us)
Async XLA Ops:
  7.2 67.3 %copy-start = (bf16[1,1,512,1536]{3,2,1,0:T(8,128)(2,1)S(1)}, bf16[1,1,512,1536]{3,2,1,0:T(8,128)(2,1)}, u32[]{:S(2)}) copy-start(bf16[1,1,512,1536]{3,2,1,0:T(8,128)(2,1)} %param.10) | copy-start | bytes 4718596
  7.2 76.9 %all-gather.2.cloned.1.call-start = ((), (), s32[]{:S(2)}) async-start(), calls=%async_computation.4 | async-start | bytes 5013504 | tf_op jit(solution)/shard_map/all_gather | solution.py:459
  8.8 5.9 %collective-permute-start = (bf16[48,96]{1,0:T(8,128)(2,1)S(1)}, bf16[48,96]{1,0:T(8,128)(2,1)S(1)}, u32[]{:S(2)}, u32[]{:S(2)}) collective-permute-start(bf16[48,96]{1,0:T(8,128)(2,1)S(1)} %maximum_maximum_fusion), channel_id=1, source_target_pairs={{0,1},{1,0},{2,3},{3,2},{4,5},{5,4},{6,7},{7,6},{8,9},{9,8},{10,11... | collective-permute-start | bytes 27656 | tf_op jit(solution)/shard_map/ppermute | solution.py:428
  8.8 1.7 copy-start.2
  10.5 0.7 copy-start.3
  11.2 3.5 %copy-start.7 = (bf16[32,96]{1,0:T(8,128)(2,1)S(1)}, bf16[32,96]{1,0:T(8,128)(2,1)}, u32[]{:S(2)}) copy-start(bf16[32,96]{1,0:T(8,128)(2,1)} %param.12) | copy-start | bytes 18436
  11.2 3.5 %copy-start.10 = (bf16[2,96]{1,0:T(2,128)(2,1)S(1)}, bf16[2,96]{1,0:T(2,128)(2,1)}, u32[]{:S(2)}) copy-start(bf16[2,96]{1,0:T(2,128)(2,1)} %param.13) | copy-start | bytes 1156
  12.4 2.2 copy-start.1
  14.7 9.4 %copy-start.9 = (s32[1,1,768]{2,1,0:T(1,128)S(1)}, s32[1,1,768]{2,1,0:T(1,128)}, u32[]{:S(2)}) copy-start(s32[1,1,768]{2,1,0:T(1,128)} %param.8) | copy-start | bytes 9220
  14.8 10.0 %collective-permute-start.1 = (bf16[2,48,96]{2,1,0:T(8,128)(2,1)S(1)}, bf16[2,48,96]{2,1,0:T(8,128)(2,1)S(1)}, u32[]{:S(2)}, u32[]{:S(2)}) collective-permute-start(bf16[2,48,96]{2,1,0:T(8,128)(2,1)S(1)} %pad_maximum_fusion.4), channel_id=1, source_target_pairs={{0,2},{1,3},{2,0},{3,1},{4,6},{5,7},{6,4},{7,5},{8,10},{9,11},{10,... | collective-permute-start | bytes 55304 | tf_op jit(solution)/shard_map/ppermute | solution.py:428
  16.8 83.4 %all-to-all-start = ((bf16[16,96,1536]{2,1,0:T(8,128)(2,1)}), bf16[16,96,1536]{2,1,0:T(8,128)(2,1)}, u32[]{:S(2)}, u32[]{:S(2)}) async-start(bf16[16,96,1536]{2,1,0:T(8,128)(2,1)} %copy-done.1), calls=%async_computation | async-start | bytes 9437184 | tf_op jit(solution)/shard_map/all_to_all | solution.py:454
  24.8 12.1 %collective-permute-start.4 = (bf16[2,2,48,96]{3,2,1,0:T(8,128)(2,1)S(1)}, bf16[2,2,48,96]{3,2,1,0:T(8,128)(2,1)S(1)}, u32[]{:S(2)}, u32[]{:S(2)}) collective-permute-start(bf16[2,2,48,96]{3,2,1,0:T(8,128)(2,1)S(1)} %pad_maximum_fusion.3), channel_id=1, source_target_pairs={{0,4},{1,5},{2,6},{3,7},{4,8},{5,9},{6,10},{7,11},{8,12},{9,13},{1... | collective-permute-start | bytes 110600 | tf_op jit(solution)/shard_map/ppermute | solution.py:431
  28.2 11.5 %collective-permute-start.3 = (bf16[2,2,48,96]{3,2,1,0:T(8,128)(2,1)S(1)}, bf16[2,2,48,96]{3,2,1,0:T(8,128)(2,1)S(1)}, u32[]{:S(2)}, u32[]{:S(2)}) collective-permute-start(bf16[2,2,48,96]{3,2,1,0:T(8,128)(2,1)S(1)} %pad_maximum_fusion.3), channel_id=1, source_target_pairs={{0,8},{1,9},{2,10},{3,11},{4,12},{5,13},{6,14},{7,15},{8,0},{9,1},... | collective-permute-start | bytes 110600 | tf_op jit(solution)/shard_map/ppermute | solution.py:431
  32.7 7.0 %collective-permute-start.2 = (bf16[2,2,48,96]{3,2,1,0:T(8,128)(2,1)S(1)}, bf16[2,2,48,96]{3,2,1,0:T(8,128)(2,1)S(1)}, u32[]{:S(2)}, u32[]{:S(2)}) collective-permute-start(bf16[2,2,48,96]{3,2,1,0:T(8,128)(2,1)S(1)} %pad_maximum_fusion.3), channel_id=1, source_target_pairs={{0,12},{1,13},{2,14},{3,15},{4,0},{5,1},{6,2},{7,3},{8,4},{9,5},{1... | collective-permute-start | bytes 110600 | tf_op jit(solution)/shard_map/ppermute | solution.py:431
  40.8 33.6 %copy-start.8 = (f32[1,1536]{1,0:T(1,128)S(1)}, f32[1,1536]{1,0:T(1,128)}, u32[]{:S(2)}) copy-start(f32[1,1536]{1,0:T(1,128)} %get-tuple-element.33) | copy-start | bytes 18436
  52.2 1.4 collective-permute-start.5
  54.3 3.7 %collective-permute-start.6 = (f32[2,1536]{1,0:T(2,128)S(1)}, f32[2,1536]{1,0:T(2,128)S(1)}, u32[]{:S(2)}, u32[]{:S(2)}) collective-permute-start(f32[2,1536]{1,0:T(2,128)S(1)} %add.110), channel_id=1, source_target_pairs={{0,2},{1,3},{2,0},{3,1},{4,6},{5,7},{6,4},{7,5},{8,10},{9,11},{10,... | collective-permute-start | bytes 36872 | tf_op jit(solution)/shard_map/ppermute | solution.py:421
  58.0 11.3 %collective-permute-start.9 = (f32[2,1536]{1,0:T(2,128)S(1)}, f32[2,1536]{1,0:T(2,128)S(1)}, u32[]{:S(2)}, u32[]{:S(2)}) collective-permute-start(f32[2,1536]{1,0:T(2,128)S(1)} %add.111), channel_id=1, source_target_pairs={{0,12},{1,13},{2,14},{3,15},{4,0},{5,1},{6,2},{7,3},{8,4},{9,5},{1... | collective-permute-start | bytes 36872 | tf_op jit(solution)/shard_map/ppermute | solution.py:421
  63.6 7.6 %collective-permute-start.8 = (f32[2,1536]{1,0:T(2,128)S(1)}, f32[2,1536]{1,0:T(2,128)S(1)}, u32[]{:S(2)}, u32[]{:S(2)}) collective-permute-start(f32[2,1536]{1,0:T(2,128)S(1)} %add.111), channel_id=1, source_target_pairs={{0,8},{1,9},{2,10},{3,11},{4,12},{5,13},{6,14},{7,15},{8,0},{9,1},... | collective-permute-start | bytes 36872 | tf_op jit(solution)/shard_map/ppermute | solution.py:421
  68.6 5.8 %collective-permute-start.7 = (f32[2,1536]{1,0:T(2,128)S(1)}, f32[2,1536]{1,0:T(2,128)S(1)}, u32[]{:S(2)}, u32[]{:S(2)}) collective-permute-start(f32[2,1536]{1,0:T(2,128)S(1)} %add.111), channel_id=1, source_target_pairs={{0,4},{1,5},{2,6},{3,7},{4,8},{5,9},{6,10},{7,11},{8,12},{9,13},{1... | collective-permute-start | bytes 36872 | tf_op jit(solution)/shard_map/ppermute | solution.py:421
  74.4 16.2 %collective-permute-start.12 = (f32[3,1536]{1,0:T(4,128)S(1)}, f32[3,1536]{1,0:T(4,128)S(1)}, u32[]{:S(2)}, u32[]{:S(2)}) collective-permute-start(f32[3,1536]{1,0:T(4,128)S(1)} %pad_maximum_fusion.5), channel_id=1, source_target_pairs={{0,48},{16,0},{32,16},{48,32},{64,112},{80,64},{96,80},{112,96},{1... | collective-permute-start | bytes 55304 | tf_op jit(solution)/shard_map/ppermute | solution.py:421
  74.7 15.9 %collective-permute-start.11 = (f32[3,1536]{1,0:T(4,128)S(1)}, f32[3,1536]{1,0:T(4,128)S(1)}, u32[]{:S(2)}, u32[]{:S(2)}) collective-permute-start(f32[3,1536]{1,0:T(4,128)S(1)} %pad_maximum_fusion.5), channel_id=1, source_target_pairs={{0,32},{16,48},{32,0},{48,16},{64,96},{80,112},{96,64},{112,80},{1... | collective-permute-start | bytes 55304 | tf_op jit(solution)/shard_map/ppermute | solution.py:421
  77.1 13.5 %collective-permute-start.10 = (f32[3,1536]{1,0:T(4,128)S(1)}, f32[3,1536]{1,0:T(4,128)S(1)}, u32[]{:S(2)}, u32[]{:S(2)}) collective-permute-start(f32[3,1536]{1,0:T(4,128)S(1)} %pad_maximum_fusion.5), channel_id=1, source_target_pairs={{0,16},{16,32},{32,48},{48,0},{64,80},{80,96},{96,112},{112,64},{1... | collective-permute-start | bytes 55304 | tf_op jit(solution)/shard_map/ppermute | solution.py:421
  90.7 4.3 %collective-permute-start.15 = (f32[3,1536]{1,0:T(4,128)S(1)}, f32[3,1536]{1,0:T(4,128)S(1)}, u32[]{:S(2)}, u32[]{:S(2)}) collective-permute-start(f32[3,1536]{1,0:T(4,128)S(1)} %add_add_fusion.1), channel_id=1, source_target_pairs={{0,192},{16,208},{32,224},{48,240},{64,0},{80,16},{96,32},{112,48}... | collective-permute-start | bytes 55304 | tf_op jit(solution)/shard_map/ppermute | solution.py:421
  90.8 5.4 %collective-permute-start.14 = (f32[3,1536]{1,0:T(4,128)S(1)}, f32[3,1536]{1,0:T(4,128)S(1)}, u32[]{:S(2)}, u32[]{:S(2)}) collective-permute-start(f32[3,1536]{1,0:T(4,128)S(1)} %add_add_fusion.1), channel_id=1, source_target_pairs={{0,128},{16,144},{32,160},{48,176},{64,192},{80,208},{96,224},{112... | collective-permute-start | bytes 55304 | tf_op jit(solution)/shard_map/ppermute | solution.py:421
  93.8 5.0 %collective-permute-start.13 = (f32[3,1536]{1,0:T(4,128)S(1)}, f32[3,1536]{1,0:T(4,128)S(1)}, u32[]{:S(2)}, u32[]{:S(2)}) collective-permute-start(f32[3,1536]{1,0:T(4,128)S(1)} %add_add_fusion.1), channel_id=1, source_target_pairs={{0,64},{16,80},{32,96},{48,112},{64,128},{80,144},{96,160},{112,17... | collective-permute-start | bytes 55304 | tf_op jit(solution)/shard_map/ppermute | solution.py:421
  94.9 5.2 %collective-permute-start.16 = (bf16[512,768]{1,0:T(8,128)(2,1)S(1)}, bf16[512,768]{1,0:T(8,128)(2,1)S(1)}, u32[]{:S(2)}, u32[]{:S(2)}) collective-permute-start(bf16[512,768]{1,0:T(8,128)(2,1)S(1)} %fusion.21), channel_id=1, source_target_pairs={{0,1},{1,0},{2,3},{3,2},{4,5},{5,4},{6,7},{7,6},{8,9},{9,8},{10,11... | collective-permute-start | bytes 2359304 | tf_op jit(solution)/shard_map/ppermute | solution.py:481
  100.1 0.9 copy-start.4
  115.3 3.6 %collective-permute-start.17 = (bf16[512,1536]{1,0:T(8,128)(2,1)}, bf16[512,1536]{1,0:T(8,128)(2,1)S(1)}, u32[]{:S(2)}, u32[]{:S(2)}) collective-permute-start(bf16[512,1536]{1,0:T(8,128)(2,1)} %get-tuple-element.44), channel_id=1, source_target_pairs={{0,1},{1,0},{2,3},{3,2},{4,5},{5,4},{6,7},{7,6},{8,9},{9,8},{10,11... | collective-permute-start | bytes 4718600 | tf_op jit(solution)/shard_map/ppermute | solution.py:491
  115.3 3.6 %copy-start.5 = (bf16[512,768]{1,0:T(8,128)(2,1)S(1)}, bf16[512,768]{1,0:T(8,128)(2,1)}, u32[]{:S(2)}) copy-start(bf16[512,768]{1,0:T(8,128)(2,1)} %copy-done.4) | copy-start | bytes 2359300
  122.3 37.5 %all-to-all-start.1 = ((bf16[16,96,768]{2,1,0:T(8,128)(2,1)}), bf16[16,96,768]{2,1,0:T(8,128)(2,1)}, u32[]{:S(2)}, u32[]{:S(2)}) async-start(bf16[16,96,768]{2,1,0:T(8,128)(2,1)} %bitcast.68), calls=%async_computation.1 | async-start | bytes 4718592 | tf_op jit(solution)/shard_map/all_to_all | solution.py:497
  127.2 22.3 %copy-start.6 = (f32[32,1536]{1,0:T(8,128)S(1)}, f32[32,1536]{1,0:T(8,128)}, u32[]{:S(2)}) copy-start(f32[32,1536]{1,0:T(8,128)} %get-tuple-element.49) | copy-start | bytes 589828
  150.8 1.8 collective-permute-start.18
  192.8 27.1 %all-to-all-start.3 = ((f32[16,200,96]{1,2,0:T(8,128)}), f32[16,200,96]{1,2,0:T(8,128)S(1)}, u32[]{:S(2)}, u32[]{:S(2)}) async-start(f32[16,200,96]{1,2,0:T(8,128)} %broadcast_in_dim.8), calls=%async_computation.3 | async-start | bytes 3145728 | tf_op jit(solution)/shard_map/all_to_all | solution.py:522
Sparse Core Ops, SparseCore 0:
  9.8 49.2 all-gather.1

commit v8 on v7

--- a/solution.py
+++ b/solution.py
@@ -509,7 +509,7 @@
     grads = lax.dynamic_index_in_dim(grads, core, 0, False) + grads_other
 
     term = jnp.sum(term.astype(F32), axis=0).reshape(share, 8, share)
-    both = jnp.concatenate([jnp.transpose(term, (1, 0, 2)), grads], axis=1)
+    both = jnp.concatenate([jnp.transpose(term, (1, 0, 2)), grads], axis=1).reshape(8, 150, LANES)
     both = lax.all_to_all(
         both,
         "zero",
@@ -522,8 +522,8 @@
     last = lax.all_to_all(
         jnp.broadcast_to(last[None], (16,) + last.shape), "dp", 0, 0, tiled=True
     )
-    part_w = last[:, :share].reshape(width, share)
-    grads = jnp.sum(last[:, share:], axis=0)
+    part_w = last[:, :72].reshape(width, share)
+    grads = jnp.sum(last[:, 72:], axis=0).reshape(104, share)
 
     own = lax.dynamic_slice_in_dim(norm, zero_id * share, share, 1)
     da_x, hat_x, x_k = grads[:KER], grads[KER : 2 * KER], grads[72 : 72 + KER]

time: 232 us -> 225 us (0.970)
  Pallas kernels: 50.7 us -> 45.4 us
  starting transfers between devices: 54.7 us -> 59.6 us
  waiting for transfers between devices: 37.5 us -> 34.2 us
  blocking collectives: 29.1 us -> 26.2 us
    pallas_call x1, Pallas kernels: 11.4 us -> 7.48 us  [stats(): pl.pallas_call(stats_kernel, grid=(width // WIDE,), out_shape=(jax.ShapeD...]
    ppermute x11, starting transfers between devices: 21.8 us -> 25.7 us  [add_from(): parts = [lax.ppermute(x, axis, step) for step in steps]]
    all_to_all x1, waiting for transfers between devices: 11.9 us -> 8.44 us  [per_device(): lax.all_to_all(jnp.broadcast_to(last[None], (16,) + last.shape), 'dp', 0,...]
    all_to_all x1, blocking collectives: 29.1 us -> 26.2 us  [per_device(): lax.all_to_all(both, 'zero', 0, 0, axis_index_groups=[[i for i in range(1...]
    unnamed x24 -> x25, local copies, waits for them, and re-layouts: 6.78 us -> 6.52 us
  transfers between devices with their start and end apart: 23 -> 23, of which waited for: 11 -> 10; matrix products, arithmetic and copies ran while one was open for 12% -> 13% of each run, Pallas kernels for 16% -> 14%
where the time goes in v8:
time: 225 us
  starting transfers between devices  59.6 us (26%)
  Pallas kernels  45.4 us (20%)
  waiting for transfers between devices  34.2 us (15%)
  blocking collectives  26.2 us (12%)
  matrix products  22.1 us (10%)
  between operations  14.5 us (6%)
  local copies, waits for them, and re-layouts  12.1 us (5%)
  other arithmetic  10.5 us (5%)
    all_to_all x1, blocking collectives, per_device(): lax.all_to_all(both, 'zero', 0, 0, axis_index_groups=[[i for i in range(1...  26.2 us
    ppermute x11, starting transfers between devices, add_from(): parts = [lax.ppermute(x, axis, step) for step in steps]  25.7 us
    pallas_call x1, Pallas kernels, terms(): pl.pallas_call(terms_kernel, grid=(width // WIDE,), out_shape=jax.ShapeDt...  21.3 us
    pallas_call x1, Pallas kernels, hidden(): pl.pallas_call(hidden_kernel, grid=(width // WIDE,), out_shape=(jax.Shape...  13.8 us
    ppermute x11, waiting for transfers between devices, add_from(): parts = [lax.ppermute(x, axis, step) for step in steps]  12.7 us
    ppermute x3, starting transfers between devices, gather_small(): lax.ppermute(x, 'zero', zero_step(step))  10.5 us
    all_to_all x1, waiting for transfers between devices, per_device(): lax.all_to_all(jnp.broadcast_to(last[None], (16,) + last.shape), 'dp', 0,...  8.44 us
    all_to_all x1, starting transfers between devices, per_device(): lax.all_to_all(jnp.broadcast_to(last[None], (16,) + last.shape), 'dp', 0,...  7.88 us
  transfers between devices with their start and end apart: 23, of which 10 were waited for; matrix products, arithmetic and copies ran while one was open for 13% of the time, Pallas kernels for 14%

profile of v8, /device:TPU:8, one launch (start us, length us, event | category | flops | bytes accessed | tf_op | source)
XLA Modules:
  0.0 224.5 jit_solution(12408756675925139929)
XLA Ops:
  7.2 0.7 all-gather.2.cloned.1.call-update
  8.0 0.8 maximum_maximum_fusion
  8.8 1.7 copy-done.2
  10.5 0.7 copy-done.3
  11.2 1.2 pack.1._
  12.4 2.2 copy-done.1
  14.7 2.0 collective-permute-start.1
  16.7 7.4 %all-to-all-start = ((bf16[16,96,1536]{2,1,0:T(8,128)(2,1)}), bf16[16,96,1536]{2,1,0:T(8,128)(2,1)}, u32[]{:S(2)}, u32[]{:S(2)}) async-start(bf16[16,96,1536]{2,1,0:T(8,128)(2,1)} %copy-done.1), calls=%async_computation | async-start | bytes 9437184 | tf_op jit(solution)/shard_map/all_to_all | solution.py:454
  24.1 0.6 reduce
  24.8 3.4 %collective-permute-start.4 = (bf16[2,2,48,96]{3,2,1,0:T(8,128)(2,1)S(1)}, bf16[2,2,48,96]{3,2,1,0:T(8,128)(2,1)S(1)}, u32[]{:S(2)}, u32[]{:S(2)}) collective-permute-start(bf16[2,2,48,96]{3,2,1,0:T(8,128)(2,1)S(1)} %pad_maximum_fusion.3), channel_id=1, source_target_pairs={{0,4},{1,5},{2,6},{3,7},{4,8},{5,9},{6,10},{7,11},{8,12},{9,13},{1... | collective-permute-start | bytes 110600 | tf_op jit(solution)/shard_map/ppermute | solution.py:431
  28.1 4.5 %collective-permute-start.3 = (bf16[2,2,48,96]{3,2,1,0:T(8,128)(2,1)S(1)}, bf16[2,2,48,96]{3,2,1,0:T(8,128)(2,1)S(1)}, u32[]{:S(2)}, u32[]{:S(2)}) collective-permute-start(bf16[2,2,48,96]{3,2,1,0:T(8,128)(2,1)S(1)} %pad_maximum_fusion.3), channel_id=1, source_target_pairs={{0,8},{1,9},{2,10},{3,11},{4,12},{5,13},{6,14},{7,15},{8,0},{9,1},... | collective-permute-start | bytes 110600 | tf_op jit(solution)/shard_map/ppermute | solution.py:431
  32.6 2.7 %collective-permute-start.2 = (bf16[2,2,48,96]{3,2,1,0:T(8,128)(2,1)S(1)}, bf16[2,2,48,96]{3,2,1,0:T(8,128)(2,1)S(1)}, u32[]{:S(2)}, u32[]{:S(2)}) collective-permute-start(bf16[2,2,48,96]{3,2,1,0:T(8,128)(2,1)S(1)} %pad_maximum_fusion.3), channel_id=1, source_target_pairs={{0,12},{1,13},{2,14},{3,15},{4,0},{5,1},{6,2},{7,3},{8,4},{9,5},{1... | collective-permute-start | bytes 110600 | tf_op jit(solution)/shard_map/ppermute | solution.py:431
  35.3 1.5 places.1
  36.9 2.8 %collective-permute-done.3 = bf16[2,2,48,96]{3,2,1,0:T(8,128)(2,1)S(1)} collective-permute-done((bf16[2,2,48,96]{3,2,1,0:T(8,128)(2,1)S(1)}, bf16[2,2,48,96]{3,2,1,0:T(8,128)(2,1)S(1)}, u32[]{:S(2)}, u32[]{:S(2)}) %collective-permute-start.3) | collective-permute-done | bytes 36896 | tf_op jit(solution)/shard_map/ppermute | solution.py:431
  40.0 0.8 slice.61.kern_ref
  40.9 7.5 %stats.1 = (f32[2,1536]{1,0:T(2,128)}, f32[32,1536]{1,0:T(8,128)}) custom-call(s32[4]{0:T(128)} %get-tuple-element.27.bounds_ref, bf16[768,1536]{1,0:T(8,128)(2,1)} %bitcast.66, f32[32,1536]{1,0:T(8,128)} %slice.61.kern_ref, bf16[16,96,1536]{2,1,0:T(8,128)(2,1)} %copy-done.1), custom_call_target="tpu_custom_call" | custom-call | flops 16499999744 | bytes 1000000 | tf_op jit(solution)/shard_map/stats/pallas_call | solution.py:218
  48.3 7.0 %collective-permute-start.5 = (f32[2,1536]{1,0:T(2,128)}, f32[2,1536]{1,0:T(2,128)S(1)}, u32[]{:S(2)}, u32[]{:S(2)}) collective-permute-start(f32[2,1536]{1,0:T(2,128)} %get-tuple-element.29), channel_id=1, source_target_pairs={{0,1},{1,0},{2,3},{3,2},{4,5},{5,4},{6,7},{7,6},{8,9},{9,8},{10,11... | collective-permute-start | bytes 36872 | tf_op jit(solution)/shard_map/ppermute | solution.py:421
  55.3 1.0 collective-permute-done.5
  56.4 0.7 add.110
  57.2 3.6 %collective-permute-done.6 = f32[2,1536]{1,0:T(2,128)S(1)} collective-permute-done((f32[2,1536]{1,0:T(2,128)S(1)}, f32[2,1536]{1,0:T(2,128)S(1)}, u32[]{:S(2)}, u32[]{:S(2)}) %collective-permute-start.6) | collective-permute-done | bytes 12320 | tf_op jit(solution)/shard_map/ppermute | solution.py:421
  60.8 4.4 %collective-permute-start.9 = (f32[2,1536]{1,0:T(2,128)S(1)}, f32[2,1536]{1,0:T(2,128)S(1)}, u32[]{:S(2)}, u32[]{:S(2)}) collective-permute-start(f32[2,1536]{1,0:T(2,128)S(1)} %add.111), channel_id=1, source_target_pairs={{0,12},{1,13},{2,14},{3,15},{4,0},{5,1},{6,2},{7,3},{8,4},{9,5},{1... | collective-permute-start | bytes 36872 | tf_op jit(solution)/shard_map/ppermute | solution.py:421
  65.2 1.1 collective-permute-start.8
  66.3 2.1 collective-permute-start.7
  68.4 4.4 %collective-permute-done.8 = f32[2,1536]{1,0:T(2,128)S(1)} collective-permute-done((f32[2,1536]{1,0:T(2,128)S(1)}, f32[2,1536]{1,0:T(2,128)S(1)}, u32[]{:S(2)}, u32[]{:S(2)}) %collective-permute-start.8) | collective-permute-done | bytes 12320 | tf_op jit(solution)/shard_map/ppermute | solution.py:421
  72.9 1.3 collective-permute-start.12
  74.3 1.5 collective-permute-start.11
  75.8 1.7 collective-permute-start.10
  77.4 1.8 fusion.21
  79.2 2.7 %fusion.18 = bf16[512,768]{1,0:T(8,128)(2,1)} fusion(bf16[512,1536]{1,0:T(8,128)(2,1)S(1)} %bitcast.65, s32[768]{0:T(1024)S(1)} %get-tuple-element.73, s32[768]{0:T(1024)S(1)} %get-tuple-element.74, pred[768]{0:T(1024)(128)(4,1)S(1)} %fusion.27, pred[]{:T(512)S(6)} %eq.85), kind=kOutput, calls=%fused_computation.21 | convolution fusion | flops 1216610304 | bytes 2366209 | tf_op jit(solution)/shard_map/dot_general | solution.py:475
  81.9 6.6 %fusion.35.rest_0_.wide_back = f32[512,1536]{1,0:T(8,128)} fusion(bf16[512,1536]{1,0:T(8,128)(2,1)S(1)} %bitcast.64, bf16[1536,1536]{1,0:T(8,128)(2,1)} %all-gather.2.cloned.1.call-done), kind=kOutput, calls=%fused_computation.71 | convolution fusion | flops 2415919104 | bytes 9437184 | tf_op jit(solution)/shard_map/dot_general | solution.py:477
  88.5 3.8 %collective-permute-start.15 = (f32[3,1536]{1,0:T(4,128)S(1)}, f32[3,1536]{1,0:T(4,128)S(1)}, u32[]{:S(2)}, u32[]{:S(2)}) collective-permute-start(f32[3,1536]{1,0:T(4,128)S(1)} %add_add_fusion.1), channel_id=1, source_target_pairs={{0,192},{16,208},{32,224},{48,240},{64,0},{80,16},{96,32},{112,48}... | collective-permute-start | bytes 55304 | tf_op jit(solution)/shard_map/ppermute | solution.py:421
  92.3 1.5 collective-permute-start.14
  93.8 1.2 collective-permute-start.13
  95.2 2.4 %collective-permute-done.14 = f32[3,1536]{1,0:T(4,128)S(1)} collective-permute-done((f32[3,1536]{1,0:T(4,128)S(1)}, f32[3,1536]{1,0:T(4,128)S(1)}, u32[]{:S(2)}, u32[]{:S(2)}) %collective-permute-start.14) | collective-permute-done | bytes 18464 | tf_op jit(solution)/shard_map/ppermute | solution.py:421
  97.6 1.2 collective-permute-done.13
  98.9 0.6 fusion.29.info_ref
  99.4 0.6 pad_maximum_fusion.6.norm_ref
  100.1 0.9 copy-done.5
  101.0 13.8 %hidden.1 = (f32[12,512,128]{2,1,0:T(8,128)}, bf16[512,1536]{1,0:T(8,128)(2,1)}) custom-call(s32[80]{0:T(128)} %fusion.29.info_ref, bf16[16,96,1536]{2,1,0:T(8,128)(2,1)} %all-to-all-done.got_ref, f32[32,1536]{1,0:T(8,128)} %slice.61.kern_ref, f32[4,1536]{1,0:T(4,128)} %pad_maximum_fusion.6.norm_ref, f32[512,1536]{1,0:T(8,128)} %fusion.35.rest_0_.wide_back, ...), custom_call_target="tpu_custom_call" | custom-call | flops 17600000000 | bytes 1000000 | tf_op jit(solution)/shard_map/hidden/pallas_call | solution.py:303
  114.8 3.1 %fusion.36 = f32[1536,768]{1,0:T(8,128)S(1)} fusion(bf16[512,1536]{1,0:T(8,128)(2,1)} %get-tuple-element.44, bf16[512,768]{1,0:T(8,128)(2,1)} %fusion.18), kind=kOutput, calls=%fused_computation.72 | convolution fusion | flops 1207959552 | bytes 7077888 | tf_op jit(solution)/shard_map/dot_general | solution.py:493
  117.9 0.5 collective-permute-done.17
  118.4 1.4 fusion.37
  119.9 1.9 add_convert_fusion
  121.8 5.9 %all-to-all-start.1 = ((bf16[16,96,768]{2,1,0:T(8,128)(2,1)}), bf16[16,96,768]{2,1,0:T(8,128)(2,1)}, u32[]{:S(2)}, u32[]{:S(2)}) async-start(bf16[16,96,768]{2,1,0:T(8,128)(2,1)} %bitcast.70), calls=%async_computation.1 | async-start | bytes 4718592 | tf_op jit(solution)/shard_map/all_to_all | solution.py:497
  127.7 21.3 %terms.1 = f32[72,1536]{1,0:T(8,128)} custom-call(s32[80]{0:T(128)} %fusion.29.info_ref, bf16[16,96,1536]{2,1,0:T(8,128)(2,1)} %all-to-all-done.got_ref, f32[12,512,128]{2,1,0:T(8,128)} %get-tuple-element.48.h_ref, f32[512,1536]{1,0:T(8,128)} %fusion.35.rest_0_.wide_back, f32[4,1536]{1,0:T(4,128)} %pad_maximum_fusion.6.norm_ref), custom_call_target="tpu_custom_call" | custom-call | flops 27499999232 | bytes 1000000 | tf_op jit(solution)/shard_map/terms/pallas_call | solution.py:384
  149.0 1.1 pad_maximum_fusion.1
  150.1 0.3 copy.20
  150.5 1.7 collective-permute-done.18
  152.2 0.8 bitcast_add_fusion
  153.0 7.4 %all-to-all-done.1 = bf16[16,96,768]{2,1,0:T(8,128)(2,1)} async-done(((bf16[16,96,768]{2,1,0:T(8,128)(2,1)}), bf16[16,96,768]{2,1,0:T(8,128)(2,1)}, u32[]{:S(2)}, u32[]{:S(2)}) %all-to-all-start.1) | async-done | bytes 2359328 | tf_op jit(solution)/shard_map/all_to_all | solution.py:497
  160.4 2.0 convert_reduce_fusion
  162.6 0.3 pad_maximum_fusion
  162.8 0.3 copy.22
  163.1 0.6 reshape.46
  163.8 26.2 %all_to_all.20 = f32[8,150,128]{2,1,0:T(8,128)S(1)} all-to-all(f32[8,150,128]{2,1,0:T(8,128)S(1)} %reshape.46), channel_id=1, replica_groups={{0,2,4,6,8,10,12,14},{1,3,5,7,9,11,13,15},{16,18,20,22,24,26,28,30},{17..., dimensions={0} | all-to-all | bytes 1228800 | tf_op jit(solution)/shard_map/all_to_all | solution.py:513
  190.0 1.2 broadcast_in_dim.8
  191.1 7.9 %all-to-all-start.3 = ((f32[16,150,128]{2,1,0:T(8,128)}), f32[16,150,128]{2,1,0:T(8,128)S(1)}, u32[]{:S(2)}, u32[]{:S(2)}) async-start(f32[16,150,128]{2,1,0:T(8,128)} %broadcast_in_dim.8), calls=%async_computation.3 | async-start | bytes 2490368 | tf_op jit(solution)/shard_map/all_to_all | solution.py:522
  199.0 0.8 constant_dynamic-slice_fusion
  199.8 6.6 %fusion.5 = bf16[1,1,512,1536]{3,2,1,0:T(8,128)(2,1)} fusion(bf16[512,1536]{1,0:T(8,128)(2,1)} %get-tuple-element.44, bf16[1536,1536]{1,0:T(8,128)(2,1)} %all-gather.2.cloned.1.call-done), kind=kOutput, calls=%fused_computation.10 | convolution fusion | flops 2416705536 | bytes 7864320 | tf_op jit(solution)/shard_map/dot_general | solution.py:500
  206.4 8.4 %all-to-all-done.3 = f32[16,150,128]{2,1,0:T(8,128)S(1)} async-done(((f32[16,150,128]{2,1,0:T(8,128)}), f32[16,150,128]{2,1,0:T(8,128)S(1)}, u32[]{:S(2)}, u32[]{:S(2)}) %all-to-all-start.3) | async-done | bytes 1228832 | tf_op jit(solution)/shard_map/all_to_all | solution.py:522
  214.9 0.6 stack.54
  215.8 0.2 reshape.47
  216.0 1.1 copy.23
  217.1 0.6 subtract_multiply_fusion
  (73 shorter events, 1.7 us)
Async XLA Ops:
  7.2 65.7 %copy-start = (bf16[1,1,512,1536]{3,2,1,0:T(8,128)(2,1)S(1)}, bf16[1,1,512,1536]{3,2,1,0:T(8,128)(2,1)}, u32[]{:S(2)}) copy-start(bf16[1,1,512,1536]{3,2,1,0:T(8,128)(2,1)} %param.10) | copy-start | bytes 4718596
  7.2 74.7 %all-gather.2.cloned.1.call-start = ((), (), s32[]{:S(2)}) async-start(), calls=%async_computation.4 | async-start | bytes 5013504 | tf_op jit(solution)/shard_map/all_gather | solution.py:459
  8.8 5.8 %collective-permute-start = (bf16[48,96]{1,0:T(8,128)(2,1)S(1)}, bf16[48,96]{1,0:T(8,128)(2,1)S(1)}, u32[]{:S(2)}, u32[]{:S(2)}) collective-permute-start(bf16[48,96]{1,0:T(8,128)(2,1)S(1)} %maximum_maximum_fusion), channel_id=1, source_target_pairs={{0,1},{1,0},{2,3},{3,2},{4,5},{5,4},{6,7},{7,6},{8,9},{9,8},{10,11... | collective-permute-start | bytes 27656 | tf_op jit(solution)/shard_map/ppermute | solution.py:428
  8.8 1.7 copy-start.2
  10.5 0.7 copy-start.3
  11.2 3.5 %copy-start.8 = (bf16[32,96]{1,0:T(8,128)(2,1)S(1)}, bf16[32,96]{1,0:T(8,128)(2,1)}, u32[]{:S(2)}) copy-start(bf16[32,96]{1,0:T(8,128)(2,1)} %param.12) | copy-start | bytes 18436
  11.2 3.5 %copy-start.11 = (bf16[2,96]{1,0:T(2,128)(2,1)S(1)}, bf16[2,96]{1,0:T(2,128)(2,1)}, u32[]{:S(2)}) copy-start(bf16[2,96]{1,0:T(2,128)(2,1)} %param.13) | copy-start | bytes 1156
  12.4 2.2 copy-start.1
  14.7 9.4 %copy-start.10 = (s32[1,1,768]{2,1,0:T(1,128)S(1)}, s32[1,1,768]{2,1,0:T(1,128)}, u32[]{:S(2)}) copy-start(s32[1,1,768]{2,1,0:T(1,128)} %param.8) | copy-start | bytes 9220
  14.7 10.0 %collective-permute-start.1 = (bf16[2,48,96]{2,1,0:T(8,128)(2,1)S(1)}, bf16[2,48,96]{2,1,0:T(8,128)(2,1)S(1)}, u32[]{:S(2)}, u32[]{:S(2)}) collective-permute-start(bf16[2,48,96]{2,1,0:T(8,128)(2,1)S(1)} %pad_maximum_fusion.4), channel_id=1, source_target_pairs={{0,2},{1,3},{2,0},{3,1},{4,6},{5,7},{6,4},{7,5},{8,10},{9,11},{10,... | collective-permute-start | bytes 55304 | tf_op jit(solution)/shard_map/ppermute | solution.py:428
  16.7 83.3 %all-to-all-start = ((bf16[16,96,1536]{2,1,0:T(8,128)(2,1)}), bf16[16,96,1536]{2,1,0:T(8,128)(2,1)}, u32[]{:S(2)}, u32[]{:S(2)}) async-start(bf16[16,96,1536]{2,1,0:T(8,128)(2,1)} %copy-done.1), calls=%async_computation | async-start | bytes 9437184 | tf_op jit(solution)/shard_map/all_to_all | solution.py:454
  24.8 12.1 %collective-permute-start.4 = (bf16[2,2,48,96]{3,2,1,0:T(8,128)(2,1)S(1)}, bf16[2,2,48,96]{3,2,1,0:T(8,128)(2,1)S(1)}, u32[]{:S(2)}, u32[]{:S(2)}) collective-permute-start(bf16[2,2,48,96]{3,2,1,0:T(8,128)(2,1)S(1)} %pad_maximum_fusion.3), channel_id=1, source_target_pairs={{0,4},{1,5},{2,6},{3,7},{4,8},{5,9},{6,10},{7,11},{8,12},{9,13},{1... | collective-permute-start | bytes 110600 | tf_op jit(solution)/shard_map/ppermute | solution.py:431
  28.1 11.5 %collective-permute-start.3 = (bf16[2,2,48,96]{3,2,1,0:T(8,128)(2,1)S(1)}, bf16[2,2,48,96]{3,2,1,0:T(8,128)(2,1)S(1)}, u32[]{:S(2)}, u32[]{:S(2)}) collective-permute-start(bf16[2,2,48,96]{3,2,1,0:T(8,128)(2,1)S(1)} %pad_maximum_fusion.3), channel_id=1, source_target_pairs={{0,8},{1,9},{2,10},{3,11},{4,12},{5,13},{6,14},{7,15},{8,0},{9,1},... | collective-permute-start | bytes 110600 | tf_op jit(solution)/shard_map/ppermute | solution.py:431
  32.6 7.0 %collective-permute-start.2 = (bf16[2,2,48,96]{3,2,1,0:T(8,128)(2,1)S(1)}, bf16[2,2,48,96]{3,2,1,0:T(8,128)(2,1)S(1)}, u32[]{:S(2)}, u32[]{:S(2)}) collective-permute-start(bf16[2,2,48,96]{3,2,1,0:T(8,128)(2,1)S(1)} %pad_maximum_fusion.3), channel_id=1, source_target_pairs={{0,12},{1,13},{2,14},{3,15},{4,0},{5,1},{6,2},{7,3},{8,4},{9,5},{1... | collective-permute-start | bytes 110600 | tf_op jit(solution)/shard_map/ppermute | solution.py:431
  40.8 32.0 %copy-start.9 = (f32[1,1536]{1,0:T(1,128)S(1)}, f32[1,1536]{1,0:T(1,128)}, u32[]{:S(2)}) copy-start(f32[1,1536]{1,0:T(1,128)} %get-tuple-element.33) | copy-start | bytes 18436
  48.3 8.0 %collective-permute-start.5 = (f32[2,1536]{1,0:T(2,128)}, f32[2,1536]{1,0:T(2,128)S(1)}, u32[]{:S(2)}, u32[]{:S(2)}) collective-permute-start(f32[2,1536]{1,0:T(2,128)} %get-tuple-element.29), channel_id=1, source_target_pairs={{0,1},{1,0},{2,3},{3,2},{4,5},{5,4},{6,7},{7,6},{8,9},{9,8},{10,11... | collective-permute-start | bytes 36872 | tf_op jit(solution)/shard_map/ppermute | solution.py:421
  57.1 3.7 %collective-permute-start.6 = (f32[2,1536]{1,0:T(2,128)S(1)}, f32[2,1536]{1,0:T(2,128)S(1)}, u32[]{:S(2)}, u32[]{:S(2)}) collective-permute-start(f32[2,1536]{1,0:T(2,128)S(1)} %add.110), channel_id=1, source_target_pairs={{0,2},{1,3},{2,0},{3,1},{4,6},{5,7},{6,4},{7,5},{8,10},{9,11},{10,... | collective-permute-start | bytes 36872 | tf_op jit(solution)/shard_map/ppermute | solution.py:421
  60.8 7.6 %collective-permute-start.9 = (f32[2,1536]{1,0:T(2,128)S(1)}, f32[2,1536]{1,0:T(2,128)S(1)}, u32[]{:S(2)}, u32[]{:S(2)}) collective-permute-start(f32[2,1536]{1,0:T(2,128)S(1)} %add.111), channel_id=1, source_target_pairs={{0,12},{1,13},{2,14},{3,15},{4,0},{5,1},{6,2},{7,3},{8,4},{9,5},{1... | collective-permute-start | bytes 36872 | tf_op jit(solution)/shard_map/ppermute | solution.py:421
  65.2 7.7 %collective-permute-start.8 = (f32[2,1536]{1,0:T(2,128)S(1)}, f32[2,1536]{1,0:T(2,128)S(1)}, u32[]{:S(2)}, u32[]{:S(2)}) collective-permute-start(f32[2,1536]{1,0:T(2,128)S(1)} %add.111), channel_id=1, source_target_pairs={{0,8},{1,9},{2,10},{3,11},{4,12},{5,13},{6,14},{7,15},{8,0},{9,1},... | collective-permute-start | bytes 36872 | tf_op jit(solution)/shard_map/ppermute | solution.py:421
  66.3 6.5 %collective-permute-start.7 = (f32[2,1536]{1,0:T(2,128)S(1)}, f32[2,1536]{1,0:T(2,128)S(1)}, u32[]{:S(2)}, u32[]{:S(2)}) collective-permute-start(f32[2,1536]{1,0:T(2,128)S(1)} %add.111), channel_id=1, source_target_pairs={{0,4},{1,5},{2,6},{3,7},{4,8},{5,9},{6,10},{7,11},{8,12},{9,13},{1... | collective-permute-start | bytes 36872 | tf_op jit(solution)/shard_map/ppermute | solution.py:421
  72.9 15.5 %collective-permute-start.12 = (f32[3,1536]{1,0:T(4,128)S(1)}, f32[3,1536]{1,0:T(4,128)S(1)}, u32[]{:S(2)}, u32[]{:S(2)}) collective-permute-start(f32[3,1536]{1,0:T(4,128)S(1)} %pad_maximum_fusion.5), channel_id=1, source_target_pairs={{0,48},{16,0},{32,16},{48,32},{64,112},{80,64},{96,80},{112,96},{1... | collective-permute-start | bytes 55304 | tf_op jit(solution)/shard_map/ppermute | solution.py:421
  74.3 14.2 %collective-permute-start.11 = (f32[3,1536]{1,0:T(4,128)S(1)}, f32[3,1536]{1,0:T(4,128)S(1)}, u32[]{:S(2)}, u32[]{:S(2)}) collective-permute-start(f32[3,1536]{1,0:T(4,128)S(1)} %pad_maximum_fusion.5), channel_id=1, source_target_pairs={{0,32},{16,48},{32,0},{48,16},{64,96},{80,112},{96,64},{112,80},{1... | collective-permute-start | bytes 55304 | tf_op jit(solution)/shard_map/ppermute | solution.py:421
  75.8 12.7 %collective-permute-start.10 = (f32[3,1536]{1,0:T(4,128)S(1)}, f32[3,1536]{1,0:T(4,128)S(1)}, u32[]{:S(2)}, u32[]{:S(2)}) collective-permute-start(f32[3,1536]{1,0:T(4,128)S(1)} %pad_maximum_fusion.5), channel_id=1, source_target_pairs={{0,16},{16,32},{32,48},{48,0},{64,80},{80,96},{96,112},{112,64},{1... | collective-permute-start | bytes 55304 | tf_op jit(solution)/shard_map/ppermute | solution.py:421
  88.5 6.7 %collective-permute-start.15 = (f32[3,1536]{1,0:T(4,128)S(1)}, f32[3,1536]{1,0:T(4,128)S(1)}, u32[]{:S(2)}, u32[]{:S(2)}) collective-permute-start(f32[3,1536]{1,0:T(4,128)S(1)} %add_add_fusion.1), channel_id=1, source_target_pairs={{0,192},{16,208},{32,224},{48,240},{64,0},{80,16},{96,32},{112,48}... | collective-permute-start | bytes 55304 | tf_op jit(solution)/shard_map/ppermute | solution.py:421
  92.3 5.3 %collective-permute-start.14 = (f32[3,1536]{1,0:T(4,128)S(1)}, f32[3,1536]{1,0:T(4,128)S(1)}, u32[]{:S(2)}, u32[]{:S(2)}) collective-permute-start(f32[3,1536]{1,0:T(4,128)S(1)} %add_add_fusion.1), channel_id=1, source_target_pairs={{0,128},{16,144},{32,160},{48,176},{64,192},{80,208},{96,224},{112... | collective-permute-start | bytes 55304 | tf_op jit(solution)/shard_map/ppermute | solution.py:421
  93.8 5.0 %collective-permute-start.13 = (f32[3,1536]{1,0:T(4,128)S(1)}, f32[3,1536]{1,0:T(4,128)S(1)}, u32[]{:S(2)}, u32[]{:S(2)}) collective-permute-start(f32[3,1536]{1,0:T(4,128)S(1)} %add_add_fusion.1), channel_id=1, source_target_pairs={{0,64},{16,80},{32,96},{48,112},{64,128},{80,144},{96,160},{112,17... | collective-permute-start | bytes 55304 | tf_op jit(solution)/shard_map/ppermute | solution.py:421
  95.1 5.0 %collective-permute-start.16 = (bf16[512,768]{1,0:T(8,128)(2,1)S(1)}, bf16[512,768]{1,0:T(8,128)(2,1)S(1)}, u32[]{:S(2)}, u32[]{:S(2)}) collective-permute-start(bf16[512,768]{1,0:T(8,128)(2,1)S(1)} %fusion.21), channel_id=1, source_target_pairs={{0,1},{1,0},{2,3},{3,2},{4,5},{5,4},{6,7},{7,6},{8,9},{9,8},{10,11... | collective-permute-start | bytes 2359304 | tf_op jit(solution)/shard_map/ppermute | solution.py:481
  100.1 0.9 copy-start.5
  114.8 3.6 %collective-permute-start.17 = (bf16[512,1536]{1,0:T(8,128)(2,1)}, bf16[512,1536]{1,0:T(8,128)(2,1)S(1)}, u32[]{:S(2)}, u32[]{:S(2)}) collective-permute-start(bf16[512,1536]{1,0:T(8,128)(2,1)} %get-tuple-element.44), channel_id=1, source_target_pairs={{0,1},{1,0},{2,3},{3,2},{4,5},{5,4},{6,7},{7,6},{8,9},{9,8},{10,11... | collective-permute-start | bytes 4718600 | tf_op jit(solution)/shard_map/ppermute | solution.py:491
  114.8 3.6 %copy-start.6 = (bf16[512,768]{1,0:T(8,128)(2,1)S(1)}, bf16[512,768]{1,0:T(8,128)(2,1)}, u32[]{:S(2)}) copy-start(bf16[512,768]{1,0:T(8,128)(2,1)} %copy-done.5) | copy-start | bytes 2359300
  121.8 38.6 %all-to-all-start.1 = ((bf16[16,96,768]{2,1,0:T(8,128)(2,1)}), bf16[16,96,768]{2,1,0:T(8,128)(2,1)}, u32[]{:S(2)}, u32[]{:S(2)}) async-start(bf16[16,96,768]{2,1,0:T(8,128)(2,1)} %bitcast.70), calls=%async_computation.1 | async-start | bytes 4718592 | tf_op jit(solution)/shard_map/all_to_all | solution.py:497
  127.7 21.3 %copy-start.7 = (f32[32,1536]{1,0:T(8,128)S(1)}, f32[32,1536]{1,0:T(8,128)}, u32[]{:S(2)}) copy-start(f32[32,1536]{1,0:T(8,128)} %get-tuple-element.49) | copy-start | bytes 589828
  150.4 1.8 collective-permute-start.18
  153.0 9.6 %copy-start.4 = (f32[8,104,96]{1,2,0:T(8,128)S(1)}, f32[8,104,96]{1,2,0:T(8,128)}, u32[]{:S(2)}) copy-start(f32[8,104,96]{1,2,0:T(8,128)} %bitcast_add_fusion) | copy-start | bytes 958468
  191.1 23.7 %all-to-all-start.3 = ((f32[16,150,128]{2,1,0:T(8,128)}), f32[16,150,128]{2,1,0:T(8,128)S(1)}, u32[]{:S(2)}, u32[]{:S(2)}) async-start(f32[16,150,128]{2,1,0:T(8,128)} %broadcast_in_dim.8), calls=%async_computation.3 | async-start | bytes 2490368 | tf_op jit(solution)/shard_map/all_to_all | solution.py:522
Sparse Core Ops, SparseCore 0:
  9.8 49.2 all-gather.1

commit v9 on v8

--- a/solution.py
+++ b/solution.py
@@ -507,9 +507,12 @@
         lax.dynamic_index_in_dim(grads, 1 - core, 0, False), "zero", swap
     )
     grads = lax.dynamic_index_in_dim(grads, core, 0, False) + grads_other
+    grads = grads.reshape(8, 78, LANES)
+    term, grads = lax.optimization_barrier((term, grads))
 
     term = jnp.sum(term.astype(F32), axis=0).reshape(share, 8, share)
-    both = jnp.concatenate([jnp.transpose(term, (1, 0, 2)), grads], axis=1).reshape(8, 150, LANES)
+    term = jnp.transpose(term, (1, 0, 2)).reshape(8, 72, LANES)
+    both = jnp.concatenate([term, grads], axis=1)
     both = lax.all_to_all(
         both,
         "zero",

time: 225 us -> 224 us (level)
  Pallas kernels: 45.4 us -> 47.9 us
    ppermute x11, waiting for transfers between devices: 12.7 us -> 9.63 us  [add_from(): parts = [lax.ppermute(x, axis, step) for step in steps]]
    all_to_all x1, starting transfers between devices: 5.87 us -> 8.76 us  [per_device(): term = lax.all_to_all(term, 'dp', 0, 0, tiled=True)]
    unnamed x25 -> x23, local copies, waits for them, and re-layouts: 6.52 us -> 6.52 us
  transfers between devices with their start and end apart: 23 -> 23, of which waited for: 10 -> 11; matrix products, arithmetic and copies ran while one was open for 13% -> 13% of each run, Pallas kernels for 14% -> 15%
where the time goes in v9:
time: 224 us
  starting transfers between devices  59.9 us (27%)
  Pallas kernels  47.9 us (21%)
  waiting for transfers between devices  32.2 us (14%)
  blocking collectives  25.4 us (11%)
  matrix products  22.1 us (10%)
  between operations  14.5 us (6%)
  local copies, waits for them, and re-layouts  12 us (5%)
  other arithmetic  9.51 us (4%)
    all_to_all x1, blocking collectives, per_device(): lax.all_to_all(both, 'zero', 0, 0, axis_index_groups=[[i for i in range(1...  25.4 us
    ppermute x11, starting transfers between devices, add_from(): parts = [lax.ppermute(x, axis, step) for step in steps]  24.1 us
    pallas_call x1, Pallas kernels, terms(): pl.pallas_call(terms_kernel, grid=(width // WIDE,), out_shape=jax.ShapeDt...  22.3 us
    pallas_call x1, Pallas kernels, hidden(): pl.pallas_call(hidden_kernel, grid=(width // WIDE,), out_shape=(jax.Shape...  14.3 us
    ppermute x11, waiting for transfers between devices, add_from(): parts = [lax.ppermute(x, axis, step) for step in steps]  9.63 us
    ppermute x3, starting transfers between devices, gather_small(): lax.ppermute(x, 'zero', zero_step(step))  9.31 us
    all_to_all x1, starting transfers between devices, per_device(): term = lax.all_to_all(term, 'dp', 0, 0, tiled=True)  8.76 us
    pallas_call x1, Pallas kernels, stats(): pl.pallas_call(stats_kernel, grid=(width // WIDE,), out_shape=(jax.ShapeD...  8.6 us
  transfers between devices with their start and end apart: 23, of which 11 were waited for; matrix products, arithmetic and copies ran while one was open for 13% of the time, Pallas kernels for 15%

profile of v9, /device:TPU:8, one launch (start us, length us, event | category | flops | bytes accessed | tf_op | source)
XLA Modules:
  0.0 223.5 jit_solution(8430530197103863294)
XLA Ops:
  7.2 0.7 all-gather.2.cloned.1.call-update
  8.0 0.8 maximum_maximum_fusion
  8.8 1.7 copy-done.2
  10.5 0.7 copy-done.3
  11.2 1.2 pack.1._
  12.4 2.2 copy-done.1
  14.7 2.0 collective-permute-start.1
  16.7 7.4 %all-to-all-start = ((bf16[16,96,1536]{2,1,0:T(8,128)(2,1)}), bf16[16,96,1536]{2,1,0:T(8,128)(2,1)}, u32[]{:S(2)}, u32[]{:S(2)}) async-start(bf16[16,96,1536]{2,1,0:T(8,128)(2,1)} %copy-done.1), calls=%async_computation | async-start | bytes 9437184 | tf_op jit(solution)/shard_map/all_to_all | solution.py:454
  24.1 0.6 reduce
  24.8 5.5 %collective-permute-start.2 = (bf16[2,2,48,96]{3,2,1,0:T(8,128)(2,1)S(1)}, bf16[2,2,48,96]{3,2,1,0:T(8,128)(2,1)S(1)}, u32[]{:S(2)}, u32[]{:S(2)}) collective-permute-start(bf16[2,2,48,96]{3,2,1,0:T(8,128)(2,1)S(1)} %pad_maximum_fusion.3), channel_id=1, source_target_pairs={{0,12},{1,13},{2,14},{3,15},{4,0},{5,1},{6,2},{7,3},{8,4},{9,5},{1... | collective-permute-start | bytes 110600 | tf_op jit(solution)/shard_map/ppermute | solution.py:431
  30.3 1.4 collective-permute-start.3
  31.7 2.4 %collective-permute-start.4 = (bf16[2,2,48,96]{3,2,1,0:T(8,128)(2,1)S(1)}, bf16[2,2,48,96]{3,2,1,0:T(8,128)(2,1)S(1)}, u32[]{:S(2)}, u32[]{:S(2)}) collective-permute-start(bf16[2,2,48,96]{3,2,1,0:T(8,128)(2,1)S(1)} %pad_maximum_fusion.3), channel_id=1, source_target_pairs={{0,4},{1,5},{2,6},{3,7},{4,8},{5,9},{6,10},{7,11},{8,12},{9,13},{1... | collective-permute-start | bytes 110600 | tf_op jit(solution)/shard_map/ppermute | solution.py:431
  34.1 1.5 places.1
  35.7 4.8 %collective-permute-done.3 = bf16[2,2,48,96]{3,2,1,0:T(8,128)(2,1)S(1)} collective-permute-done((bf16[2,2,48,96]{3,2,1,0:T(8,128)(2,1)S(1)}, bf16[2,2,48,96]{3,2,1,0:T(8,128)(2,1)S(1)}, u32[]{:S(2)}, u32[]{:S(2)}) %collective-permute-start.3) | collective-permute-done | bytes 36896 | tf_op jit(solution)/shard_map/ppermute | solution.py:431
  40.9 0.8 slice.61.kern_ref
  41.7 8.6 %stats.1 = (f32[2,1536]{1,0:T(2,128)}, f32[32,1536]{1,0:T(8,128)}) custom-call(s32[4]{0:T(128)} %get-tuple-element.29.bounds_ref, bf16[768,1536]{1,0:T(8,128)(2,1)} %bitcast.64, f32[32,1536]{1,0:T(8,128)} %slice.61.kern_ref, bf16[16,96,1536]{2,1,0:T(8,128)(2,1)} %copy-done.1), custom_call_target="tpu_custom_call" | custom-call | flops 16499999744 | bytes 1000000 | tf_op jit(solution)/shard_map/stats/pallas_call | solution.py:218
  50.3 2.6 %collective-permute-start.5 = (f32[2,1536]{1,0:T(2,128)}, f32[2,1536]{1,0:T(2,128)S(1)}, u32[]{:S(2)}, u32[]{:S(2)}) collective-permute-start(f32[2,1536]{1,0:T(2,128)} %get-tuple-element.31), channel_id=1, source_target_pairs={{0,1},{1,0},{2,3},{3,2},{4,5},{5,4},{6,7},{7,6},{8,9},{9,8},{10,11... | collective-permute-start | bytes 36872 | tf_op jit(solution)/shard_map/ppermute | solution.py:421
  52.9 1.0 collective-permute-done.5
  53.9 0.7 add.110
  54.7 3.1 %collective-permute-start.6 = (f32[2,1536]{1,0:T(2,128)S(1)}, f32[2,1536]{1,0:T(2,128)S(1)}, u32[]{:S(2)}, u32[]{:S(2)}) collective-permute-start(f32[2,1536]{1,0:T(2,128)S(1)} %add.110), channel_id=1, source_target_pairs={{0,2},{1,3},{2,0},{3,1},{4,6},{5,7},{6,4},{7,5},{8,10},{9,11},{10,... | collective-permute-start | bytes 36872 | tf_op jit(solution)/shard_map/ppermute | solution.py:421
  57.7 1.7 collective-permute-done.6
  59.4 2.8 %collective-permute-start.7 = (f32[2,1536]{1,0:T(2,128)S(1)}, f32[2,1536]{1,0:T(2,128)S(1)}, u32[]{:S(2)}, u32[]{:S(2)}) collective-permute-start(f32[2,1536]{1,0:T(2,128)S(1)} %add.111), channel_id=1, source_target_pairs={{0,4},{1,5},{2,6},{3,7},{4,8},{5,9},{6,10},{7,11},{8,12},{9,13},{1... | collective-permute-start | bytes 36872 | tf_op jit(solution)/shard_map/ppermute | solution.py:421
  62.2 7.0 %collective-permute-start.8 = (f32[2,1536]{1,0:T(2,128)S(1)}, f32[2,1536]{1,0:T(2,128)S(1)}, u32[]{:S(2)}, u32[]{:S(2)}) collective-permute-start(f32[2,1536]{1,0:T(2,128)S(1)} %add.111), channel_id=1, source_target_pairs={{0,8},{1,9},{2,10},{3,11},{4,12},{5,13},{6,14},{7,15},{8,0},{9,1},... | collective-permute-start | bytes 36872 | tf_op jit(solution)/shard_map/ppermute | solution.py:421
  69.2 1.9 collective-permute-done.8
  71.1 2.7 %collective-permute-done.9 = f32[2,1536]{1,0:T(2,128)S(1)} collective-permute-done((f32[2,1536]{1,0:T(2,128)S(1)}, f32[2,1536]{1,0:T(2,128)S(1)}, u32[]{:S(2)}, u32[]{:S(2)}) %collective-permute-start.9) | collective-permute-done | bytes 12320 | tf_op jit(solution)/shard_map/ppermute | solution.py:421
  73.9 2.4 %collective-permute-start.11 = (f32[3,1536]{1,0:T(4,128)S(1)}, f32[3,1536]{1,0:T(4,128)S(1)}, u32[]{:S(2)}, u32[]{:S(2)}) collective-permute-start(f32[3,1536]{1,0:T(4,128)S(1)} %pad_maximum_fusion.5), channel_id=1, source_target_pairs={{0,32},{16,48},{32,0},{48,16},{64,96},{80,112},{96,64},{112,80},{1... | collective-permute-start | bytes 55304 | tf_op jit(solution)/shard_map/ppermute | solution.py:421
  76.3 1.9 collective-permute-start.12
  78.2 2.7 %fusion.18 = bf16[512,768]{1,0:T(8,128)(2,1)} fusion(bf16[512,1536]{1,0:T(8,128)(2,1)S(1)} %bitcast.63, s32[768]{0:T(1024)S(1)} %get-tuple-element.73, s32[768]{0:T(1024)S(1)} %get-tuple-element.74, pred[768]{0:T(1024)(128)(4,1)S(1)} %fusion.27, pred[]{:T(512)S(6)} %eq.85), kind=kOutput, calls=%fused_computation.21 | convolution fusion | flops 1216610304 | bytes 2366209 | tf_op jit(solution)/shard_map/dot_general | solution.py:475
  80.8 1.8 fusion.21
  82.6 6.6 %fusion.35.rest_0_.wide_back = f32[512,1536]{1,0:T(8,128)} fusion(bf16[512,1536]{1,0:T(8,128)(2,1)S(1)} %bitcast.62, bf16[1536,1536]{1,0:T(8,128)(2,1)} %all-gather.2.cloned.1.call-done), kind=kOutput, calls=%fused_computation.71 | convolution fusion | flops 2415919104 | bytes 9437184 | tf_op jit(solution)/shard_map/dot_general | solution.py:477
  89.2 1.5 collective-permute-start.13
  90.8 0.7 collective-permute-start.14
  91.5 2.1 collective-permute-start.15
  93.8 0.6 collective-permute-done.13
  94.4 1.8 collective-permute-done.14
  96.2 0.6 fusion.29.info_ref
  96.8 0.6 pad_maximum_fusion.6.norm_ref
  97.4 0.9 copy-done.4
  98.3 14.3 %hidden.1 = (f32[12,512,128]{2,1,0:T(8,128)}, bf16[512,1536]{1,0:T(8,128)(2,1)}) custom-call(s32[80]{0:T(128)} %fusion.29.info_ref, bf16[16,96,1536]{2,1,0:T(8,128)(2,1)} %all-to-all-done.got_ref, f32[32,1536]{1,0:T(8,128)} %slice.61.kern_ref, f32[4,1536]{1,0:T(4,128)} %pad_maximum_fusion.6.norm_ref, f32[512,1536]{1,0:T(8,128)} %fusion.35.rest_0_.wide_back, ...), custom_call_target="tpu_custom_call" | custom-call | flops 17600000000 | bytes 1000000 | tf_op jit(solution)/shard_map/hidden/pallas_call | solution.py:303
  112.6 3.1 %fusion.36 = f32[1536,768]{1,0:T(8,128)S(1)} fusion(bf16[512,1536]{1,0:T(8,128)(2,1)} %get-tuple-element.46, bf16[512,768]{1,0:T(8,128)(2,1)} %fusion.18), kind=kOutput, calls=%fused_computation.72 | convolution fusion | flops 1207959552 | bytes 7077888 | tf_op jit(solution)/shard_map/dot_general | solution.py:493
  115.7 0.5 collective-permute-done.17
  116.2 1.4 fusion.37
  117.6 1.9 add_convert_fusion
  119.6 8.8 %all-to-all-start.1 = ((bf16[16,96,768]{2,1,0:T(8,128)(2,1)}), bf16[16,96,768]{2,1,0:T(8,128)(2,1)}, u32[]{:S(2)}, u32[]{:S(2)}) async-start(bf16[16,96,768]{2,1,0:T(8,128)(2,1)} %bitcast.68), calls=%async_computation.1 | async-start | bytes 4718592 | tf_op jit(solution)/shard_map/all_to_all | solution.py:497
  128.3 22.3 %terms.1 = f32[72,1536]{1,0:T(8,128)} custom-call(s32[80]{0:T(128)} %fusion.29.info_ref, bf16[16,96,1536]{2,1,0:T(8,128)(2,1)} %all-to-all-done.got_ref, f32[12,512,128]{2,1,0:T(8,128)} %get-tuple-element.50.h_ref, f32[512,1536]{1,0:T(8,128)} %fusion.35.rest_0_.wide_back, f32[4,1536]{1,0:T(4,128)} %pad_maximum_fusion.6.norm_ref), custom_call_target="tpu_custom_call" | custom-call | flops 27499999232 | bytes 1000000 | tf_op jit(solution)/shard_map/terms/pallas_call | solution.py:384
  150.6 1.1 pad_maximum_fusion
  151.7 0.3 copy.14
  152.1 1.7 collective-permute-done.18
  153.8 0.2 copy.16
  154.0 0.3 reshape.48
  154.3 6.7 %all-to-all-done.1 = bf16[16,96,768]{2,1,0:T(8,128)(2,1)} async-done(((bf16[16,96,768]{2,1,0:T(8,128)(2,1)}), bf16[16,96,768]{2,1,0:T(8,128)(2,1)}, u32[]{:S(2)}, u32[]{:S(2)}) %all-to-all-start.1) | async-done | bytes 2359328 | tf_op jit(solution)/shard_map/all_to_all | solution.py:497
  161.0 2.0 convert_reduce_fusion
  163.0 0.2 reshape.49
  163.3 0.2 reshape.50
  163.6 25.4 %all_to_all.20 = f32[8,150,128]{2,1,0:T(8,128)S(1)} all-to-all(f32[8,150,128]{2,1,0:T(8,128)S(1)} %pad_maximum_fusion.1), channel_id=1, replica_groups={{0,2,4,6,8,10,12,14},{1,3,5,7,9,11,13,15},{16,18,20,22,24,26,28,30},{17..., dimensions={0} | all-to-all | bytes 1228800 | tf_op jit(solution)/shard_map/all_to_all | solution.py:516
  189.1 1.2 broadcast_in_dim.8
  190.2 8.1 %all-to-all-start.3 = ((f32[16,150,128]{2,1,0:T(8,128)}), f32[16,150,128]{2,1,0:T(8,128)S(1)}, u32[]{:S(2)}, u32[]{:S(2)}) async-start(f32[16,150,128]{2,1,0:T(8,128)} %broadcast_in_dim.8), calls=%async_computation.3 | async-start | bytes 2490368 | tf_op jit(solution)/shard_map/all_to_all | solution.py:525
  198.3 0.8 constant_dynamic-slice_fusion
  199.1 6.6 %fusion.5 = bf16[1,1,512,1536]{3,2,1,0:T(8,128)(2,1)} fusion(bf16[512,1536]{1,0:T(8,128)(2,1)} %get-tuple-element.46, bf16[1536,1536]{1,0:T(8,128)(2,1)} %all-gather.2.cloned.1.call-done), kind=kOutput, calls=%fused_computation.10 | convolution fusion | flops 2416705536 | bytes 7864320 | tf_op jit(solution)/shard_map/dot_general | solution.py:500
  205.7 8.1 %all-to-all-done.3 = f32[16,150,128]{2,1,0:T(8,128)S(1)} async-done(((f32[16,150,128]{2,1,0:T(8,128)}), f32[16,150,128]{2,1,0:T(8,128)S(1)}, u32[]{:S(2)}, u32[]{:S(2)}) %all-to-all-start.3) | async-done | bytes 1228832 | tf_op jit(solution)/shard_map/all_to_all | solution.py:525
  213.9 0.6 stack.54
  214.8 0.2 reshape.51
  215.0 1.1 copy.18
  216.1 0.6 subtract_multiply_fusion
  (73 shorter events, 1.8 us)
Async XLA Ops:
  7.2 66.6 %copy-start = (bf16[1,1,512,1536]{3,2,1,0:T(8,128)(2,1)S(1)}, bf16[1,1,512,1536]{3,2,1,0:T(8,128)(2,1)}, u32[]{:S(2)}) copy-start(bf16[1,1,512,1536]{3,2,1,0:T(8,128)(2,1)} %param.10) | copy-start | bytes 4718596
  7.2 75.4 %all-gather.2.cloned.1.call-start = ((), (), s32[]{:S(2)}) async-start(), calls=%async_computation.4 | async-start | bytes 5013504 | tf_op jit(solution)/shard_map/all_gather | solution.py:459
  8.8 5.8 %collective-permute-start = (bf16[48,96]{1,0:T(8,128)(2,1)S(1)}, bf16[48,96]{1,0:T(8,128)(2,1)S(1)}, u32[]{:S(2)}, u32[]{:S(2)}) collective-permute-start(bf16[48,96]{1,0:T(8,128)(2,1)S(1)} %maximum_maximum_fusion), channel_id=1, source_target_pairs={{0,1},{1,0},{2,3},{3,2},{4,5},{5,4},{6,7},{7,6},{8,9},{9,8},{10,11... | collective-permute-start | bytes 27656 | tf_op jit(solution)/shard_map/ppermute | solution.py:428
  8.8 1.7 copy-start.2
  10.5 0.7 copy-start.3
  11.2 3.5 %copy-start.7 = (bf16[32,96]{1,0:T(8,128)(2,1)S(1)}, bf16[32,96]{1,0:T(8,128)(2,1)}, u32[]{:S(2)}) copy-start(bf16[32,96]{1,0:T(8,128)(2,1)} %param.12) | copy-start | bytes 18436
  11.2 3.5 %copy-start.10 = (bf16[2,96]{1,0:T(2,128)(2,1)S(1)}, bf16[2,96]{1,0:T(2,128)(2,1)}, u32[]{:S(2)}) copy-start(bf16[2,96]{1,0:T(2,128)(2,1)} %param.13) | copy-start | bytes 1156
  12.4 2.2 copy-start.1
  14.7 9.4 %copy-start.9 = (s32[1,1,768]{2,1,0:T(1,128)S(1)}, s32[1,1,768]{2,1,0:T(1,128)}, u32[]{:S(2)}) copy-start(s32[1,1,768]{2,1,0:T(1,128)} %param.8) | copy-start | bytes 9220
  14.7 10.0 %collective-permute-start.1 = (bf16[2,48,96]{2,1,0:T(8,128)(2,1)S(1)}, bf16[2,48,96]{2,1,0:T(8,128)(2,1)S(1)}, u32[]{:S(2)}, u32[]{:S(2)}) collective-permute-start(bf16[2,48,96]{2,1,0:T(8,128)(2,1)S(1)} %pad_maximum_fusion.4), channel_id=1, source_target_pairs={{0,2},{1,3},{2,0},{3,1},{4,6},{5,7},{6,4},{7,5},{8,10},{9,11},{10,... | collective-permute-start | bytes 55304 | tf_op jit(solution)/shard_map/ppermute | solution.py:428
  16.7 80.7 %all-to-all-start = ((bf16[16,96,1536]{2,1,0:T(8,128)(2,1)}), bf16[16,96,1536]{2,1,0:T(8,128)(2,1)}, u32[]{:S(2)}, u32[]{:S(2)}) async-start(bf16[16,96,1536]{2,1,0:T(8,128)(2,1)} %copy-done.1), calls=%async_computation | async-start | bytes 9437184 | tf_op jit(solution)/shard_map/all_to_all | solution.py:454
  24.8 10.9 %collective-permute-start.2 = (bf16[2,2,48,96]{3,2,1,0:T(8,128)(2,1)S(1)}, bf16[2,2,48,96]{3,2,1,0:T(8,128)(2,1)S(1)}, u32[]{:S(2)}, u32[]{:S(2)}) collective-permute-start(bf16[2,2,48,96]{3,2,1,0:T(8,128)(2,1)S(1)} %pad_maximum_fusion.3), channel_id=1, source_target_pairs={{0,12},{1,13},{2,14},{3,15},{4,0},{5,1},{6,2},{7,3},{8,4},{9,5},{1... | collective-permute-start | bytes 110600 | tf_op jit(solution)/shard_map/ppermute | solution.py:431
  30.3 10.3 %collective-permute-start.3 = (bf16[2,2,48,96]{3,2,1,0:T(8,128)(2,1)S(1)}, bf16[2,2,48,96]{3,2,1,0:T(8,128)(2,1)S(1)}, u32[]{:S(2)}, u32[]{:S(2)}) collective-permute-start(bf16[2,2,48,96]{3,2,1,0:T(8,128)(2,1)S(1)} %pad_maximum_fusion.3), channel_id=1, source_target_pairs={{0,8},{1,9},{2,10},{3,11},{4,12},{5,13},{6,14},{7,15},{8,0},{9,1},... | collective-permute-start | bytes 110600 | tf_op jit(solution)/shard_map/ppermute | solution.py:431
  31.7 8.8 %collective-permute-start.4 = (bf16[2,2,48,96]{3,2,1,0:T(8,128)(2,1)S(1)}, bf16[2,2,48,96]{3,2,1,0:T(8,128)(2,1)S(1)}, u32[]{:S(2)}, u32[]{:S(2)}) collective-permute-start(bf16[2,2,48,96]{3,2,1,0:T(8,128)(2,1)S(1)} %pad_maximum_fusion.3), channel_id=1, source_target_pairs={{0,4},{1,5},{2,6},{3,7},{4,8},{5,9},{6,10},{7,11},{8,12},{9,13},{1... | collective-permute-start | bytes 110600 | tf_op jit(solution)/shard_map/ppermute | solution.py:431
  41.7 32.0 %copy-start.8 = (f32[1,1536]{1,0:T(1,128)S(1)}, f32[1,1536]{1,0:T(1,128)}, u32[]{:S(2)}) copy-start(f32[1,1536]{1,0:T(1,128)} %get-tuple-element.35) | copy-start | bytes 18436
  50.3 3.6 %collective-permute-start.5 = (f32[2,1536]{1,0:T(2,128)}, f32[2,1536]{1,0:T(2,128)S(1)}, u32[]{:S(2)}, u32[]{:S(2)}) collective-permute-start(f32[2,1536]{1,0:T(2,128)} %get-tuple-element.31), channel_id=1, source_target_pairs={{0,1},{1,0},{2,3},{3,2},{4,5},{5,4},{6,7},{7,6},{8,9},{9,8},{10,11... | collective-permute-start | bytes 36872 | tf_op jit(solution)/shard_map/ppermute | solution.py:421
  54.7 4.7 %collective-permute-start.6 = (f32[2,1536]{1,0:T(2,128)S(1)}, f32[2,1536]{1,0:T(2,128)S(1)}, u32[]{:S(2)}, u32[]{:S(2)}) collective-permute-start(f32[2,1536]{1,0:T(2,128)S(1)} %add.110), channel_id=1, source_target_pairs={{0,2},{1,3},{2,0},{3,1},{4,6},{5,7},{6,4},{7,5},{8,10},{9,11},{10,... | collective-permute-start | bytes 36872 | tf_op jit(solution)/shard_map/ppermute | solution.py:421
  59.4 9.8 %collective-permute-start.7 = (f32[2,1536]{1,0:T(2,128)S(1)}, f32[2,1536]{1,0:T(2,128)S(1)}, u32[]{:S(2)}, u32[]{:S(2)}) collective-permute-start(f32[2,1536]{1,0:T(2,128)S(1)} %add.111), channel_id=1, source_target_pairs={{0,4},{1,5},{2,6},{3,7},{4,8},{5,9},{6,10},{7,11},{8,12},{9,13},{1... | collective-permute-start | bytes 36872 | tf_op jit(solution)/shard_map/ppermute | solution.py:421
  62.2 8.9 %collective-permute-start.8 = (f32[2,1536]{1,0:T(2,128)S(1)}, f32[2,1536]{1,0:T(2,128)S(1)}, u32[]{:S(2)}, u32[]{:S(2)}) collective-permute-start(f32[2,1536]{1,0:T(2,128)S(1)} %add.111), channel_id=1, source_target_pairs={{0,8},{1,9},{2,10},{3,11},{4,12},{5,13},{6,14},{7,15},{8,0},{9,1},... | collective-permute-start | bytes 36872 | tf_op jit(solution)/shard_map/ppermute | solution.py:421
  69.1 4.6 %collective-permute-start.9 = (f32[2,1536]{1,0:T(2,128)S(1)}, f32[2,1536]{1,0:T(2,128)S(1)}, u32[]{:S(2)}, u32[]{:S(2)}) collective-permute-start(f32[2,1536]{1,0:T(2,128)S(1)} %add.111), channel_id=1, source_target_pairs={{0,12},{1,13},{2,14},{3,15},{4,0},{5,1},{6,2},{7,3},{8,4},{9,5},{1... | collective-permute-start | bytes 36872 | tf_op jit(solution)/shard_map/ppermute | solution.py:421
  73.8 15.4 %collective-permute-start.10 = (f32[3,1536]{1,0:T(4,128)S(1)}, f32[3,1536]{1,0:T(4,128)S(1)}, u32[]{:S(2)}, u32[]{:S(2)}) collective-permute-start(f32[3,1536]{1,0:T(4,128)S(1)} %pad_maximum_fusion.5), channel_id=1, source_target_pairs={{0,16},{16,32},{32,48},{48,0},{64,80},{80,96},{96,112},{112,64},{1... | collective-permute-start | bytes 55304 | tf_op jit(solution)/shard_map/ppermute | solution.py:421
  73.9 15.3 %collective-permute-start.11 = (f32[3,1536]{1,0:T(4,128)S(1)}, f32[3,1536]{1,0:T(4,128)S(1)}, u32[]{:S(2)}, u32[]{:S(2)}) collective-permute-start(f32[3,1536]{1,0:T(4,128)S(1)} %pad_maximum_fusion.5), channel_id=1, source_target_pairs={{0,32},{16,48},{32,0},{48,16},{64,96},{80,112},{96,64},{112,80},{1... | collective-permute-start | bytes 55304 | tf_op jit(solution)/shard_map/ppermute | solution.py:421
  76.3 12.9 %collective-permute-start.12 = (f32[3,1536]{1,0:T(4,128)S(1)}, f32[3,1536]{1,0:T(4,128)S(1)}, u32[]{:S(2)}, u32[]{:S(2)}) collective-permute-start(f32[3,1536]{1,0:T(4,128)S(1)} %pad_maximum_fusion.5), channel_id=1, source_target_pairs={{0,48},{16,0},{32,16},{48,32},{64,112},{80,64},{96,80},{112,96},{1... | collective-permute-start | bytes 55304 | tf_op jit(solution)/shard_map/ppermute | solution.py:421
  89.2 5.1 %collective-permute-start.13 = (f32[3,1536]{1,0:T(4,128)S(1)}, f32[3,1536]{1,0:T(4,128)S(1)}, u32[]{:S(2)}, u32[]{:S(2)}) collective-permute-start(f32[3,1536]{1,0:T(4,128)S(1)} %add_add_fusion.1), channel_id=1, source_target_pairs={{0,64},{16,80},{32,96},{48,112},{64,128},{80,144},{96,160},{112,17... | collective-permute-start | bytes 55304 | tf_op jit(solution)/shard_map/ppermute | solution.py:421
  90.8 5.3 %collective-permute-start.14 = (f32[3,1536]{1,0:T(4,128)S(1)}, f32[3,1536]{1,0:T(4,128)S(1)}, u32[]{:S(2)}, u32[]{:S(2)}) collective-permute-start(f32[3,1536]{1,0:T(4,128)S(1)} %add_add_fusion.1), channel_id=1, source_target_pairs={{0,128},{16,144},{32,160},{48,176},{64,192},{80,208},{96,224},{112... | collective-permute-start | bytes 55304 | tf_op jit(solution)/shard_map/ppermute | solution.py:421
  91.5 4.6 %collective-permute-start.15 = (f32[3,1536]{1,0:T(4,128)S(1)}, f32[3,1536]{1,0:T(4,128)S(1)}, u32[]{:S(2)}, u32[]{:S(2)}) collective-permute-start(f32[3,1536]{1,0:T(4,128)S(1)} %add_add_fusion.1), channel_id=1, source_target_pairs={{0,192},{16,208},{32,224},{48,240},{64,0},{80,16},{96,32},{112,48}... | collective-permute-start | bytes 55304 | tf_op jit(solution)/shard_map/ppermute | solution.py:421
  93.7 3.7 %collective-permute-start.16 = (bf16[512,768]{1,0:T(8,128)(2,1)S(1)}, bf16[512,768]{1,0:T(8,128)(2,1)S(1)}, u32[]{:S(2)}, u32[]{:S(2)}) collective-permute-start(bf16[512,768]{1,0:T(8,128)(2,1)S(1)} %fusion.21), channel_id=1, source_target_pairs={{0,1},{1,0},{2,3},{3,2},{4,5},{5,4},{6,7},{7,6},{8,9},{9,8},{10,11... | collective-permute-start | bytes 2359304 | tf_op jit(solution)/shard_map/ppermute | solution.py:481
  97.4 0.9 copy-start.4
  112.6 3.6 %collective-permute-start.17 = (bf16[512,1536]{1,0:T(8,128)(2,1)}, bf16[512,1536]{1,0:T(8,128)(2,1)S(1)}, u32[]{:S(2)}, u32[]{:S(2)}) collective-permute-start(bf16[512,1536]{1,0:T(8,128)(2,1)} %get-tuple-element.46), channel_id=1, source_target_pairs={{0,1},{1,0},{2,3},{3,2},{4,5},{5,4},{6,7},{7,6},{8,9},{9,8},{10,11... | collective-permute-start | bytes 4718600 | tf_op jit(solution)/shard_map/ppermute | solution.py:491
  112.6 3.6 %copy-start.5 = (bf16[512,768]{1,0:T(8,128)(2,1)S(1)}, bf16[512,768]{1,0:T(8,128)(2,1)}, u32[]{:S(2)}) copy-start(bf16[512,768]{1,0:T(8,128)(2,1)} %copy-done.4) | copy-start | bytes 2359300
  119.6 41.5 %all-to-all-start.1 = ((bf16[16,96,768]{2,1,0:T(8,128)(2,1)}), bf16[16,96,768]{2,1,0:T(8,128)(2,1)}, u32[]{:S(2)}, u32[]{:S(2)}) async-start(bf16[16,96,768]{2,1,0:T(8,128)(2,1)} %bitcast.68), calls=%async_computation.1 | async-start | bytes 4718592 | tf_op jit(solution)/shard_map/all_to_all | solution.py:497
  128.3 22.3 %copy-start.6 = (f32[32,1536]{1,0:T(8,128)S(1)}, f32[32,1536]{1,0:T(8,128)}, u32[]{:S(2)}) copy-start(f32[32,1536]{1,0:T(8,128)} %get-tuple-element.51) | copy-start | bytes 589828
  152.0 1.8 collective-permute-start.18
  190.2 23.6 %all-to-all-start.3 = ((f32[16,150,128]{2,1,0:T(8,128)}), f32[16,150,128]{2,1,0:T(8,128)S(1)}, u32[]{:S(2)}, u32[]{:S(2)}) async-start(f32[16,150,128]{2,1,0:T(8,128)} %broadcast_in_dim.8), calls=%async_computation.3 | async-start | bytes 2490368 | tf_op jit(solution)/shard_map/all_to_all | solution.py:525
Sparse Core Ops, SparseCore 0:
  9.8 49.7 all-gather.1
